TPU v7x, 32 devices: a whole 2x2x4 slice. The times are simulated.
32 devices in a mesh: batch: 2 (over x), seq: 16 (over z, y, core).
Axes of the slice: x: 2, y: 2, z: 4, core: 2. Of those that a mesh axis runs over, the one named last changes fastest.
Arguments:
- tokens: bfloat16 [2, 8192, 1152], P('batch', 'seq'), may hold values from -6 to 6
- cotangent: bfloat16 [2, 8192, 1152], P('batch', 'seq'), may hold values from -6 to 6
- doc_ids: int32 [2, 8192], P('batch'), may hold values from 0 to 7, never falling along the last dimension, each value on 1 to 2048 neighbouring positions
- w_query: bfloat16 [1152, 1024], P(('batch', 'seq')), may hold values from -0.1875 to 0.1875
- w_key: bfloat16 [1152, 256], P(('batch', 'seq')), may hold values from -0.1875 to 0.1875
- w_value: bfloat16 [1152, 256], P(('batch', 'seq')), may hold values from -0.1875 to 0.1875
- w_out: bfloat16 [1024, 1152], P(('batch', 'seq')), may hold values from -0.1875 to 0.1875
- w_gate: bfloat16 [1152, 6912], P(('batch', 'seq')), may hold values from -0.1875 to 0.1875
- w_up: bfloat16 [1152, 6912], P(('batch', 'seq')), may hold values from -0.1875 to 0.1875
- w_down: bfloat16 [6912, 1152], P(('batch', 'seq')), may hold values from -0.078125 to 0.078125
- gain_attn_in: bfloat16 [1152], P(('batch', 'seq')), may hold values from 0.25 to 1.75
- gain_attn_out: bfloat16 [1152], P(('batch', 'seq')), may hold values from 0.25 to 1.75
- gain_mlp_in: bfloat16 [1152], P(('batch', 'seq')), may hold values from 0.25 to 1.75
- gain_mlp_out: bfloat16 [1152], P(('batch', 'seq')), may hold values from 0.25 to 1.75
- gain_query: bfloat16 [256], P(('batch', 'seq')), may hold values from 0.25 to 1.75
- gain_key: bfloat16 [256], P(('batch', 'seq')), may hold values from 0.25 to 1.75
Outputs:
- layer_out: bfloat16 [2, 8192, 1152], P('batch', 'seq')
- grad_tokens: bfloat16 [2, 8192, 1152], P('batch', 'seq')
- grad_w_query: float32 [1152, 1024], P(('batch', 'seq'))
- grad_w_key: float32 [1152, 256], P(('batch', 'seq'))
- grad_w_value: float32 [1152, 256], P(('batch', 'seq'))
- grad_w_out: float32 [1024, 1152], P(('batch', 'seq'))
- grad_w_gate: float32 [1152, 6912], P(('batch', 'seq'))
- grad_w_up: float32 [1152, 6912], P(('batch', 'seq'))
- grad_w_down: float32 [6912, 1152], P(('batch', 'seq'))
- grad_gain_attn_in: float32 [1152], P(('batch', 'seq'))
- grad_gain_attn_out: float32 [1152], P(('batch', 'seq'))
- grad_gain_mlp_in: float32 [1152], P(('batch', 'seq'))
- grad_gain_mlp_out: float32 [1152], P(('batch', 'seq'))
- grad_gain_query: float32 [256], P(('batch', 'seq'))
- grad_gain_key: float32 [256], P(('batch', 'seq'))
Inputs may be any that keep to these rules, and one draw needn't show every extreme that they name: `doc_ids`: within each sequence the ids never fall; each of the 8 documents holds 1 to 2048 tokens, and one holds exactly 2048.
All inputs are finite; a program needn't handle non-finite values.
Results may differ from a plain program's by a relative error of at most 0.018.
Values may be sent and summed in bfloat16 or wider, within the bound.
No kernel may reach another device: no remote copies, remote signals or barrier semaphores. Data moves between devices by JAX's collectives and lax.ppermute only.
A program may use at most 384 MiB of HBM per device.

v0:
```python
import jax
import jax.numpy as jnp
from jax import lax
from jax.sharding import PartitionSpec as P

HEAD = 256
WINDOW = 512


EPSILON = 1e-06
ROPE_BASE = 10000.0


def passed_along(array, axis, by):
    size = lax.axis_size(axis)
    pairs = [(i, i + by) for i in range(size) if 0 <= i + by < size]
    return lax.ppermute(array, axis, pairs)


def norm_gain(values, gain_vec):
    return (
        values * lax.rsqrt(jnp.mean(values * values, axis=-1, keepdims=True) + EPSILON) * gain_vec
    )


def rotate(values, cosine_table, sine_table):
    half_size = values.shape[-1] // 2
    turned = jnp.concatenate([-values[..., half_size:], values[..., :half_size]], axis=-1)
    return values * cosine_table + turned * sine_table


def rope_tables(first_row, row_count, head_size):
    places = (first_row + jnp.arange(row_count, dtype=jnp.int32)).astype(jnp.float32)
    frequency = ROPE_BASE ** (-(jnp.arange(head_size // 2, dtype=jnp.float32) * 2.0) / head_size)
    angles = places[:, None] * frequency[None, :]
    angles = jnp.concatenate([angles, angles], axis=-1)
    return (jnp.cos(angles), jnp.sin(angles))


def prepare_query(raw_value, gain_vec, cosine_table, sine_table):
    split_heads = raw_value.reshape(raw_value.shape[0], -1, gain_vec.shape[0])
    return rotate(
        norm_gain(split_heads, gain_vec), cosine_table[:, None, :], sine_table[:, None, :]
    )


def prepare_key(raw_value, gain_vec, cosine_table, sine_table):
    return rotate(norm_gain(raw_value, gain_vec), cosine_table, sine_table)


def gated_unit(gate_raw, up_raw):
    return jax.nn.gelu(gate_raw, approximate=True) * up_raw


def matmul(left_side, right_side):
    return jnp.dot(left_side, right_side, preferred_element_type=jnp.float32)


def over_rows(left_side, right_side):
    return lax.dot_general(
        left_side, right_side, (((0,), (0,)), ((), ())), preferred_element_type=jnp.float32
    )


def by_transpose(left_side, right_side):
    return lax.dot_general(
        left_side, right_side, (((1,), (1,)), ((), ())), preferred_element_type=jnp.float32
    )


def block_mask(query_ids, key_ids, window_rows):
    query_place = window_rows + jnp.arange(window_rows, dtype=jnp.int32)
    key_place = jnp.arange(2 * window_rows, dtype=jnp.int32)
    distance = query_place[:, None] - key_place[None, :]
    same_doc = query_ids[:, None] == key_ids[None, :]
    return (distance >= 0) & (distance < window_rows) & same_doc


def block_parts(block_start, window_rows, queries, key_pad, value_pad, ids_pad):
    query_part = lax.dynamic_slice_in_dim(queries, block_start, window_rows, 0)
    key_part = lax.dynamic_slice_in_dim(key_pad, block_start, 2 * window_rows, 0)
    value_part = lax.dynamic_slice_in_dim(value_pad, block_start, 2 * window_rows, 0)
    query_ids = lax.dynamic_slice_in_dim(ids_pad, block_start + window_rows, window_rows, 0)
    return (query_part, key_part, value_part, block_mask(query_ids, ids_pad, window_rows))


def attend_forward(queries, key_pad, value_pad, ids_pad, window_rows, attn_scale):
    row_count, head_count, head_size = queries.shape

    def one_block(block_index):
        query_part, key_part, value_part, allowed = block_parts(
            block_index * window_rows, window_rows, queries, key_pad, value_pad, ids_pad
        )
        scores = (
            jnp.einsum("qhd,kd->hqk", query_part, key_part, preferred_element_type=jnp.float32)
            * attn_scale
        )
        scores = jnp.where(allowed[None], scores, -1e30)
        row_max = jnp.max(scores, axis=-1, keepdims=True)
        weights = jnp.exp(scores - row_max)
        row_total = jnp.sum(weights, axis=-1, keepdims=True)
        probabilities = (weights / row_total).astype(jnp.bfloat16)
        attended = jnp.einsum(
            "hqk,kd->qhd", probabilities, value_part, preferred_element_type=jnp.float32
        )
        return (attended, (row_max + jnp.log(row_total))[..., 0])

    attended, log_total = lax.map(one_block, jnp.arange(row_count // window_rows, dtype=jnp.int32))
    return (attended.reshape(row_count, head_count * head_size), log_total)


def attend_backward(
    queries, key_pad, value_pad, ids_pad, log_total, grad_attended, window_rows, attn_scale
):
    row_count, head_count, head_size = queries.shape
    grad_heads = grad_attended.reshape(row_count, head_count, head_size)

    def one_block(carried, block_item):
        key_grad, value_grad = carried
        block_index, block_total = block_item
        block_start = block_index * window_rows
        query_part, key_part, value_part, allowed = block_parts(
            block_start, window_rows, queries, key_pad, value_pad, ids_pad
        )
        grad_part = lax.dynamic_slice_in_dim(grad_heads, block_start, window_rows, 0)
        scores = (
            jnp.einsum("qhd,kd->hqk", query_part, key_part, preferred_element_type=jnp.float32)
            * attn_scale
        )
        probabilities = jnp.where(allowed[None], jnp.exp(scores - block_total[..., None]), 0.0)
        grad_prob = jnp.einsum(
            "qhd,kd->hqk", grad_part, value_part, preferred_element_type=jnp.float32
        )
        inner_sum = jnp.sum(probabilities * grad_prob, axis=-1, keepdims=True)
        grad_score = (probabilities * (grad_prob - inner_sum)).astype(jnp.bfloat16)
        grad_query = (
            jnp.einsum("hqk,kd->qhd", grad_score, key_part, preferred_element_type=jnp.float32)
            * attn_scale
        )
        grad_key = (
            jnp.einsum("hqk,qhd->kd", grad_score, query_part, preferred_element_type=jnp.float32)
            * attn_scale
        )
        grad_value = jnp.einsum(
            "hqk,qhd->kd",
            probabilities.astype(jnp.bfloat16),
            grad_part,
            preferred_element_type=jnp.float32,
        )
        key_grad = lax.dynamic_update_slice_in_dim(
            key_grad,
            lax.dynamic_slice_in_dim(key_grad, block_start, 2 * window_rows, 0) + grad_key,
            block_start,
            0,
        )
        value_grad = lax.dynamic_update_slice_in_dim(
            value_grad,
            lax.dynamic_slice_in_dim(value_grad, block_start, 2 * window_rows, 0) + grad_value,
            block_start,
            0,
        )
        return ((key_grad, value_grad), grad_query)

    empty = jnp.zeros((row_count + window_rows, head_size), jnp.float32)
    block_count = row_count // window_rows
    (key_grad, value_grad), grad_query = lax.scan(
        one_block, (empty, empty), (jnp.arange(block_count, dtype=jnp.int32), log_total)
    )
    return (grad_query.reshape(row_count, head_count, head_size), key_grad, value_grad)


def forward(
    layer_in,
    attn_weights,
    mlp_weights,
    send_halo,
    ids_pad,
    cosine_table,
    sine_table,
    window_rows,
    attn_scale,
):
    w_query, w_key, w_value, w_out, gain_attn_in, gain_attn_out, gain_query, gain_key = attn_weights
    w_gate, w_up, w_down, gain_mlp_in, gain_mlp_out = mlp_weights
    normed = norm_gain(layer_in, gain_attn_in.astype(jnp.float32)).astype(jnp.bfloat16)
    query_raw = matmul(normed, w_query)
    key_raw = matmul(normed, w_key)
    value_raw = matmul(normed, w_value)
    queries = prepare_query(
        query_raw, gain_query.astype(jnp.float32), cosine_table, sine_table
    ).astype(jnp.bfloat16)
    keys = prepare_key(key_raw, gain_key.astype(jnp.float32), cosine_table, sine_table).astype(
        jnp.bfloat16
    )
    values = value_raw.astype(jnp.bfloat16)
    halo_rows = send_halo(jnp.stack([keys, values]))
    key_pad = jnp.concatenate([halo_rows[0], keys])
    value_pad = jnp.concatenate([halo_rows[1], values])
    attended, log_total = attend_forward(
        queries, key_pad, value_pad, ids_pad, window_rows, attn_scale
    )
    attended = attended.astype(jnp.bfloat16)
    branch = matmul(attended, w_out)
    middle = layer_in + norm_gain(branch, gain_attn_out.astype(jnp.float32))
    normed_mlp = norm_gain(middle, gain_mlp_in.astype(jnp.float32)).astype(jnp.bfloat16)
    gate_raw = matmul(normed_mlp, w_gate)
    up_raw = matmul(normed_mlp, w_up)
    hidden = gated_unit(gate_raw, up_raw).astype(jnp.bfloat16)
    mixed = matmul(hidden, w_down)
    layer_out = middle + norm_gain(mixed, gain_mlp_out.astype(jnp.float32))
    return dict(
        normed=normed,
        query_raw=query_raw,
        key_raw=key_raw,
        queries=queries,
        key_pad=key_pad,
        value_pad=value_pad,
        log_total=log_total,
        attended=attended,
        branch=branch,
        middle=middle,
        normed_mlp=normed_mlp,
        gate_raw=gate_raw,
        up_raw=up_raw,
        hidden=hidden,
        mixed=mixed,
        layer_out=layer_out,
    )


def backward(
    stored,
    layer_in,
    grad_out,
    attn_weights,
    mlp_weights,
    send_back,
    ids_pad,
    cosine_table,
    sine_table,
    window_rows,
    attn_scale,
):
    w_query, w_key, w_value, w_out, gain_attn_in, gain_attn_out, gain_query, gain_key = attn_weights
    w_gate, w_up, w_down, gain_mlp_in, gain_mlp_out = mlp_weights
    _, pullback = jax.vjp(norm_gain, stored["mixed"], gain_mlp_out.astype(jnp.float32))
    grad_mixed, grad_gain_mlp_out = pullback(grad_out)
    grad_mixed = grad_mixed.astype(jnp.bfloat16)
    grad_w_down = over_rows(stored["hidden"], grad_mixed)
    grad_hidden = by_transpose(grad_mixed, w_down)
    _, pullback = jax.vjp(gated_unit, stored["gate_raw"], stored["up_raw"])
    grad_gate, grad_up = pullback(grad_hidden)
    grad_gate = grad_gate.astype(jnp.bfloat16)
    grad_up = grad_up.astype(jnp.bfloat16)
    grad_w_gate = over_rows(stored["normed_mlp"], grad_gate)
    grad_w_up = over_rows(stored["normed_mlp"], grad_up)
    grad_normed_mlp = by_transpose(grad_gate, w_gate) + by_transpose(grad_up, w_up)
    _, pullback = jax.vjp(norm_gain, stored["middle"], gain_mlp_in.astype(jnp.float32))
    grad_from_mlp, grad_gain_mlp_in = pullback(grad_normed_mlp)
    grad_middle = grad_out + grad_from_mlp
    _, pullback = jax.vjp(norm_gain, stored["branch"], gain_attn_out.astype(jnp.float32))
    grad_branch, grad_gain_attn_out = pullback(grad_middle)
    grad_branch = grad_branch.astype(jnp.bfloat16)
    grad_w_out = over_rows(stored["attended"], grad_branch)
    grad_attended = by_transpose(grad_branch, w_out).astype(jnp.bfloat16)
    grad_queries, key_grad, value_grad = attend_backward(
        stored["queries"],
        stored["key_pad"],
        stored["value_pad"],
        ids_pad,
        stored["log_total"],
        grad_attended,
        window_rows,
        attn_scale,
    )
    returned = send_back(jnp.stack([key_grad[:window_rows], value_grad[:window_rows]]))
    grad_keys = key_grad[window_rows:]
    grad_values = value_grad[window_rows:]
    grad_keys = jnp.concatenate([grad_keys[:-window_rows], grad_keys[-window_rows:] + returned[0]])
    grad_values = jnp.concatenate(
        [grad_values[:-window_rows], grad_values[-window_rows:] + returned[1]]
    )

    def key_piece(raw_value, gain_vec):
        return prepare_key(raw_value, gain_vec, cosine_table, sine_table)

    def query_piece(raw_value, gain_vec):
        return prepare_query(raw_value, gain_vec, cosine_table, sine_table)

    _, pullback = jax.vjp(key_piece, stored["key_raw"], gain_key.astype(jnp.float32))
    grad_key_raw, grad_gain_key = pullback(grad_keys)
    _, pullback = jax.vjp(query_piece, stored["query_raw"], gain_query.astype(jnp.float32))
    grad_query_raw, grad_gain_query = pullback(grad_queries)
    grad_key_raw = grad_key_raw.astype(jnp.bfloat16)
    grad_query_raw = grad_query_raw.astype(jnp.bfloat16)
    grad_value_raw = grad_values.astype(jnp.bfloat16)
    grad_w_query = over_rows(stored["normed"], grad_query_raw)
    grad_w_key = over_rows(stored["normed"], grad_key_raw)
    grad_w_value = over_rows(stored["normed"], grad_value_raw)
    grad_normed = (
        by_transpose(grad_query_raw, w_query)
        + by_transpose(grad_key_raw, w_key)
        + by_transpose(grad_value_raw, w_value)
    )
    _, pullback = jax.vjp(norm_gain, layer_in, gain_attn_in.astype(jnp.float32))
    grad_from_attn, grad_gain_attn_in = pullback(grad_normed)
    grad_in = grad_middle + grad_from_attn
    terms = (
        grad_w_query,
        grad_w_key,
        grad_w_value,
        grad_w_out,
        grad_w_gate,
        grad_w_up,
        grad_w_down,
        grad_gain_attn_in,
        grad_gain_attn_out,
        grad_gain_mlp_in,
        grad_gain_mlp_out,
        grad_gain_query,
        grad_gain_key,
    )
    return (grad_in, terms)


def reduce_group(group_terms):
    return lax.psum_scatter(group_terms, ("batch", "seq"), scatter_dimension=0, tiled=True)


def on_device(
    tokens,
    cotangent,
    doc_ids,
    w_query,
    w_key,
    w_value,
    w_out,
    w_gate,
    w_up,
    w_down,
    gain_attn_in,
    gain_attn_out,
    gain_mlp_in,
    gain_mlp_out,
    gain_query,
    gain_key,
):
    row_count = tokens.shape[1]
    window_rows = WINDOW
    attn_scale = HEAD ** (-0.5)
    seq_place = lax.axis_index("seq")
    first_row = seq_place * row_count
    ids_all = doc_ids[0]
    ids_own = lax.dynamic_slice_in_dim(ids_all, first_row, row_count, 0)
    ids_prev = lax.dynamic_slice_in_dim(
        ids_all, jnp.maximum(first_row - window_rows, 0), window_rows, 0
    )
    ids_prev = jnp.where(seq_place > 0, ids_prev, -1)
    ids_pad = jnp.concatenate([ids_prev, ids_own])
    cosine_table, sine_table = rope_tables(first_row, row_count, HEAD)
    layer_in = tokens[0].astype(jnp.float32)
    grad_out = cotangent[0].astype(jnp.float32)
    attn_shards = (
        w_query,
        w_key,
        w_value,
        w_out,
        gain_attn_in,
        gain_attn_out,
        gain_query,
        gain_key,
    )
    mlp_shards = (w_gate, w_up, w_down, gain_mlp_in, gain_mlp_out)
    attn_weights = (
        lax.all_gather(attn_shards[0], ("batch", "seq"), axis=0, tiled=True),
        lax.all_gather(attn_shards[1], ("batch", "seq"), axis=0, tiled=True),
        lax.all_gather(attn_shards[2], ("batch", "seq"), axis=0, tiled=True),
        lax.all_gather(attn_shards[3], ("batch", "seq"), axis=0, tiled=True),
        lax.all_gather(attn_shards[4], ("batch", "seq"), axis=0, tiled=True),
        lax.all_gather(attn_shards[5], ("batch", "seq"), axis=0, tiled=True),
        lax.all_gather(attn_shards[6], ("batch", "seq"), axis=0, tiled=True),
        lax.all_gather(attn_shards[7], ("batch", "seq"), axis=0, tiled=True),
    )
    mlp_weights = (
        lax.all_gather(mlp_shards[0], ("batch", "seq"), axis=0, tiled=True),
        lax.all_gather(mlp_shards[1], ("batch", "seq"), axis=0, tiled=True),
        lax.all_gather(mlp_shards[2], ("batch", "seq"), axis=0, tiled=True),
        lax.all_gather(mlp_shards[3], ("batch", "seq"), axis=0, tiled=True),
        lax.all_gather(mlp_shards[4], ("batch", "seq"), axis=0, tiled=True),
    )
    stored = forward(
        layer_in,
        attn_weights,
        mlp_weights,
        lambda stacked: passed_along(stacked, "seq", 1),
        ids_pad,
        cosine_table,
        sine_table,
        window_rows,
        attn_scale,
    )
    layer_out = stored["layer_out"]
    grad_in, terms = backward(
        stored,
        layer_in,
        grad_out,
        attn_weights,
        mlp_weights,
        lambda stacked: passed_along(stacked.astype(jnp.bfloat16), "seq", -1).astype(stacked.dtype),
        ids_pad,
        cosine_table,
        sine_table,
        window_rows,
        attn_scale,
    )
    down_share = reduce_group((terms[6],))
    gate_share = reduce_group((terms[4],))
    up_share = reduce_group((terms[5],))
    attn_share = reduce_group(
        (
            terms[0],
            terms[1],
            terms[2],
            terms[3],
            terms[7],
            terms[8],
            terms[9],
            terms[10],
            terms[11],
            terms[12],
        )
    )
    shares = (
        attn_share[0],
        attn_share[1],
        attn_share[2],
        attn_share[3],
        gate_share[0],
        up_share[0],
        down_share[0],
        attn_share[4],
        attn_share[5],
        attn_share[6],
        attn_share[7],
        attn_share[8],
        attn_share[9],
    )
    return (layer_out.astype(jnp.bfloat16)[None], grad_in.astype(jnp.bfloat16)[None]) + shares


def solution(mesh):
    return jax.shard_map(
        on_device,
        mesh=mesh,
        in_specs=(
            P("batch", "seq", None),
            P("batch", "seq", None),
            P("batch", None),
            P(("batch", "seq"), None),
            P(("batch", "seq"), None),
            P(("batch", "seq"), None),
            P(("batch", "seq"), None),
            P(("batch", "seq"), None),
            P(("batch", "seq"), None),
            P(("batch", "seq"), None),
            P(("batch", "seq")),
            P(("batch", "seq")),
            P(("batch", "seq")),
            P(("batch", "seq")),
            P(("batch", "seq")),
            P(("batch", "seq")),
        ),
        out_specs=(
            P("batch", "seq", None),
            P("batch", "seq", None),
            P(("batch", "seq"), None),
            P(("batch", "seq"), None),
            P(("batch", "seq"), None),
            P(("batch", "seq"), None),
            P(("batch", "seq"), None),
            P(("batch", "seq"), None),
            P(("batch", "seq"), None),
            P(("batch", "seq")),
            P(("batch", "seq")),
            P(("batch", "seq")),
            P(("batch", "seq")),
            P(("batch", "seq")),
            P(("batch", "seq")),
        ),
        check_vma=False,
    )
```

profile of v0, /device:TPU:13, one launch (start us, length us, event | category | flops | bytes accessed | tf_op | source)
XLA Modules:
  0.0 1836.0 jit_solution(14655989670294815910)
XLA Ops:
  15.7 40.0 %all-reduce.28 = (bf16[1152]{0:T(1024)(128)(2,1)S(1)}, bf16[256]{0:T(256)(128)(2,1)S(1)}, bf16[256]{0:T(256)(128)(2,1)S(1)}, bf16[1152]{0:T(1024)(128)(2,1)S(1)}...) all-reduce(bf16[1152]{0:T(1024)(128)(2,1)S(1)} %dynamic-update-slic, ...), channel_id=1, replica_groups=mesh['batch'=2,'seq'=16] {'batch','seq'}, use_global_device_ids=true, to_apply=%add.4 | all-reduce | flops 5120 | bytes 20480
  55.8 36.7 %all-gather = bf16[32,36,256]{2,1,0:T(8,128)(2,1)S(1)} all-gather(bf16[1,36,256]{2,1,0:T(8,128)(2,1)} %bitcast.227), channel_id=1, replica_groups=mesh['batch'=2,'seq'=16] {'batch','seq'}, dimensions={0}, use_global_device_ids=true | all-gather | bytes 608256 | tf_op jit(solution)/shard_map/all_gather | solution.py:376
  92.6 42.8 %all-gather.1 = bf16[32,36,256]{2,1,0:T(8,128)(2,1)S(1)} all-gather(bf16[1,36,256]{2,1,0:T(8,128)(2,1)S(1)} %bitcast.228), channel_id=1, replica_groups=mesh['batch'=2,'seq'=16] {'batch','seq'}, dimensions={0}, use_global_device_ids=true | all-gather | bytes 608256 | tf_op jit(solution)/shard_map/all_gather | solution.py:377
  186.5 65.8 %all-gather.17.cloned.1.call-done = bf16[32,36,6912]{2,1,0:T(8,128)(2,1)} async-done(((bf16[1,36,6912]{2,1,0:T(8,128)(2,1)}), bf16[32,36,6912]{2,1,0:T(8,128)(2,1)}) %all-gather.17.cloned.1.call-update) | async-done | bytes 15925264 | tf_op jit(solution)/shard_map/all_gather | solution.py:385
  252.3 18.5 %reshape.354 = bf16[1152,6912]{1,0:T(8,128)(2,1)} reshape(bf16[32,36,6912]{2,1,0:T(8,128)(2,1)} %all-gather.17.cloned.1.call-done) | data formatting | bytes 31850496
  270.8 101.7 %all-gather.19.cloned.1.call-done = bf16[32,36,6912]{2,1,0:T(8,128)(2,1)} async-done(((bf16[1,36,6912]{2,1,0:T(8,128)(2,1)}), bf16[32,36,6912]{2,1,0:T(8,128)(2,1)}) %all-gather.19.cloned.1.call-update) | async-done | bytes 15925264 | tf_op jit(solution)/shard_map/all_gather | solution.py:386
  372.5 18.5 %reshape.356 = bf16[1152,6912]{1,0:T(8,128)(2,1)} reshape(bf16[32,36,6912]{2,1,0:T(8,128)(2,1)} %all-gather.19.cloned.1.call-done) | data formatting | bytes 31850496
  391.0 16.2 fusion.111
  407.2 21.4 %multiply_convert_fusion.1 = (bf16[512,6912]{1,0:T(8,128)(2,1)}, f32[512,6912]{1,0:T(8,128)}) fusion(f32[512,6912]{1,0:T(8,128)} %fusion.111, bf16[512,1152]{1,0:T(8,128)(2,1)S(1)} %multiply_convert_fusion.2, bf16[1152,6912]{1,0:T(8,128)(2,1)} %reshape.356), kind=kOutput, calls=%fused_computation.10 | convolution fusion | flops 8189116416 | bytes 52494336 | tf_op jit(solution)/shard_map/dot_general | solution.py:56
  428.6 56.0 %all-gather.13.cloned.1.call-done = bf16[6912,1152]{1,0:T(8,128)(2,1)} async-done(((bf16[216,1152]{1,0:T(8,128)(2,1)}), bf16[6912,1152]{1,0:T(8,128)(2,1)}) %all-gather.13.cloned.1.call-update) | async-done | bytes 15925264 | tf_op jit(solution)/shard_map/all_gather | solution.py:387
  484.6 14.6 multiply_reduce_fusion.4
  503.0 27.9 %multiply_convert_fusion = (bf16[512,6912]{1,0:T(8,128)(2,1)}, bf16[512,6912]{1,0:T(8,128)(2,1)}) fusion(f32[512,6912]{1,0:T(8,128)} %fusion.111, f32[512,6912]{1,0:T(8,128)} %get-tuple-element.135, bf16[512,1152]{1,0:T(8,128)(2,1)} %get-tuple-element.105, bf16[6912,1152]{1,0:T(8,128)(2,1)} %all-gather.13.cloned.1.call-done), kind=kOutput, calls=%fused_computation.9 | convolution fusion | flops 8238661632 | bytes 59572224 | tf_op jit(solution)/shard_map/dot_general | solution.py:66
  530.9 14.3 fusion.112
  545.3 16.7 multiply_reduce_fusion
  571.0 19.3 %fusion.117 = f32[6912,1152]{1,0:T(8,128)} fusion(bf16[512,6912]{1,0:T(8,128)(2,1)} %get-tuple-element.134, bf16[512,1152]{1,0:T(8,128)(2,1)S(1)} %copy-done.36), kind=kOutput, calls=%fused_computation.193 | convolution fusion | flops 8153726976 | bytes 40108032 | tf_op jit(solution)/shard_map/dot_general | solution.py:60
  610.7 17.3 fusion.116
  628.0 451.4 %fusion.4 = f32[40,6912]{1,0:T(8,128)} fusion(f32[1152,6912]{1,0:T(8,128)} %fusion.116), kind=kCustom, calls=%all-reduce-scatter.4 | all-reduce-scatter fusion | flops 8847361 | bytes 32956416
  1079.4 17.1 fusion.115
  1132.0 461.4 %fusion.106 = (f32[40,1024]{1,0:T(8,128)}, f32[40,256]{1,0:T(8,128)}, f32[40,256]{1,0:T(8,128)}, f32[40,6912]{1,0:T(8,128)}) fusion(f32[1152,1024]{1,0:T(8,128)} %fusion.63, f32[1152,256]{1,0:T(8,128)} %fusion.101, f32[1152,256]{1,0:T(8,128)} %fusion.99, f32[1152,6912]{1,0:T(8,128)} %fusion.115), kind=kCustom, calls=%all-reduce-scatter.5 | all-reduce-scatter fusion | flops 10813441 | bytes 40280064
  1594.1 12.9 collective-permute-start.8
  1654.5 65.7 %all-reduce.27 = (f32[1152]{0:T(1024)S(1)}, f32[1152]{0:T(1024)S(1)}, f32[1152]{0:T(1024)S(1)}, f32[1152]{0:T(1024)S(1)}, f32[256]{0:T(256)S(1)}, /*index=5*/f32[256]{0:T(256)S(1)}) all-reduce(f32[1152]{0:T(1024)} %get-tuple-element.74, f32[1152]{0:T(1024)} %get-tuple-element.68, ...), channel_id=9, replica_groups=mesh['batch'=2,'seq'=16] {'batch','seq'}, use_global_device_ids=true, to_apply=%region_23.24.clone | all-reduce | flops 5120 | bytes 40960
  1764.0 23.1 %concatenate.36 = f32[164,6912]{1,0:T(8,128)} concatenate(f32[4,6912]{1,0:T(4,128)} %collective-permute-done.21, f32[40,6912]{1,0:T(8,128)} %collective-permute-done.20, f32[40,6912]{1,0:T(8,128)S(1)} %collective-permute-done.19, f32[40,6912]{1,0:T(8,128)} %collective-permute-done.18, f32[40,6912]{1,0:T(8,128)} %fusion.4), dimensions={0} | concatenate | bytes 9068544
  1789.5 15.5 collective-permute-done.17
  1805.0 21.6 %concatenate.35 = f32[164,6912]{1,0:T(8,128)} concatenate(f32[4,6912]{1,0:T(4,128)S(1)} %collective-permute-done.17, f32[40,6912]{1,0:T(8,128)S(1)} %collective-permute-done.16, f32[40,6912]{1,0:T(8,128)} %collective-permute-done.15, f32[40,6912]{1,0:T(8,128)} %collective-permute-done.14, f32[40,6912]{1,0:T(8,128)S(1)} %copy-done.23), dimensions={0} | concatenate | bytes 9068544
  (376 shorter events, 223.4 us)
Async XLA Ops:
  7.2 152.9 %all-gather.15.cloned.1.call-start = ((), (), s32[]{:S(2)}) async-start(), calls=%async_computation.5 | async-start | bytes 2703360 | tf_op jit(solution)/shard_map/all_gather | solution.py:375
  7.9 172.1 %all-gather.11.cloned.1.call-start = ((), (), s32[]{:S(2)}) async-start(), calls=%async_computation.2 | async-start | bytes 2433024 | tf_op jit(solution)/shard_map/all_gather | solution.py:378
  8.7 243.6 %all-gather.17.cloned.1.call-start = ((), (), s32[]{:S(2)}) async-start(), calls=%async_computation.6 | async-start | bytes 18247680 | tf_op jit(solution)/shard_map/all_gather | solution.py:385
  9.4 363.1 %all-gather.19.cloned.1.call-start = ((), (), s32[]{:S(2)}) async-start(), calls=%async_computation.7 | async-start | bytes 18247680 | tf_op jit(solution)/shard_map/all_gather | solution.py:386
  10.0 474.6 %all-gather.13.cloned.1.call-start = ((), (), s32[]{:S(2)}) async-start(), calls=%async_computation.3 | async-start | bytes 16422912 | tf_op jit(solution)/shard_map/all_gather | solution.py:387
  10.6 1818.4 %reduce-scatter.15.cloned.1.call-start = ((), (), s32[]{:S(2)}) async-start(), calls=%async_computation.4 | async-start | bytes 4866048 | tf_op jit(solution)/shard_map/reduce_scatter | solution.py:327
  141.4 17.8 collective-permute-start
  569.7 1259.3 %reduce-scatter.17.cloned.1.call-start = ((), (), s32[]{:S(2)}) async-start(), calls=%async_computation.8 | async-start | bytes 32845824
  608.5 504.2 %collective-permute-start.1 = (bf16[2,512,256]{1,2,0:T(8,128)(2,1)}, bf16[2,512,256]{1,2,0:T(8,128)(2,1)}, u32[]{:S(2)}, u32[]{:S(2)}) collective-permute-start(bf16[2,512,256]{1,2,0:T(8,128)(2,1)} %pad_maximum_fusion.2), channel_id=1, source_target_pairs={{1,0},{2,1},{3,2},{4,3},{5,4},{6,5},{7,6},{8,7},{9,8},{10,9},{11,1... | collective-permute-start | bytes 1572872 | tf_op jit(solution)/shard_map/ppermute | solution.py:17
  1096.5 648.4 %collective-permute-start.20 = (f32[40,6912]{1,0:T(8,128)}, f32[40,6912]{1,0:T(8,128)}, u32[]{:S(2)}, u32[]{:S(2)}) collective-permute-start(f32[40,6912]{1,0:T(8,128)} %fusion.4), channel_id=1, source_target_pairs={{0,3},{1,4},{2,5},{3,6},{4,7},{5,8},{6,9},{7,10},{8,11},{9,12},{10... | collective-permute-start | bytes 3317768
  1110.8 508.7 %collective-permute-start.21 = (f32[4,6912]{1,0:T(4,128)}, f32[4,6912]{1,0:T(4,128)}, u32[]{:S(2)}, u32[]{:S(2)}) collective-permute-start(f32[4,6912]{1,0:T(4,128)} %slice.67), channel_id=1, source_target_pairs={{0,4},{1,5},{2,6},{3,7},{4,8},{5,9},{6,10},{7,11},{8,12},{9,13},{1... | collective-permute-start | bytes 331784
  1594.1 37.8 %collective-permute-start.8 = (f32[40,256]{1,0:T(8,128)}, f32[40,256]{1,0:T(8,128)S(1)}, u32[]{:S(2)}, u32[]{:S(2)}) collective-permute-start(f32[40,256]{1,0:T(8,128)} %get-tuple-element.95), channel_id=1, source_target_pairs={{0,3},{1,4},{2,5},{3,6},{4,7},{5,8},{6,9},{7,10},{8,11},{9,12},{10... | collective-permute-start | bytes 122888
  1607.7 13.8 collective-permute-start.13
  1610.4 15.1 collective-permute-start.9
  1619.5 15.3 collective-permute-start.7
  1621.6 15.7 collective-permute-start.6
  1641.5 118.0 %collective-permute-start.19 = (f32[40,6912]{1,0:T(8,128)}, f32[40,6912]{1,0:T(8,128)S(1)}, u32[]{:S(2)}, u32[]{:S(2)}) collective-permute-start(f32[40,6912]{1,0:T(8,128)} %fusion.4), channel_id=1, source_target_pairs={{0,2},{1,3},{2,4},{3,5},{4,6},{5,7},{6,8},{7,9},{8,10},{9,11},{10,... | collective-permute-start | bytes 3317768
  1643.6 120.3 %collective-permute-start.18 = (f32[40,6912]{1,0:T(8,128)}, f32[40,6912]{1,0:T(8,128)}, u32[]{:S(2)}, u32[]{:S(2)}) collective-permute-start(f32[40,6912]{1,0:T(8,128)} %fusion.4), channel_id=1, source_target_pairs={{0,1},{1,2},{2,3},{3,4},{4,5},{5,6},{6,7},{7,8},{8,9},{9,10},{10,1... | collective-permute-start | bytes 3317768
  1648.5 89.9 %collective-permute-start.3 = (f32[40,1024]{1,0:T(8,128)S(1)}, f32[40,1024]{1,0:T(8,128)}, u32[]{:S(2)}, u32[]{:S(2)}) collective-permute-start(f32[40,1024]{1,0:T(8,128)S(1)} %copy-done.51), channel_id=1, source_target_pairs={{0,2},{1,3},{2,4},{3,5},{4,6},{5,7},{6,8},{7,9},{8,10},{9,11},{10,... | collective-permute-start | bytes 491528
  1650.4 91.5 %collective-permute-start.2 = (f32[40,1024]{1,0:T(8,128)S(1)}, f32[40,1024]{1,0:T(8,128)}, u32[]{:S(2)}, u32[]{:S(2)}) collective-permute-start(f32[40,1024]{1,0:T(8,128)S(1)} %copy-done.51), channel_id=1, source_target_pairs={{0,1},{1,2},{2,3},{3,4},{4,5},{5,6},{6,7},{7,8},{8,9},{9,10},{10,1... | collective-permute-start | bytes 491528
  1738.4 66.6 %collective-permute-start.16 = (f32[40,6912]{1,0:T(8,128)S(1)}, f32[40,6912]{1,0:T(8,128)S(1)}, u32[]{:S(2)}, u32[]{:S(2)}) collective-permute-start(f32[40,6912]{1,0:T(8,128)S(1)} %copy-done.23), channel_id=1, source_target_pairs={{0,3},{1,4},{2,5},{3,6},{4,7},{5,8},{6,9},{7,10},{8,11},{9,12},{10... | collective-permute-start | bytes 3317768
  1742.0 62.9 %collective-permute-start.15 = (f32[40,6912]{1,0:T(8,128)S(1)}, f32[40,6912]{1,0:T(8,128)}, u32[]{:S(2)}, u32[]{:S(2)}) collective-permute-start(f32[40,6912]{1,0:T(8,128)S(1)} %copy-done.23), channel_id=1, source_target_pairs={{0,2},{1,3},{2,4},{3,5},{4,6},{5,7},{6,8},{7,9},{8,10},{9,11},{10,... | collective-permute-start | bytes 3317768
  1744.9 60.0 %collective-permute-start.14 = (f32[40,6912]{1,0:T(8,128)S(1)}, f32[40,6912]{1,0:T(8,128)}, u32[]{:S(2)}, u32[]{:S(2)}) collective-permute-start(f32[40,6912]{1,0:T(8,128)S(1)} %copy-done.23), channel_id=1, source_target_pairs={{0,1},{1,2},{2,3},{3,4},{4,5},{5,6},{6,7},{7,8},{8,9},{9,10},{10,1... | collective-permute-start | bytes 3317768
  1759.5 45.4 %collective-permute-start.17 = (f32[4,6912]{1,0:T(4,128)}, f32[4,6912]{1,0:T(4,128)S(1)}, u32[]{:S(2)}, u32[]{:S(2)}) collective-permute-start(f32[4,6912]{1,0:T(4,128)} %slice.66), channel_id=1, source_target_pairs={{0,4},{1,5},{2,6},{3,7},{4,8},{5,9},{6,10},{7,11},{8,12},{9,13},{1... | collective-permute-start | bytes 331784
  (109 other events, 1920.8 us)
Sparse Core Ops, SparseCore 0:
  10.9 58.3 all-gather.14
  72.3 56.5 all-gather.10
  131.8 120.4 all-gather.16
  255.0 117.4 all-gather.18
  375.2 109.3 all-gather.12
  569.8 129.7 reduce-scatter.14
  707.8 453.0 reduce-scatter.16
where the time goes:
time: 1850 us; the launch traced here: 1840 us
  blocking collectives  1100 us (59%)
  waiting for transfers between devices  255 us (14%)
  matrix products  207 us (11%)
  local copies, waits for them, and re-layouts  145 us (8%)
  starting transfers between devices  83.6 us (5%)
  other arithmetic  31.5 us (2%)
    unnamed x4, blocking collectives  1020 us
    unnamed x246, local copies, waits for them, and re-layouts  142 us
    all_gather x1, waiting for transfers between devices, on_device(): lax.all_gather(mlp_shards[1], ('batch', 'seq'), axis=0, tiled=True)  102 us
    unnamed x21, starting transfers between devices  79.1 us
    all_gather x1, waiting for transfers between devices, on_device(): lax.all_gather(mlp_shards[0], ('batch', 'seq'), axis=0, tiled=True)  65.8 us
    dot_general x7, matrix products, by_transpose(): lax.dot_general(left_side, right_side, (((1,), (1,)), ((), ())), preferre...  65.5 us
    dot_general x7, matrix products, over_rows(): lax.dot_general(left_side, right_side, (((0,), (0,)), ((), ())), preferre...  64.5 us
    dot_general x7, matrix products, matmul(): return jnp.dot(left_side, right_side, preferred_element_type=jnp.float32)  60.6 us
  transfers between devices with their start and end apart: 29, of which 6 were waited for; matrix products, arithmetic and copies ran while one was open for 65% of the time, Pallas kernels for 0%

commit v1 on v0

v1 whole, which is shorter than its diff:
```python
import jax
import jax.numpy as jnp
from jax import lax
from jax.sharding import Mesh
from jax.sharding import PartitionSpec as P

HEAD = 256
WINDOW = 512
EPSILON = 1e-06
ROPE_BASE = 10000.0
ALL = ("x", "g", "y", "c")
PLANE = ("x", "y", "c")
BF = jnp.bfloat16
F32 = jnp.float32


def norm_gain(values, gain_vec):
    return (
        values * lax.rsqrt(jnp.mean(values * values, axis=-1, keepdims=True) + EPSILON) * gain_vec
    )


def rotate(values, cosine_table, sine_table):
    half_size = values.shape[-1] // 2
    turned = jnp.concatenate([-values[..., half_size:], values[..., :half_size]], axis=-1)
    return values * cosine_table + turned * sine_table


def rope_tables(first_row, row_count, head_size):
    places = (first_row + jnp.arange(row_count, dtype=jnp.int32)).astype(F32)
    frequency = ROPE_BASE ** (-(jnp.arange(head_size // 2, dtype=F32) * 2.0) / head_size)
    angles = places[:, None] * frequency[None, :]
    angles = jnp.concatenate([angles, angles], axis=-1)
    return (jnp.cos(angles), jnp.sin(angles))


def prepare_query(raw_value, gain_vec, cosine_table, sine_table):
    split_heads = raw_value.reshape(raw_value.shape[0], -1, gain_vec.shape[0])
    return rotate(
        norm_gain(split_heads, gain_vec), cosine_table[:, None, :], sine_table[:, None, :]
    )


def prepare_key(raw_value, gain_vec, cosine_table, sine_table):
    return rotate(norm_gain(raw_value, gain_vec), cosine_table, sine_table)


def matmul(left_side, right_side):
    return jnp.dot(left_side, right_side, preferred_element_type=F32)


def over_rows(left_side, right_side):
    return lax.dot_general(
        left_side, right_side, (((0,), (0,)), ((), ())), preferred_element_type=F32
    )


def by_transpose(left_side, right_side):
    return lax.dot_general(
        left_side, right_side, (((1,), (1,)), ((), ())), preferred_element_type=F32
    )


def block_mask(ids_pad, rows):
    query_place = rows + jnp.arange(rows, dtype=jnp.int32)
    key_place = jnp.arange(2 * rows, dtype=jnp.int32)
    distance = query_place[:, None] - key_place[None, :]
    same_doc = ids_pad[rows:][:, None] == ids_pad[None, :]
    return (distance >= 0) & (distance < WINDOW) & same_doc


def attend_forward(queries, key_pad, value_pad, allowed, attn_scale):
    row_count, head_count, head_size = queries.shape
    scores = jnp.einsum("qhd,kd->hqk", queries, key_pad, preferred_element_type=F32) * attn_scale
    scores = jnp.where(allowed[None], scores, -1e30)
    row_max = jnp.max(scores, axis=-1, keepdims=True)
    weights = jnp.exp(scores - row_max)
    row_total = jnp.sum(weights, axis=-1, keepdims=True)
    probabilities = (weights / row_total).astype(BF)
    attended = jnp.einsum("hqk,kd->qhd", probabilities, value_pad, preferred_element_type=F32)
    return (
        attended.reshape(row_count, head_count * head_size),
        (row_max + jnp.log(row_total))[..., 0],
    )


def attend_backward(queries, key_pad, value_pad, allowed, log_total, grad_attended, attn_scale):
    row_count, head_count, head_size = queries.shape
    grad_part = grad_attended.reshape(row_count, head_count, head_size)
    scores = jnp.einsum("qhd,kd->hqk", queries, key_pad, preferred_element_type=F32) * attn_scale
    probabilities = jnp.where(allowed[None], jnp.exp(scores - log_total[..., None]), 0.0)
    grad_prob = jnp.einsum("qhd,kd->hqk", grad_part, value_pad, preferred_element_type=F32)
    inner_sum = jnp.sum(probabilities * grad_prob, axis=-1, keepdims=True)
    grad_score = (probabilities * (grad_prob - inner_sum)).astype(BF)
    grad_query = (
        jnp.einsum("hqk,kd->qhd", grad_score, key_pad, preferred_element_type=F32) * attn_scale
    )
    grad_key = (
        jnp.einsum("hqk,qhd->kd", grad_score, queries, preferred_element_type=F32) * attn_scale
    )
    grad_value = jnp.einsum(
        "hqk,qhd->kd", probabilities.astype(BF), grad_part, preferred_element_type=F32
    )
    return (grad_query, grad_key, grad_value)


def swap(array, axis):
    return lax.ppermute(array, axis, [(0, 1), (1, 0)])


def plane_gather(own):
    half = own.shape[0] // 2
    from_x = swap(own, "x")
    from_y = swap(own, "y")
    far_top = swap(from_x[:half], "y")
    far_low = swap(from_y[half:], "x")
    mine = jnp.concatenate([own, from_x, from_y, far_top, far_low])
    return jnp.concatenate([mine, swap(mine, "c")])


def plane_reduce(parts):
    rows = parts.shape[0] // 8
    half = rows // 2
    mine = parts[: 4 * rows].astype(F32) + swap(parts[4 * rows :].astype(BF), "c").astype(F32)
    own, to_x, to_y, far = (mine[i * rows : (i + 1) * rows] for i in range(4))
    far = far.astype(BF)
    top = swap(far[:half], "y").astype(F32)
    low = swap(far[half:], "x").astype(F32)
    to_x = jnp.concatenate([to_x[:half] + top, to_x[half:]]).astype(BF)
    to_y = jnp.concatenate([to_y[:half], to_y[half:] + low]).astype(BF)
    return own + swap(to_x, "x").astype(F32) + swap(to_y, "y").astype(F32)


def on_device(
    tokens,
    cotangent,
    doc_ids,
    w_query,
    w_key,
    w_value,
    w_out,
    w_gate,
    w_up,
    w_down,
    gain_attn_in,
    gain_attn_out,
    gain_mlp_in,
    gain_mlp_out,
    gain_query,
    gain_key,
):
    row_count = tokens.shape[1]
    width = tokens.shape[2]
    devices = lax.axis_size(ALL)
    groups = lax.axis_size("g")
    members = lax.axis_size(PLANE)
    shard_rows = w_query.shape[0]
    head_rows = gain_query.shape[0]
    hidden_all = w_gate.shape[1]
    hidden_own = hidden_all // members
    piece = hidden_own // groups
    q_cols, k_cols = w_query.shape[1], w_key.shape[1]
    qkv_cols = q_cols + 2 * k_cols
    attn_scale = HEAD ** (-0.5)

    def gain_columns(d_gains, h_gains):
        columns = list(d_gains) + [
            jnp.pad(h, ((0, 0), (0, shard_rows - head_rows))) for h in h_gains
        ]
        block = jnp.stack(columns, axis=-1)
        return jnp.pad(block, ((0, 0), (0, 0), (0, 128 - len(columns))))

    gains = gain_columns(
        [g[None] for g in (gain_attn_in, gain_attn_out, gain_mlp_in, gain_mlp_out)],
        [gain_query[None], gain_key[None]],
    )
    packed = jnp.concatenate([w_query, w_key, w_value, gains[0]], axis=1)
    packed = lax.all_gather(packed, ALL, axis=0)
    w_o = lax.all_gather(w_out, ALL, axis=0, tiled=True)
    gain_block = packed[:, :, qkv_cols:].astype(F32)
    d_gains = gain_block[:, :, :4].reshape(width, 4).T
    g_attn_in, g_attn_out, g_mlp_in, g_mlp_out = (d_gains[i : i + 1] for i in range(4))
    g_query = gain_block[:, :head_rows, 4].reshape(HEAD)
    g_key = gain_block[:, :head_rows, 5].reshape(HEAD)
    w_qkv = packed[:, :, :qkv_cols].reshape(width, qkv_cols)

    down = lax.all_gather(w_down, "g", axis=0, tiled=True)

    def spread(weight):
        cut = weight.reshape(shard_rows, 2, groups, members // 2, piece)
        return cut.transpose(1, 3, 0, 2, 4).reshape(members, shard_rows, hidden_own)

    sent = jnp.stack([spread(w_gate), spread(w_up)], axis=1)
    sent = lax.all_to_all(sent, PLANE, split_axis=0, concat_axis=0, tiled=True)
    sent = sent.transpose(1, 0, 2, 3).reshape(2, members * shard_rows, hidden_own)
    both = lax.all_gather(sent, "g", axis=0)
    both = both.reshape(groups, 2, 2, members // 2 * shard_rows, hidden_own)
    gate = both[:, 0].transpose(1, 0, 2, 3).reshape(width, hidden_own)
    up = both[:, 1].transpose(1, 0, 2, 3).reshape(width, hidden_own)

    seq_place = lax.axis_index(("g", "y", "c"))
    seq_size = lax.axis_size(("g", "y", "c"))
    first_row = seq_place * row_count
    ids_all = doc_ids[0]
    ids_own = lax.dynamic_slice_in_dim(ids_all, first_row, row_count, 0)
    ids_prev = lax.dynamic_slice_in_dim(
        ids_all, jnp.maximum(first_row - row_count, 0), row_count, 0
    )
    ids_prev = jnp.where(seq_place > 0, ids_prev, -1)
    ids_pad = jnp.concatenate([ids_prev, ids_own])
    allowed = block_mask(ids_pad, row_count)
    cosine_table, sine_table = rope_tables(first_row, row_count, HEAD)
    layer_in = tokens[0].astype(F32)
    grad_out = cotangent[0].astype(F32)

    normed = norm_gain(layer_in, g_attn_in).astype(BF)
    qkv_raw = matmul(normed, w_qkv)
    query_raw = qkv_raw[:, :q_cols]
    key_raw = qkv_raw[:, q_cols : q_cols + k_cols]
    queries = prepare_query(query_raw, g_query, cosine_table, sine_table).astype(BF)
    keys = prepare_key(key_raw, g_key, cosine_table, sine_table).astype(BF)
    values = qkv_raw[:, q_cols + k_cols :].astype(BF)
    key_value = jnp.concatenate([keys, values], axis=1)
    halo = lax.ppermute(key_value, ("g", "y", "c"), [(i, i + 1) for i in range(seq_size - 1)])
    key_pad = jnp.concatenate([halo[:, :k_cols], keys])
    value_pad = jnp.concatenate([halo[:, k_cols:], values])
    attended, log_total = attend_forward(queries, key_pad, value_pad, allowed, attn_scale)
    attended = attended.astype(BF)
    branch = matmul(attended, w_o)
    middle = layer_in + norm_gain(branch, g_attn_out)
    normed_mlp = norm_gain(middle, g_mlp_in).astype(BF)

    normed_all = plane_gather(normed_mlp)
    gate_raw = matmul(normed_all, gate)
    up_raw = matmul(normed_all, up)
    gelu, gelu_pull = jax.vjp(lambda u: jax.nn.gelu(u, approximate=True), gate_raw)
    hidden = (gelu * up_raw).astype(BF)
    slope = gelu_pull(up_raw)[0].astype(BF)
    gelu = gelu.astype(BF)
    mixed = plane_reduce(matmul(hidden, down))
    layer_out = middle + norm_gain(mixed, g_mlp_out)

    _, pullback = jax.vjp(norm_gain, mixed, g_mlp_out)
    grad_mixed, grad_gain_mlp_out = pullback(grad_out)
    grad_mixed_all = plane_gather(grad_mixed.astype(BF))
    grad_down = over_rows(hidden, grad_mixed_all).astype(BF)
    grad_down = lax.psum_scatter(grad_down, "g", scatter_dimension=0, tiled=True)
    grad_hidden = by_transpose(grad_mixed_all, down)
    grad_gate = (grad_hidden * slope.astype(F32)).astype(BF)
    grad_up = (grad_hidden * gelu.astype(F32)).astype(BF)

    def collect(term):
        term = term.astype(BF).reshape(2, groups, members // 2 * shard_rows, hidden_own)
        term = term.transpose(1, 0, 2, 3).reshape(groups * members * shard_rows, hidden_own)
        term = lax.psum_scatter(term, "g", scatter_dimension=0, tiled=True)
        term = term.reshape(members, shard_rows, hidden_own)
        term = lax.all_to_all(term, PLANE, split_axis=0, concat_axis=0, tiled=True)
        term = term.reshape(2, members // 2, shard_rows, groups, piece)
        return term.transpose(2, 0, 3, 1, 4).reshape(shard_rows, hidden_all).astype(F32)

    grad_w_gate = collect(over_rows(normed_all, grad_gate))
    grad_w_up = collect(over_rows(normed_all, grad_up))
    grad_normed_mlp = plane_reduce(by_transpose(grad_gate, gate) + by_transpose(grad_up, up))
    _, pullback = jax.vjp(norm_gain, middle, g_mlp_in)
    grad_from_mlp, grad_gain_mlp_in = pullback(grad_normed_mlp)
    grad_middle = grad_out + grad_from_mlp

    _, pullback = jax.vjp(norm_gain, branch, g_attn_out)
    grad_branch, grad_gain_attn_out = pullback(grad_middle)
    grad_branch = grad_branch.astype(BF)
    grad_w_out = lax.psum_scatter(
        over_rows(attended, grad_branch).astype(BF), ALL, scatter_dimension=0, tiled=True
    )
    grad_attended = by_transpose(grad_branch, w_o).astype(BF)
    grad_queries, grad_key_pad, grad_value_pad = attend_backward(
        queries, key_pad, value_pad, allowed, log_total, grad_attended, attn_scale
    )
    returned = lax.ppermute(
        jnp.concatenate([grad_key_pad[:row_count], grad_value_pad[:row_count]], axis=1).astype(BF),
        ("g", "y", "c"),
        [(i + 1, i) for i in range(seq_size - 1)],
    ).astype(F32)
    grad_keys = grad_key_pad[row_count:] + returned[:, :k_cols]
    grad_values = grad_value_pad[row_count:] + returned[:, k_cols:]
    _, pullback = jax.vjp(
        lambda raw, gain: prepare_key(raw, gain, cosine_table, sine_table), key_raw, g_key
    )
    grad_key_raw, grad_gain_key = pullback(grad_keys)
    _, pullback = jax.vjp(
        lambda raw, gain: prepare_query(raw, gain, cosine_table, sine_table), query_raw, g_query
    )
    grad_query_raw, grad_gain_query = pullback(grad_queries)
    grad_qkv_raw = jnp.concatenate([grad_query_raw, grad_key_raw, grad_values], axis=1).astype(BF)
    grad_w_qkv = over_rows(normed, grad_qkv_raw).astype(BF)
    grad_normed = by_transpose(grad_qkv_raw, w_qkv)
    _, pullback = jax.vjp(norm_gain, layer_in, g_attn_in)
    grad_from_attn, grad_gain_attn_in = pullback(grad_normed)
    grad_in = grad_middle + grad_from_attn

    terms = gain_columns(
        [
            g.reshape(devices, shard_rows)
            for g in (grad_gain_attn_in, grad_gain_attn_out, grad_gain_mlp_in, grad_gain_mlp_out)
        ],
        [g.reshape(devices, head_rows) for g in (grad_gain_query, grad_gain_key)],
    ).astype(BF)
    terms = jnp.concatenate([grad_w_qkv.reshape(devices, shard_rows, qkv_cols), terms], axis=2)
    share = lax.psum_scatter(terms, ALL, scatter_dimension=0, tiled=True)[0].astype(F32)
    return (
        layer_out.astype(BF)[None],
        grad_in.astype(BF)[None],
        share[:, :q_cols],
        share[:, q_cols : q_cols + k_cols],
        share[:, q_cols + k_cols : qkv_cols],
        grad_w_out.astype(F32),
        grad_w_gate,
        grad_w_up,
        grad_down.astype(F32),
        share[:, qkv_cols],
        share[:, qkv_cols + 1],
        share[:, qkv_cols + 2],
        share[:, qkv_cols + 3],
        share[:head_rows, qkv_cols + 4],
        share[:head_rows, qkv_cols + 5],
    )


def solution(mesh):
    batch, seq = mesh.devices.shape
    fine = Mesh(mesh.devices.reshape(batch, seq // 4, 2, 2), ALL)
    rows = ("g", "y", "c")
    return jax.shard_map(
        on_device,
        mesh=fine,
        in_specs=(P("x", rows, None),) * 2
        + (P("x", None),)
        + (P(ALL, None),) * 7
        + (P(ALL),) * 6,
        out_specs=(P("x", rows, None),) * 2 + (P(ALL, None),) * 7 + (P(ALL),) * 6,
        check_vma=False,
    )
```

time: 1850 us -> 919 us (0.50)
  the two profiles are of different devices: /device:TPU:13 before, /device:TPU:0 now
where the time goes in v1:
time: 919 us; the launch traced here: 909 us
  waiting for transfers between devices  410 us (45%)
  matrix products  209 us (23%)
  local copies, waits for them, and re-layouts  131 us (14%)
  other arithmetic  95.6 us (10%)
  starting transfers between devices  46.8 us (5%)
  between operations  17.4 us (2%)
    unnamed x11, waiting for transfers between devices  149 us
    ppermute x20, waiting for transfers between devices, swap(): return lax.ppermute(array, axis, [(0, 1), (1, 0)])  145 us
    dot_general x5, matrix products, by_transpose(): lax.dot_general(left_side, right_side, (((1,), (1,)), ((), ())), preferre...  73.8 us
    dot_general x5, matrix products, matmul(): return jnp.dot(left_side, right_side, preferred_element_type=F32)  60.4 us
    dot_general x5, matrix products, over_rows(): lax.dot_general(left_side, right_side, (((0,), (0,)), ((), ())), preferre...  54.2 us
    all_gather x1, waiting for transfers between devices, on_device(): packed = lax.all_gather(packed, ALL, axis=0)  48.7 us
    all_gather x1, waiting for transfers between devices, on_device(): both = lax.all_gather(sent, 'g', axis=0)  30.8 us
    unnamed x215, local copies, waits for them, and re-layouts  29.6 us
  transfers between devices with their start and end apart: 34, of which 22 were waited for; matrix products, arithmetic and copies ran while one was open for 32% of the time, Pallas kernels for 0%

profile of v1, /device:TPU:0, one launch (start us, length us, event | category | flops | bytes accessed | tf_op | source)
XLA Modules:
  0.0 909.3 jit_solution(13672174091658792706)
XLA Ops:
  28.7 48.7 %all-gather.13.cloned.1.call-done = bf16[32,36,1664]{2,1,0:T(8,128)(2,1)} async-done(((bf16[1,36,1664]{2,1,0:T(8,128)(2,1)}), bf16[32,36,1664]{2,1,0:T(8,128)(2,1)}) %all-gather.13.cloned.1.call-update) | async-done | bytes 3833872 | tf_op jit(solution)/shard_map/all_gather | solution.py:178
  147.1 23.7 %collective-permute-done.2 = bf16[512,1152]{1,0:T(8,128)(2,1)} collective-permute-done((bf16[512,1152]{1,0:T(8,128)(2,1)S(1)}, bf16[512,1152]{1,0:T(8,128)(2,1)}, u32[]{:S(2)}, u32[]{:S(2)}) %collective-permute-start.2) | collective-permute-done | bytes 1179680 | tf_op jit(solution)/shard_map/ppermute | solution.py:108
  180.2 8.8 collective-permute-done.3
  194.6 30.8 %all-gather.9.cloned.1.call-done = bf16[4,2,288,864]{3,2,1,0:T(8,128)(2,1)} async-done(((bf16[1,2,288,864]{3,2,1,0:T(8,128)(2,1)}), bf16[4,2,288,864]{3,2,1,0:T(8,128)(2,1)}) %all-gather.9.cloned.1.call-update) | async-done | bytes 3981328 | tf_op jit(solution)/shard_map/all_gather | solution.py:196
  235.2 13.1 %fusion.112 = f32[4096,864]{0,1:T(8,128)} fusion(bf16[4096,1152]{1,0:T(8,128)(2,1)S(1)} %constant_dynamic-update-slice_fusion.5, bf16[1152,864]{1,0:T(8,128)(2,1)S(1)} %bitcast.234), kind=kOutput, calls=%fused_computation.260 | convolution fusion | flops 8153726976 | bytes 25583616 | tf_op jit(solution)/shard_map/dot_general | solution.py:49
  248.4 22.2 %multiply_convert_fusion.2 = (bf16[4096,864]{0,1:T(8,128)(2,1)}, f32[4096,864]{0,1:T(8,128)}) fusion(f32[4096,864]{0,1:T(8,128)} %fusion.112, bf16[4096,1152]{1,0:T(8,128)(2,1)} %copy-done.50, bf16[1152,864]{1,0:T(8,128)(2,1)} %bitcast.236), kind=kOutput, calls=%fused_computation.12 | convolution fusion | flops 8189116416 | bytes 46817280 | tf_op jit(solution)/shard_map/dot_general | solution.py:49
  270.6 17.5 %fusion.113 = f32[4096,1152]{1,0:T(8,128)} fusion(bf16[4096,864]{0,1:T(8,128)(2,1)} %get-tuple-element.112, bf16[864,1152]{1,0:T(8,128)(2,1)} %all-gather.11.cloned.1.call-done), kind=kOutput, calls=%fused_computation.261 | convolution fusion | flops 8153726976 | bytes 27942912 | tf_op jit(solution)/shard_map/dot_general | solution.py:49
  300.3 11.1 %fusion.103 = (bf16[2048,1152]{1,0:T(8,128)(2,1)}, f32[2048,1152]{1,0:T(8,128)}) fusion(bf16[2048,1152]{1,0:T(8,128)(2,1)} %collective-permute-done.6, f32[4096,1152]{1,0:T(8,128)} %fusion.113), kind=kLoop, calls=%fused_computation.252 | loop fusion | flops 7077888 | bytes 28311552 | tf_op jit(solution)/shard_map/convert.51
  316.3 12.4 %collective-permute-done.7 = bf16[256,1152]{1,0:T(8,128)(2,1)S(1)} collective-permute-done((bf16[256,1152]{1,0:T(8,128)(2,1)S(1)}, bf16[256,1152]{1,0:T(8,128)(2,1)S(1)}, u32[]{:S(2)}, u32[]{:S(2)}) %collective-permute-start.7) | collective-permute-done | bytes 589856 | tf_op jit(solution)/shard_map/ppermute | solution.py:108
  334.2 24.7 %collective-permute-done.10 = bf16[512,1152]{1,0:T(8,128)(2,1)S(1)} collective-permute-done((bf16[512,1152]{1,0:T(8,128)(2,1)S(1)}, bf16[512,1152]{1,0:T(8,128)(2,1)S(1)}, u32[]{:S(2)}, u32[]{:S(2)}) %collective-permute-start.10) | collective-permute-done | bytes 1179680 | tf_op jit(solution)/shard_map/ppermute | solution.py:108
  367.7 22.7 %collective-permute-done.12 = bf16[512,1152]{1,0:T(8,128)(2,1)S(1)} collective-permute-done((bf16[512,1152]{1,0:T(8,128)(2,1)S(1)}, bf16[512,1152]{1,0:T(8,128)(2,1)S(1)}, u32[]{:S(2)}, u32[]{:S(2)}) %collective-permute-start.12) | collective-permute-done | bytes 1179680 | tf_op jit(solution)/shard_map/ppermute | solution.py:108
  394.2 9.8 %collective-permute-done.13 = bf16[256,1152]{1,0:T(8,128)(2,1)S(1)} collective-permute-done((bf16[256,1152]{1,0:T(8,128)(2,1)S(1)}, bf16[256,1152]{1,0:T(8,128)(2,1)S(1)}, u32[]{:S(2)}, u32[]{:S(2)}) %collective-permute-start.13) | collective-permute-done | bytes 589856 | tf_op jit(solution)/shard_map/ppermute | solution.py:108
  416.6 27.6 %multiply_convert_fusion = (bf16[4096,864]{0,1:T(8,128)(2,1)}, bf16[4096,864]{0,1:T(8,128)(2,1)}) fusion(f32[4096,864]{0,1:T(8,128)} %fusion.112, f32[4096,864]{0,1:T(8,128)} %get-tuple-element.113, bf16[4096,1152]{1,0:T(8,128)(2,1)} %copy-done.51, bf16[864,1152]{1,0:T(8,128)(2,1)S(1)} %copy-done.96), kind=kOutput, calls=%fused_computation.10 | convolution fusion | flops 8252817408 | bytes 53895168 | tf_op jit(solution)/shard_map/dot_general | solution.py:59
  444.2 17.5 %fusion.114 = f32[4096,1152]{1,0:T(8,128)} fusion(bf16[4096,864]{0,1:T(8,128)(2,1)} %get-tuple-element.55, bf16[1152,864]{1,0:T(8,128)(2,1)S(1)} %bitcast.235), kind=kOutput, calls=%fused_computation.262 | convolution fusion | flops 8153726976 | bytes 27942912 | tf_op jit(solution)/shard_map/dot_general | solution.py:59
  461.7 21.5 %convolution_add_fusion = f32[4096,1152]{1,0:T(8,128)} fusion(f32[4096,1152]{1,0:T(8,128)} %fusion.114, bf16[4096,864]{0,1:T(8,128)(2,1)} %get-tuple-element.54, bf16[1152,864]{1,0:T(8,128)(2,1)S(1)} %bitcast.237), kind=kOutput, calls=%fused_computation.2 | convolution fusion | flops 8158445568 | bytes 46817280 | tf_op jit(solution)/shard_map/dot_general | solution.py:59
  489.8 14.3 %convolution_convert_fusion.2 = bf16[1152,864]{0,1:T(8,128)(2,1)} fusion(bf16[4096,864]{0,1:T(8,128)(2,1)S(1)} %copy-done.97, bf16[4096,1152]{1,0:T(8,128)(2,1)} %copy-done.50), kind=kOutput, calls=%fused_computation.47 | convolution fusion | flops 8154722304 | bytes 18505728 | tf_op jit(solution)/shard_map/dot_general | solution.py:53
  508.6 15.3 %convolution_convert_fusion.3 = bf16[1152,864]{0,1:T(8,128)(2,1)} fusion(bf16[4096,864]{0,1:T(8,128)(2,1)} %get-tuple-element.55, bf16[4096,1152]{1,0:T(8,128)(2,1)} %copy-done.50), kind=kOutput, calls=%fused_computation.48 | convolution fusion | flops 8154722304 | bytes 18505728 | tf_op jit(solution)/shard_map/dot_general | solution.py:53
  528.3 11.3 %fusion.100 = (bf16[2048,1152]{1,0:T(8,128)(2,1)}, f32[2048,1152]{1,0:T(8,128)}) fusion(bf16[2048,1152]{1,0:T(8,128)(2,1)} %collective-permute-done.16, f32[4096,1152]{1,0:T(8,128)} %convolution_add_fusion), kind=kLoop, calls=%fused_computation.251 | loop fusion | flops 7077888 | bytes 28311552 | tf_op jit(solution)/shard_map/convert.43
  543.8 13.2 %collective-permute-done.17 = bf16[256,1152]{1,0:T(8,128)(2,1)S(1)} collective-permute-done((bf16[256,1152]{1,0:T(8,128)(2,1)S(1)}, bf16[256,1152]{1,0:T(8,128)(2,1)S(1)}, u32[]{:S(2)}, u32[]{:S(2)}) %collective-permute-start.17) | collective-permute-done | bytes 589856 | tf_op jit(solution)/shard_map/ppermute | solution.py:108
  564.4 15.1 %convolution_convert_fusion.4 = bf16[864,1152]{1,0:T(8,128)(2,1)} fusion(bf16[4096,864]{0,1:T(8,128)(2,1)} %get-tuple-element.112, bf16[4096,1152]{1,0:T(8,128)(2,1)} %copy-done.51), kind=kOutput, calls=%fused_computation.49 | convolution fusion | flops 8154722304 | bytes 18505728 | tf_op jit(solution)/shard_map/dot_general | solution.py:53
  677.6 13.2 %all-to-all-start.2 = ((bf16[8,36,864]{2,1,0:T(8,128)(2,1)}), bf16[8,36,864]{2,1,0:T(8,128)(2,1)S(1)}, u32[]{:S(2)}, u32[]{:S(2)}) async-start(bf16[8,36,864]{2,1,0:T(8,128)(2,1)} %reshape.404), calls=%async_computation.5 | async-start | bytes 1146880 | tf_op jit(solution)/shard_map/all_to_all | solution.py:257
  692.8 11.0 %all-to-all-done.2 = bf16[8,36,864]{2,1,0:T(8,128)(2,1)S(1)} async-done(((bf16[8,36,864]{2,1,0:T(8,128)(2,1)}), bf16[8,36,864]{2,1,0:T(8,128)(2,1)S(1)}, u32[]{:S(2)}, u32[]{:S(2)}) %all-to-all-start.2) | async-done | bytes 497696 | tf_op jit(solution)/shard_map/all_to_all | solution.py:257
  731.1 17.4 %reduce-scatter.11.cloned.1.call-done = bf16[32,1152]{1,0:T(8,128)(2,1)} async-done(((bf16[1024,1152]{1,0:T(8,128)(2,1)}), bf16[32,1152]{1,0:T(8,128)(2,1)}) %reduce-scatter.11.cloned.1.call-update) | async-done | bytes 73744 | tf_op jit(solution)/shard_map/reduce_scatter | solution.py:271
  750.1 147.9 %reduce-scatter.17.cloned.1.call-done = bf16[1,36,1664]{2,1,0:T(8,128)(2,1)} async-done(((bf16[32,36,1664]{2,1,0:T(8,128)(2,1)}), bf16[1,36,1664]{2,1,0:T(8,128)(2,1)}) %reduce-scatter.17.cloned.1.call-update) | async-done | bytes 119824
  (431 shorter events, 320.9 us)
Async XLA Ops:
  8.0 69.4 %all-gather.13.cloned.1.call-start = ((), (), s32[]{:S(2)}) async-start(), calls=%async_computation.14 | async-start | bytes 4392960 | tf_op jit(solution)/shard_map/all_gather | solution.py:178
  19.3 125.4 %all-to-all-start = ((bf16[8,2,36,864]{3,1,2,0:T(2,128)(2,1)}), bf16[8,2,36,864]{3,1,2,0:T(2,128)(2,1)}, u32[]{:S(2)}, u32[]{:S(2)}) async-start(bf16[8,2,36,864]{3,1,2,0:T(2,128)(2,1)} %copy.268), calls=%async_computation | async-start | bytes 2064384 | tf_op jit(solution)/shard_map/all_to_all | solution.py:194
  24.4 111.8 %all-gather.7.cloned.1.call-start = ((), (), s32[]{:S(2)}) async-start(), calls=%async_computation.8 | async-start | bytes 2433024 | tf_op jit(solution)/shard_map/all_gather | solution.py:179
  25.2 200.3 %all-gather.9.cloned.1.call-start = ((), (), s32[]{:S(2)}) async-start(), calls=%async_computation.9 | async-start | bytes 5160960 | tf_op jit(solution)/shard_map/all_gather | solution.py:196
  142.6 28.2 %collective-permute-start.2 = (bf16[512,1152]{1,0:T(8,128)(2,1)S(1)}, bf16[512,1152]{1,0:T(8,128)(2,1)}, u32[]{:S(2)}, u32[]{:S(2)}) collective-permute-start(bf16[512,1152]{1,0:T(8,128)(2,1)S(1)} %get-tuple-element.51), channel_id=1, source_target_pairs={{0,2},{2,0},{1,3},{3,1},{4,6},{6,4},{5,7},{7,5},{8,10},{10,8},{9,1... | collective-permute-start | bytes 3538952 | tf_op jit(solution)/shard_map/ppermute | solution.py:108
  144.1 29.4 %collective-permute-start.1 = (bf16[512,1152]{1,0:T(8,128)(2,1)S(1)}, bf16[512,1152]{1,0:T(8,128)(2,1)}, u32[]{:S(2)}, u32[]{:S(2)}) collective-permute-start(bf16[512,1152]{1,0:T(8,128)(2,1)S(1)} %get-tuple-element.51), channel_id=1, source_target_pairs={{0,16},{16,0},{1,17},{17,1},{2,18},{18,2},{3,19},{19,3},{4,20},{20... | collective-permute-start | bytes 3538952 | tf_op jit(solution)/shard_map/ppermute | solution.py:108
  146.9 123.6 %all-gather.11.cloned.1.call-start = ((), (), s32[]{:S(2)}) async-start(), calls=%async_computation.10 | async-start | bytes 2488320 | tf_op jit(solution)/shard_map/all_gather | solution.py:187
  172.0 18.0 %collective-permute-start.4 = (bf16[256,1152]{1,0:T(8,128)(2,1)S(1)}, bf16[256,1152]{1,0:T(8,128)(2,1)S(1)}, u32[]{:S(2)}, u32[]{:S(2)}) collective-permute-start(bf16[256,1152]{1,0:T(8,128)(2,1)S(1)} %slice.275), channel_id=1, source_target_pairs={{0,16},{16,0},{1,17},{17,1},{2,18},{18,2},{3,19},{19,3},{4,20},{20... | collective-permute-start | bytes 1769480 | tf_op jit(solution)/shard_map/ppermute | solution.py:108
  194.5 35.3 %collective-permute-start.5 = (bf16[2048,1152]{1,0:T(8,128)(2,1)}, bf16[2048,1152]{1,0:T(8,128)(2,1)}, u32[]{:S(2)}, u32[]{:S(2)}) collective-permute-start(bf16[2048,1152]{1,0:T(8,128)(2,1)} %get-tuple-element.88), channel_id=1, source_target_pairs={{0,1},{1,0},{2,3},{3,2},{4,5},{5,4},{6,7},{7,6},{8,9},{9,8},{10,11... | collective-permute-start | bytes 14155784 | tf_op jit(solution)/shard_map/ppermute | solution.py:108
  194.6 481.1 %reduce-scatter.15.cloned.1.call-start = ((), (), s32[]{:S(2)}) async-start(), calls=%async_computation.13 | async-start | bytes 2580480 | tf_op jit(solution)/shard_map/reduce_scatter | solution.py:255
  331.9 26.9 %collective-permute-start.10 = (bf16[512,1152]{1,0:T(8,128)(2,1)S(1)}, bf16[512,1152]{1,0:T(8,128)(2,1)S(1)}, u32[]{:S(2)}, u32[]{:S(2)}) collective-permute-start(bf16[512,1152]{1,0:T(8,128)(2,1)S(1)} %pad_maximum_fusion.2), channel_id=1, source_target_pairs={{0,2},{2,0},{1,3},{3,1},{4,6},{6,4},{5,7},{7,5},{8,10},{10,8},{9,1... | collective-permute-start | bytes 3538952 | tf_op jit(solution)/shard_map/ppermute | solution.py:108
  332.6 26.7 %collective-permute-start.8 = (bf16[512,1152]{1,0:T(8,128)(2,1)S(1)}, bf16[512,1152]{1,0:T(8,128)(2,1)S(1)}, u32[]{:S(2)}, u32[]{:S(2)}) collective-permute-start(bf16[512,1152]{1,0:T(8,128)(2,1)S(1)} %pad_maximum_fusion.1), channel_id=1, source_target_pairs={{0,16},{16,0},{1,17},{17,1},{2,18},{18,2},{3,19},{19,3},{4,20},{20... | collective-permute-start | bytes 3538952 | tf_op jit(solution)/shard_map/ppermute | solution.py:108
  364.7 25.8 %collective-permute-start.12 = (bf16[512,1152]{1,0:T(8,128)(2,1)S(1)}, bf16[512,1152]{1,0:T(8,128)(2,1)S(1)}, u32[]{:S(2)}, u32[]{:S(2)}) collective-permute-start(bf16[512,1152]{1,0:T(8,128)(2,1)S(1)} %get-tuple-element.45), channel_id=1, source_target_pairs={{0,2},{2,0},{1,3},{3,1},{4,6},{6,4},{5,7},{7,5},{8,10},{10,8},{9,1... | collective-permute-start | bytes 3538952 | tf_op jit(solution)/shard_map/ppermute | solution.py:108
  366.1 26.7 %collective-permute-start.11 = (bf16[512,1152]{1,0:T(8,128)(2,1)S(1)}, bf16[512,1152]{1,0:T(8,128)(2,1)S(1)}, u32[]{:S(2)}, u32[]{:S(2)}) collective-permute-start(bf16[512,1152]{1,0:T(8,128)(2,1)S(1)} %get-tuple-element.45), channel_id=1, source_target_pairs={{0,16},{16,0},{1,17},{17,1},{2,18},{18,2},{3,19},{19,3},{4,20},{20... | collective-permute-start | bytes 3538952 | tf_op jit(solution)/shard_map/ppermute | solution.py:108
  489.6 38.7 %collective-permute-start.16 = (bf16[2048,1152]{1,0:T(8,128)(2,1)}, bf16[2048,1152]{1,0:T(8,128)(2,1)}, u32[]{:S(2)}, u32[]{:S(2)}) collective-permute-start(bf16[2048,1152]{1,0:T(8,128)(2,1)} %slice.379), channel_id=1, source_target_pairs={{0,1},{1,0},{2,3},{3,2},{4,5},{5,4},{6,7},{7,6},{8,9},{9,8},{10,11... | collective-permute-start | bytes 14155784 | tf_op jit(solution)/shard_map/ppermute | solution.py:108
  508.5 182.3 %reduce-scatter.13.cloned.1.call-start = ((), (), s32[]{:S(2)}) async-start(), calls=%async_computation.12 | async-start | bytes 2580480 | tf_op jit(solution)/shard_map/reduce_scatter | solution.py:255
  528.2 180.0 %reduce-scatter.19.cloned.1.call-start = ((), (), s32[]{:S(2)}) async-start(), calls=%async_computation.16 | async-start | bytes 2488320
  541.4 15.6 %collective-permute-start.17 = (bf16[256,1152]{1,0:T(8,128)(2,1)S(1)}, bf16[256,1152]{1,0:T(8,128)(2,1)S(1)}, u32[]{:S(2)}, u32[]{:S(2)}) collective-permute-start(bf16[256,1152]{1,0:T(8,128)(2,1)S(1)} %get-tuple-element.60), channel_id=1, source_target_pairs={{0,2},{2,0},{1,3},{3,1},{4,6},{6,4},{5,7},{7,5},{8,10},{10,8},{9,1... | collective-permute-start | bytes 1769480 | tf_op jit(solution)/shard_map/ppermute | solution.py:108
  542.5 15.4 %collective-permute-start.19 = (bf16[256,1152]{1,0:T(8,128)(2,1)S(1)}, bf16[256,1152]{1,0:T(8,128)(2,1)S(1)}, u32[]{:S(2)}, u32[]{:S(2)}) collective-permute-start(bf16[256,1152]{1,0:T(8,128)(2,1)S(1)} %get-tuple-element.61), channel_id=1, source_target_pairs={{0,16},{16,0},{1,17},{17,1},{2,18},{18,2},{3,19},{19,3},{4,20},{20... | collective-permute-start | bytes 1769480 | tf_op jit(solution)/shard_map/ppermute | solution.py:108
  561.0 27.6 %collective-permute-start.20 = (bf16[512,1152]{1,0:T(8,128)(2,1)}, bf16[512,1152]{1,0:T(8,128)(2,1)}, u32[]{:S(2)}, u32[]{:S(2)}) collective-permute-start(bf16[512,1152]{1,0:T(8,128)(2,1)} %pad_maximum_fusion.4), channel_id=1, source_target_pairs={{0,2},{2,0},{1,3},{3,1},{4,6},{6,4},{5,7},{7,5},{8,10},{10,8},{9,1... | collective-permute-start | bytes 3538952 | tf_op jit(solution)/shard_map/ppermute | solution.py:108
  562.9 27.4 %collective-permute-start.18 = (bf16[512,1152]{1,0:T(8,128)(2,1)}, bf16[512,1152]{1,0:T(8,128)(2,1)}, u32[]{:S(2)}, u32[]{:S(2)}) collective-permute-start(bf16[512,1152]{1,0:T(8,128)(2,1)} %pad_maximum_fusion.3), channel_id=1, source_target_pairs={{0,16},{16,0},{1,17},{17,1},{2,18},{18,2},{3,19},{19,3},{4,20},{20... | collective-permute-start | bytes 3538952 | tf_op jit(solution)/shard_map/ppermute | solution.py:108
  579.5 169.0 %reduce-scatter.11.cloned.1.call-start = ((), (), s32[]{:S(2)}) async-start(), calls=%async_computation.11 | async-start | bytes 2433024 | tf_op jit(solution)/shard_map/reduce_scatter | solution.py:271
  630.2 267.8 %reduce-scatter.17.cloned.1.call-start = ((), (), s32[]{:S(2)}) async-start(), calls=%async_computation.15 | async-start | bytes 4392960
  677.6 26.2 %all-to-all-start.2 = ((bf16[8,36,864]{2,1,0:T(8,128)(2,1)}), bf16[8,36,864]{2,1,0:T(8,128)(2,1)S(1)}, u32[]{:S(2)}, u32[]{:S(2)}) async-start(bf16[8,36,864]{2,1,0:T(8,128)(2,1)} %reshape.404), calls=%async_computation.5 | async-start | bytes 1146880 | tf_op jit(solution)/shard_map/all_to_all | solution.py:257
  (111 other events, 1157.0 us)
Sparse Core Ops, SparseCore 0:
  12.4 65.0 all-gather.12
  80.3 55.8 all-gather.6
Sparse Core Ops, SparseCore 1:
  147.0 78.4 all-gather.8
  226.9 42.3 all-gather.10
  508.6 40.5 reduce-scatter.14
  551.6 42.2 reduce-scatter.12
  596.2 45.7 reduce-scatter.18
  647.2 101.3 reduce-scatter.10
  750.8 147.1 reduce-scatter.16

commit v2 on v1

--- a/solution.py
+++ b/solution.py
@@ -129,6 +129,50 @@
     to_x = jnp.concatenate([to_x[:half] + top, to_x[half:]]).astype(BF)
     to_y = jnp.concatenate([to_y[:half], to_y[half:] + low]).astype(BF)
     return own + swap(to_x, "x").astype(F32) + swap(to_y, "y").astype(F32)
+
+
+def in_order(own, other, place):
+    both = jnp.concatenate([own[None], other[None], own[None]])
+    return lax.dynamic_slice_in_dim(both, place, 2, 0)
+
+
+def group_gather(own):
+    size = lax.axis_size("g")
+    parts = [own] + [
+        lax.ppermute(own, "g", [((i + k) % size, i) for i in range(size)]) for k in range(1, size)
+    ]
+    both = jnp.stack(parts + parts[:-1])
+    place = lax.axis_index("g")
+    return lax.dynamic_slice_in_dim(both, lax.rem(size - place, size), size, 0)
+
+
+def plane_weights(blocks):
+    x, y = lax.axis_index("x"), lax.axis_index("y")
+    half = blocks.shape[0] // 2
+    first, second = blocks[:half], blocks[half:]
+    first = in_order(first, swap(first, "x"), x)
+    second = in_order(second, swap(second, "y"), y)
+    first = in_order(first, swap(first, "y"), y)
+    second = in_order(second, swap(second, "x"), x)
+    first = first.transpose(1, 2, 0, 3, 4)
+    second = second.transpose(0, 2, 1, 3, 4)
+    return jnp.concatenate([first, second], axis=1)
+
+
+def fold(term, axis, dim):
+    place = lax.axis_index(axis)
+    mine = lax.dynamic_index_in_dim(term, place, dim, keepdims=False)
+    other = lax.dynamic_index_in_dim(term, 1 - place, dim, keepdims=False)
+    return (mine.astype(F32) + swap(other.astype(BF), axis).astype(F32)).astype(BF)
+
+
+def plane_terms(term):
+    half = term.shape[1] // 2
+    first = fold(fold(term[:, :half], "x", 0), "y", 1)
+    second = fold(fold(term[:, half:], "y", 2), "x", 0)
+    term = jnp.concatenate([first, second])
+    term = term.reshape(-1, term.shape[-1])
+    return lax.psum_scatter(term, "g", scatter_dimension=0, tiled=True)
 
 
 def on_device(
@@ -160,7 +204,6 @@
     hidden_own = hidden_all // members
     piece = hidden_own // groups
     q_cols, k_cols = w_query.shape[1], w_key.shape[1]
-    qkv_cols = q_cols + 2 * k_cols
     attn_scale = HEAD ** (-0.5)
 
     def gain_columns(d_gains, h_gains):
@@ -170,21 +213,36 @@
         block = jnp.stack(columns, axis=-1)
         return jnp.pad(block, ((0, 0), (0, 0), (0, 128 - len(columns))))
 
+    core = lax.axis_index("c")
+    half_cols = q_cols // 2 + k_cols + 128
     gains = gain_columns(
         [g[None] for g in (gain_attn_in, gain_attn_out, gain_mlp_in, gain_mlp_out)],
         [gain_query[None], gain_key[None]],
     )
-    packed = jnp.concatenate([w_query, w_key, w_value, gains[0]], axis=1)
-    packed = lax.all_gather(packed, ALL, axis=0)
-    w_o = lax.all_gather(w_out, ALL, axis=0, tiled=True)
-    gain_block = packed[:, :, qkv_cols:].astype(F32)
-    d_gains = gain_block[:, :, :4].reshape(width, 4).T
+    halves = jnp.stack(
+        [
+            jnp.concatenate([w_query[:, : q_cols // 2], w_key, gains[0]], axis=1),
+            jnp.concatenate([w_query[:, q_cols // 2 :], w_value, jnp.zeros_like(gains[0])], axis=1),
+        ]
+    )
+    mine = lax.dynamic_index_in_dim(halves, core, 0, keepdims=False)
+    other = lax.dynamic_index_in_dim(halves, 1 - core, 0, keepdims=False)
+    mine = in_order(mine, swap(other, "c"), core).reshape(2 * shard_rows, half_cols)
+    mine = plane_weights(group_gather(mine)).reshape(width, half_cols)
+    w_first, w_second = in_order(mine, swap(mine, "c"), core)
+    gain_block = w_first[:, q_cols // 2 + k_cols :].astype(F32)
+    d_gains = gain_block[:, :4].T
     g_attn_in, g_attn_out, g_mlp_in, g_mlp_out = (d_gains[i : i + 1] for i in range(4))
-    g_query = gain_block[:, :head_rows, 4].reshape(HEAD)
-    g_key = gain_block[:, :head_rows, 5].reshape(HEAD)
-    w_qkv = packed[:, :, :qkv_cols].reshape(width, qkv_cols)
-
-    down = lax.all_gather(w_down, "g", axis=0, tiled=True)
+    h_gains = gain_block[:, 4:6].reshape(devices, shard_rows, 2)[:, :head_rows]
+    g_query = h_gains[:, :, 0].reshape(HEAD)
+    g_key = h_gains[:, :, 1].reshape(HEAD)
+    w_first = w_first[:, : q_cols // 2 + k_cols]
+    w_second = w_second[:, : q_cols // 2 + k_cols]
+
+    down = lax.all_gather(jnp.concatenate([w_down, w_out]), "g", axis=0)
+    w_o = plane_weights(down[:, w_down.shape[0] :])
+    down = down[:, : w_down.shape[0]].reshape(-1, width)
+    w_o = in_order(w_o, swap(w_o, "c"), core).transpose(1, 2, 3, 0, 4, 5).reshape(q_cols, width)
 
     def spread(weight):
         cut = weight.reshape(shard_rows, 2, groups, members // 2, piece)
@@ -214,12 +272,13 @@
     grad_out = cotangent[0].astype(F32)
 
     normed = norm_gain(layer_in, g_attn_in).astype(BF)
-    qkv_raw = matmul(normed, w_qkv)
-    query_raw = qkv_raw[:, :q_cols]
-    key_raw = qkv_raw[:, q_cols : q_cols + k_cols]
+    raw_first = matmul(normed, w_first)
+    raw_second = matmul(normed, w_second)
+    query_raw = jnp.concatenate([raw_first[:, : q_cols // 2], raw_second[:, : q_cols // 2]], axis=1)
+    key_raw = raw_first[:, q_cols // 2 :]
     queries = prepare_query(query_raw, g_query, cosine_table, sine_table).astype(BF)
     keys = prepare_key(key_raw, g_key, cosine_table, sine_table).astype(BF)
-    values = qkv_raw[:, q_cols + k_cols :].astype(BF)
+    values = raw_second[:, q_cols // 2 :].astype(BF)
     key_value = jnp.concatenate([keys, values], axis=1)
     halo = lax.ppermute(key_value, ("g", "y", "c"), [(i, i + 1) for i in range(seq_size - 1)])
     key_pad = jnp.concatenate([halo[:, :k_cols], keys])
@@ -268,9 +327,9 @@
     _, pullback = jax.vjp(norm_gain, branch, g_attn_out)
     grad_branch, grad_gain_attn_out = pullback(grad_middle)
     grad_branch = grad_branch.astype(BF)
-    grad_w_out = lax.psum_scatter(
-        over_rows(attended, grad_branch).astype(BF), ALL, scatter_dimension=0, tiled=True
-    )
+    grad_w_out = over_rows(attended, grad_branch).astype(BF)
+    grad_w_out = grad_w_out.reshape(2, groups, 2, 2, w_out.shape[0], width)
+    grad_w_out = plane_terms(fold(grad_w_out, "c", 3))
     grad_attended = by_transpose(grad_branch, w_o).astype(BF)
     grad_queries, grad_key_pad, grad_value_pad = attend_backward(
         queries, key_pad, value_pad, allowed, log_total, grad_attended, attn_scale
@@ -290,9 +349,12 @@
         lambda raw, gain: prepare_query(raw, gain, cosine_table, sine_table), query_raw, g_query
     )
     grad_query_raw, grad_gain_query = pullback(grad_queries)
-    grad_qkv_raw = jnp.concatenate([grad_query_raw, grad_key_raw, grad_values], axis=1).astype(BF)
-    grad_w_qkv = over_rows(normed, grad_qkv_raw).astype(BF)
-    grad_normed = by_transpose(grad_qkv_raw, w_qkv)
+    grad_query_raw = grad_query_raw.astype(BF)
+    grad_first = jnp.concatenate([grad_query_raw[:, : q_cols // 2], grad_key_raw.astype(BF)], axis=1)
+    grad_second = jnp.concatenate([grad_query_raw[:, q_cols // 2 :], grad_values.astype(BF)], axis=1)
+    grad_w_first = over_rows(normed, grad_first).astype(BF)
+    grad_w_second = over_rows(normed, grad_second).astype(BF)
+    grad_normed = by_transpose(grad_first, w_first) + by_transpose(grad_second, w_second)
     _, pullback = jax.vjp(norm_gain, layer_in, g_attn_in)
     grad_from_attn, grad_gain_attn_in = pullback(grad_normed)
     grad_in = grad_middle + grad_from_attn
@@ -304,24 +366,36 @@
         ],
         [g.reshape(devices, head_rows) for g in (grad_gain_query, grad_gain_key)],
     ).astype(BF)
-    terms = jnp.concatenate([grad_w_qkv.reshape(devices, shard_rows, qkv_cols), terms], axis=2)
-    share = lax.psum_scatter(terms, ALL, scatter_dimension=0, tiled=True)[0].astype(F32)
+    terms = terms.reshape(width, 128)
+    terms = jnp.stack(
+        [
+            jnp.concatenate([grad_w_first, terms], axis=1),
+            jnp.concatenate([grad_w_second, jnp.zeros_like(terms)], axis=1),
+        ]
+    )
+    share = plane_terms(fold(terms, "c", 0).reshape(2, groups, 2, 2 * shard_rows, half_cols))
+    share = share.reshape(2, shard_rows, half_cols)
+    mine = lax.dynamic_index_in_dim(share, core, 0, keepdims=False)
+    other = lax.dynamic_index_in_dim(share, 1 - core, 0, keepdims=False)
+    first, second = in_order(mine, swap(other, "c"), core).astype(F32)
+    half = q_cols // 2
+    d_terms = first[:, half + k_cols :]
     return (
         layer_out.astype(BF)[None],
         grad_in.astype(BF)[None],
-        share[:, :q_cols],
-        share[:, q_cols : q_cols + k_cols],
-        share[:, q_cols + k_cols : qkv_cols],
+        jnp.concatenate([first[:, :half], second[:, :half]], axis=1),
+        first[:, half : half + k_cols],
+        second[:, half : half + k_cols],
         grad_w_out.astype(F32),
         grad_w_gate,
         grad_w_up,
         grad_down.astype(F32),
-        share[:, qkv_cols],
-        share[:, qkv_cols + 1],
-        share[:, qkv_cols + 2],
-        share[:, qkv_cols + 3],
-        share[:head_rows, qkv_cols + 4],
-        share[:head_rows, qkv_cols + 5],
+        d_terms[:, 0],
+        d_terms[:, 1],
+        d_terms[:, 2],
+        d_terms[:, 3],
+        d_terms[:head_rows, 4],
+        d_terms[:head_rows, 5],
     )
 
 

time: 919 us -> 820 us (0.89)
  the two profiles are of different devices: /device:TPU:0 before, /device:TPU:13 now
where the time goes in v2:
time: 820 us; the launch traced here: 805 us
  waiting for transfers between devices  264 us (32%)
  matrix products  207 us (25%)
  local copies, waits for them, and re-layouts  135 us (16%)
  other arithmetic  110 us (13%)
  starting transfers between devices  72.5 us (9%)
  between operations  16.6 us (2%)
    ppermute x42, waiting for transfers between devices, swap(): return lax.ppermute(array, axis, [(0, 1), (1, 0)])  166 us
    dot_general x6, matrix products, by_transpose(): lax.dot_general(left_side, right_side, (((1,), (1,)), ((), ())), preferre...  74.6 us
    dot_general x6, matrix products, matmul(): return jnp.dot(left_side, right_side, preferred_element_type=F32)  58.1 us
    dot_general x6, matrix products, over_rows(): lax.dot_general(left_side, right_side, (((0,), (0,)), ((), ())), preferre...  50 us
    unnamed x9, waiting for transfers between devices  44.4 us
    ppermute x42, starting transfers between devices, swap(): return lax.ppermute(array, axis, [(0, 1), (1, 0)])  41.4 us
    unnamed x227, local copies, waits for them, and re-layouts  31 us
    all_gather x1, waiting for transfers between devices, on_device(): both = lax.all_gather(sent, 'g', axis=0)  28.5 us
  transfers between devices with their start and end apart: 57, of which 28 were waited for; matrix products, arithmetic and copies ran while one was open for 32% of the time, Pallas kernels for 0%

profile of v2, /device:TPU:13, one launch (start us, length us, event | category | flops | bytes accessed | tf_op | source)
XLA Modules:
  0.0 805.3 jit_solution(12239532663098628269)
XLA Ops:
  33.0 9.5 %collective-permute-done.5 = bf16[2,2,72,896]{3,2,1,0:T(8,128)(2,1)S(1)} collective-permute-done((bf16[2,2,72,896]{3,2,1,0:T(8,128)(2,1)S(1)}, bf16[2,2,72,896]{3,2,1,0:T(8,128)(2,1)S(1)}, u32[]{:S(2)}, u32[]{:S(2)}) %collective-permute-start.5) | collective-permute-done | bytes 516128 | tf_op jit(solution)/shard_map/ppermute | solution.py:108
  144.9 22.6 %collective-permute-done.16 = bf16[512,1152]{1,0:T(8,128)(2,1)} collective-permute-done((bf16[512,1152]{1,0:T(8,128)(2,1)S(1)}, bf16[512,1152]{1,0:T(8,128)(2,1)}, u32[]{:S(2)}, u32[]{:S(2)}) %collective-permute-start.16) | collective-permute-done | bytes 1179680 | tf_op jit(solution)/shard_map/ppermute | solution.py:108
  193.7 28.5 %all-gather.4.cloned.1.call-done = bf16[4,2,288,864]{3,2,1,0:T(8,128)(2,1)} async-done(((bf16[1,2,288,864]{3,2,1,0:T(8,128)(2,1)}), bf16[4,2,288,864]{3,2,1,0:T(8,128)(2,1)}) %all-gather.4.cloned.1.call-update) | async-done | bytes 3981328 | tf_op jit(solution)/shard_map/all_gather | solution.py:254
  231.7 12.9 %fusion.158 = f32[4096,864]{0,1:T(8,128)} fusion(bf16[4096,1152]{1,0:T(8,128)(2,1)S(1)} %constant_dynamic-update-slice_fusion.7, bf16[1152,864]{1,0:T(8,128)(2,1)S(1)} %bitcast.359), kind=kOutput, calls=%fused_computation.405 | convolution fusion | flops 8153726976 | bytes 25583616 | tf_op jit(solution)/shard_map/dot_general | solution.py:49
  244.6 21.9 %multiply_convert_fusion.2 = (bf16[4096,864]{0,1:T(8,128)(2,1)}, f32[4096,864]{0,1:T(8,128)}) fusion(f32[4096,864]{0,1:T(8,128)} %fusion.158, bf16[4096,1152]{1,0:T(8,128)(2,1)} %copy-done.58, bf16[1152,864]{1,0:T(8,128)(2,1)} %bitcast.361), kind=kOutput, calls=%fused_computation.12 | convolution fusion | flops 8189116416 | bytes 46817280 | tf_op jit(solution)/shard_map/dot_general | solution.py:49
  266.5 17.6 %fusion.159 = f32[4096,1152]{1,0:T(8,128)} fusion(bf16[4096,864]{0,1:T(8,128)(2,1)} %get-tuple-element.138, bf16[864,1152]{1,0:T(8,128)(2,1)} %bitcast.364), kind=kOutput, calls=%fused_computation.406 | convolution fusion | flops 8153726976 | bytes 27942912 | tf_op jit(solution)/shard_map/dot_general | solution.py:49
  289.1 7.7 collective-permute-done.20
  296.7 11.2 %fusion.145 = (bf16[2048,1152]{1,0:T(8,128)(2,1)}, f32[2048,1152]{1,0:T(8,128)}) fusion(bf16[2048,1152]{1,0:T(8,128)(2,1)} %collective-permute-done.20, f32[4096,1152]{1,0:T(8,128)} %fusion.159), kind=kLoop, calls=%fused_computation.392 | loop fusion | flops 7077888 | bytes 28311552 | tf_op jit(solution)/shard_map/convert.56
  311.2 13.1 %collective-permute-done.21 = bf16[256,1152]{1,0:T(8,128)(2,1)S(1)} collective-permute-done((bf16[256,1152]{1,0:T(8,128)(2,1)S(1)}, bf16[256,1152]{1,0:T(8,128)(2,1)S(1)}, u32[]{:S(2)}, u32[]{:S(2)}) %collective-permute-start.21) | collective-permute-done | bytes 589856 | tf_op jit(solution)/shard_map/ppermute | solution.py:108
  328.9 23.7 %collective-permute-done.24 = bf16[512,1152]{1,0:T(8,128)(2,1)S(1)} collective-permute-done((bf16[512,1152]{1,0:T(8,128)(2,1)S(1)}, bf16[512,1152]{1,0:T(8,128)(2,1)S(1)}, u32[]{:S(2)}, u32[]{:S(2)}) %collective-permute-start.24) | collective-permute-done | bytes 1179680 | tf_op jit(solution)/shard_map/ppermute | solution.py:108
  360.4 23.1 %collective-permute-done.26 = bf16[512,1152]{1,0:T(8,128)(2,1)S(1)} collective-permute-done((bf16[512,1152]{1,0:T(8,128)(2,1)S(1)}, bf16[512,1152]{1,0:T(8,128)(2,1)S(1)}, u32[]{:S(2)}, u32[]{:S(2)}) %collective-permute-start.26) | collective-permute-done | bytes 1179680 | tf_op jit(solution)/shard_map/ppermute | solution.py:108
  386.0 9.8 %collective-permute-done.27 = bf16[256,1152]{1,0:T(8,128)(2,1)S(1)} collective-permute-done((bf16[256,1152]{1,0:T(8,128)(2,1)S(1)}, bf16[256,1152]{1,0:T(8,128)(2,1)S(1)}, u32[]{:S(2)}, u32[]{:S(2)}) %collective-permute-start.27) | collective-permute-done | bytes 589856 | tf_op jit(solution)/shard_map/ppermute | solution.py:108
  412.9 27.0 %multiply_convert_fusion = (bf16[4096,864]{0,1:T(8,128)(2,1)S(1)}, bf16[4096,864]{0,1:T(8,128)(2,1)}) fusion(f32[4096,864]{0,1:T(8,128)} %fusion.158, f32[4096,864]{0,1:T(8,128)} %get-tuple-element.139, bf16[4096,1152]{1,0:T(8,128)(2,1)} %copy-done.59, bf16[864,1152]{1,0:T(8,128)(2,1)S(1)} %bitcast.365), kind=kOutput, calls=%fused_computation.10 | convolution fusion | flops 8252817408 | bytes 53895168 | tf_op jit(solution)/shard_map/dot_general | solution.py:59
  442.7 14.5 %convolution_convert_fusion.1 = bf16[1152,864]{0,1:T(8,128)(2,1)} fusion(bf16[4096,864]{0,1:T(8,128)(2,1)S(1)} %get-tuple-element.52, bf16[4096,1152]{1,0:T(8,128)(2,1)} %copy-done.58), kind=kOutput, calls=%fused_computation.62 | convolution fusion | flops 8154722304 | bytes 18505728 | tf_op jit(solution)/shard_map/dot_general | solution.py:53
  461.7 17.5 %fusion.160 = f32[4096,1152]{1,0:T(8,128)} fusion(bf16[4096,864]{0,1:T(8,128)(2,1)} %get-tuple-element.53, bf16[1152,864]{1,0:T(8,128)(2,1)} %bitcast.360), kind=kOutput, calls=%fused_computation.407 | convolution fusion | flops 8153726976 | bytes 27942912 | tf_op jit(solution)/shard_map/dot_general | solution.py:59
  479.2 21.5 %convolution_add_fusion = f32[4096,1152]{1,0:T(8,128)} fusion(f32[4096,1152]{1,0:T(8,128)} %fusion.160, bf16[4096,864]{0,1:T(8,128)(2,1)} %copy-done.101, bf16[1152,864]{1,0:T(8,128)(2,1)S(1)} %bitcast.362), kind=kOutput, calls=%fused_computation.2 | convolution fusion | flops 8158445568 | bytes 46817280 | tf_op jit(solution)/shard_map/dot_general | solution.py:59
  507.5 15.3 %convolution_convert_fusion.2 = bf16[1152,864]{0,1:T(8,128)(2,1)} fusion(bf16[4096,864]{0,1:T(8,128)(2,1)} %get-tuple-element.53, bf16[4096,1152]{1,0:T(8,128)(2,1)} %copy-done.58), kind=kOutput, calls=%fused_computation.63 | convolution fusion | flops 8154722304 | bytes 18505728 | tf_op jit(solution)/shard_map/dot_general | solution.py:53
  527.2 14.9 %convolution_convert_fusion.3 = bf16[864,1152]{1,0:T(8,128)(2,1)} fusion(bf16[4096,864]{0,1:T(8,128)(2,1)} %get-tuple-element.138, bf16[4096,1152]{1,0:T(8,128)(2,1)} %copy-done.59), kind=kOutput, calls=%fused_computation.64 | convolution fusion | flops 8154722304 | bytes 18505728 | tf_op jit(solution)/shard_map/dot_general | solution.py:53
  542.2 11.3 %fusion.142 = (bf16[2048,1152]{1,0:T(8,128)(2,1)}, f32[2048,1152]{1,0:T(8,128)}) fusion(bf16[2048,1152]{1,0:T(8,128)(2,1)} %collective-permute-done.30, f32[4096,1152]{1,0:T(8,128)} %convolution_add_fusion), kind=kLoop, calls=%fused_computation.391 | loop fusion | flops 7077888 | bytes 28311552 | tf_op jit(solution)/shard_map/convert.48
  578.1 7.7 all-to-all-start.1
  586.6 26.3 %reduce-scatter.18.cloned.1.call-done = bf16[216,1152]{1,0:T(8,128)(2,1)} async-done(((bf16[864,1152]{1,0:T(8,128)(2,1)}), bf16[216,1152]{1,0:T(8,128)(2,1)}) %reduce-scatter.18.cloned.1.call-update) | async-done | bytes 497680
  731.2 10.6 %collective-permute-done.39 = bf16[2,2,72,896]{3,2,1,0:T(8,128)(2,1)S(1)} collective-permute-done((bf16[2,2,72,896]{3,2,1,0:T(8,128)(2,1)S(1)}, bf16[2,2,72,896]{3,2,1,0:T(8,128)(2,1)S(1)}, u32[]{:S(2)}, u32[]{:S(2)}) %collective-permute-start.39) | collective-permute-done | bytes 516128 | tf_op jit(solution)/shard_map/ppermute | solution.py:108
  753.3 18.0 %reduce-scatter.16.cloned.1.call-done = bf16[72,896]{1,0:T(8,128)(2,1)} async-done(((bf16[288,896]{1,0:T(8,128)(2,1)}), bf16[72,896]{1,0:T(8,128)(2,1)}) %reduce-scatter.16.cloned.1.call-update) | async-done | bytes 129040
  779.3 12.7 %reduce-scatter.10.cloned.1.call-done = bf16[32,1152]{1,0:T(8,128)(2,1)} async-done(((bf16[128,1152]{1,0:T(8,128)(2,1)}), bf16[32,1152]{1,0:T(8,128)(2,1)}) %reduce-scatter.10.cloned.1.call-update) | async-done | bytes 73744 | tf_op jit(solution)/shard_map/reduce_scatter | solution.py:175
  (555 shorter events, 390.1 us)
Async XLA Ops:
  7.2 103.8 %all-gather.6.cloned.1.call-start = ((), (), s32[]{:S(2)}) async-start(), calls=%async_computation.12 | async-start | bytes 2856960 | tf_op jit(solution)/shard_map/all_gather | solution.py:242
  44.1 22.7 %collective-permute-start.8 = (bf16[1152,896]{1,0:T(8,128)(2,1)S(1)}, bf16[1152,896]{1,0:T(8,128)(2,1)}, u32[]{:S(2)}, u32[]{:S(2)}) collective-permute-start(bf16[1152,896]{1,0:T(8,128)(2,1)S(1)} %bitcast.337), channel_id=1, source_target_pairs={{0,1},{1,0},{2,3},{3,2},{4,5},{5,4},{6,7},{7,6},{8,9},{9,8},{10,11... | collective-permute-start | bytes 6193160 | tf_op jit(solution)/shard_map/ppermute | solution.py:108
  58.0 84.4 %all-to-all-start = ((bf16[8,2,36,864]{3,1,2,0:T(2,128)(2,1)}), bf16[8,2,36,864]{3,1,2,0:T(2,128)(2,1)}, u32[]{:S(2)}, u32[]{:S(2)}) async-start(bf16[8,2,36,864]{3,1,2,0:T(2,128)(2,1)} %copy.317), calls=%async_computation | async-start | bytes 2064384 | tf_op jit(solution)/shard_map/all_to_all | solution.py:252
  63.2 159.0 %all-gather.4.cloned.1.call-start = ((), (), s32[]{:S(2)}) async-start(), calls=%async_computation.8 | async-start | bytes 5160960 | tf_op jit(solution)/shard_map/all_gather | solution.py:254
  139.8 27.7 %collective-permute-start.16 = (bf16[512,1152]{1,0:T(8,128)(2,1)S(1)}, bf16[512,1152]{1,0:T(8,128)(2,1)}, u32[]{:S(2)}, u32[]{:S(2)}) collective-permute-start(bf16[512,1152]{1,0:T(8,128)(2,1)S(1)} %get-tuple-element.49), channel_id=1, source_target_pairs={{0,2},{2,0},{1,3},{3,1},{4,6},{6,4},{5,7},{7,5},{8,10},{10,8},{9,1... | collective-permute-start | bytes 3538952 | tf_op jit(solution)/shard_map/ppermute | solution.py:108
  141.0 28.8 %collective-permute-start.15 = (bf16[512,1152]{1,0:T(8,128)(2,1)S(1)}, bf16[512,1152]{1,0:T(8,128)(2,1)}, u32[]{:S(2)}, u32[]{:S(2)}) collective-permute-start(bf16[512,1152]{1,0:T(8,128)(2,1)S(1)} %get-tuple-element.49), channel_id=1, source_target_pairs={{0,16},{16,0},{1,17},{17,1},{2,18},{18,2},{3,19},{19,3},{4,20},{20... | collective-permute-start | bytes 3538952 | tf_op jit(solution)/shard_map/ppermute | solution.py:108
  144.7 412.2 %reduce-scatter.14.cloned.1.call-start = ((), (), s32[]{:S(2)}) async-start(), calls=%async_computation.11 | async-start | bytes 2580480 | tf_op jit(solution)/shard_map/reduce_scatter | solution.py:314
  190.3 36.3 %collective-permute-start.19 = (bf16[2048,1152]{1,0:T(8,128)(2,1)}, bf16[2048,1152]{1,0:T(8,128)(2,1)}, u32[]{:S(2)}, u32[]{:S(2)}) collective-permute-start(bf16[2048,1152]{1,0:T(8,128)(2,1)} %get-tuple-element.107), channel_id=1, source_target_pairs={{0,1},{1,0},{2,3},{3,2},{4,5},{5,4},{6,7},{7,6},{8,9},{9,8},{10,11... | collective-permute-start | bytes 14155784 | tf_op jit(solution)/shard_map/ppermute | solution.py:108
  326.3 26.2 %collective-permute-start.24 = (bf16[512,1152]{1,0:T(8,128)(2,1)S(1)}, bf16[512,1152]{1,0:T(8,128)(2,1)S(1)}, u32[]{:S(2)}, u32[]{:S(2)}) collective-permute-start(bf16[512,1152]{1,0:T(8,128)(2,1)S(1)} %pad_maximum_fusion.4), channel_id=1, source_target_pairs={{0,2},{2,0},{1,3},{3,1},{4,6},{6,4},{5,7},{7,5},{8,10},{10,8},{9,1... | collective-permute-start | bytes 3538952 | tf_op jit(solution)/shard_map/ppermute | solution.py:108
  327.6 25.7 %collective-permute-start.22 = (bf16[512,1152]{1,0:T(8,128)(2,1)S(1)}, bf16[512,1152]{1,0:T(8,128)(2,1)S(1)}, u32[]{:S(2)}, u32[]{:S(2)}) collective-permute-start(bf16[512,1152]{1,0:T(8,128)(2,1)S(1)} %pad_maximum_fusion.3), channel_id=1, source_target_pairs={{0,16},{16,0},{1,17},{17,1},{2,18},{18,2},{3,19},{19,3},{4,20},{20... | collective-permute-start | bytes 3538952 | tf_op jit(solution)/shard_map/ppermute | solution.py:108
  358.7 24.8 %collective-permute-start.26 = (bf16[512,1152]{1,0:T(8,128)(2,1)S(1)}, bf16[512,1152]{1,0:T(8,128)(2,1)S(1)}, u32[]{:S(2)}, u32[]{:S(2)}) collective-permute-start(bf16[512,1152]{1,0:T(8,128)(2,1)S(1)} %get-tuple-element.43), channel_id=1, source_target_pairs={{0,2},{2,0},{1,3},{3,1},{4,6},{6,4},{5,7},{7,5},{8,10},{10,8},{9,1... | collective-permute-start | bytes 3538952 | tf_op jit(solution)/shard_map/ppermute | solution.py:108
  359.3 25.5 %collective-permute-start.25 = (bf16[512,1152]{1,0:T(8,128)(2,1)S(1)}, bf16[512,1152]{1,0:T(8,128)(2,1)S(1)}, u32[]{:S(2)}, u32[]{:S(2)}) collective-permute-start(bf16[512,1152]{1,0:T(8,128)(2,1)S(1)} %get-tuple-element.43), channel_id=1, source_target_pairs={{0,16},{16,0},{1,17},{17,1},{2,18},{18,2},{3,19},{19,3},{4,20},{20... | collective-permute-start | bytes 3538952 | tf_op jit(solution)/shard_map/ppermute | solution.py:108
  461.6 114.6 %reduce-scatter.12.cloned.1.call-start = ((), (), s32[]{:S(2)}) async-start(), calls=%async_computation.10 | async-start | bytes 2580480 | tf_op jit(solution)/shard_map/reduce_scatter | solution.py:314
  507.1 35.1 %collective-permute-start.30 = (bf16[2048,1152]{1,0:T(8,128)(2,1)}, bf16[2048,1152]{1,0:T(8,128)(2,1)}, u32[]{:S(2)}, u32[]{:S(2)}) collective-permute-start(bf16[2048,1152]{1,0:T(8,128)(2,1)} %slice.482), channel_id=1, source_target_pairs={{0,1},{1,0},{2,3},{3,2},{4,5},{5,4},{6,7},{7,6},{8,9},{9,8},{10,11... | collective-permute-start | bytes 14155784 | tf_op jit(solution)/shard_map/ppermute | solution.py:108
  527.2 85.7 %reduce-scatter.18.cloned.1.call-start = ((), (), s32[]{:S(2)}) async-start(), calls=%async_computation.14 | async-start | bytes 2488320
  558.9 19.2 %all-to-all-start.2 = ((bf16[8,36,864]{2,1,0:T(8,128)(2,1)}), bf16[8,36,864]{2,1,0:T(8,128)(2,1)S(1)}, u32[]{:S(2)}, u32[]{:S(2)}) async-start(bf16[8,36,864]{2,1,0:T(8,128)(2,1)} %reshape.438), calls=%async_computation.5 | async-start | bytes 1146880 | tf_op jit(solution)/shard_map/all_to_all | solution.py:316
  573.5 55.8 %collective-permute-start.34 = (bf16[512,1152]{1,0:T(8,128)(2,1)}, bf16[512,1152]{1,0:T(8,128)(2,1)S(1)}, u32[]{:S(2)}, u32[]{:S(2)}) collective-permute-start(bf16[512,1152]{1,0:T(8,128)(2,1)} %pad_maximum_fusion.6), channel_id=1, source_target_pairs={{0,2},{2,0},{1,3},{3,1},{4,6},{6,4},{5,7},{7,5},{8,10},{10,8},{9,1... | collective-permute-start | bytes 3538952 | tf_op jit(solution)/shard_map/ppermute | solution.py:108
  575.7 53.6 %collective-permute-start.32 = (bf16[512,1152]{1,0:T(8,128)(2,1)}, bf16[512,1152]{1,0:T(8,128)(2,1)}, u32[]{:S(2)}, u32[]{:S(2)}) collective-permute-start(bf16[512,1152]{1,0:T(8,128)(2,1)} %pad_maximum_fusion.5), channel_id=1, source_target_pairs={{0,16},{16,0},{1,17},{17,1},{2,18},{18,2},{3,19},{19,3},{4,20},{20... | collective-permute-start | bytes 3538952 | tf_op jit(solution)/shard_map/ppermute | solution.py:108
  578.1 41.6 %all-to-all-start.1 = ((bf16[8,36,864]{2,1,0:T(8,128)(2,1)}), bf16[8,36,864]{2,1,0:T(8,128)(2,1)}, u32[]{:S(2)}, u32[]{:S(2)}) async-start(bf16[8,36,864]{2,1,0:T(8,128)(2,1)} %reshape.435), calls=%async_computation.3 | async-start | bytes 1146880 | tf_op jit(solution)/shard_map/all_to_all | solution.py:316
  585.8 185.4 %reduce-scatter.16.cloned.1.call-start = ((), (), s32[]{:S(2)}) async-start(), calls=%async_computation.13 | async-start | bytes 645120
  673.8 36.6 %collective-permute-start.42 = (bf16[2,4,2,32,1152]{4,3,2,1,0:T(8,128)(2,1)}, bf16[2,4,2,32,1152]{4,3,2,1,0:T(8,128)(2,1)}, u32[]{:S(2)}, u32[]{:S(2)}) collective-permute-start(bf16[2,4,2,32,1152]{4,3,2,1,0:T(8,128)(2,1)} %dynamic-slice_bitcast_fusion), channel_id=1, source_target_pairs={{0,1},{1,0},{2,3},{3,2},{4,5},{5,4},{6,7},{7,6},{8,9},{9,8},{10,11... | collective-permute-start | bytes 3538952 | tf_op jit(solution)/shard_map/ppermute | solution.py:108
  722.7 26.6 %collective-permute-start.46 = (bf16[2,32,1152]{2,1,0:T(8,128)(2,1)}, bf16[2,32,1152]{2,1,0:T(8,128)(2,1)}, u32[]{:S(2)}, u32[]{:S(2)}) collective-permute-start(bf16[2,32,1152]{2,1,0:T(8,128)(2,1)} %dynamic-slice_bitcast_fusion.5), channel_id=1, source_target_pairs={{0,16},{16,0},{1,17},{17,1},{2,18},{18,2},{3,19},{19,3},{4,20},{20... | collective-permute-start | bytes 442376 | tf_op jit(solution)/shard_map/ppermute | solution.py:108
  749.3 42.8 %reduce-scatter.10.cloned.1.call-start = ((), (), s32[]{:S(2)}) async-start(), calls=%async_computation.9 | async-start | bytes 368640 | tf_op jit(solution)/shard_map/reduce_scatter | solution.py:175
  774.4 19.2 %collective-permute-start.41 = (bf16[36,896]{1,0:T(8,128)(2,1)}, bf16[36,896]{1,0:T(8,128)(2,1)}, u32[]{:S(2)}, u32[]{:S(2)}) collective-permute-start(bf16[36,896]{1,0:T(8,128)(2,1)} %get-tuple-element.124), channel_id=1, source_target_pairs={{0,1},{1,0},{2,3},{3,2},{4,5},{5,4},{6,7},{7,6},{8,9},{9,8},{10,11... | collective-permute-start | bytes 193544 | tf_op jit(solution)/shard_map/ppermute | solution.py:108
  (137 other events, 1330.7 us)
Sparse Core Ops, SparseCore 0:
  48.3 50.5 all-gather.5
  144.8 77.3 all-gather.3
  461.7 41.0 reduce-scatter.13
  527.3 41.8 reduce-scatter.11
  571.4 41.4 reduce-scatter.17
  749.4 21.8 reduce-scatter.15
  773.6 18.3 reduce-scatter.9

commit v3 on v2

--- a/solution.py
+++ b/solution.py
@@ -1,6 +1,8 @@
 import jax
 import jax.numpy as jnp
 from jax import lax
+from jax.experimental import pallas as pl
+from jax.experimental.pallas import tpu as pltpu
 from jax.sharding import Mesh
 from jax.sharding import PartitionSpec as P
 
@@ -108,26 +110,178 @@
     return lax.ppermute(array, axis, [(0, 1), (1, 0)])
 
 
+GELU_A = 0.7978845608028654
+GELU_B = 0.044715
+TILE = 512
+PARAMS = pltpu.CompilerParams(vmem_limit_bytes=58 << 20)
+
+
+def whole_block(shape):
+    return pl.BlockSpec(shape, lambda i: (0,) * len(shape), pipeline_mode=pl.Buffered(1))
+
+
+def row_block(rows, columns):
+    return pl.BlockSpec((rows, columns), lambda i: (i, 0))
+
+
+def mlp_forward_kernel(normed, gate_up, down, hidden, gelu, slope, mixed):
+    own = down.shape[0]
+    raw = matmul(normed[...], gate_up[...])
+    gate_raw, up_raw = raw[:, :own], raw[:, own:]
+    square = gate_raw * gate_raw
+    bend = jnp.tanh(GELU_A * (gate_raw + GELU_B * square * gate_raw))
+    half = 0.5 + 0.5 * bend
+    active = gate_raw * half
+    turn = 0.5 * gate_raw * (1.0 - bend * bend) * (GELU_A * (1.0 + 3.0 * GELU_B * square))
+    low = (active * up_raw).astype(BF)
+    hidden[...] = low
+    gelu[...] = active.astype(BF)
+    slope[...] = ((half + turn) * up_raw).astype(BF)
+    mixed[...] = matmul(low, down[...]).astype(BF)
+
+
+def mlp_forward(normed, gate_up, down):
+    rows, width = normed.shape
+    own = down.shape[0]
+    flat = jax.ShapeDtypeStruct((rows, own), BF)
+    return pl.pallas_call(
+        mlp_forward_kernel,
+        grid=(rows // TILE,),
+        in_specs=[row_block(TILE, width), whole_block(gate_up.shape), whole_block(down.shape)],
+        out_specs=[row_block(TILE, own)] * 3 + [row_block(TILE, width)],
+        out_shape=[flat, flat, flat, jax.ShapeDtypeStruct((rows, width), BF)],
+        compiler_params=PARAMS,
+        cost_estimate=pl.CostEstimate(
+            flops=6 * rows * width * own, bytes_accessed=rows * (4 * width + 6 * own), transcendentals=0
+        ),
+    )(normed, gate_up, down)
+
+
+def mlp_backward_kernel(grad_mixed, gelu, slope, gate_up, down, grad_raw, grad_normed):
+    own = down.shape[0]
+    grad_hidden = by_transpose(grad_mixed[...], down[...])
+    grad_gate = (grad_hidden * slope[...].astype(F32)).astype(BF)
+    grad_up = (grad_hidden * gelu[...].astype(F32)).astype(BF)
+    grad_raw[:, :own] = grad_gate
+    grad_raw[:, own:] = grad_up
+    grad_normed[...] = (
+        by_transpose(grad_gate, gate_up[:, :own]) + by_transpose(grad_up, gate_up[:, own:])
+    ).astype(BF)
+
+
+def mlp_backward(grad_mixed, gelu, slope, gate_up, down):
+    rows, width = grad_mixed.shape
+    own = down.shape[0]
+    return pl.pallas_call(
+        mlp_backward_kernel,
+        grid=(rows // TILE,),
+        in_specs=[
+            row_block(TILE, width),
+            row_block(TILE, own),
+            row_block(TILE, own),
+            whole_block(gate_up.shape),
+            whole_block(down.shape),
+        ],
+        out_specs=[row_block(TILE, 2 * own), row_block(TILE, width)],
+        out_shape=[
+            jax.ShapeDtypeStruct((rows, 2 * own), BF),
+            jax.ShapeDtypeStruct((rows, width), BF),
+        ],
+        compiler_params=PARAMS,
+        cost_estimate=pl.CostEstimate(
+            flops=6 * rows * width * own, bytes_accessed=rows * (4 * width + 8 * own), transcendentals=0
+        ),
+    )(grad_mixed, gelu, slope, gate_up, down)
+
+
+def down_terms_kernel(*refs):
+    *ins, out = refs
+    half = len(ins) // 2
+    total = over_rows(ins[0][...], ins[half][...])
+    for left, right in zip(ins[1:half], ins[half + 1 :]):
+        total = total + over_rows(left[...], right[...])
+    out[...] = total.astype(BF)
+
+
+def down_terms(hidden, grad_mixed):
+    own, width = hidden[0].shape[1], grad_mixed[0].shape[1]
+    rows = sum(part.shape[0] for part in hidden)
+    return pl.pallas_call(
+        down_terms_kernel,
+        grid=(own // 128,),
+        in_specs=[pl.BlockSpec((part.shape[0], 128), lambda i: (0, i)) for part in hidden]
+        + [whole_block(part.shape) for part in grad_mixed],
+        out_specs=row_block(128, width),
+        out_shape=jax.ShapeDtypeStruct((own, width), BF),
+        compiler_params=PARAMS,
+        cost_estimate=pl.CostEstimate(
+            flops=2 * rows * width * own, bytes_accessed=2 * rows * (width + own), transcendentals=0
+        ),
+    )(*hidden, *grad_mixed)
+
+
+def gate_terms_kernel(*refs):
+    *ins, out = refs
+    half = len(ins) // 2
+    total = over_rows(ins[0][...], ins[half][...])
+    for left, right in zip(ins[1:half], ins[half + 1 :]):
+        total = total + over_rows(left[...], right[...])
+    total = total.astype(BF)
+    groups, sides, rows, _ = out.shape
+    for side in range(sides):
+        for group in range(groups):
+            first = (side * groups + group) * rows
+            out[group, side] = total[first : first + rows]
+
+
+def gate_terms(normed, grad_raw, groups):
+    width, both = normed[0].shape[1], grad_raw[0].shape[1]
+    rows = sum(part.shape[0] for part in normed)
+    shape = (groups, 2, width // (2 * groups))
+    return pl.pallas_call(
+        gate_terms_kernel,
+        grid=(both // 256,),
+        in_specs=[whole_block(part.shape) for part in normed]
+        + [pl.BlockSpec((part.shape[0], 256), lambda i: (0, i)) for part in grad_raw],
+        out_specs=pl.BlockSpec(shape + (256,), lambda i: (0, 0, 0, i)),
+        out_shape=jax.ShapeDtypeStruct(shape + (both,), BF),
+        compiler_params=PARAMS,
+        cost_estimate=pl.CostEstimate(
+            flops=2 * rows * width * both, bytes_accessed=2 * rows * (width + both), transcendentals=0
+        ),
+    )(*normed, *grad_raw)
+
+
+def with_core(part):
+    return jnp.concatenate([part, swap(part, "c")])
+
+
 def plane_gather(own):
     half = own.shape[0] // 2
     from_x = swap(own, "x")
     from_y = swap(own, "y")
     far_top = swap(from_x[:half], "y")
     far_low = swap(from_y[half:], "x")
-    mine = jnp.concatenate([own, from_x, from_y, far_top, far_low])
-    return jnp.concatenate([mine, swap(mine, "c")])
-
-
-def plane_reduce(parts):
-    rows = parts.shape[0] // 8
+    near = jnp.concatenate([from_x, from_y])
+    far = jnp.concatenate([far_top, far_low])
+    return [with_core(own), with_core(near), with_core(far)]
+
+
+def core_sum(part):
+    half = part.shape[0] // 2
+    return part[:half].astype(F32) + swap(part[half:], "c").astype(F32)
+
+
+def plane_reduce(own, near, far):
+    far = core_sum(far).astype(BF)
+    rows = far.shape[0]
     half = rows // 2
-    mine = parts[: 4 * rows].astype(F32) + swap(parts[4 * rows :].astype(BF), "c").astype(F32)
-    own, to_x, to_y, far = (mine[i * rows : (i + 1) * rows] for i in range(4))
-    far = far.astype(BF)
     top = swap(far[:half], "y").astype(F32)
     low = swap(far[half:], "x").astype(F32)
-    to_x = jnp.concatenate([to_x[:half] + top, to_x[half:]]).astype(BF)
-    to_y = jnp.concatenate([to_y[:half], to_y[half:] + low]).astype(BF)
+    near = core_sum(near)
+    to_x = jnp.concatenate([near[:half] + top, near[half:rows]]).astype(BF)
+    to_y = jnp.concatenate([near[rows : rows + half], near[rows + half :] + low]).astype(BF)
+    own = core_sum(own)
     return own + swap(to_x, "x").astype(F32) + swap(to_y, "y").astype(F32)
 
 
@@ -202,6 +356,7 @@
     head_rows = gain_query.shape[0]
     hidden_all = w_gate.shape[1]
     hidden_own = hidden_all // members
+    hidden_pad = -(-hidden_own // 128) * 128
     piece = hidden_own // groups
     q_cols, k_cols = w_query.shape[1], w_key.shape[1]
     attn_scale = HEAD ** (-0.5)
@@ -242,19 +397,20 @@
     down = lax.all_gather(jnp.concatenate([w_down, w_out]), "g", axis=0)
     w_o = plane_weights(down[:, w_down.shape[0] :])
     down = down[:, : w_down.shape[0]].reshape(-1, width)
+    down = jnp.pad(down, ((0, hidden_pad - hidden_own), (0, 0)))
     w_o = in_order(w_o, swap(w_o, "c"), core).transpose(1, 2, 3, 0, 4, 5).reshape(q_cols, width)
 
     def spread(weight):
         cut = weight.reshape(shard_rows, 2, groups, members // 2, piece)
-        return cut.transpose(1, 3, 0, 2, 4).reshape(members, shard_rows, hidden_own)
-
-    sent = jnp.stack([spread(w_gate), spread(w_up)], axis=1)
+        cut = cut.transpose(1, 3, 0, 2, 4).reshape(members, shard_rows, hidden_own)
+        return jnp.pad(cut, ((0, 0), (0, 0), (0, hidden_pad - hidden_own)))
+
+    sent = jnp.concatenate([spread(w_gate), spread(w_up)], axis=2)
     sent = lax.all_to_all(sent, PLANE, split_axis=0, concat_axis=0, tiled=True)
-    sent = sent.transpose(1, 0, 2, 3).reshape(2, members * shard_rows, hidden_own)
+    sent = sent.reshape(members * shard_rows, 2 * hidden_pad)
     both = lax.all_gather(sent, "g", axis=0)
-    both = both.reshape(groups, 2, 2, members // 2 * shard_rows, hidden_own)
-    gate = both[:, 0].transpose(1, 0, 2, 3).reshape(width, hidden_own)
-    up = both[:, 1].transpose(1, 0, 2, 3).reshape(width, hidden_own)
+    both = both.reshape(groups, 2, members // 2 * shard_rows, 2 * hidden_pad)
+    gate_up = both.transpose(1, 0, 2, 3).reshape(width, 2 * hidden_pad)
 
     seq_place = lax.axis_index(("g", "y", "c"))
     seq_size = lax.axis_size(("g", "y", "c"))
@@ -290,36 +446,31 @@
     normed_mlp = norm_gain(middle, g_mlp_in).astype(BF)
 
     normed_all = plane_gather(normed_mlp)
-    gate_raw = matmul(normed_all, gate)
-    up_raw = matmul(normed_all, up)
-    gelu, gelu_pull = jax.vjp(lambda u: jax.nn.gelu(u, approximate=True), gate_raw)
-    hidden = (gelu * up_raw).astype(BF)
-    slope = gelu_pull(up_raw)[0].astype(BF)
-    gelu = gelu.astype(BF)
-    mixed = plane_reduce(matmul(hidden, down))
+    results = [mlp_forward(part, gate_up, down) for part in normed_all]
+    mixed = plane_reduce(*(r[3] for r in results))
     layer_out = middle + norm_gain(mixed, g_mlp_out)
 
     _, pullback = jax.vjp(norm_gain, mixed, g_mlp_out)
     grad_mixed, grad_gain_mlp_out = pullback(grad_out)
     grad_mixed_all = plane_gather(grad_mixed.astype(BF))
-    grad_down = over_rows(hidden, grad_mixed_all).astype(BF)
+    grads = [
+        mlp_backward(part, r[1], r[2], gate_up, down) for part, r in zip(grad_mixed_all, results)
+    ]
+    grad_down = down_terms([r[0] for r in results], grad_mixed_all)[:hidden_own]
     grad_down = lax.psum_scatter(grad_down, "g", scatter_dimension=0, tiled=True)
-    grad_hidden = by_transpose(grad_mixed_all, down)
-    grad_gate = (grad_hidden * slope.astype(F32)).astype(BF)
-    grad_up = (grad_hidden * gelu.astype(F32)).astype(BF)
-
-    def collect(term):
-        term = term.astype(BF).reshape(2, groups, members // 2 * shard_rows, hidden_own)
-        term = term.transpose(1, 0, 2, 3).reshape(groups * members * shard_rows, hidden_own)
-        term = lax.psum_scatter(term, "g", scatter_dimension=0, tiled=True)
-        term = term.reshape(members, shard_rows, hidden_own)
-        term = lax.all_to_all(term, PLANE, split_axis=0, concat_axis=0, tiled=True)
-        term = term.reshape(2, members // 2, shard_rows, groups, piece)
-        return term.transpose(2, 0, 3, 1, 4).reshape(shard_rows, hidden_all).astype(F32)
-
-    grad_w_gate = collect(over_rows(normed_all, grad_gate))
-    grad_w_up = collect(over_rows(normed_all, grad_up))
-    grad_normed_mlp = plane_reduce(by_transpose(grad_gate, gate) + by_transpose(grad_up, up))
+    term = gate_terms(normed_all, [g[0] for g in grads], groups)
+    term = term.reshape(groups * members * shard_rows, 2 * hidden_pad)
+    term = lax.psum_scatter(term, "g", scatter_dimension=0, tiled=True)
+    term = term.reshape(members, shard_rows, 2 * hidden_pad)
+    term = lax.all_to_all(term, PLANE, split_axis=0, concat_axis=0, tiled=True)
+
+    def collect(cut):
+        cut = cut[:, :, :hidden_own].reshape(2, members // 2, shard_rows, groups, piece)
+        return cut.transpose(2, 0, 3, 1, 4).reshape(shard_rows, hidden_all).astype(F32)
+
+    grad_w_gate = collect(term[:, :, :hidden_pad])
+    grad_w_up = collect(term[:, :, hidden_pad:])
+    grad_normed_mlp = plane_reduce(*(g[1] for g in grads))
     _, pullback = jax.vjp(norm_gain, middle, g_mlp_in)
     grad_from_mlp, grad_gain_mlp_in = pullback(grad_normed_mlp)
     grad_middle = grad_out + grad_from_mlp

time: 820 us -> 814 us (level)
  matrix products: 207 us -> 43 us
  Pallas kernels: 0 us -> 138 us
  waiting for transfers between devices: 264 us -> 316 us
  local copies, waits for them, and re-layouts: 135 us -> 117 us
  starting transfers between devices: 72.5 us -> 64.3 us
    pallas_call x0 -> x8, Pallas kernels: none -> 138 us  [the longest x3 49 us: mlp_backward(): pl.pallas_call(mlp_backward_kernel, grid=(rows // TILE,), in_specs=[row_b...]
    dot_general x6 -> x3, matrix products: 74.6 us -> 8.87 us  [by_transpose(): lax.dot_general(left_side, right_side, (((1,), (1,)), ((), ())), preferre...]
    dot_general x6 -> x3, matrix products: 58.1 us -> 4.16 us  [matmul(): return jnp.dot(left_side, right_side, preferred_element_type=F32)]
    reduce_scatter x2 -> x1, waiting for transfers between devices: 0.01 us -> 52.4 us  [on_device(): term = lax.psum_scatter(term, 'g', scatter_dimension=0, tiled=True)]
    unnamed x9 -> x8, waiting for transfers between devices: 44.4 us -> 0.12 us
    dot_general x6 -> x3, matrix products: 50 us -> 6.97 us  [over_rows(): lax.dot_general(left_side, right_side, (((0,), (0,)), ((), ())), preferre...]
    ppermute x42 -> x50, waiting for transfers between devices: 166 us -> 202 us  [swap(): return lax.ppermute(array, axis, [(0, 1), (1, 0)])]
    all_gather x1, waiting for transfers between devices: 28.5 us -> 0.01 us  [on_device(): both = lax.all_gather(sent, 'g', axis=0)]
  transfers between devices with their start and end apart: 57 -> 63, of which waited for: 28 -> 36; matrix products, arithmetic and copies ran while one was open for 32% -> 21% of each run, Pallas kernels for 0% -> 17%
where the time goes in v3:
time: 814 us; the launch traced here: 798 us
  waiting for transfers between devices  316 us (39%)
  Pallas kernels  138 us (17%)
  local copies, waits for them, and re-layouts  117 us (14%)
  other arithmetic  103 us (13%)
  starting transfers between devices  64.3 us (8%)
  matrix products  43 us (5%)
  between operations  16.6 us (2%)
    ppermute x50, waiting for transfers between devices, swap(): return lax.ppermute(array, axis, [(0, 1), (1, 0)])  202 us
    reduce_scatter x1, waiting for transfers between devices, on_device(): term = lax.psum_scatter(term, 'g', scatter_dimension=0, tiled=True)  52.4 us
    pallas_call x3, Pallas kernels, mlp_backward(): pl.pallas_call(mlp_backward_kernel, grid=(rows // TILE,), in_specs=[row_b...  49 us
    pallas_call x3, Pallas kernels, mlp_forward(): pl.pallas_call(mlp_forward_kernel, grid=(rows // TILE,), in_specs=[row_bl...  48.1 us
    ppermute x50, starting transfers between devices, swap(): return lax.ppermute(array, axis, [(0, 1), (1, 0)])  38.3 us
    pallas_call x1, Pallas kernels, gate_terms(): pl.pallas_call(gate_terms_kernel, grid=(both // 256,), in_specs=[whole_bl...  24.4 us
    unnamed x229, local copies, waits for them, and re-layouts  21 us
  transfers between devices with their start and end apart: 63, of which 36 were waited for; matrix products, arithmetic and copies ran while one was open for 21% of the time, Pallas kernels for 17%

profile of v3, /device:TPU:13, one launch (start us, length us, event | category | flops | bytes accessed | tf_op | source)
XLA Modules:
  0.0 798.1 jit_solution(12574151611431791881)
XLA Ops:
  24.9 9.6 %collective-permute-done.3 = bf16[72,896]{1,0:T(8,128)(2,1)S(1)} collective-permute-done((bf16[72,896]{1,0:T(8,128)(2,1)S(1)}, bf16[72,896]{1,0:T(8,128)(2,1)S(1)}, u32[]{:S(2)}, u32[]{:S(2)}) %collective-permute-start.3) | collective-permute-done | bytes 129056 | tf_op jit(solution)/shard_map/ppermute | solution.py:296
  44.7 10.0 %collective-permute-done.5 = bf16[2,2,72,896]{3,2,1,0:T(8,128)(2,1)S(1)} collective-permute-done((bf16[2,2,72,896]{3,2,1,0:T(8,128)(2,1)S(1)}, bf16[2,2,72,896]{3,2,1,0:T(8,128)(2,1)S(1)}, u32[]{:S(2)}, u32[]{:S(2)}) %collective-permute-start.5) | collective-permute-done | bytes 516128 | tf_op jit(solution)/shard_map/ppermute | solution.py:110
  76.4 11.7 %all-to-all-done = bf16[8,36,1792]{2,1,0:T(8,128)(2,1)} async-done(((bf16[8,36,1792]{2,1,0:T(8,128)(2,1)}), bf16[8,36,1792]{2,1,0:T(8,128)(2,1)}, u32[]{:S(2)}, u32[]{:S(2)}) %all-to-all-start) | async-done | bytes 1032224 | tf_op jit(solution)/shard_map/all_to_all | solution.py:409
  139.3 16.1 %collective-permute-done.9 = bf16[512,512]{1,0:T(8,128)(2,1)} collective-permute-done((bf16[512,512]{1,0:T(8,128)(2,1)}, bf16[512,512]{1,0:T(8,128)(2,1)}, u32[]{:S(2)}, u32[]{:S(2)}) %collective-permute-start.9) | collective-permute-done | bytes 524320 | tf_op jit(solution)/shard_map/ppermute | solution.py:439
  178.9 26.6 %collective-permute-done.17 = bf16[512,1152]{1,0:T(8,128)(2,1)S(1)} collective-permute-done((bf16[512,1152]{1,0:T(8,128)(2,1)}, bf16[512,1152]{1,0:T(8,128)(2,1)S(1)}, u32[]{:S(2)}, u32[]{:S(2)}) %collective-permute-start.17) | collective-permute-done | bytes 1179680 | tf_op jit(solution)/shard_map/ppermute | solution.py:110
  210.1 14.0 %collective-permute-done.21 = bf16[256,1152]{1,0:T(8,128)(2,1)S(1)} collective-permute-done((bf16[256,1152]{1,0:T(8,128)(2,1)S(1)}, bf16[256,1152]{1,0:T(8,128)(2,1)S(1)}, u32[]{:S(2)}, u32[]{:S(2)}) %collective-permute-start.21) | collective-permute-done | bytes 589856 | tf_op jit(solution)/shard_map/ppermute | solution.py:110
  242.0 22.1 %shard_map.272 = (bf16[2048,896]{1,0:T(8,128)(2,1)}, bf16[2048,896]{1,0:T(8,128)(2,1)}, bf16[2048,896]{1,0:T(8,128)(2,1)}, bf16[2048,1152]{1,0:T(8,128)(2,1)}) custom-call(bf16[2048,1152]{1,0:T(8,128)(2,1)} %constant_dynamic-update-slice_fusion.2.normed.refs_1_, bf16[1152,1792]{1,0:T(8,128)(2,1)} %bitcast.311, bf16[896,1152]{1,0:T(8,128)(2,1)} %pad.54.down), custom_call_target="tpu_custom_call" | custom-call | flops 12683575296 | bytes 20447232 | tf_op jit(solution)/shard_map/pallas_call | solution.py:147
  266.5 12.9 %shard_map.273 = (bf16[1024,896]{1,0:T(8,128)(2,1)}, bf16[1024,896]{1,0:T(8,128)(2,1)}, bf16[1024,896]{1,0:T(8,128)(2,1)}, bf16[1024,1152]{1,0:T(8,128)(2,1)}) custom-call(bf16[1024,1152]{1,0:T(8,128)(2,1)} %constant_dynamic-update-slice_fusion.5.normed.refs_2_, bf16[1152,1792]{1,0:T(8,128)(2,1)} %bitcast.312, bf16[896,1152]{1,0:T(8,128)(2,1)} %pad.54.down), custom_call_target="tpu_custom_call" | custom-call | flops 6341787648 | bytes 10223616 | tf_op jit(solution)/shard_map/pallas_call | solution.py:147
  285.1 13.1 %shard_map.271 = (bf16[1024,896]{1,0:T(8,128)(2,1)}, bf16[1024,896]{1,0:T(8,128)(2,1)}, bf16[1024,896]{1,0:T(8,128)(2,1)}, bf16[1024,1152]{1,0:T(8,128)(2,1)}) custom-call(bf16[1024,1152]{1,0:T(8,128)(2,1)} %pad_maximum_fusion.normed.refs_0_, bf16[1152,1792]{1,0:T(8,128)(2,1)} %bitcast.313, bf16[896,1152]{1,0:T(8,128)(2,1)} %pad.54.down), custom_call_target="tpu_custom_call" | custom-call | flops 6341787648 | bytes 10223616 | tf_op jit(solution)/shard_map/pallas_call | solution.py:147
  307.4 9.1 %collective-permute-done.25 = bf16[256,1152]{1,0:T(8,128)(2,1)S(1)} collective-permute-done((bf16[256,1152]{1,0:T(8,128)(2,1)S(1)}, bf16[256,1152]{1,0:T(8,128)(2,1)S(1)}, u32[]{:S(2)}, u32[]{:S(2)}) %collective-permute-start.25) | collective-permute-done | bytes 589856 | tf_op jit(solution)/shard_map/ppermute | solution.py:110
  319.3 24.6 %collective-permute-done.26 = bf16[512,1152]{1,0:T(8,128)(2,1)S(1)} collective-permute-done((bf16[512,1152]{1,0:T(8,128)(2,1)S(1)}, bf16[512,1152]{1,0:T(8,128)(2,1)S(1)}, u32[]{:S(2)}, u32[]{:S(2)}) %collective-permute-start.26) | collective-permute-done | bytes 1179680 | tf_op jit(solution)/shard_map/ppermute | solution.py:110
  350.4 23.7 %collective-permute-done.31 = bf16[512,1152]{1,0:T(8,128)(2,1)S(1)} collective-permute-done((bf16[512,1152]{1,0:T(8,128)(2,1)}, bf16[512,1152]{1,0:T(8,128)(2,1)S(1)}, u32[]{:S(2)}, u32[]{:S(2)}) %collective-permute-start.31) | collective-permute-done | bytes 1179680 | tf_op jit(solution)/shard_map/ppermute | solution.py:110
  380.3 13.5 %collective-permute-done.35 = bf16[256,1152]{1,0:T(8,128)(2,1)S(1)} collective-permute-done((bf16[256,1152]{1,0:T(8,128)(2,1)S(1)}, bf16[256,1152]{1,0:T(8,128)(2,1)S(1)}, u32[]{:S(2)}, u32[]{:S(2)}) %collective-permute-start.35) | collective-permute-done | bytes 589856 | tf_op jit(solution)/shard_map/ppermute | solution.py:110
  402.9 22.0 %shard_map.275 = (bf16[2048,1792]{1,0:T(8,128)(2,1)}, bf16[2048,1152]{1,0:T(8,128)(2,1)}) custom-call(bf16[2048,1152]{1,0:T(8,128)(2,1)} %copy-done.57, bf16[2048,896]{1,0:T(8,128)(2,1)} %get-tuple-element.39.gelu, bf16[2048,896]{1,0:T(8,128)(2,1)} %get-tuple-element.40.slope, bf16[1152,1792]{1,0:T(8,128)(2,1)} %bitcast.314, bf16[896,1152]{1,0:T(8,128)(2,1)} %pad.54.down), custom_call_target="tpu_custom_call" | custom-call | flops 12683575296 | bytes 24117248 | tf_op jit(solution)/shard_map/pallas_call | solution.py:175
  428.6 13.6 %shard_map.276 = (bf16[1024,1792]{1,0:T(8,128)(2,1)}, bf16[1024,1152]{1,0:T(8,128)(2,1)}) custom-call(bf16[1024,1152]{1,0:T(8,128)(2,1)} %copy-done.60, bf16[1024,896]{1,0:T(8,128)(2,1)} %get-tuple-element.42.gelu, bf16[1024,896]{1,0:T(8,128)(2,1)} %get-tuple-element.43.slope, bf16[1152,1792]{1,0:T(8,128)(2,1)} %bitcast.315, bf16[896,1152]{1,0:T(8,128)(2,1)} %pad.54.down), custom_call_target="tpu_custom_call" | custom-call | flops 6341787648 | bytes 12058624 | tf_op jit(solution)/shard_map/pallas_call | solution.py:175
  447.0 13.5 %shard_map.274 = (bf16[1024,1792]{1,0:T(8,128)(2,1)}, bf16[1024,1152]{1,0:T(8,128)(2,1)}) custom-call(bf16[1024,1152]{1,0:T(8,128)(2,1)} %pad_maximum_fusion.2.grad_mixed.refs_3_, bf16[1024,896]{1,0:T(8,128)(2,1)} %get-tuple-element.36.gelu, bf16[1024,896]{1,0:T(8,128)(2,1)} %get-tuple-element.37.slope, bf16[1152,1792]{1,0:T(8,128)(2,1)} %bitcast.316, ...), custom_call_target="tpu_custom_call" | custom-call | flops 6341787648 | bytes 12058624 | tf_op jit(solution)/shard_map/pallas_call | solution.py:175
  469.1 9.7 %collective-permute-done.39 = bf16[256,1152]{1,0:T(8,128)(2,1)S(1)} collective-permute-done((bf16[256,1152]{1,0:T(8,128)(2,1)S(1)}, bf16[256,1152]{1,0:T(8,128)(2,1)S(1)}, u32[]{:S(2)}, u32[]{:S(2)}) %collective-permute-start.39) | collective-permute-done | bytes 589856 | tf_op jit(solution)/shard_map/ppermute | solution.py:110
  481.9 23.8 %collective-permute-done.40 = bf16[512,1152]{1,0:T(8,128)(2,1)S(1)} collective-permute-done((bf16[512,1152]{1,0:T(8,128)(2,1)S(1)}, bf16[512,1152]{1,0:T(8,128)(2,1)S(1)}, u32[]{:S(2)}, u32[]{:S(2)}) %collective-permute-start.40) | collective-permute-done | bytes 1179680 | tf_op jit(solution)/shard_map/ppermute | solution.py:110
  543.5 10.0 %collective-permute-done.43 = bf16[512,512]{1,0:T(8,128)(2,1)S(1)} collective-permute-done((bf16[512,512]{1,0:T(8,128)(2,1)S(1)}, bf16[512,512]{1,0:T(8,128)(2,1)S(1)}, u32[]{:S(2)}, u32[]{:S(2)}) %collective-permute-start.43) | collective-permute-done | bytes 524320 | tf_op jit(solution)/shard_map/ppermute | solution.py:488
  596.3 16.2 %shard_map.278 = bf16[896,1152]{1,0:T(8,128)(2,1)} custom-call(bf16[1024,896]{1,0:T(8,128)(2,1)} %get-tuple-element.48.refs_0_, bf16[2048,896]{1,0:T(8,128)(2,1)} %get-tuple-element.49.refs_1_, bf16[1024,896]{1,0:T(8,128)(2,1)} %get-tuple-element.50.refs_2_, bf16[1024,1152]{1,0:T(8,128)(2,1)} %pad_maximum_fusion.2.grad_mixed.refs_3_, ...), custom_call_target="tpu_custom_call" | custom-call | flops 8455716864 | bytes 16777216 | tf_op jit(solution)/shard_map/pallas_call | solution.py:209
  625.8 11.1 %collective-permute-done.45 = bf16[2,2,72,896]{3,2,0,1:T(8,128)(2,1)S(1)} collective-permute-done((bf16[2,2,72,896]{3,2,0,1:T(8,128)(2,1)}, bf16[2,2,72,896]{3,2,0,1:T(8,128)(2,1)S(1)}, u32[]{:S(2)}, u32[]{:S(2)}) %collective-permute-start.45) | collective-permute-done | bytes 516128 | tf_op jit(solution)/shard_map/ppermute | solution.py:110
  647.2 24.4 %shard_map.277 = bf16[4,2,144,1792]{3,2,1,0:T(8,128)(2,1)} custom-call(bf16[1024,1152]{1,0:T(8,128)(2,1)} %pad_maximum_fusion.normed.refs_0_, bf16[2048,1152]{1,0:T(8,128)(2,1)} %constant_dynamic-update-slice_fusion.2.normed.refs_1_, bf16[1024,1152]{1,0:T(8,128)(2,1)} %constant_dynamic-update-slice_fusion.5.normed.refs_2_, ...), custom_call_target="tpu_custom_call" | custom-call | flops 16911433728 | bytes 24117248 | tf_op jit(solution)/shard_map/pallas_call | solution.py:241
  704.4 52.4 %reduce-scatter.11.cloned.1.call-done = bf16[288,1792]{1,0:T(8,128)(2,1)} async-done(((bf16[1152,1792]{1,0:T(8,128)(2,1)}), bf16[288,1792]{1,0:T(8,128)(2,1)}) %reduce-scatter.11.cloned.1.call-update) | async-done | bytes 1032208 | tf_op jit(solution)/shard_map/reduce_scatter | solution.py:463
  767.3 8.8 %reduce-scatter.9.cloned.1.call-done = bf16[32,1152]{1,0:T(8,128)(2,1)} async-done(((bf16[128,1152]{1,0:T(8,128)(2,1)}), bf16[32,1152]{1,0:T(8,128)(2,1)}) %reduce-scatter.9.cloned.1.call-update) | async-done | bytes 73744 | tf_op jit(solution)/shard_map/reduce_scatter | solution.py:329
  (578 shorter events, 369.2 us)
Async XLA Ops:
  7.2 129.7 %all-gather.6.cloned.1.call-start = ((), (), s32[]{:S(2)}) async-start(), calls=%async_computation.9 | async-start | bytes 2856960 | tf_op jit(solution)/shard_map/all_gather | solution.py:397
  56.2 34.3 %collective-permute-start.8 = (bf16[1152,896]{1,0:T(8,128)(2,1)S(1)}, bf16[1152,896]{1,0:T(8,128)(2,1)}, u32[]{:S(2)}, u32[]{:S(2)}) collective-permute-start(bf16[1152,896]{1,0:T(8,128)(2,1)S(1)} %bitcast.300), channel_id=1, source_target_pairs={{0,1},{1,0},{2,3},{3,2},{4,5},{5,4},{6,7},{7,6},{8,9},{9,8},{10,11... | collective-permute-start | bytes 6193160 | tf_op jit(solution)/shard_map/ppermute | solution.py:110
  73.6 158.3 %all-gather.4.cloned.1.call-start = ((), (), s32[]{:S(2)}) async-start(), calls=%async_computation.6 | async-start | bytes 5160960 | tf_op jit(solution)/shard_map/all_gather | solution.py:411
  90.3 588.6 %reduce-scatter.15.cloned.1.call-start = ((), (), s32[]{:S(2)}) async-start(), calls=%async_computation.11 | async-start | bytes 2488320
  121.6 33.8 %collective-permute-start.9 = (bf16[512,512]{1,0:T(8,128)(2,1)}, bf16[512,512]{1,0:T(8,128)(2,1)}, u32[]{:S(2)}, u32[]{:S(2)}) collective-permute-start(bf16[512,512]{1,0:T(8,128)(2,1)} %pad_maximum_fusion.17), channel_id=1, source_target_pairs={{0,1},{1,2},{2,3},{3,4},{4,5},{5,6},{6,7},{7,8},{8,9},{9,10},{10,1... | collective-permute-start | bytes 1572872 | tf_op jit(solution)/shard_map/ppermute | solution.py:439
  138.0 25.3 %collective-permute-start.10 = (bf16[2,32,1152]{2,1,0:T(8,128)(2,1)S(1)}, bf16[2,32,1152]{2,1,0:T(8,128)(2,1)S(1)}, u32[]{:S(2)}, u32[]{:S(2)}) collective-permute-start(bf16[2,32,1152]{2,1,0:T(8,128)(2,1)S(1)} %get-tuple-element.96), channel_id=1, source_target_pairs={{0,16},{16,0},{1,17},{17,1},{2,18},{18,2},{3,19},{19,3},{4,20},{20... | collective-permute-start | bytes 442376 | tf_op jit(solution)/shard_map/ppermute | solution.py:110
  178.2 27.3 %collective-permute-start.17 = (bf16[512,1152]{1,0:T(8,128)(2,1)}, bf16[512,1152]{1,0:T(8,128)(2,1)S(1)}, u32[]{:S(2)}, u32[]{:S(2)}) collective-permute-start(bf16[512,1152]{1,0:T(8,128)(2,1)} %multiply_convert_fusion), channel_id=1, source_target_pairs={{0,16},{16,0},{1,17},{17,1},{2,18},{18,2},{3,19},{19,3},{4,20},{20... | collective-permute-start | bytes 3538952 | tf_op jit(solution)/shard_map/ppermute | solution.py:110
  178.9 27.0 %collective-permute-start.18 = (bf16[512,1152]{1,0:T(8,128)(2,1)}, bf16[512,1152]{1,0:T(8,128)(2,1)S(1)}, u32[]{:S(2)}, u32[]{:S(2)}) collective-permute-start(bf16[512,1152]{1,0:T(8,128)(2,1)} %multiply_convert_fusion), channel_id=1, source_target_pairs={{0,2},{2,0},{1,3},{3,1},{4,6},{6,4},{5,7},{7,5},{8,10},{10,8},{9,1... | collective-permute-start | bytes 3538952 | tf_op jit(solution)/shard_map/ppermute | solution.py:110
  207.4 31.3 %collective-permute-start.19 = (bf16[1024,1152]{1,0:T(8,128)(2,1)}, bf16[1024,1152]{1,0:T(8,128)(2,1)}, u32[]{:S(2)}, u32[]{:S(2)}) collective-permute-start(bf16[1024,1152]{1,0:T(8,128)(2,1)} %pad_maximum_fusion.1), channel_id=1, source_target_pairs={{0,1},{1,0},{2,3},{3,2},{4,5},{5,4},{6,7},{7,6},{8,9},{9,8},{10,11... | collective-permute-start | bytes 7077896 | tf_op jit(solution)/shard_map/ppermute | solution.py:110
  227.8 54.0 %collective-permute-start.15 = (bf16[512,1152]{1,0:T(8,128)(2,1)}, bf16[512,1152]{1,0:T(8,128)(2,1)}, u32[]{:S(2)}, u32[]{:S(2)}) collective-permute-start(bf16[512,1152]{1,0:T(8,128)(2,1)} %multiply_convert_fusion), channel_id=1, source_target_pairs={{0,1},{1,0},{2,3},{3,2},{4,5},{5,4},{6,7},{7,6},{8,9},{9,8},{10,11... | collective-permute-start | bytes 3538952 | tf_op jit(solution)/shard_map/ppermute | solution.py:110
  265.9 38.3 %collective-permute-start.20 = (bf16[1024,1152]{1,0:T(8,128)(2,1)S(1)}, bf16[1024,1152]{1,0:T(8,128)(2,1)}, u32[]{:S(2)}, u32[]{:S(2)}) collective-permute-start(bf16[1024,1152]{1,0:T(8,128)(2,1)S(1)} %slice.297), channel_id=1, source_target_pairs={{0,1},{1,0},{2,3},{3,2},{4,5},{5,4},{6,7},{7,6},{8,9},{9,8},{10,11... | collective-permute-start | bytes 7077896 | tf_op jit(solution)/shard_map/ppermute | solution.py:110
  317.9 25.9 %collective-permute-start.26 = (bf16[512,1152]{1,0:T(8,128)(2,1)S(1)}, bf16[512,1152]{1,0:T(8,128)(2,1)S(1)}, u32[]{:S(2)}, u32[]{:S(2)}) collective-permute-start(bf16[512,1152]{1,0:T(8,128)(2,1)S(1)} %pad_maximum_fusion.8), channel_id=1, source_target_pairs={{0,16},{16,0},{1,17},{17,1},{2,18},{18,2},{3,19},{19,3},{4,20},{20... | collective-permute-start | bytes 3538952 | tf_op jit(solution)/shard_map/ppermute | solution.py:110
  318.9 25.7 %collective-permute-start.28 = (bf16[512,1152]{1,0:T(8,128)(2,1)S(1)}, bf16[512,1152]{1,0:T(8,128)(2,1)S(1)}, u32[]{:S(2)}, u32[]{:S(2)}) collective-permute-start(bf16[512,1152]{1,0:T(8,128)(2,1)S(1)} %pad_maximum_fusion.9), channel_id=1, source_target_pairs={{0,2},{2,0},{1,3},{3,1},{4,6},{6,4},{5,7},{7,5},{8,10},{10,8},{9,1... | collective-permute-start | bytes 3538952 | tf_op jit(solution)/shard_map/ppermute | solution.py:110
  349.2 24.9 %collective-permute-start.31 = (bf16[512,1152]{1,0:T(8,128)(2,1)}, bf16[512,1152]{1,0:T(8,128)(2,1)S(1)}, u32[]{:S(2)}, u32[]{:S(2)}) collective-permute-start(bf16[512,1152]{1,0:T(8,128)(2,1)} %get-tuple-element.90), channel_id=1, source_target_pairs={{0,16},{16,0},{1,17},{17,1},{2,18},{18,2},{3,19},{19,3},{4,20},{20... | collective-permute-start | bytes 3538952 | tf_op jit(solution)/shard_map/ppermute | solution.py:110
  349.8 24.6 %collective-permute-start.32 = (bf16[512,1152]{1,0:T(8,128)(2,1)}, bf16[512,1152]{1,0:T(8,128)(2,1)S(1)}, u32[]{:S(2)}, u32[]{:S(2)}) collective-permute-start(bf16[512,1152]{1,0:T(8,128)(2,1)} %get-tuple-element.90), channel_id=1, source_target_pairs={{0,2},{2,0},{1,3},{3,1},{4,6},{6,4},{5,7},{7,5},{8,10},{10,8},{9,1... | collective-permute-start | bytes 3538952 | tf_op jit(solution)/shard_map/ppermute | solution.py:110
  374.6 25.8 %collective-permute-start.33 = (bf16[1024,1152]{1,0:T(8,128)(2,1)S(1)}, bf16[1024,1152]{1,0:T(8,128)(2,1)S(1)}, u32[]{:S(2)}, u32[]{:S(2)}) collective-permute-start(bf16[1024,1152]{1,0:T(8,128)(2,1)S(1)} %pad_maximum_fusion.3), channel_id=1, source_target_pairs={{0,1},{1,0},{2,3},{3,2},{4,5},{5,4},{6,7},{7,6},{8,9},{9,8},{10,11... | collective-permute-start | bytes 7077896 | tf_op jit(solution)/shard_map/ppermute | solution.py:110
  395.4 48.5 %collective-permute-start.29 = (bf16[512,1152]{1,0:T(8,128)(2,1)}, bf16[512,1152]{1,0:T(8,128)(2,1)}, u32[]{:S(2)}, u32[]{:S(2)}) collective-permute-start(bf16[512,1152]{1,0:T(8,128)(2,1)} %get-tuple-element.90), channel_id=1, source_target_pairs={{0,1},{1,0},{2,3},{3,2},{4,5},{5,4},{6,7},{7,6},{8,9},{9,8},{10,11... | collective-permute-start | bytes 3538952 | tf_op jit(solution)/shard_map/ppermute | solution.py:110
  428.2 37.7 %collective-permute-start.34 = (bf16[1024,1152]{1,0:T(8,128)(2,1)}, bf16[1024,1152]{1,0:T(8,128)(2,1)}, u32[]{:S(2)}, u32[]{:S(2)}) collective-permute-start(bf16[1024,1152]{1,0:T(8,128)(2,1)} %slice.312), channel_id=1, source_target_pairs={{0,1},{1,0},{2,3},{3,2},{4,5},{5,4},{6,7},{7,6},{8,9},{9,8},{10,11... | collective-permute-start | bytes 7077896 | tf_op jit(solution)/shard_map/ppermute | solution.py:110
  479.7 26.0 %collective-permute-start.40 = (bf16[512,1152]{1,0:T(8,128)(2,1)S(1)}, bf16[512,1152]{1,0:T(8,128)(2,1)S(1)}, u32[]{:S(2)}, u32[]{:S(2)}) collective-permute-start(bf16[512,1152]{1,0:T(8,128)(2,1)S(1)} %pad_maximum_fusion.11), channel_id=1, source_target_pairs={{0,16},{16,0},{1,17},{17,1},{2,18},{18,2},{3,19},{19,3},{4,20},{20... | collective-permute-start | bytes 3538952 | tf_op jit(solution)/shard_map/ppermute | solution.py:110
  480.7 25.7 %collective-permute-start.42 = (bf16[512,1152]{1,0:T(8,128)(2,1)S(1)}, bf16[512,1152]{1,0:T(8,128)(2,1)S(1)}, u32[]{:S(2)}, u32[]{:S(2)}) collective-permute-start(bf16[512,1152]{1,0:T(8,128)(2,1)S(1)} %pad_maximum_fusion.12), channel_id=1, source_target_pairs={{0,2},{2,0},{1,3},{3,1},{4,6},{6,4},{5,7},{7,5},{8,10},{10,8},{9,1... | collective-permute-start | bytes 3538952 | tf_op jit(solution)/shard_map/ppermute | solution.py:110
  615.5 83.5 %reduce-scatter.13.cloned.1.call-start = ((), (), s32[]{:S(2)}) async-start(), calls=%async_computation.10 | async-start | bytes 645120
  647.1 109.7 %reduce-scatter.11.cloned.1.call-start = ((), (), s32[]{:S(2)}) async-start(), calls=%async_computation.8 | async-start | bytes 5160960 | tf_op jit(solution)/shard_map/reduce_scatter | solution.py:463
  671.6 104.5 %reduce-scatter.9.cloned.1.call-start = ((), (), s32[]{:S(2)}) async-start(), calls=%async_computation.7 | async-start | bytes 368640 | tf_op jit(solution)/shard_map/reduce_scatter | solution.py:329
  702.3 75.3 %collective-permute-start.49 = (bf16[36,896]{1,0:T(8,128)(2,1)}, bf16[36,896]{1,0:T(8,128)(2,1)}, u32[]{:S(2)}, u32[]{:S(2)}) collective-permute-start(bf16[36,896]{1,0:T(8,128)(2,1)} %get-tuple-element.139), channel_id=1, source_target_pairs={{0,1},{1,0},{2,3},{3,2},{4,5},{5,4},{6,7},{7,6},{8,9},{9,8},{10,11... | collective-permute-start | bytes 193544 | tf_op jit(solution)/shard_map/ppermute | solution.py:110
  (144 other events, 1383.6 us)
Sparse Core Ops, SparseCore 0:
  15.2 49.6 all-gather.5
  90.4 83.3 all-gather.3
  615.6 40.0 reduce-scatter.14
  658.4 17.9 reduce-scatter.12
  678.7 78.1 reduce-scatter.10
  759.6 16.4 reduce-scatter.8

commit v4 on v3

--- a/solution.py
+++ b/solution.py
@@ -124,7 +124,7 @@
     return pl.BlockSpec((rows, columns), lambda i: (i, 0))
 
 
-def mlp_forward_kernel(normed, gate_up, down, hidden, gelu, slope, mixed):
+def mlp_forward_kernel(normed, gate_up, down, _, hidden, gelu, slope, mixed):
     own = down.shape[0]
     raw = matmul(normed[...], gate_up[...])
     gate_raw, up_raw = raw[:, :own], raw[:, own:]
@@ -140,24 +140,29 @@
     mixed[...] = matmul(low, down[...]).astype(BF)
 
 
-def mlp_forward(normed, gate_up, down):
+def mlp_forward(normed, gate_up, down, earlier):
     rows, width = normed.shape
     own = down.shape[0]
     flat = jax.ShapeDtypeStruct((rows, own), BF)
     return pl.pallas_call(
         mlp_forward_kernel,
         grid=(rows // TILE,),
-        in_specs=[row_block(TILE, width), whole_block(gate_up.shape), whole_block(down.shape)],
+        in_specs=[
+            row_block(TILE, width),
+            whole_block(gate_up.shape),
+            whole_block(down.shape),
+            pl.BlockSpec(memory_space=pl.ANY),
+        ],
         out_specs=[row_block(TILE, own)] * 3 + [row_block(TILE, width)],
         out_shape=[flat, flat, flat, jax.ShapeDtypeStruct((rows, width), BF)],
         compiler_params=PARAMS,
         cost_estimate=pl.CostEstimate(
             flops=6 * rows * width * own, bytes_accessed=rows * (4 * width + 6 * own), transcendentals=0
         ),
-    )(normed, gate_up, down)
-
-
-def mlp_backward_kernel(grad_mixed, gelu, slope, gate_up, down, grad_raw, grad_normed):
+    )(normed, gate_up, down, earlier)
+
+
+def mlp_backward_kernel(grad_mixed, gelu, slope, gate_up, down, _, grad_raw, grad_normed):
     own = down.shape[0]
     grad_hidden = by_transpose(grad_mixed[...], down[...])
     grad_gate = (grad_hidden * slope[...].astype(F32)).astype(BF)
@@ -169,7 +174,7 @@
     ).astype(BF)
 
 
-def mlp_backward(grad_mixed, gelu, slope, gate_up, down):
+def mlp_backward(grad_mixed, gelu, slope, gate_up, down, earlier):
     rows, width = grad_mixed.shape
     own = down.shape[0]
     return pl.pallas_call(
@@ -181,6 +186,7 @@
             row_block(TILE, own),
             whole_block(gate_up.shape),
             whole_block(down.shape),
+            pl.BlockSpec(memory_space=pl.ANY),
         ],
         out_specs=[row_block(TILE, 2 * own), row_block(TILE, width)],
         out_shape=[
@@ -191,7 +197,7 @@
         cost_estimate=pl.CostEstimate(
             flops=6 * rows * width * own, bytes_accessed=rows * (4 * width + 8 * own), transcendentals=0
         ),
-    )(grad_mixed, gelu, slope, gate_up, down)
+    )(grad_mixed, gelu, slope, gate_up, down, earlier)
 
 
 def down_terms_kernel(*refs):
@@ -252,6 +258,10 @@
     )(*normed, *grad_raw)
 
 
+def after(value, *earlier):
+    return lax.optimization_barrier((value, *earlier))[0]
+
+
 def with_core(part):
     return jnp.concatenate([part, swap(part, "c")])
 
@@ -320,12 +330,12 @@
     return (mine.astype(F32) + swap(other.astype(BF), axis).astype(F32)).astype(BF)
 
 
-def plane_terms(term):
+def plane_terms(term, earlier):
     half = term.shape[1] // 2
     first = fold(fold(term[:, :half], "x", 0), "y", 1)
     second = fold(fold(term[:, half:], "y", 2), "x", 0)
     term = jnp.concatenate([first, second])
-    term = term.reshape(-1, term.shape[-1])
+    term = after(term.reshape(-1, term.shape[-1]), earlier)
     return lax.psum_scatter(term, "g", scatter_dimension=0, tiled=True)
 
 
@@ -368,6 +378,14 @@
         block = jnp.stack(columns, axis=-1)
         return jnp.pad(block, ((0, 0), (0, 0), (0, 128 - len(columns))))
 
+    def spread(weight):
+        cut = weight.reshape(shard_rows, 2, groups, members // 2, piece)
+        cut = cut.transpose(1, 3, 0, 2, 4).reshape(members, shard_rows, hidden_own)
+        return jnp.pad(cut, ((0, 0), (0, 0), (0, hidden_pad - hidden_own)))
+
+    sent = jnp.concatenate([spread(w_gate), spread(w_up)], axis=2)
+    sent = lax.all_to_all(sent, PLANE, split_axis=0, concat_axis=0, tiled=True)
+    sent = sent.reshape(members * shard_rows, 2 * hidden_pad)
     core = lax.axis_index("c")
     half_cols = q_cols // 2 + k_cols + 128
     gains = gain_columns(
@@ -383,7 +401,8 @@
     mine = lax.dynamic_index_in_dim(halves, core, 0, keepdims=False)
     other = lax.dynamic_index_in_dim(halves, 1 - core, 0, keepdims=False)
     mine = in_order(mine, swap(other, "c"), core).reshape(2 * shard_rows, half_cols)
-    mine = plane_weights(group_gather(mine)).reshape(width, half_cols)
+    mine, sent = lax.optimization_barrier((group_gather(mine), sent))
+    mine = plane_weights(mine).reshape(width, half_cols)
     w_first, w_second = in_order(mine, swap(mine, "c"), core)
     gain_block = w_first[:, q_cols // 2 + k_cols :].astype(F32)
     d_gains = gain_block[:, :4].T
@@ -400,14 +419,6 @@
     down = jnp.pad(down, ((0, hidden_pad - hidden_own), (0, 0)))
     w_o = in_order(w_o, swap(w_o, "c"), core).transpose(1, 2, 3, 0, 4, 5).reshape(q_cols, width)
 
-    def spread(weight):
-        cut = weight.reshape(shard_rows, 2, groups, members // 2, piece)
-        cut = cut.transpose(1, 3, 0, 2, 4).reshape(members, shard_rows, hidden_own)
-        return jnp.pad(cut, ((0, 0), (0, 0), (0, hidden_pad - hidden_own)))
-
-    sent = jnp.concatenate([spread(w_gate), spread(w_up)], axis=2)
-    sent = lax.all_to_all(sent, PLANE, split_axis=0, concat_axis=0, tiled=True)
-    sent = sent.reshape(members * shard_rows, 2 * hidden_pad)
     both = lax.all_gather(sent, "g", axis=0)
     both = both.reshape(groups, 2, members // 2 * shard_rows, 2 * hidden_pad)
     gate_up = both.transpose(1, 0, 2, 3).reshape(width, 2 * hidden_pad)
@@ -446,21 +457,29 @@
     normed_mlp = norm_gain(middle, g_mlp_in).astype(BF)
 
     normed_all = plane_gather(normed_mlp)
-    results = [mlp_forward(part, gate_up, down) for part in normed_all]
+    far_result = mlp_forward(normed_all[2], gate_up, down, normed_all[2])
+    near_result = mlp_forward(normed_all[1], gate_up, down, far_result[3])
+    own_result = mlp_forward(normed_all[0], gate_up, down, near_result[3])
+    results = [own_result, near_result, far_result]
     mixed = plane_reduce(*(r[3] for r in results))
     layer_out = middle + norm_gain(mixed, g_mlp_out)
 
     _, pullback = jax.vjp(norm_gain, mixed, g_mlp_out)
     grad_mixed, grad_gain_mlp_out = pullback(grad_out)
     grad_mixed_all = plane_gather(grad_mixed.astype(BF))
-    grads = [
-        mlp_backward(part, r[1], r[2], gate_up, down) for part, r in zip(grad_mixed_all, results)
-    ]
+    grads = []
+    earlier = down
+    for part, result in zip(grad_mixed_all, results):
+        grads.append(mlp_backward(part, result[1], result[2], gate_up, down, earlier))
+        earlier = grads[-1][1]
     grad_down = down_terms([r[0] for r in results], grad_mixed_all)[:hidden_own]
+    grad_down_terms = grad_down
     grad_down = lax.psum_scatter(grad_down, "g", scatter_dimension=0, tiled=True)
     term = gate_terms(normed_all, [g[0] for g in grads], groups)
-    term = term.reshape(groups * members * shard_rows, 2 * hidden_pad)
+    gate_up_terms = term
+    term = after(term.reshape(groups * members * shard_rows, 2 * hidden_pad), grad_down)
     term = lax.psum_scatter(term, "g", scatter_dimension=0, tiled=True)
+    gate_up_share = term
     term = term.reshape(members, shard_rows, 2 * hidden_pad)
     term = lax.all_to_all(term, PLANE, split_axis=0, concat_axis=0, tiled=True)
 
@@ -471,6 +490,7 @@
     grad_w_gate = collect(term[:, :, :hidden_pad])
     grad_w_up = collect(term[:, :, hidden_pad:])
     grad_normed_mlp = plane_reduce(*(g[1] for g in grads))
+    grad_normed_mlp = after(grad_normed_mlp, grad_down_terms, gate_up_terms)
     _, pullback = jax.vjp(norm_gain, middle, g_mlp_in)
     grad_from_mlp, grad_gain_mlp_in = pullback(grad_normed_mlp)
     grad_middle = grad_out + grad_from_mlp
@@ -480,7 +500,7 @@
     grad_branch = grad_branch.astype(BF)
     grad_w_out = over_rows(attended, grad_branch).astype(BF)
     grad_w_out = grad_w_out.reshape(2, groups, 2, 2, w_out.shape[0], width)
-    grad_w_out = plane_terms(fold(grad_w_out, "c", 3))
+    grad_w_out = plane_terms(fold(grad_w_out, "c", 3), gate_up_share)
     grad_attended = by_transpose(grad_branch, w_o).astype(BF)
     grad_queries, grad_key_pad, grad_value_pad = attend_backward(
         queries, key_pad, value_pad, allowed, log_total, grad_attended, attn_scale
@@ -500,7 +520,7 @@
         lambda raw, gain: prepare_query(raw, gain, cosine_table, sine_table), query_raw, g_query
     )
     grad_query_raw, grad_gain_query = pullback(grad_queries)
-    grad_query_raw = grad_query_raw.astype(BF)
+    grad_query_raw = after(grad_query_raw.astype(BF), grad_down)
     grad_first = jnp.concatenate([grad_query_raw[:, : q_cols // 2], grad_key_raw.astype(BF)], axis=1)
     grad_second = jnp.concatenate([grad_query_raw[:, q_cols // 2 :], grad_values.astype(BF)], axis=1)
     grad_w_first = over_rows(normed, grad_first).astype(BF)
@@ -524,7 +544,8 @@
             jnp.concatenate([grad_w_second, jnp.zeros_like(terms)], axis=1),
         ]
     )
-    share = plane_terms(fold(terms, "c", 0).reshape(2, groups, 2, 2 * shard_rows, half_cols))
+    terms = fold(terms, "c", 0).reshape(2, groups, 2, 2 * shard_rows, half_cols)
+    share = plane_terms(terms, grad_w_out)
     share = share.reshape(2, shard_rows, half_cols)
     mine = lax.dynamic_index_in_dim(share, core, 0, keepdims=False)
     other = lax.dynamic_index_in_dim(share, 1 - core, 0, keepdims=False)

time: 814 us -> 714 us (0.88)
  waiting for transfers between devices: 316 us -> 217 us
    ppermute x50, waiting for transfers between devices: 202 us -> 136 us  [swap(): return lax.ppermute(array, axis, [(0, 1), (1, 0)])]
    reduce_scatter x1, waiting for transfers between devices: 52.4 us -> 4.95 us  [on_device(): term = lax.psum_scatter(term, 'g', scatter_dimension=0, tiled=True)]
    unnamed x8, waiting for transfers between devices: 0.12 us -> 17.2 us
    all_to_all x1, waiting for transfers between devices: 11.7 us -> 0.01 us  [on_device(): sent = lax.all_to_all(sent, PLANE, split_axis=0, concat_axis=0, tiled=True)]
    unnamed x229 -> x221, local copies, waits for them, and re-layouts: 21 us -> 26.4 us
  transfers between devices with their start and end apart: 63 -> 63, of which waited for: 36 -> 27; matrix products, arithmetic and copies ran while one was open for 21% -> 32% of each run, Pallas kernels for 17% -> 17%
where the time goes in v4:
time: 714 us; the launch traced here: 700 us
  waiting for transfers between devices  217 us (30%)
  Pallas kernels  139 us (19%)
  local copies, waits for them, and re-layouts  125 us (18%)
  other arithmetic  101 us (14%)
  starting transfers between devices  64.5 us (9%)
  matrix products  36.9 us (5%)
  between operations  16.7 us (2%)
    ppermute x50, waiting for transfers between devices, swap(): return lax.ppermute(array, axis, [(0, 1), (1, 0)])  136 us
    pallas_call x3, Pallas kernels, mlp_backward(): pl.pallas_call(mlp_backward_kernel, grid=(rows // TILE,), in_specs=[row_b...  49.2 us
    pallas_call x3, Pallas kernels, mlp_forward(): pl.pallas_call(mlp_forward_kernel, grid=(rows // TILE,), in_specs=[row_bl...  48.2 us
    ppermute x50, starting transfers between devices, swap(): return lax.ppermute(array, axis, [(0, 1), (1, 0)])  40.5 us
    unnamed x221, local copies, waits for them, and re-layouts  26.4 us
    pallas_call x1, Pallas kernels, gate_terms(): pl.pallas_call(gate_terms_kernel, grid=(both // 256,), in_specs=[whole_bl...  25 us
    ppermute x1, waiting for transfers between devices, on_device(): lax.ppermute(key_value, ('g', 'y', 'c'), [(i, i + 1) for i in range(seq_s...  22.1 us
    ppermute x3, waiting for transfers between devices, group_gather(): lax.ppermute(own, 'g', [((i + k) % size, i) for i in range(size)])  20.1 us
  transfers between devices with their start and end apart: 63, of which 27 were waited for; matrix products, arithmetic and copies ran while one was open for 32% of the time, Pallas kernels for 17%

profile of v4, /device:TPU:13, one launch (start us, length us, event | category | flops | bytes accessed | tf_op | source)
XLA Modules:
  0.0 699.9 jit_solution(18149238494349675779)
XLA Ops:
  30.1 5.7 collective-permute-done.1
  35.8 14.4 %collective-permute-done.2 = bf16[72,896]{1,0:T(8,128)(2,1)S(1)} collective-permute-done((bf16[72,896]{1,0:T(8,128)(2,1)S(1)}, bf16[72,896]{1,0:T(8,128)(2,1)S(1)}, u32[]{:S(2)}, u32[]{:S(2)}) %collective-permute-start.2) | collective-permute-done | bytes 129056 | tf_op jit(solution)/shard_map/ppermute | solution.py:306
  60.0 9.9 %collective-permute-done.5 = bf16[2,2,72,896]{3,2,1,0:T(8,128)(2,1)S(1)} collective-permute-done((bf16[2,2,72,896]{3,2,1,0:T(8,128)(2,1)S(1)}, bf16[2,2,72,896]{3,2,1,0:T(8,128)(2,1)S(1)}, u32[]{:S(2)}, u32[]{:S(2)}) %collective-permute-start.5) | collective-permute-done | bytes 516128 | tf_op jit(solution)/shard_map/ppermute | solution.py:110
  143.5 22.1 %collective-permute-done.9 = bf16[512,512]{1,0:T(8,128)(2,1)S(1)} collective-permute-done((bf16[512,512]{1,0:T(8,128)(2,1)S(1)}, bf16[512,512]{1,0:T(8,128)(2,1)S(1)}, u32[]{:S(2)}, u32[]{:S(2)}) %collective-permute-start.9) | collective-permute-done | bytes 524320 | tf_op jit(solution)/shard_map/ppermute | solution.py:450
  179.2 20.5 %collective-permute-done.17 = bf16[512,1152]{1,0:T(8,128)(2,1)S(1)} collective-permute-done((bf16[512,1152]{1,0:T(8,128)(2,1)S(1)}, bf16[512,1152]{1,0:T(8,128)(2,1)S(1)}, u32[]{:S(2)}, u32[]{:S(2)}) %collective-permute-start.17) | collective-permute-done | bytes 1179680 | tf_op jit(solution)/shard_map/ppermute | solution.py:110
  199.9 5.5 collective-permute-done.16
  207.1 6.0 collective-permute-done.20
  227.8 13.0 %shard_map.271 = (bf16[1024,896]{1,0:T(8,128)(2,1)}, bf16[1024,896]{1,0:T(8,128)(2,1)}, bf16[1024,896]{1,0:T(8,128)(2,1)}, bf16[1024,1152]{1,0:T(8,128)(2,1)}) custom-call(bf16[1024,1152]{1,0:T(8,128)(2,1)} %constant_dynamic-update-slice_fusion.5.normed._.refs_2_, bf16[1152,1792]{1,0:T(8,128)(2,1)} %bitcast.314, bf16[896,1152]{1,0:T(8,128)(2,1)} %pad.54.down._, ...), custom_call_target="tpu_custom_call" | custom-call | flops 6341787648 | bytes 10223616 | tf_op jit(solution)/shard_map/pallas_call | solution.py:147
  244.1 22.1 %shard_map.272 = (bf16[2048,896]{1,0:T(8,128)(2,1)}, bf16[2048,896]{1,0:T(8,128)(2,1)}, bf16[2048,896]{1,0:T(8,128)(2,1)}, bf16[2048,1152]{1,0:T(8,128)(2,1)}) custom-call(bf16[2048,1152]{1,0:T(8,128)(2,1)} %constant_dynamic-update-slice_fusion.2.normed.refs_1_, bf16[1152,1792]{1,0:T(8,128)(2,1)} %bitcast.315, bf16[896,1152]{1,0:T(8,128)(2,1)} %pad.54.down._, ...), custom_call_target="tpu_custom_call" | custom-call | flops 12683575296 | bytes 20447232 | tf_op jit(solution)/shard_map/pallas_call | solution.py:147
  274.1 13.1 %shard_map.273 = (bf16[1024,896]{1,0:T(8,128)(2,1)}, bf16[1024,896]{1,0:T(8,128)(2,1)}, bf16[1024,896]{1,0:T(8,128)(2,1)}, bf16[1024,1152]{1,0:T(8,128)(2,1)}) custom-call(bf16[1024,1152]{1,0:T(8,128)(2,1)} %pad_maximum_fusion.normed.refs_0_, bf16[1152,1792]{1,0:T(8,128)(2,1)} %bitcast.316, bf16[896,1152]{1,0:T(8,128)(2,1)} %pad.54.down._, ...), custom_call_target="tpu_custom_call" | custom-call | flops 6341787648 | bytes 10223616 | tf_op jit(solution)/shard_map/pallas_call | solution.py:147
  294.5 10.4 %collective-permute-done.25 = bf16[256,1152]{1,0:T(8,128)(2,1)S(1)} collective-permute-done((bf16[256,1152]{1,0:T(8,128)(2,1)S(1)}, bf16[256,1152]{1,0:T(8,128)(2,1)S(1)}, u32[]{:S(2)}, u32[]{:S(2)}) %collective-permute-start.25) | collective-permute-done | bytes 589856 | tf_op jit(solution)/shard_map/ppermute | solution.py:110
  307.4 23.9 %collective-permute-done.28 = bf16[512,1152]{1,0:T(8,128)(2,1)S(1)} collective-permute-done((bf16[512,1152]{1,0:T(8,128)(2,1)S(1)}, bf16[512,1152]{1,0:T(8,128)(2,1)S(1)}, u32[]{:S(2)}, u32[]{:S(2)}) %collective-permute-start.28) | collective-permute-done | bytes 1179680 | tf_op jit(solution)/shard_map/ppermute | solution.py:110
  340.8 20.1 %collective-permute-done.32 = bf16[512,1152]{1,0:T(8,128)(2,1)S(1)} collective-permute-done((bf16[512,1152]{1,0:T(8,128)(2,1)S(1)}, bf16[512,1152]{1,0:T(8,128)(2,1)S(1)}, u32[]{:S(2)}, u32[]{:S(2)}) %collective-permute-start.32) | collective-permute-done | bytes 1179680 | tf_op jit(solution)/shard_map/ppermute | solution.py:110
  381.5 13.5 %shard_map.274 = (bf16[1024,1792]{1,0:T(8,128)(2,1)}, bf16[1024,1152]{1,0:T(8,128)(2,1)}) custom-call(bf16[1024,1152]{1,0:T(8,128)(2,1)} %pad_maximum_fusion.2.grad_mixed.refs_3_, bf16[1024,896]{1,0:T(8,128)(2,1)} %get-tuple-element.45.gelu, bf16[1024,896]{1,0:T(8,128)(2,1)} %get-tuple-element.46.slope, bf16[1152,1792]{1,0:T(8,128)(2,1)} %bitcast.317, ...), custom_call_target="tpu_custom_call" | custom-call | flops 6341787648 | bytes 12058624 | tf_op jit(solution)/shard_map/pallas_call | solution.py:180
  402.8 22.2 %shard_map.275 = (bf16[2048,1792]{1,0:T(8,128)(2,1)}, bf16[2048,1152]{1,0:T(8,128)(2,1)}) custom-call(bf16[2048,1152]{1,0:T(8,128)(2,1)} %constant_dynamic-update-slice_fusion.8.grad_mixed.refs_4_, bf16[2048,896]{1,0:T(8,128)(2,1)} %get-tuple-element.48.gelu, bf16[2048,896]{1,0:T(8,128)(2,1)} %get-tuple-element.49.slope, bf16[1152,1792]{1,0:T(8,128)(2,1)} %bitcast.318, ...), custom_call_target="tpu_custom_call" | custom-call | flops 12683575296 | bytes 24117248 | tf_op jit(solution)/shard_map/pallas_call | solution.py:180
  428.3 13.5 %shard_map.276 = (bf16[1024,1792]{1,0:T(8,128)(2,1)}, bf16[1024,1152]{1,0:T(8,128)(2,1)}) custom-call(bf16[1024,1152]{1,0:T(8,128)(2,1)} %constant_dynamic-update-slice_fusion.11.grad_mixed.refs_5_, bf16[1024,896]{1,0:T(8,128)(2,1)} %get-tuple-element.51.gelu, bf16[1024,896]{1,0:T(8,128)(2,1)} %get-tuple-element.52.slope, bf16[1152,1792]{1,0:T(8,128)(2,1)} %bitcast.319, ...), custom_call_target="tpu_custom_call" | custom-call | flops 6341787648 | bytes 12058624 | tf_op jit(solution)/shard_map/pallas_call | solution.py:180
  449.7 16.2 %shard_map.277 = bf16[896,1152]{1,0:T(8,128)(2,1)} custom-call(bf16[1024,896]{1,0:T(8,128)(2,1)} %get-tuple-element.54.refs_0_, bf16[2048,896]{1,0:T(8,128)(2,1)} %get-tuple-element.55.refs_1_, bf16[1024,896]{1,0:T(8,128)(2,1)} %get-tuple-element.56.refs_2_, bf16[1024,1152]{1,0:T(8,128)(2,1)} %pad_maximum_fusion.2.grad_mixed.refs_3_, ...), custom_call_target="tpu_custom_call" | custom-call | flops 8455716864 | bytes 16777216 | tf_op jit(solution)/shard_map/pallas_call | solution.py:215
  475.9 9.7 %collective-permute-done.39 = bf16[256,1152]{1,0:T(8,128)(2,1)S(1)} collective-permute-done((bf16[256,1152]{1,0:T(8,128)(2,1)S(1)}, bf16[256,1152]{1,0:T(8,128)(2,1)S(1)}, u32[]{:S(2)}, u32[]{:S(2)}) %collective-permute-start.39) | collective-permute-done | bytes 589856 | tf_op jit(solution)/shard_map/ppermute | solution.py:110
  490.0 25.0 %shard_map.278 = bf16[4,2,144,1792]{3,2,1,0:T(8,128)(2,1)} custom-call(bf16[1024,1152]{1,0:T(8,128)(2,1)} %pad_maximum_fusion.normed.refs_0_, bf16[2048,1152]{1,0:T(8,128)(2,1)} %constant_dynamic-update-slice_fusion.2.normed.refs_1_, bf16[1024,1152]{1,0:T(8,128)(2,1)} %constant_dynamic-update-slice_fusion.5.normed._.refs_2_, ...), custom_call_target="tpu_custom_call" | custom-call | flops 16911433728 | bytes 24117248 | tf_op jit(solution)/shard_map/pallas_call | solution.py:247
  534.2 6.0 fusion
  556.9 8.4 %collective-permute-done.43 = bf16[512,512]{1,0:T(8,128)(2,1)S(1)} collective-permute-done((bf16[512,512]{1,0:T(8,128)(2,1)S(1)}, bf16[512,512]{1,0:T(8,128)(2,1)S(1)}, u32[]{:S(2)}, u32[]{:S(2)}) %collective-permute-start.43) | collective-permute-done | bytes 524320 | tf_op jit(solution)/shard_map/ppermute | solution.py:508
  617.8 9.5 %collective-permute-done.47 = bf16[2,2,72,896]{3,2,1,0:T(8,128)(2,1)S(1)} collective-permute-done((bf16[2,2,72,896]{3,2,1,0:T(8,128)(2,1)S(1)}, bf16[2,2,72,896]{3,2,1,0:T(8,128)(2,1)S(1)}, u32[]{:S(2)}, u32[]{:S(2)}) %collective-permute-start.47) | collective-permute-done | bytes 516128 | tf_op jit(solution)/shard_map/ppermute | solution.py:110
  647.3 8.3 %reduce-scatter.11.cloned.1.call-done = bf16[32,1152]{1,0:T(8,128)(2,1)} async-done(((bf16[128,1152]{1,0:T(8,128)(2,1)}), bf16[32,1152]{1,0:T(8,128)(2,1)}) %reduce-scatter.11.cloned.1.call-update) | async-done | bytes 73744 | tf_op jit(solution)/shard_map/reduce_scatter | solution.py:339
  661.1 17.1 %reduce-scatter.15.cloned.1.call-done = bf16[72,896]{1,0:T(8,128)(2,1)} async-done(((bf16[288,896]{1,0:T(8,128)(2,1)}), bf16[72,896]{1,0:T(8,128)(2,1)}) %reduce-scatter.15.cloned.1.call-update) | async-done | bytes 129040
  (573 shorter events, 347.2 us)
Async XLA Ops:
  7.2 69.0 %all-gather.5.cloned.1.call-start = ((), (), s32[]{:S(2)}) async-start(), calls=%async_computation.8 | async-start | bytes 2856960 | tf_op jit(solution)/shard_map/all_gather | solution.py:416
  20.2 30.2 %all-to-all-start = ((bf16[8,36,1792]{2,1,0:T(8,128)(2,1)}), bf16[8,36,1792]{2,1,0:T(8,128)(2,1)S(1)}, u32[]{:S(2)}, u32[]{:S(2)}) async-start(bf16[8,36,1792]{2,1,0:T(8,128)(2,1)} %copy.274), calls=%async_computation | async-start | bytes 2293760 | tf_op jit(solution)/shard_map/all_to_all | solution.py:387
  24.2 196.9 %all-gather.7.cloned.1.call-start = ((), (), s32[]{:S(2)}) async-start(), calls=%async_computation.9 | async-start | bytes 5160960 | tf_op jit(solution)/shard_map/all_gather | solution.py:422
  24.6 25.6 %collective-permute-start.3 = (bf16[72,896]{1,0:T(8,128)(2,1)S(1)}, bf16[72,896]{1,0:T(8,128)(2,1)S(1)}, u32[]{:S(2)}, u32[]{:S(2)}) collective-permute-start(bf16[72,896]{1,0:T(8,128)(2,1)S(1)} %reshape.403), channel_id=1, source_target_pairs={{12,0},{0,4},{4,8},{8,12},{13,1},{1,5},{5,9},{9,13},{14,2},{2,6},{... | collective-permute-start | bytes 387080 | tf_op jit(solution)/shard_map/ppermute | solution.py:306
  78.3 476.5 %reduce-scatter.13.cloned.1.call-start = ((), (), s32[]{:S(2)}) async-start(), calls=%async_computation.10 | async-start | bytes 2488320
  84.6 57.4 %collective-permute-start.11 = (bf16[2,2,32,1152]{3,2,1,0:T(8,128)(2,1)}, bf16[2,2,32,1152]{3,2,1,0:T(8,128)(2,1)}, u32[]{:S(2)}, u32[]{:S(2)}) collective-permute-start(bf16[2,2,32,1152]{3,2,1,0:T(8,128)(2,1)} %fusion.100), channel_id=1, source_target_pairs={{0,2},{2,0},{1,3},{3,1},{4,6},{6,4},{5,7},{7,5},{8,10},{10,8},{9,1... | collective-permute-start | bytes 884744 | tf_op jit(solution)/shard_map/ppermute | solution.py:110
  86.6 53.6 %collective-permute-start.13 = (bf16[2,2,32,1152]{3,2,0,1:T(8,128)(2,1)}, bf16[2,2,32,1152]{3,2,0,1:T(8,128)(2,1)}, u32[]{:S(2)}, u32[]{:S(2)}) collective-permute-start(bf16[2,2,32,1152]{3,2,0,1:T(8,128)(2,1)} %fusion.98), channel_id=1, source_target_pairs={{0,16},{16,0},{1,17},{17,1},{2,18},{18,2},{3,19},{19,3},{4,20},{20... | collective-permute-start | bytes 884744 | tf_op jit(solution)/shard_map/ppermute | solution.py:110
  132.9 32.6 %collective-permute-start.9 = (bf16[512,512]{1,0:T(8,128)(2,1)S(1)}, bf16[512,512]{1,0:T(8,128)(2,1)S(1)}, u32[]{:S(2)}, u32[]{:S(2)}) collective-permute-start(bf16[512,512]{1,0:T(8,128)(2,1)S(1)} %pad_maximum_fusion.17), channel_id=1, source_target_pairs={{0,1},{1,2},{2,3},{3,4},{4,5},{5,6},{6,7},{7,8},{8,9},{9,10},{10,1... | collective-permute-start | bytes 1572872 | tf_op jit(solution)/shard_map/ppermute | solution.py:450
  143.3 30.3 %collective-permute-start.14 = (bf16[2,4,2,32,1152]{4,3,2,1,0:T(8,128)(2,1)S(1)}, bf16[2,4,2,32,1152]{4,3,2,1,0:T(8,128)(2,1)S(1)}, u32[]{:S(2)}, u32[]{:S(2)}) collective-permute-start(bf16[2,4,2,32,1152]{4,3,2,1,0:T(8,128)(2,1)S(1)} %get-tuple-element.126), channel_id=1, source_target_pairs={{0,1},{1,0},{2,3},{3,2},{4,5},{5,4},{6,7},{7,6},{8,9},{9,8},{10,11... | collective-permute-start | bytes 3538952 | tf_op jit(solution)/shard_map/ppermute | solution.py:110
  178.3 27.0 %collective-permute-start.16 = (bf16[512,1152]{1,0:T(8,128)(2,1)S(1)}, bf16[512,1152]{1,0:T(8,128)(2,1)S(1)}, u32[]{:S(2)}, u32[]{:S(2)}) collective-permute-start(bf16[512,1152]{1,0:T(8,128)(2,1)S(1)} %multiply_convert_fusion), channel_id=1, source_target_pairs={{0,16},{16,0},{1,17},{17,1},{2,18},{18,2},{3,19},{19,3},{4,20},{20... | collective-permute-start | bytes 3538952 | tf_op jit(solution)/shard_map/ppermute | solution.py:110
  207.1 33.7 %collective-permute-start.18 = (bf16[1024,1152]{1,0:T(8,128)(2,1)}, bf16[1024,1152]{1,0:T(8,128)(2,1)}, u32[]{:S(2)}, u32[]{:S(2)}) collective-permute-start(bf16[1024,1152]{1,0:T(8,128)(2,1)} %pad_maximum_fusion.1), channel_id=1, source_target_pairs={{0,1},{1,0},{2,3},{3,2},{4,5},{5,4},{6,7},{7,6},{8,9},{9,8},{10,11... | collective-permute-start | bytes 7077896 | tf_op jit(solution)/shard_map/ppermute | solution.py:110
  217.1 54.2 %collective-permute-start.15 = (bf16[512,1152]{1,0:T(8,128)(2,1)S(1)}, bf16[512,1152]{1,0:T(8,128)(2,1)}, u32[]{:S(2)}, u32[]{:S(2)}) collective-permute-start(bf16[512,1152]{1,0:T(8,128)(2,1)S(1)} %multiply_convert_fusion), channel_id=1, source_target_pairs={{0,1},{1,0},{2,3},{3,2},{4,5},{5,4},{6,7},{7,6},{8,9},{9,8},{10,11... | collective-permute-start | bytes 3538952 | tf_op jit(solution)/shard_map/ppermute | solution.py:110
  305.2 26.1 %collective-permute-start.28 = (bf16[512,1152]{1,0:T(8,128)(2,1)S(1)}, bf16[512,1152]{1,0:T(8,128)(2,1)S(1)}, u32[]{:S(2)}, u32[]{:S(2)}) collective-permute-start(bf16[512,1152]{1,0:T(8,128)(2,1)S(1)} %pad_maximum_fusion.9), channel_id=1, source_target_pairs={{0,2},{2,0},{1,3},{3,1},{4,6},{6,4},{5,7},{7,5},{8,10},{10,8},{9,1... | collective-permute-start | bytes 3538952 | tf_op jit(solution)/shard_map/ppermute | solution.py:110
  306.5 25.6 %collective-permute-start.26 = (bf16[512,1152]{1,0:T(8,128)(2,1)S(1)}, bf16[512,1152]{1,0:T(8,128)(2,1)S(1)}, u32[]{:S(2)}, u32[]{:S(2)}) collective-permute-start(bf16[512,1152]{1,0:T(8,128)(2,1)S(1)} %pad_maximum_fusion.8), channel_id=1, source_target_pairs={{0,16},{16,0},{1,17},{17,1},{2,18},{18,2},{3,19},{19,3},{4,20},{20... | collective-permute-start | bytes 3538952 | tf_op jit(solution)/shard_map/ppermute | solution.py:110
  337.6 31.7 %collective-permute-start.29 = (bf16[512,1152]{1,0:T(8,128)(2,1)S(1)}, bf16[512,1152]{1,0:T(8,128)(2,1)S(1)}, u32[]{:S(2)}, u32[]{:S(2)}) collective-permute-start(bf16[512,1152]{1,0:T(8,128)(2,1)S(1)} %get-tuple-element.104), channel_id=1, source_target_pairs={{0,1},{1,0},{2,3},{3,2},{4,5},{5,4},{6,7},{7,6},{8,9},{9,8},{10,11... | collective-permute-start | bytes 3538952 | tf_op jit(solution)/shard_map/ppermute | solution.py:110
  364.3 36.9 %collective-permute-start.33 = (bf16[1024,1152]{1,0:T(8,128)(2,1)}, bf16[1024,1152]{1,0:T(8,128)(2,1)S(1)}, u32[]{:S(2)}, u32[]{:S(2)}) collective-permute-start(bf16[1024,1152]{1,0:T(8,128)(2,1)} %pad_maximum_fusion.3), channel_id=1, source_target_pairs={{0,1},{1,0},{2,3},{3,2},{4,5},{5,4},{6,7},{7,6},{8,9},{9,8},{10,11... | collective-permute-start | bytes 7077896 | tf_op jit(solution)/shard_map/ppermute | solution.py:110
  428.3 44.5 %collective-permute-start.34 = (bf16[1024,1152]{1,0:T(8,128)(2,1)}, bf16[1024,1152]{1,0:T(8,128)(2,1)}, u32[]{:S(2)}, u32[]{:S(2)}) collective-permute-start(bf16[1024,1152]{1,0:T(8,128)(2,1)} %slice.312), channel_id=1, source_target_pairs={{0,1},{1,0},{2,3},{3,2},{4,5},{5,4},{6,7},{7,6},{8,9},{9,8},{10,11... | collective-permute-start | bytes 7077896 | tf_op jit(solution)/shard_map/ppermute | solution.py:110
  449.7 65.2 %collective-permute-start.30 = (bf16[512,1152]{1,0:T(8,128)(2,1)}, bf16[512,1152]{1,0:T(8,128)(2,1)}, u32[]{:S(2)}, u32[]{:S(2)}) collective-permute-start(bf16[512,1152]{1,0:T(8,128)(2,1)} %slice.310), channel_id=1, source_target_pairs={{0,1},{1,0},{2,3},{3,2},{4,5},{5,4},{6,7},{7,6},{8,9},{9,8},{10,11... | collective-permute-start | bytes 3538952 | tf_op jit(solution)/shard_map/ppermute | solution.py:110
  468.9 167.4 %reduce-scatter.9.cloned.1.call-start = ((), (), s32[]{:S(2)}) async-start(), calls=%async_computation.6 | async-start | bytes 5160960 | tf_op jit(solution)/shard_map/reduce_scatter | solution.py:481
  487.5 27.5 %collective-permute-start.42 = (bf16[512,1152]{1,0:T(8,128)(2,1)}, bf16[512,1152]{1,0:T(8,128)(2,1)}, u32[]{:S(2)}, u32[]{:S(2)}) collective-permute-start(bf16[512,1152]{1,0:T(8,128)(2,1)} %pad_maximum_fusion.12), channel_id=1, source_target_pairs={{0,2},{2,0},{1,3},{3,1},{4,6},{6,4},{5,7},{7,5},{8,10},{10,8},{9,1... | collective-permute-start | bytes 3538952 | tf_op jit(solution)/shard_map/ppermute | solution.py:110
  489.1 26.0 %collective-permute-start.40 = (bf16[512,1152]{1,0:T(8,128)(2,1)}, bf16[512,1152]{1,0:T(8,128)(2,1)}, u32[]{:S(2)}, u32[]{:S(2)}) collective-permute-start(bf16[512,1152]{1,0:T(8,128)(2,1)} %pad_maximum_fusion.11), channel_id=1, source_target_pairs={{0,16},{16,0},{1,17},{17,1},{2,18},{18,2},{3,19},{19,3},{4,20},{20... | collective-permute-start | bytes 3538952 | tf_op jit(solution)/shard_map/ppermute | solution.py:110
  554.8 39.1 %collective-permute-start.49 = (bf16[2,4,2,32,1152]{4,3,2,1,0:T(8,128)(2,1)}, bf16[2,4,2,32,1152]{4,3,2,1,0:T(8,128)(2,1)}, u32[]{:S(2)}, u32[]{:S(2)}) collective-permute-start(bf16[2,4,2,32,1152]{4,3,2,1,0:T(8,128)(2,1)} %dynamic-slice_bitcast_fusion), channel_id=1, source_target_pairs={{0,1},{1,0},{2,3},{3,2},{4,5},{5,4},{6,7},{7,6},{8,9},{9,8},{10,11... | collective-permute-start | bytes 3538952 | tf_op jit(solution)/shard_map/ppermute | solution.py:110
  554.8 100.8 %reduce-scatter.11.cloned.1.call-start = ((), (), s32[]{:S(2)}) async-start(), calls=%async_computation.7 | async-start | bytes 368640 | tf_op jit(solution)/shard_map/reduce_scatter | solution.py:339
  644.4 33.8 %reduce-scatter.15.cloned.1.call-start = ((), (), s32[]{:S(2)}) async-start(), calls=%async_computation.11 | async-start | bytes 645120
  (140 other events, 1203.4 us)
Sparse Core Ops, SparseCore 0:
  14.0 57.5 all-gather.4
  78.4 88.2 all-gather.6
  469.0 46.7 reduce-scatter.12
  555.0 81.2 reduce-scatter.8
  639.1 16.4 reduce-scatter.10
  658.5 19.6 reduce-scatter.14

commit v5 on v4

v5 whole, which is shorter than its diff:
```python
import functools

import jax
import jax.numpy as jnp
from jax import lax
from jax.experimental import pallas as pl
from jax.experimental.pallas import tpu as pltpu
from jax.sharding import Mesh
from jax.sharding import PartitionSpec as P

HEAD = 256
WINDOW = 512
EPSILON = 1e-06
ROPE_BASE = 10000.0
ALL = ("x", "g", "y", "c")
PLANE = ("x", "y", "c")
BF = jnp.bfloat16
F32 = jnp.float32


def norm_gain(values, gain_vec):
    return (
        values * lax.rsqrt(jnp.mean(values * values, axis=-1, keepdims=True) + EPSILON) * gain_vec
    )


def rope_tables(first_row, row_count, head_size):
    places = (first_row + jnp.arange(row_count, dtype=jnp.int32)).astype(F32)
    frequency = ROPE_BASE ** (-(jnp.arange(head_size // 2, dtype=F32) * 2.0) / head_size)
    angles = places[:, None] * frequency[None, :]
    return (jnp.cos(angles), jnp.sin(angles))


def matmul(left_side, right_side):
    return jnp.dot(left_side, right_side, preferred_element_type=F32)


def over_rows(left_side, right_side):
    return lax.dot_general(
        left_side, right_side, (((0,), (0,)), ((), ())), preferred_element_type=F32
    )


def by_transpose(left_side, right_side):
    return lax.dot_general(
        left_side, right_side, (((1,), (1,)), ((), ())), preferred_element_type=F32
    )


def swap(array, axis):
    return lax.ppermute(array, axis, [(0, 1), (1, 0)])


GELU_A = 0.7978845608028654
GELU_B = 0.044715
TILE = 512
PARAMS = pltpu.CompilerParams(vmem_limit_bytes=58 << 20)


def whole_block(shape):
    return pl.BlockSpec(shape, lambda i: (0,) * len(shape), pipeline_mode=pl.Buffered(1))


def row_block(rows, columns):
    return pl.BlockSpec((rows, columns), lambda i: (i, 0))


def mlp_forward_kernel(normed, gate_up, down, _, hidden, gelu, slope, mixed):
    own = down.shape[0]
    raw = matmul(normed[...], gate_up[...])
    gate_raw, up_raw = raw[:, :own], raw[:, own:]
    square = gate_raw * gate_raw
    bend = jnp.tanh(GELU_A * (gate_raw + GELU_B * square * gate_raw))
    half = 0.5 + 0.5 * bend
    active = gate_raw * half
    turn = 0.5 * gate_raw * (1.0 - bend * bend) * (GELU_A * (1.0 + 3.0 * GELU_B * square))
    low = (active * up_raw).astype(BF)
    hidden[...] = low
    gelu[...] = active.astype(BF)
    slope[...] = ((half + turn) * up_raw).astype(BF)
    mixed[...] = matmul(low, down[...]).astype(BF)


def mlp_forward(normed, gate_up, down, earlier):
    rows, width = normed.shape
    own = down.shape[0]
    flat = jax.ShapeDtypeStruct((rows, own), BF)
    return pl.pallas_call(
        mlp_forward_kernel,
        grid=(rows // TILE,),
        in_specs=[
            row_block(TILE, width),
            whole_block(gate_up.shape),
            whole_block(down.shape),
            pl.BlockSpec(memory_space=pl.ANY),
        ],
        out_specs=[row_block(TILE, own)] * 3 + [row_block(TILE, width)],
        out_shape=[flat, flat, flat, jax.ShapeDtypeStruct((rows, width), BF)],
        compiler_params=PARAMS,
        cost_estimate=pl.CostEstimate(
            flops=6 * rows * width * own, bytes_accessed=rows * (4 * width + 6 * own), transcendentals=0
        ),
    )(normed, gate_up, down, earlier)


def mlp_backward_kernel(grad_mixed, gelu, slope, gate_up, down, _, grad_raw, grad_normed):
    own = down.shape[0]
    grad_hidden = by_transpose(grad_mixed[...], down[...])
    grad_gate = (grad_hidden * slope[...].astype(F32)).astype(BF)
    grad_up = (grad_hidden * gelu[...].astype(F32)).astype(BF)
    grad_raw[:, :own] = grad_gate
    grad_raw[:, own:] = grad_up
    grad_normed[...] = (
        by_transpose(grad_gate, gate_up[:, :own]) + by_transpose(grad_up, gate_up[:, own:])
    ).astype(BF)


def mlp_backward(grad_mixed, gelu, slope, gate_up, down, earlier):
    rows, width = grad_mixed.shape
    own = down.shape[0]
    return pl.pallas_call(
        mlp_backward_kernel,
        grid=(rows // TILE,),
        in_specs=[
            row_block(TILE, width),
            row_block(TILE, own),
            row_block(TILE, own),
            whole_block(gate_up.shape),
            whole_block(down.shape),
            pl.BlockSpec(memory_space=pl.ANY),
        ],
        out_specs=[row_block(TILE, 2 * own), row_block(TILE, width)],
        out_shape=[
            jax.ShapeDtypeStruct((rows, 2 * own), BF),
            jax.ShapeDtypeStruct((rows, width), BF),
        ],
        compiler_params=PARAMS,
        cost_estimate=pl.CostEstimate(
            flops=6 * rows * width * own, bytes_accessed=rows * (4 * width + 8 * own), transcendentals=0
        ),
    )(grad_mixed, gelu, slope, gate_up, down, earlier)


def down_terms_kernel(*refs):
    *ins, out = refs
    half = len(ins) // 2
    total = over_rows(ins[0][...], ins[half][...])
    for left, right in zip(ins[1:half], ins[half + 1 :]):
        total = total + over_rows(left[...], right[...])
    out[...] = total.astype(BF)


def down_terms(hidden, grad_mixed, keep):
    own, width = hidden[0].shape[1], grad_mixed[0].shape[1]
    rows = sum(part.shape[0] for part in hidden)
    return pl.pallas_call(
        down_terms_kernel,
        grid=(own // 128,),
        in_specs=[pl.BlockSpec((part.shape[0], 128), lambda i: (0, i)) for part in hidden]
        + [whole_block(part.shape) for part in grad_mixed],
        out_specs=row_block(128, width),
        out_shape=jax.ShapeDtypeStruct((keep, width), BF),
        compiler_params=PARAMS,
        cost_estimate=pl.CostEstimate(
            flops=2 * rows * width * own, bytes_accessed=2 * rows * (width + own), transcendentals=0
        ),
    )(*hidden, *grad_mixed)


def gate_terms_kernel(*refs):
    *ins, _, out = refs
    half = len(ins) // 2
    total = over_rows(ins[0][...], ins[half][...])
    for left, right in zip(ins[1:half], ins[half + 1 :]):
        total = total + over_rows(left[...], right[...])
    total = total.astype(BF)
    groups, sides, rows, _ = out.shape
    for side in range(sides):
        for group in range(groups):
            first = (side * groups + group) * rows
            out[group, side] = total[first : first + rows]


def gate_terms(normed, grad_raw, groups, earlier):
    width, both = normed[0].shape[1], grad_raw[0].shape[1]
    rows = sum(part.shape[0] for part in normed)
    shape = (groups, 2, width // (2 * groups))
    return pl.pallas_call(
        gate_terms_kernel,
        grid=(both // 256,),
        in_specs=[whole_block(part.shape) for part in normed]
        + [pl.BlockSpec((part.shape[0], 256), lambda i: (0, i)) for part in grad_raw]
        + [pl.BlockSpec(memory_space=pl.ANY)],
        out_specs=pl.BlockSpec(shape + (256,), lambda i: (0, 0, 0, i)),
        out_shape=jax.ShapeDtypeStruct(shape + (both,), BF),
        compiler_params=PARAMS,
        cost_estimate=pl.CostEstimate(
            flops=2 * rows * width * both, bytes_accessed=2 * rows * (width + both), transcendentals=0
        ),
    )(*normed, *grad_raw, earlier)


def after(value, *earlier):
    return lax.optimization_barrier((value, *earlier))[0]


def with_core(part):
    return jnp.concatenate([part, swap(part, "c")])


def core_sum(part):
    half = part.shape[0] // 2
    return part[:half].astype(F32) + swap(part[half:], "c").astype(F32)


def send_far(far):
    half = far.shape[0] // 2
    return swap(far[:half], "y").astype(F32), swap(far[half:], "x").astype(F32)


def sum_near(near, top, low):
    near = core_sum(near)
    rows = near.shape[0] // 2
    half = rows // 2
    to_x = jnp.concatenate([near[:half] + top, near[half:rows]]).astype(BF)
    to_y = jnp.concatenate([near[rows : rows + half], near[rows + half :] + low]).astype(BF)
    return to_x, to_y


def sum_own(own, to_x, to_y):
    return core_sum(own) + swap(to_x, "x").astype(F32) + swap(to_y, "y").astype(F32)


def in_order(own, other, place):
    both = jnp.concatenate([own[None], other[None], own[None]])
    return lax.dynamic_slice_in_dim(both, place, 2, 0)


def group_gather(own):
    size = lax.axis_size("g")
    parts = [own] + [
        lax.ppermute(own, "g", [((i + k) % size, i) for i in range(size)]) for k in range(1, size)
    ]
    both = jnp.stack(parts + parts[:-1])
    place = lax.axis_index("g")
    return lax.dynamic_slice_in_dim(both, lax.rem(size - place, size), size, 0)


def plane_weights(blocks):
    x, y = lax.axis_index("x"), lax.axis_index("y")
    half = blocks.shape[0] // 2
    first, second = blocks[:half], blocks[half:]
    first = in_order(first, swap(first, "x"), x)
    second = in_order(second, swap(second, "y"), y)
    first = in_order(first, swap(first, "y"), y)
    second = in_order(second, swap(second, "x"), x)
    first = first.transpose(1, 2, 0, 3, 4)
    second = second.transpose(0, 2, 1, 3, 4)
    return jnp.concatenate([first, second], axis=1)


def fold(term, axis, dim):
    place = lax.axis_index(axis)
    mine = lax.dynamic_index_in_dim(term, place, dim, keepdims=False)
    other = lax.dynamic_index_in_dim(term, 1 - place, dim, keepdims=False)
    return (mine.astype(F32) + swap(other.astype(BF), axis).astype(F32)).astype(BF)


def plane_terms(term):
    half = term.shape[1] // 2
    first = fold(fold(term[:, :half], "x", 0), "y", 1)
    second = fold(fold(term[:, half:], "y", 2), "x", 0)
    return jnp.concatenate([first, second])


def rms_scale(values):
    return lax.rsqrt(jnp.mean(values * values, axis=-1, keepdims=True) + EPSILON)


def rms_backward(values, scale, gain, grad):
    weighted = grad * gain
    inner = jnp.mean(weighted * values, axis=-1, keepdims=True)
    terms = jnp.sum(grad * values * scale, axis=0, keepdims=True)
    return weighted * scale - values * (scale * scale * scale * inner), terms


def turn_forward(values, cosine, sine):
    half = cosine.shape[1]
    low, high = values[:, :half], values[:, half:]
    return jnp.concatenate([low * cosine - high * sine, high * cosine + low * sine], axis=1)


def turn_backward(grad, cosine, sine):
    half = cosine.shape[1]
    low, high = grad[:, :half], grad[:, half:]
    return jnp.concatenate([low * cosine + high * sine, high * cosine - low * sine], axis=1)


def gain_places(width, columns, shard_rows):
    heads = columns // (width // shard_rows)
    row = lax.broadcasted_iota(jnp.int32, (width, columns), 0)
    column = lax.broadcasted_iota(jnp.int32, (width, columns), 1)
    place = (column // heads) * shard_rows + lax.rem(column, heads)
    return jnp.where(row == place, 1.0, 0.0).astype(BF)


def project_kernel(
    shard_rows, core, tokens, own, other, cosine, sine,
    normed, query_raw, key_raw, queries, key_value, d_gains, h_gains,
):
    width = tokens.shape[1]
    k_cols = key_raw.shape[1]
    half = query_raw.shape[1] // 2
    first_is_own = core[0] == 0
    block = jnp.where(
        first_is_own, own[:, half + k_cols :].astype(F32), other[:, half + k_cols :].astype(F32)
    )
    flat = block.T[:8]
    d_gains[...] = flat
    chosen = matmul(flat.astype(BF), gain_places(width, k_cols, shard_rows))
    h_gains[...] = chosen
    values = tokens[...].astype(F32)
    low = (values * rms_scale(values) * flat[0:1]).astype(BF)
    normed[...] = low
    raw_own = matmul(low, own[:, : half + k_cols])
    raw_other = matmul(low, other[:, : half + k_cols])
    first = jnp.where(first_is_own, raw_own, raw_other)
    second = jnp.where(first_is_own, raw_other, raw_own)
    raw_query = jnp.concatenate([first[:, :half], second[:, :half]], axis=1)
    raw_key = first[:, half:]
    query_raw[...] = raw_query
    key_raw[...] = raw_key
    cos, sin = cosine[...], sine[...]
    for head in range(2 * half // k_cols):
        at = slice(head * k_cols, (head + 1) * k_cols)
        part = raw_query[:, at]
        part = part * rms_scale(part) * chosen[4:5]
        queries[:, at] = turn_forward(part, cos, sin).astype(BF)
    part = raw_key * rms_scale(raw_key) * chosen[5:6]
    key_value[:, :k_cols] = turn_forward(part, cos, sin).astype(BF)
    key_value[:, k_cols:] = second[:, half:].astype(BF)


def project(core, tokens, own, other, cosine, sine, shard_rows, q_cols, k_cols):
    rows, width = tokens.shape
    vmem = pl.BlockSpec(memory_space=pltpu.VMEM)
    return pl.pallas_call(
        functools.partial(project_kernel, shard_rows),
        in_specs=[pl.BlockSpec(memory_space=pltpu.SMEM)] + [vmem] * 5,
        out_specs=[vmem] * 7,
        out_shape=[
            jax.ShapeDtypeStruct((rows, width), BF),
            jax.ShapeDtypeStruct((rows, q_cols), F32),
            jax.ShapeDtypeStruct((rows, k_cols), F32),
            jax.ShapeDtypeStruct((rows, q_cols), BF),
            jax.ShapeDtypeStruct((rows, 2 * k_cols), BF),
            jax.ShapeDtypeStruct((8, width), F32),
            jax.ShapeDtypeStruct((8, k_cols), F32),
        ],
        compiler_params=PARAMS,
        cost_estimate=pl.CostEstimate(
            flops=2 * rows * width * (q_cols + 2 * k_cols), bytes_accessed=16 * rows * width, transcendentals=0
        ),
    )(core, tokens, own, other, cosine, sine)


def tile_mask(first, rows, first_key, keys, query_ids, key_ids, pad):
    query_place = pad + first + lax.broadcasted_iota(jnp.int32, (rows, keys), 0)
    key_place = first_key + lax.broadcasted_iota(jnp.int32, (rows, keys), 1)
    distance = query_place - key_place
    same_doc = query_ids[first : first + rows, :] == key_ids[:, first_key : first_key + keys]
    return (distance >= 0) & (distance < WINDOW) & same_doc


def attend_kernel(
    scale, queries, halo, key_value, query_ids, key_ids, w_o, tokens, d_gains,
    attended, log_total, branch, middle, normed_mlp, keys, values,
):
    pad, k_cols = halo.shape[0], halo.shape[1] // 2
    rows, q_cols = queries.shape
    keys[:pad] = halo[:, :k_cols]
    keys[pad:] = key_value[:, :k_cols]
    values[:pad] = halo[:, k_cols:]
    values[pad:] = key_value[:, k_cols:]
    tile = rows // 2
    span = pad + tile
    lane = lax.broadcasted_iota(jnp.int32, (tile, 128), 1)
    for first in (0, tile):
        at = slice(first, first + tile)
        seen = slice(first, first + span)
        allowed = tile_mask(first, tile, first, span, query_ids, key_ids, pad)
        logs = jnp.zeros((tile, 128), F32)
        for head in range(q_cols // k_cols):
            columns = slice(head * k_cols, (head + 1) * k_cols)
            scores = by_transpose(queries[at, columns], keys[seen]) * scale
            scores = jnp.where(allowed, scores, -1e30)
            row_max = jnp.max(scores, axis=-1, keepdims=True)
            weights = jnp.exp(scores - row_max)
            row_total = jnp.sum(weights, axis=-1, keepdims=True)
            probabilities = (weights * (1.0 / row_total)).astype(BF)
            attended[at, columns] = matmul(probabilities, values[seen]).astype(BF)
            logs = jnp.where(lane == head, row_max + jnp.log(row_total), logs)
        log_total[at] = logs
    out = matmul(attended[...], w_o[...])
    branch[...] = out
    total = tokens[...].astype(F32) + out * rms_scale(out) * d_gains[1:2]
    middle[...] = total
    normed_mlp[...] = (total * rms_scale(total) * d_gains[2:3]).astype(BF)


def attend(queries, halo, key_value, query_ids, key_ids, w_o, tokens, d_gains, scale):
    rows, q_cols = queries.shape
    width = tokens.shape[1]
    k_cols = halo.shape[1] // 2
    pad = halo.shape[0]
    vmem = pl.BlockSpec(memory_space=pltpu.VMEM)
    return pl.pallas_call(
        functools.partial(attend_kernel, scale),
        in_specs=[vmem] * 8,
        out_specs=[vmem] * 5,
        out_shape=[
            jax.ShapeDtypeStruct((rows, q_cols), BF),
            jax.ShapeDtypeStruct((rows, 128), F32),
            jax.ShapeDtypeStruct((rows, width), F32),
            jax.ShapeDtypeStruct((rows, width), F32),
            jax.ShapeDtypeStruct((rows, width), BF),
        ],
        scratch_shapes=[pltpu.VMEM((pad + rows, k_cols), BF), pltpu.VMEM((pad + rows, k_cols), BF)],
        compiler_params=PARAMS,
        cost_estimate=pl.CostEstimate(
            flops=2 * rows * q_cols * (width + 2 * (pad + rows)), bytes_accessed=20 * rows * width, transcendentals=0
        ),
    )(queries, halo, key_value, query_ids, key_ids, w_o, tokens, d_gains)


def attend_backward_kernel(
    scale, grad_normed_mlp, cotangent, middle, branch, d_gains, w_o,
    queries, halo, key_value, query_ids, key_ids, log_total,
    grad_middle, grad_branch, grad_queries, grad_key_value, returned, terms,
    keys, values, grad_keys, grad_values, grad_attended,
):
    pad, k_cols = halo.shape[0], halo.shape[1] // 2
    rows, q_cols = queries.shape
    total = middle[...]
    from_mlp, mlp_terms = rms_backward(total, rms_scale(total), d_gains[2:3], grad_normed_mlp[...])
    grad_total = cotangent[...].astype(F32) + from_mlp
    grad_middle[...] = grad_total
    out = branch[...]
    grad_out, out_terms = rms_backward(out, rms_scale(out), d_gains[1:2], grad_total)
    low = grad_out.astype(BF)
    grad_branch[...] = low
    terms[...] = jnp.concatenate([out_terms, mlp_terms, jnp.zeros((6, out.shape[1]), F32)], axis=0)
    grad_attended[...] = by_transpose(low, w_o[...]).astype(BF)
    keys[:pad] = halo[:, :k_cols]
    keys[pad:] = key_value[:, :k_cols]
    values[:pad] = halo[:, k_cols:]
    values[pad:] = key_value[:, k_cols:]
    grad_keys[...] = jnp.zeros_like(grad_keys)
    grad_values[...] = jnp.zeros_like(grad_values)
    tile = rows // 2
    span = pad + tile
    for first in (0, tile):
        at = slice(first, first + tile)
        seen = slice(first, first + span)
        allowed = tile_mask(first, tile, first, span, query_ids, key_ids, pad)
        key_total = jnp.zeros((span, k_cols), F32)
        value_total = jnp.zeros((span, k_cols), F32)
        for head in range(q_cols // k_cols):
            columns = slice(head * k_cols, (head + 1) * k_cols)
            query = queries[at, columns]
            grad = grad_attended[at, columns]
            scores = by_transpose(query, keys[seen]) * scale
            probabilities = jnp.where(
                allowed, jnp.exp(scores - log_total[at, head : head + 1]), 0.0
            )
            grad_prob = by_transpose(grad, values[seen])
            inner = jnp.sum(probabilities * grad_prob, axis=-1, keepdims=True)
            grad_score = (probabilities * (grad_prob - inner)).astype(BF)
            grad_queries[at, columns] = matmul(grad_score, keys[seen]) * scale
            key_total = key_total + over_rows(grad_score, query)
            value_total = value_total + over_rows(probabilities.astype(BF), grad)
        grad_keys[seen] = grad_keys[seen] + key_total * scale
        grad_values[seen] = grad_values[seen] + value_total
    returned[:, :k_cols] = grad_keys[:pad].astype(BF)
    returned[:, k_cols:] = grad_values[:pad].astype(BF)
    grad_key_value[:, :k_cols] = grad_keys[pad:]
    grad_key_value[:, k_cols:] = grad_values[pad:]


def attend_backward(
    grad_normed_mlp, cotangent, middle, branch, d_gains, w_o,
    queries, halo, key_value, query_ids, key_ids, log_total, scale,
):
    rows, q_cols = queries.shape
    width = middle.shape[1]
    k_cols = halo.shape[1] // 2
    pad = halo.shape[0]
    vmem = pl.BlockSpec(memory_space=pltpu.VMEM)
    return pl.pallas_call(
        functools.partial(attend_backward_kernel, scale),
        in_specs=[vmem] * 12,
        out_specs=[vmem] * 6,
        out_shape=[
            jax.ShapeDtypeStruct((rows, width), F32),
            jax.ShapeDtypeStruct((rows, width), BF),
            jax.ShapeDtypeStruct((rows, q_cols), F32),
            jax.ShapeDtypeStruct((rows, 2 * k_cols), F32),
            jax.ShapeDtypeStruct((pad, 2 * k_cols), BF),
            jax.ShapeDtypeStruct((8, width), F32),
        ],
        scratch_shapes=[
            pltpu.VMEM((pad + rows, k_cols), BF),
            pltpu.VMEM((pad + rows, k_cols), BF),
            pltpu.VMEM((pad + rows, k_cols), F32),
            pltpu.VMEM((pad + rows, k_cols), F32),
            pltpu.VMEM((rows, q_cols), BF),
        ],
        compiler_params=PARAMS,
        cost_estimate=pl.CostEstimate(
            flops=2 * rows * q_cols * (width + 5 * (pad + rows)), bytes_accessed=30 * rows * width, transcendentals=0
        ),
    )(
        grad_normed_mlp, cotangent, middle, branch, d_gains, w_o,
        queries, halo, key_value, query_ids, key_ids, log_total,
    )


def project_backward_kernel(
    shard_rows, core, grad_queries, grad_key_value, returned, query_raw, key_raw, cosine, sine,
    h_gains, normed, own, other, grad_middle, tokens, d_gains, terms, mixed_terms,
    grad_tokens, mine, sent,
):
    width = tokens.shape[1]
    k_cols = key_raw.shape[1]
    half = query_raw.shape[1] // 2
    first_is_own = core[0] == 0
    cos, sin = cosine[...], sine[...]
    query_terms = jnp.zeros((1, k_cols), F32)
    parts = []
    for head in range(2 * half // k_cols):
        at = slice(head * k_cols, (head + 1) * k_cols)
        raw = query_raw[:, at]
        grad = turn_backward(grad_queries[:, at], cos, sin)
        grad, term = rms_backward(raw, rms_scale(raw), h_gains[4:5], grad)
        query_terms = query_terms + term
        parts.append(grad.astype(BF))
    total = grad_key_value[...] + returned[...].astype(F32)
    raw = key_raw[...]
    grad = turn_backward(total[:, :k_cols], cos, sin)
    grad, key_terms = rms_backward(raw, rms_scale(raw), h_gains[5:6], grad)
    both = len(parts) // 2
    first = jnp.concatenate(parts[:both] + [grad.astype(BF)], axis=1)
    second = jnp.concatenate(parts[both:] + [total[:, k_cols:].astype(BF)], axis=1)
    grad_own = jnp.where(first_is_own, first, second)
    grad_other = jnp.where(first_is_own, second, first)
    cols = half + k_cols
    grad_normed = by_transpose(grad_own, own[:, :cols]) + by_transpose(grad_other, other[:, :cols])
    values = tokens[...].astype(F32)
    from_attn, in_terms = rms_backward(values, rms_scale(values), d_gains[0:1], grad_normed)
    grad_tokens[...] = (grad_middle[...] + from_attn).astype(BF)
    mine[:, :cols] = over_rows(normed[...], grad_own).astype(BF)
    sent[:, :cols] = over_rows(normed[...], grad_other).astype(BF)
    heads = jnp.concatenate([query_terms, key_terms, jnp.zeros((6, k_cols), F32)], axis=0)
    placed = by_transpose(heads.astype(BF), gain_places(width, k_cols, shard_rows))
    block = jnp.concatenate(
        [in_terms, terms[0:2], mixed_terms[0:1], placed[0:2], jnp.zeros((122, width), F32)], axis=0
    ).T
    mine[:, cols:] = jnp.where(first_is_own, block, 0.0).astype(BF)
    sent[:, cols:] = jnp.where(first_is_own, 0.0, block).astype(BF)


def project_backward(
    core, grad_queries, grad_key_value, returned, query_raw, key_raw, cosine, sine,
    h_gains, normed, own, other, grad_middle, tokens, d_gains, terms, mixed_terms, shard_rows,
):
    rows, width = tokens.shape
    vmem = pl.BlockSpec(memory_space=pltpu.VMEM)
    return pl.pallas_call(
        functools.partial(project_backward_kernel, shard_rows),
        in_specs=[pl.BlockSpec(memory_space=pltpu.SMEM)] + [vmem] * 16,
        out_specs=[vmem] * 3,
        out_shape=[
            jax.ShapeDtypeStruct((rows, width), BF),
            jax.ShapeDtypeStruct(own.shape, BF),
            jax.ShapeDtypeStruct(own.shape, BF),
        ],
        compiler_params=PARAMS,
        cost_estimate=pl.CostEstimate(
            flops=8 * rows * width * own.shape[1], bytes_accessed=30 * rows * width, transcendentals=0
        ),
    )(
        core, grad_queries, grad_key_value, returned, query_raw, key_raw, cosine, sine,
        h_gains, normed, own, other, grad_middle, tokens, d_gains, terms, mixed_terms,
    )


def on_device(
    tokens,
    cotangent,
    doc_ids,
    w_query,
    w_key,
    w_value,
    w_out,
    w_gate,
    w_up,
    w_down,
    gain_attn_in,
    gain_attn_out,
    gain_mlp_in,
    gain_mlp_out,
    gain_query,
    gain_key,
):
    row_count = tokens.shape[1]
    width = tokens.shape[2]
    groups = lax.axis_size("g")
    members = lax.axis_size(PLANE)
    shard_rows = w_query.shape[0]
    head_rows = gain_query.shape[0]
    hidden_all = w_gate.shape[1]
    hidden_own = hidden_all // members
    hidden_pad = -(-hidden_own // 128) * 128
    piece = hidden_own // groups
    q_cols, k_cols = w_query.shape[1], w_key.shape[1]
    attn_scale = HEAD ** (-0.5)

    def gain_columns(d_gains, h_gains):
        columns = list(d_gains) + [
            jnp.pad(h, ((0, 0), (0, shard_rows - head_rows))) for h in h_gains
        ]
        block = jnp.stack(columns, axis=-1)
        return jnp.pad(block, ((0, 0), (0, 0), (0, 128 - len(columns))))

    def spread(weight):
        cut = weight.reshape(shard_rows, 2, groups, members // 2, piece)
        cut = cut.transpose(1, 3, 0, 2, 4).reshape(members, shard_rows, hidden_own)
        return jnp.pad(cut, ((0, 0), (0, 0), (0, hidden_pad - hidden_own)))

    sent = jnp.concatenate([spread(w_gate), spread(w_up)], axis=2)
    sent = lax.all_to_all(sent, PLANE, split_axis=0, concat_axis=0, tiled=True)
    sent = sent.reshape(members * shard_rows, 2 * hidden_pad)
    core = lax.axis_index("c")
    half_cols = q_cols // 2 + k_cols + 128
    gains = gain_columns(
        [g[None] for g in (gain_attn_in, gain_attn_out, gain_mlp_in, gain_mlp_out)],
        [gain_query[None], gain_key[None]],
    )
    halves = jnp.stack(
        [
            jnp.concatenate([w_query[:, : q_cols // 2], w_key, gains[0]], axis=1),
            jnp.concatenate([w_query[:, q_cols // 2 :], w_value, jnp.zeros_like(gains[0])], axis=1),
        ]
    )
    mine = lax.dynamic_index_in_dim(halves, core, 0, keepdims=False)
    other = lax.dynamic_index_in_dim(halves, 1 - core, 0, keepdims=False)
    mine = in_order(mine, swap(other, "c"), core).reshape(2 * shard_rows, half_cols)
    mine, sent = lax.optimization_barrier((group_gather(mine), sent))
    mine = plane_weights(mine).reshape(width, half_cols)
    other = swap(mine, "c")

    down = lax.all_gather(jnp.concatenate([w_down, w_out]), "g", axis=0)
    w_o = plane_weights(down[:, w_down.shape[0] :])
    down = down[:, : w_down.shape[0]].reshape(-1, width)
    down = jnp.pad(down, ((0, hidden_pad - hidden_own), (0, 0)))
    w_o = in_order(w_o, swap(w_o, "c"), core).transpose(1, 2, 3, 0, 4, 5).reshape(q_cols, width)

    both = lax.all_gather(sent, "g", axis=0)
    both = both.reshape(groups, 2, members // 2 * shard_rows, 2 * hidden_pad)
    gate_up = both.transpose(1, 0, 2, 3).reshape(width, 2 * hidden_pad)

    seq_place = lax.axis_index(("g", "y", "c"))
    seq_size = lax.axis_size(("g", "y", "c"))
    first_row = seq_place * row_count
    ids_all = doc_ids[0]
    ids_own = lax.dynamic_slice_in_dim(ids_all, first_row, row_count, 0)
    ids_prev = lax.dynamic_slice_in_dim(
        ids_all, jnp.maximum(first_row - row_count, 0), row_count, 0
    )
    ids_prev = jnp.where(seq_place > 0, ids_prev, -1)
    ids_pad = jnp.concatenate([ids_prev, ids_own])
    query_ids, key_ids = ids_own[:, None], ids_pad[None]
    cosine_table, sine_table = rope_tables(first_row, row_count, HEAD)
    places = jnp.full((1,), core, jnp.int32)
    layer_in, grad_out = tokens[0], cotangent[0]

    normed, query_raw, key_raw, queries, key_value, d_gains, h_gains = project(
        places, layer_in, mine, other, cosine_table, sine_table, shard_rows, q_cols, k_cols
    )
    halo = lax.ppermute(key_value, ("g", "y", "c"), [(i, i + 1) for i in range(seq_size - 1)])
    attended, log_total, branch, middle, normed_mlp = attend(
        queries, halo, key_value, query_ids, key_ids, w_o, layer_in, d_gains, attn_scale
    )

    half = row_count // 2
    from_x, from_y = swap(normed_mlp, "x"), swap(normed_mlp, "y")
    normed_far = jnp.concatenate([swap(from_x[:half], "y"), swap(from_y[half:], "x")])
    normed_near = jnp.concatenate([from_x, from_y])
    normed_all = [with_core(part) for part in (normed_mlp, normed_near, normed_far)]
    far_result = mlp_forward(normed_all[2], gate_up, down, normed_all[2])
    far_sum = core_sum(far_result[3]).astype(BF)
    near_result = mlp_forward(normed_all[1], gate_up, down, far_sum)
    to_x, to_y = sum_near(near_result[3], *send_far(far_sum))
    own_result = mlp_forward(normed_all[0], gate_up, down, to_x)
    mixed = sum_own(own_result[3], to_x, to_y)
    layer_out = middle + norm_gain(mixed, d_gains[3:4])

    _, pullback = jax.vjp(norm_gain, mixed, d_gains[3:4])
    grad_mixed, mixed_terms = pullback(grad_out.astype(F32))
    grad_mixed = grad_mixed.astype(BF)
    from_x, from_y = swap(grad_mixed, "x"), swap(grad_mixed, "y")
    grad_own = with_core(grad_mixed)
    own_grads = mlp_backward(grad_own, own_result[1], own_result[2], gate_up, down, down)
    from_x, from_y = lax.optimization_barrier((from_x, from_y, own_grads[1]))[:2]
    grad_far = with_core(jnp.concatenate([swap(from_x[:half], "y"), swap(from_y[half:], "x")]))
    grad_near = with_core(jnp.concatenate([from_x, from_y]))
    grad_down_terms = down_terms(
        [r[0] for r in (own_result, near_result, far_result)],
        [grad_own, grad_near, grad_far],
        hidden_own,
    )
    grad_down = lax.psum_scatter(grad_down_terms, "g", scatter_dimension=0, tiled=True)
    far_grads = mlp_backward(
        grad_far, far_result[1], far_result[2], gate_up, down, grad_down_terms
    )
    far_sum = core_sum(far_grads[1]).astype(BF)
    near_grads = mlp_backward(grad_near, near_result[1], near_result[2], gate_up, down, far_sum)
    to_x, to_y = sum_near(near_grads[1], *send_far(far_sum))
    gate_up_terms = gate_terms(
        normed_all, [g[0] for g in (own_grads, near_grads, far_grads)], groups, to_x
    )
    grad_normed_mlp = sum_own(own_grads[1], to_x, to_y)
    grad_normed_mlp = after(grad_normed_mlp, gate_up_terms, grad_down)
    term = gate_up_terms.reshape(groups * members * shard_rows, 2 * hidden_pad)
    gate_up_share = lax.psum_scatter(after(term, grad_down), "g", scatter_dimension=0, tiled=True)
    term = gate_up_share.reshape(members, shard_rows, 2 * hidden_pad)
    term = lax.all_to_all(term, PLANE, split_axis=0, concat_axis=0, tiled=True)

    def collect(cut):
        cut = cut[:, :, :hidden_own].reshape(2, members // 2, shard_rows, groups, piece)
        return cut.transpose(2, 0, 3, 1, 4).reshape(shard_rows, hidden_all).astype(F32)

    grad_w_gate = collect(term[:, :, :hidden_pad])
    grad_w_up = collect(term[:, :, hidden_pad:])

    grad_middle, grad_branch, grad_queries, grad_key_value, returned, terms = attend_backward(
        grad_normed_mlp, grad_out, middle, branch, d_gains, w_o,
        queries, halo, key_value, query_ids, key_ids, log_total, attn_scale,
    )
    returned = lax.ppermute(returned, ("g", "y", "c"), [(i + 1, i) for i in range(seq_size - 1)])
    out_terms = over_rows(attended, grad_branch).astype(BF)
    out_terms = out_terms.reshape(2, groups, 2, 2, w_out.shape[0], width)
    out_terms = plane_terms(fold(out_terms, "c", 3))
    grad_in, mine, sent = project_backward(
        places, grad_queries, grad_key_value, returned, query_raw, key_raw,
        cosine_table, sine_table, h_gains, normed, mine, other,
        grad_middle, layer_in, d_gains, terms, mixed_terms, shard_rows,
    )
    mine = (mine.astype(F32) + swap(sent, "c").astype(F32)).astype(BF)
    qkv_terms = plane_terms(mine.reshape(2, groups, 2, 2 * shard_rows, half_cols))
    qkv_terms = qkv_terms.reshape(groups, -1, width)
    share = jnp.concatenate([out_terms, qkv_terms], axis=1)
    share = jnp.pad(share, ((0, 0), (0, -share.shape[1] % 32), (0, 0))).reshape(-1, width)
    share = lax.psum_scatter(after(share, gate_up_share), "g", scatter_dimension=0, tiled=True)
    grad_w_out = share[: w_out.shape[0]].astype(F32)
    qkv_rows = qkv_terms.shape[1]
    share = share[w_out.shape[0] :][:qkv_rows].reshape(2, shard_rows, half_cols)
    mine = lax.dynamic_index_in_dim(share, core, 0, keepdims=False)
    other = lax.dynamic_index_in_dim(share, 1 - core, 0, keepdims=False)
    first, second = in_order(mine, swap(other, "c"), core).astype(F32)
    half = q_cols // 2
    d_terms = first[:, half + k_cols :]
    return (
        layer_out.astype(BF)[None],
        grad_in[None],
        jnp.concatenate([first[:, :half], second[:, :half]], axis=1),
        first[:, half : half + k_cols],
        second[:, half : half + k_cols],
        grad_w_out,
        grad_w_gate,
        grad_w_up,
        grad_down.astype(F32),
        d_terms[:, 0],
        d_terms[:, 1],
        d_terms[:, 2],
        d_terms[:, 3],
        d_terms[:head_rows, 4],
        d_terms[:head_rows, 5],
    )


def solution(mesh):
    batch, seq = mesh.devices.shape
    fine = Mesh(mesh.devices.reshape(batch, seq // 4, 2, 2), ALL)
    rows = ("g", "y", "c")
    return jax.shard_map(
        on_device,
        mesh=fine,
        in_specs=(P("x", rows, None),) * 2
        + (P("x", None),)
        + (P(ALL, None),) * 7
        + (P(ALL),) * 6,
        out_specs=(P("x", rows, None),) * 2 + (P(ALL, None),) * 7 + (P(ALL),) * 6,
        check_vma=False,
    )
```

time: 714 us -> 624 us (0.87); the launches traced: 700 us -> 618 us
  local copies, waits for them, and re-layouts: 125 us -> 59.9 us
  other arithmetic: 101 us -> 45.3 us
  Pallas kernels: 139 us -> 184 us
  matrix products: 36.9 us -> 2.83 us
  waiting for transfers between devices: 217 us -> 246 us
    pallas_call x0 -> x4, Pallas kernels: none -> 46.5 us  [the longest x1 16 us: attend_backward(): pl.pallas_call(functools.partial(attend_backward_kernel, scale), in_specs...]
    dot_general x12 -> x0, matrix products: 32.7 us -> none  [the longest x3 8.16 us: by_transpose(): lax.dot_general(left_side, right_side, (((1,), (1,)), ((), ())), preferre...]
    ppermute x1, waiting for transfers between devices: 8.42 us -> 36.2 us  [on_device(): lax.ppermute(returned, ('g', 'y', 'c'), [(i + 1, i) for i in range(seq_si...]
    unnamed x221 -> x63, local copies, waits for them, and re-layouts: 26.4 us -> 9.81 us
    all_to_all x1, waiting for transfers between devices: 0.01 us -> 13.4 us  [on_device(): term = lax.all_to_all(term, PLANE, split_axis=0, concat_axis=0, tiled=True)]
    reduce_scatter x2, waiting for transfers between devices: 13.3 us -> 0.01 us  [the longest x1 0.01 us: on_device(): lax.psum_scatter(after(term, grad_down), 'g', scatter_dimension=0, tiled=...]
    slice x21 -> x10, local copies, waits for them, and re-layouts: 12.9 us -> 2.26 us  [the longest x1 0.91 us: on_device(): share = share[w_out.shape[0]:][:qkv_rows].reshape(2, shard_rows, half_cols)]
    reshape x13 -> x4, local copies, waits for them, and re-layouts: 13.9 us -> 3.56 us  [the longest x1 2.21 us: on_device(): term = gate_up_share.reshape(members, shard_rows, 2 * hidden_pad)]
  transfers between devices with their start and end apart: 63 -> 62, of which waited for: 27 -> 34; matrix products, arithmetic and copies ran while one was open for 32% -> 13% of each run, Pallas kernels for 17% -> 18%
where the time goes in v5:
time: 624 us; the launch traced here: 618 us
  waiting for transfers between devices  246 us (39%)
  Pallas kernels  184 us (29%)
  starting transfers between devices  64.4 us (10%)
  local copies, waits for them, and re-layouts  59.9 us (10%)
  other arithmetic  45.3 us (7%)
  between operations  15.1 us (2%)
    ppermute x50, waiting for transfers between devices, swap(): return lax.ppermute(array, axis, [(0, 1), (1, 0)])  143 us
    pallas_call x3, Pallas kernels, mlp_backward(): pl.pallas_call(mlp_backward_kernel, grid=(rows // TILE,), in_specs=[row_b...  48.9 us
    pallas_call x3, Pallas kernels, mlp_forward(): pl.pallas_call(mlp_forward_kernel, grid=(rows // TILE,), in_specs=[row_bl...  48.1 us
    ppermute x50, starting transfers between devices, swap(): return lax.ppermute(array, axis, [(0, 1), (1, 0)])  39.4 us
    ppermute x1, waiting for transfers between devices, on_device(): lax.ppermute(returned, ('g', 'y', 'c'), [(i + 1, i) for i in range(seq_si...  36.2 us
    ppermute x1, waiting for transfers between devices, on_device(): lax.ppermute(key_value, ('g', 'y', 'c'), [(i, i + 1) for i in range(seq_s...  25.8 us
    pallas_call x1, Pallas kernels, gate_terms(): pl.pallas_call(gate_terms_kernel, grid=(both // 256,), in_specs=[whole_bl...  24.4 us
    ppermute x3, waiting for transfers between devices, group_gather(): lax.ppermute(own, 'g', [((i + k) % size, i) for i in range(size)])  19.5 us
  transfers between devices with their start and end apart: 62, of which 34 were waited for; matrix products, arithmetic and copies ran while one was open for 13% of the time, Pallas kernels for 18%

profile of v5, /device:TPU:13, one launch (start us, length us, event | category | flops | bytes accessed | tf_op | source)
XLA Modules:
  0.0 617.7 jit_solution(5017616796712806266)
XLA Ops:
  29.4 9.4 %collective-permute-done.2 = bf16[72,896]{1,0:T(8,128)(2,1)S(1)} collective-permute-done((bf16[72,896]{1,0:T(8,128)(2,1)S(1)}, bf16[72,896]{1,0:T(8,128)(2,1)S(1)}, u32[]{:S(2)}, u32[]{:S(2)}) %collective-permute-start.2) | collective-permute-done | bytes 129056 | tf_op jit(solution)/shard_map/ppermute | solution.py:242
  38.8 10.1 %collective-permute-done.3 = bf16[72,896]{1,0:T(8,128)(2,1)S(1)} collective-permute-done((bf16[72,896]{1,0:T(8,128)(2,1)S(1)}, bf16[72,896]{1,0:T(8,128)(2,1)S(1)}, u32[]{:S(2)}, u32[]{:S(2)}) %collective-permute-start.3) | collective-permute-done | bytes 129056 | tf_op jit(solution)/shard_map/ppermute | solution.py:242
  60.0 8.4 %collective-permute-done.7 = bf16[2,2,72,896]{3,2,1,0:T(8,128)(2,1)S(1)} collective-permute-done((bf16[2,2,72,896]{3,2,1,0:T(8,128)(2,1)S(1)}, bf16[2,2,72,896]{3,2,1,0:T(8,128)(2,1)S(1)}, u32[]{:S(2)}, u32[]{:S(2)}) %collective-permute-start.7) | collective-permute-done | bytes 516128 | tf_op jit(solution)/shard_map/ppermute | solution.py:51
  95.7 7.5 %shard_map.271 = (bf16[512,1152]{1,0:T(8,128)(2,1)}, f32[512,1024]{1,0:T(8,128)}, f32[512,256]{1,0:T(8,128)}, bf16[512,1024]{1,0:T(8,128)(2,1)}, bf16[512,512]{1...) custom-call(s32[1]{0:T(128)} %bitcast.core, bf16[512,1152]{1,0:T(8,128)(2,1)} %bitcast.197, ...), custom_call_target="tpu_custom_call" | custom-call | flops 1811939328 | bytes 9437184 | tf_op jit(solution)/shard_map/pallas_call | solution.py:347
  114.3 25.8 %collective-permute-done.9.halo = bf16[512,512]{1,0:T(8,128)(2,1)S(1)} collective-permute-done((bf16[512,512]{1,0:T(8,128)(2,1)}, bf16[512,512]{1,0:T(8,128)(2,1)S(1)}, u32[]{:S(2)}, u32[]{:S(2)}) %collective-permute-start.9) | collective-permute-done | bytes 524320 | tf_op jit(solution)/shard_map/ppermute | solution.py:690
  140.9 9.7 %shard_map.272 = (bf16[512,1024]{1,0:T(8,128)(2,1)}, f32[512,128]{1,0:T(8,128)}, f32[512,1152]{1,0:T(8,128)}, f32[512,1152]{1,0:T(8,128)}, bf16[512,1152]{1,0:T(8,128)(2,1)}) custom-call(bf16[512,1024]{1,0:T(8,128)(2,1)} %get-tuple-element.62.queries, bf16[512,512]{1,0:T(8,128)(2,1)} %copy-done.21, bf16[512,512]{1,0:T(8,128)(2,1)} %get-tuple-element.63.key_value, ...), custom_call_target="tpu_custom_call" | custom-call | flops 3355443200 | bytes 11796480 | tf_op jit(solution)/shard_map/pallas_call | solution.py:417
  150.6 21.6 %collective-permute-done.16 = bf16[512,1152]{1,0:T(8,128)(2,1)S(1)} collective-permute-done((bf16[512,1152]{1,0:T(8,128)(2,1)}, bf16[512,1152]{1,0:T(8,128)(2,1)S(1)}, u32[]{:S(2)}, u32[]{:S(2)}) %collective-permute-start.16) | collective-permute-done | bytes 1179680 | tf_op jit(solution)/shard_map/ppermute | solution.py:51
  193.8 13.1 %shard_map.273 = (bf16[1024,896]{1,0:T(8,128)(2,1)}, bf16[1024,896]{1,0:T(8,128)(2,1)}, bf16[1024,896]{1,0:T(8,128)(2,1)}, bf16[1024,1152]{1,0:T(8,128)(2,1)}) custom-call(bf16[1024,1152]{1,0:T(8,128)(2,1)} %constant_dynamic-update-slice_fusion.7.normed._.refs_2_, bf16[1152,1792]{1,0:T(8,128)(2,1)} %bitcast.181, bf16[896,1152]{1,0:T(8,128)(2,1)} %pad.31.down._, ...), custom_call_target="tpu_custom_call" | custom-call | flops 6341787648 | bytes 10223616 | tf_op jit(solution)/shard_map/pallas_call | solution.py:88
  214.4 21.8 %shard_map.274 = (bf16[2048,896]{1,0:T(8,128)(2,1)}, bf16[2048,896]{1,0:T(8,128)(2,1)}, bf16[2048,896]{1,0:T(8,128)(2,1)}, bf16[2048,1152]{1,0:T(8,128)(2,1)}) custom-call(bf16[2048,1152]{1,0:T(8,128)(2,1)} %copy-done.18, bf16[1152,1792]{1,0:T(8,128)(2,1)} %bitcast.182, bf16[896,1152]{1,0:T(8,128)(2,1)} %pad.31.down._, bf16[512,1152]{1,0:T(8,128)(2,1)} %add_convert_fusion.3._), custom_call_target="tpu_custom_call" | custom-call | flops 12683575296 | bytes 20447232 | tf_op jit(solution)/shard_map/pallas_call | solution.py:88
  247.1 12.3 %collective-permute-done.24 = bf16[256,1152]{1,0:T(8,128)(2,1)S(1)} collective-permute-done((bf16[256,1152]{1,0:T(8,128)(2,1)S(1)}, bf16[256,1152]{1,0:T(8,128)(2,1)S(1)}, u32[]{:S(2)}, u32[]{:S(2)}) %collective-permute-start.24) | collective-permute-done | bytes 589856 | tf_op jit(solution)/shard_map/ppermute | solution.py:51
  262.4 13.2 %shard_map.275 = (bf16[1024,896]{1,0:T(8,128)(2,1)}, bf16[1024,896]{1,0:T(8,128)(2,1)}, bf16[1024,896]{1,0:T(8,128)(2,1)}, bf16[1024,1152]{1,0:T(8,128)(2,1)}) custom-call(bf16[1024,1152]{1,0:T(8,128)(2,1)} %copy-done.14, bf16[1152,1792]{1,0:T(8,128)(2,1)} %bitcast.183, bf16[896,1152]{1,0:T(8,128)(2,1)} %pad.31.down._, bf16[512,1152]{1,0:T(8,128)(2,1)} %copy-done.13), custom_call_target="tpu_custom_call" | custom-call | flops 6341787648 | bytes 10223616 | tf_op jit(solution)/shard_map/pallas_call | solution.py:88
  298.3 13.4 %shard_map.276 = (bf16[1024,1792]{1,0:T(8,128)(2,1)}, bf16[1024,1152]{1,0:T(8,128)(2,1)}) custom-call(bf16[1024,1152]{1,0:T(8,128)(2,1)} %pad_maximum_fusion.1.grad_mixed.refs_3_, bf16[1024,896]{1,0:T(8,128)(2,1)} %get-tuple-element.71.gelu, bf16[1024,896]{1,0:T(8,128)(2,1)} %get-tuple-element.72.slope, bf16[1152,1792]{1,0:T(8,128)(2,1)} %bitcast.184, ...), custom_call_target="tpu_custom_call" | custom-call | flops 6341787648 | bytes 12058624 | tf_op jit(solution)/shard_map/pallas_call | solution.py:121
  311.7 10.1 %collective-permute-done.31 = bf16[512,1152]{1,0:T(8,128)(2,1)S(1)} collective-permute-done((bf16[512,1152]{1,0:T(8,128)(2,1)S(1)}, bf16[512,1152]{1,0:T(8,128)(2,1)S(1)}, u32[]{:S(2)}, u32[]{:S(2)}) %collective-permute-start.31) | collective-permute-done | bytes 1179680 | tf_op jit(solution)/shard_map/ppermute | solution.py:51
  325.7 13.4 %collective-permute-done.34 = bf16[256,1152]{1,0:T(8,128)(2,1)S(1)} collective-permute-done((bf16[256,1152]{1,0:T(8,128)(2,1)S(1)}, bf16[256,1152]{1,0:T(8,128)(2,1)S(1)}, u32[]{:S(2)}, u32[]{:S(2)}) %collective-permute-start.34) | collective-permute-done | bytes 589856 | tf_op jit(solution)/shard_map/ppermute | solution.py:51
  346.4 16.6 %shard_map.277._ = bf16[864,1152]{1,0:T(8,128)(2,1)} custom-call(bf16[1024,896]{1,0:T(8,128)(2,1)} %get-tuple-element.80.refs_0_, bf16[2048,896]{1,0:T(8,128)(2,1)} %get-tuple-element.81.refs_1_, bf16[1024,896]{1,0:T(8,128)(2,1)} %get-tuple-element.82.refs_2_, bf16[1024,1152]{1,0:T(8,128)(2,1)} %pad_maximum_fusion.1.grad_mixed.refs_3_, ...), custom_call_target="tpu_custom_call" | custom-call | flops 8455716864 | bytes 16777216 | tf_op jit(solution)/shard_map/pallas_call | solution.py:156
  363.0 13.5 %shard_map.278 = (bf16[1024,1792]{1,0:T(8,128)(2,1)}, bf16[1024,1152]{1,0:T(8,128)(2,1)}) custom-call(bf16[1024,1152]{1,0:T(8,128)(2,1)} %copy-done.20, bf16[1024,896]{1,0:T(8,128)(2,1)} %get-tuple-element.78.gelu, bf16[1024,896]{1,0:T(8,128)(2,1)} %get-tuple-element.79.slope, bf16[1152,1792]{1,0:T(8,128)(2,1)} %bitcast.185, bf16[896,1152]{1,0:T(8,128)(2,1)} %pad.31.down._, ...), custom_call_target="tpu_custom_call" | custom-call | flops 6341787648 | bytes 12058624 | tf_op jit(solution)/shard_map/pallas_call | solution.py:121
  382.2 22.0 %shard_map.279 = (bf16[2048,1792]{1,0:T(8,128)(2,1)}, bf16[2048,1152]{1,0:T(8,128)(2,1)}) custom-call(bf16[2048,1152]{1,0:T(8,128)(2,1)} %copy-done.19, bf16[2048,896]{1,0:T(8,128)(2,1)} %get-tuple-element.76.gelu, bf16[2048,896]{1,0:T(8,128)(2,1)} %get-tuple-element.77.slope, bf16[1152,1792]{1,0:T(8,128)(2,1)} %bitcast.186, bf16[896,1152]{1,0:T(8,128)(2,1)} %pad.31.down._, ...), custom_call_target="tpu_custom_call" | custom-call | flops 12683575296 | bytes 24117248 | tf_op jit(solution)/shard_map/pallas_call | solution.py:121
  415.6 8.4 %collective-permute-done.39 = bf16[256,1152]{1,0:T(8,128)(2,1)S(1)} collective-permute-done((bf16[256,1152]{1,0:T(8,128)(2,1)S(1)}, bf16[256,1152]{1,0:T(8,128)(2,1)S(1)}, u32[]{:S(2)}, u32[]{:S(2)}) %collective-permute-start.39) | collective-permute-done | bytes 589856 | tf_op jit(solution)/shard_map/ppermute | solution.py:51
  428.8 24.4 %shard_map.280 = bf16[4,2,144,1792]{3,2,1,0:T(8,128)(2,1)} custom-call(bf16[1024,1152]{1,0:T(8,128)(2,1)} %copy-done.14, bf16[2048,1152]{1,0:T(8,128)(2,1)} %copy-done.18, bf16[1024,1152]{1,0:T(8,128)(2,1)} %constant_dynamic-update-slice_fusion.7.normed._.refs_2_, bf16[1024,1792]{1,0:T(8,128)(2,1)} %get-tuple-element.85.refs_3_, ...), custom_call_target="tpu_custom_call" | custom-call | flops 16911433728 | bytes 24117248 | tf_op jit(solution)/shard_map/pallas_call | solution.py:188
  464.6 16.0 %shard_map.281 = (f32[512,1152]{1,0:T(8,128)}, bf16[512,1152]{1,0:T(8,128)(2,1)}, f32[512,1024]{1,0:T(8,128)}, f32[512,512]{1,0:T(8,128)}, bf16[512,512]{1,0:T(8,128)(2,1)}, /*index=5*/f32[8,1152]{1,0:T(8,128)}) custom-call(f32[512,1152]{1,0:T(8,128)} %convert_add_fusion.3.grad_normed_mlp, bf16[512,1152]{1,0:T(8,128)(2,1)} %bitcast.177, ...), custom_call_target="tpu_custom_call" | custom-call | flops 6576668672 | bytes 17694720 | tf_op jit(solution)/shard_map/pallas_call | solution.py:499
  486.9 36.2 %collective-permute-done.43.returned = bf16[512,512]{1,0:T(8,128)(2,1)} collective-permute-done((bf16[512,512]{1,0:T(8,128)(2,1)}, bf16[512,512]{1,0:T(8,128)(2,1)}, u32[]{:S(2)}, u32[]{:S(2)}) %collective-permute-start.43) | collective-permute-done | bytes 524320 | tf_op jit(solution)/shard_map/ppermute | solution.py:750
  523.1 13.3 %shard_map.282 = (bf16[512,1152]{1,0:T(8,128)(2,1)}, bf16[1152,896]{1,0:T(8,128)(2,1)}, bf16[1152,896]{1,0:T(8,128)(2,1)}) custom-call(s32[1]{0:T(128)} %bitcast.core, f32[512,1024]{1,0:T(8,128)} %get-tuple-element.91.grad_queries, f32[512,512]{1,0:T(8,128)} %get-tuple-element.92.grad_key_value, bf16[512,512]{1,0:T(8,128)(2,1)} %collective-permute-done.43.returned, ...), custom_call_target="tpu_custom_call" | custom-call | flops 4227858432 | bytes 17694720 | tf_op jit(solution)/shard_map/pallas_call | solution.py:578
  553.1 11.2 %collective-permute-done.52 = bf16[2,2,72,896]{3,2,1,0:T(8,128)(2,1)S(1)} collective-permute-done((bf16[2,2,72,896]{3,2,1,0:T(8,128)(2,1)S(1)}, bf16[2,2,72,896]{3,2,1,0:T(8,128)(2,1)S(1)}, u32[]{:S(2)}, u32[]{:S(2)}) %collective-permute-start.52) | collective-permute-done | bytes 516128 | tf_op jit(solution)/shard_map/ppermute | solution.py:51
  582.9 13.4 %all-to-all-done.1 = bf16[8,36,1792]{2,1,0:T(8,128)(2,1)S(1)} async-done(((bf16[8,36,1792]{2,1,0:T(8,128)(2,1)}), bf16[8,36,1792]{2,1,0:T(8,128)(2,1)S(1)}, u32[]{:S(2)}, u32[]{:S(2)}) %all-to-all-start.1) | async-done | bytes 1032224 | tf_op jit(solution)/shard_map/all_to_all | solution.py:737
  (322 shorter events, 238.1 us)
Async XLA Ops:
  7.2 62.7 %all-gather.5.cloned.1.call-start = ((), (), s32[]{:S(2)}) async-start(), calls=%async_computation.7 | async-start | bytes 2856960 | tf_op jit(solution)/shard_map/all_gather | solution.py:662
  20.6 28.5 %all-to-all-start = ((bf16[8,36,1792]{2,1,0:T(8,128)(2,1)}), bf16[8,36,1792]{2,1,0:T(8,128)(2,1)S(1)}, u32[]{:S(2)}, u32[]{:S(2)}) async-start(bf16[8,36,1792]{2,1,0:T(8,128)(2,1)} %copy.107), calls=%async_computation | async-start | bytes 2293760 | tf_op jit(solution)/shard_map/all_to_all | solution.py:641
  24.7 163.5 %all-gather.7.cloned.1.call-start = ((), (), s32[]{:S(2)}) async-start(), calls=%async_computation.8 | async-start | bytes 5160960 | tf_op jit(solution)/shard_map/all_gather | solution.py:668
  27.1 21.7 %collective-permute-start.3 = (bf16[72,896]{1,0:T(8,128)(2,1)S(1)}, bf16[72,896]{1,0:T(8,128)(2,1)S(1)}, u32[]{:S(2)}, u32[]{:S(2)}) collective-permute-start(bf16[72,896]{1,0:T(8,128)(2,1)S(1)} %reshape.151), channel_id=1, source_target_pairs={{12,0},{0,4},{4,8},{8,12},{13,1},{1,5},{5,9},{9,13},{14,2},{2,6},{... | collective-permute-start | bytes 387080 | tf_op jit(solution)/shard_map/ppermute | solution.py:242
  59.0 401.7 %reduce-scatter.10.cloned.1.call-start = ((), (), s32[]{:S(2)}) async-start(), calls=%async_computation.9 | async-start | bytes 2488320
  73.0 22.7 %collective-permute-start.8 = (bf16[1152,896]{1,0:T(8,128)(2,1)S(1)}, bf16[1152,896]{1,0:T(8,128)(2,1)}, u32[]{:S(2)}, u32[]{:S(2)}) collective-permute-start(bf16[1152,896]{1,0:T(8,128)(2,1)S(1)} %bitcast.173), channel_id=1, source_target_pairs={{0,1},{1,0},{2,3},{3,2},{4,5},{5,4},{6,7},{7,6},{8,9},{9,8},{10,11... | collective-permute-start | bytes 6193160 | tf_op jit(solution)/shard_map/ppermute | solution.py:51
  89.9 20.5 %collective-permute-start.14 = (bf16[2,4,2,32,1152]{4,3,2,1,0:T(8,128)(2,1)}, bf16[2,4,2,32,1152]{4,3,2,1,0:T(8,128)(2,1)}, u32[]{:S(2)}, u32[]{:S(2)}) collective-permute-start(bf16[2,4,2,32,1152]{4,3,2,1,0:T(8,128)(2,1)} %get-tuple-element.143), channel_id=1, source_target_pairs={{0,1},{1,0},{2,3},{3,2},{4,5},{5,4},{6,7},{7,6},{8,9},{9,8},{10,11... | collective-permute-start | bytes 3538952 | tf_op jit(solution)/shard_map/ppermute | solution.py:51
  103.2 36.9 %collective-permute-start.9 = (bf16[512,512]{1,0:T(8,128)(2,1)}, bf16[512,512]{1,0:T(8,128)(2,1)S(1)}, u32[]{:S(2)}, u32[]{:S(2)}) collective-permute-start(bf16[512,512]{1,0:T(8,128)(2,1)} %get-tuple-element.63.key_value), channel_id=1, source_target_pairs={{0,1},{1,2},{2,3},{3,4},{4,5},{5,6},{6,7},{7,8},{8,9},{9,10},{10,1... | collective-permute-start | bytes 1572872 | tf_op jit(solution)/shard_map/ppermute | solution.py:690
  150.6 21.6 %collective-permute-start.16 = (bf16[512,1152]{1,0:T(8,128)(2,1)}, bf16[512,1152]{1,0:T(8,128)(2,1)S(1)}, u32[]{:S(2)}, u32[]{:S(2)}) collective-permute-start(bf16[512,1152]{1,0:T(8,128)(2,1)} %get-tuple-element.66), channel_id=1, source_target_pairs={{0,16},{16,0},{1,17},{17,1},{2,18},{18,2},{3,19},{19,3},{4,20},{20... | collective-permute-start | bytes 3538952 | tf_op jit(solution)/shard_map/ppermute | solution.py:51
  150.6 21.7 %collective-permute-start.17 = (bf16[512,1152]{1,0:T(8,128)(2,1)}, bf16[512,1152]{1,0:T(8,128)(2,1)S(1)}, u32[]{:S(2)}, u32[]{:S(2)}) collective-permute-start(bf16[512,1152]{1,0:T(8,128)(2,1)} %get-tuple-element.66), channel_id=1, source_target_pairs={{0,2},{2,0},{1,3},{3,1},{4,6},{6,4},{5,7},{7,5},{8,10},{10,8},{9,1... | collective-permute-start | bytes 3538952 | tf_op jit(solution)/shard_map/ppermute | solution.py:51
  183.9 24.8 %collective-permute-start.18 = (bf16[1024,1152]{1,0:T(8,128)(2,1)}, bf16[1024,1152]{1,0:T(8,128)(2,1)}, u32[]{:S(2)}, u32[]{:S(2)}) collective-permute-start(bf16[1024,1152]{1,0:T(8,128)(2,1)} %pad_maximum_fusion), channel_id=1, source_target_pairs={{0,1},{1,0},{2,3},{3,2},{4,5},{5,4},{6,7},{7,6},{8,9},{9,8},{10,11... | collective-permute-start | bytes 7077896 | tf_op jit(solution)/shard_map/ppermute | solution.py:51
  260.9 26.0 %collective-permute-start.28 = (bf16[512,1152]{1,0:T(8,128)(2,1)S(1)}, bf16[512,1152]{1,0:T(8,128)(2,1)S(1)}, u32[]{:S(2)}, u32[]{:S(2)}) collective-permute-start(bf16[512,1152]{1,0:T(8,128)(2,1)S(1)} %pad_maximum_fusion.7), channel_id=1, source_target_pairs={{0,2},{2,0},{1,3},{3,1},{4,6},{6,4},{5,7},{7,5},{8,10},{10,8},{9,1... | collective-permute-start | bytes 3538952 | tf_op jit(solution)/shard_map/ppermute | solution.py:51
  261.4 26.0 %collective-permute-start.26 = (bf16[512,1152]{1,0:T(8,128)(2,1)S(1)}, bf16[512,1152]{1,0:T(8,128)(2,1)S(1)}, u32[]{:S(2)}, u32[]{:S(2)}) collective-permute-start(bf16[512,1152]{1,0:T(8,128)(2,1)S(1)} %pad_maximum_fusion.6._), channel_id=1, source_target_pairs={{0,16},{16,0},{1,17},{17,1},{2,18},{18,2},{3,19},{19,3},{4,20},{20... | collective-permute-start | bytes 3538952 | tf_op jit(solution)/shard_map/ppermute | solution.py:51
  294.2 27.6 %collective-permute-start.31 = (bf16[512,1152]{1,0:T(8,128)(2,1)S(1)}, bf16[512,1152]{1,0:T(8,128)(2,1)S(1)}, u32[]{:S(2)}, u32[]{:S(2)}) collective-permute-start(bf16[512,1152]{1,0:T(8,128)(2,1)S(1)} %get-tuple-element.125), channel_id=1, source_target_pairs={{0,16},{16,0},{1,17},{17,1},{2,18},{18,2},{3,19},{19,3},{4,20},{20... | collective-permute-start | bytes 3538952 | tf_op jit(solution)/shard_map/ppermute | solution.py:51
  295.3 27.3 %collective-permute-start.32 = (bf16[512,1152]{1,0:T(8,128)(2,1)S(1)}, bf16[512,1152]{1,0:T(8,128)(2,1)S(1)}, u32[]{:S(2)}, u32[]{:S(2)}) collective-permute-start(bf16[512,1152]{1,0:T(8,128)(2,1)S(1)} %get-tuple-element.125), channel_id=1, source_target_pairs={{0,2},{2,0},{1,3},{3,1},{4,6},{6,4},{5,7},{7,5},{8,10},{10,8},{9,1... | collective-permute-start | bytes 3538952 | tf_op jit(solution)/shard_map/ppermute | solution.py:51
  322.7 20.2 %collective-permute-start.33 = (bf16[1024,1152]{1,0:T(8,128)(2,1)S(1)}, bf16[1024,1152]{1,0:T(8,128)(2,1)S(1)}, u32[]{:S(2)}, u32[]{:S(2)}) collective-permute-start(bf16[1024,1152]{1,0:T(8,128)(2,1)S(1)} %pad_maximum_fusion.2), channel_id=1, source_target_pairs={{0,1},{1,0},{2,3},{3,2},{4,5},{5,4},{6,7},{7,6},{8,9},{9,8},{10,11... | collective-permute-start | bytes 7077896 | tf_op jit(solution)/shard_map/ppermute | solution.py:51
  409.1 51.9 %collective-permute-start.30 = (bf16[512,1152]{1,0:T(8,128)(2,1)}, bf16[512,1152]{1,0:T(8,128)(2,1)}, u32[]{:S(2)}, u32[]{:S(2)}) collective-permute-start(bf16[512,1152]{1,0:T(8,128)(2,1)} %slice.206), channel_id=1, source_target_pairs={{0,1},{1,0},{2,3},{3,2},{4,5},{5,4},{6,7},{7,6},{8,9},{9,8},{10,11... | collective-permute-start | bytes 3538952 | tf_op jit(solution)/shard_map/ppermute | solution.py:51
  409.2 163.6 %reduce-scatter.6.cloned.1.call-start = ((), (), s32[]{:S(2)}) async-start(), calls=%async_computation.5 | async-start | bytes 5160960 | tf_op jit(solution)/shard_map/reduce_scatter | solution.py:735
  426.2 34.8 %collective-permute-start.42 = (bf16[512,1152]{1,0:T(8,128)(2,1)}, bf16[512,1152]{1,0:T(8,128)(2,1)S(1)}, u32[]{:S(2)}, u32[]{:S(2)}) collective-permute-start(bf16[512,1152]{1,0:T(8,128)(2,1)} %pad_maximum_fusion.10), channel_id=1, source_target_pairs={{0,2},{2,0},{1,3},{3,1},{4,6},{6,4},{5,7},{7,5},{8,10},{10,8},{9,1... | collective-permute-start | bytes 3538952 | tf_op jit(solution)/shard_map/ppermute | solution.py:51
  427.6 33.4 %collective-permute-start.40 = (bf16[512,1152]{1,0:T(8,128)(2,1)}, bf16[512,1152]{1,0:T(8,128)(2,1)}, u32[]{:S(2)}, u32[]{:S(2)}) collective-permute-start(bf16[512,1152]{1,0:T(8,128)(2,1)} %pad_maximum_fusion.9.refs_6_), channel_id=1, source_target_pairs={{0,16},{16,0},{1,17},{17,1},{2,18},{18,2},{3,19},{19,3},{4,20},{20... | collective-permute-start | bytes 3538952 | tf_op jit(solution)/shard_map/ppermute | solution.py:51
  460.8 143.0 %reduce-scatter.8.cloned.1.call-start = ((), (), s32[]{:S(2)}) async-start(), calls=%async_computation.6 | async-start | bytes 1105920 | tf_op jit(solution)/shard_map/reduce_scatter | solution.py:764
  483.6 52.9 %collective-permute-start.44 = (bf16[2,4,2,32,1152]{4,3,2,1,0:T(8,128)(2,1)S(1)}, bf16[2,4,2,32,1152]{4,3,2,1,0:T(8,128)(2,1)}, u32[]{:S(2)}, u32[]{:S(2)}) collective-permute-start(bf16[2,4,2,32,1152]{4,3,2,1,0:T(8,128)(2,1)S(1)} %dynamic-slice_bitcast_fusion), channel_id=1, source_target_pairs={{0,1},{1,0},{2,3},{3,2},{4,5},{5,4},{6,7},{7,6},{8,9},{9,8},{10,11... | collective-permute-start | bytes 3538952 | tf_op jit(solution)/shard_map/ppermute | solution.py:51
  484.2 38.9 %collective-permute-start.43 = (bf16[512,512]{1,0:T(8,128)(2,1)}, bf16[512,512]{1,0:T(8,128)(2,1)}, u32[]{:S(2)}, u32[]{:S(2)}) collective-permute-start(bf16[512,512]{1,0:T(8,128)(2,1)} %get-tuple-element.93), channel_id=1, source_target_pairs={{1,0},{2,1},{3,2},{4,3},{5,4},{6,5},{7,6},{8,7},{9,8},{10,9},{11,1... | collective-permute-start | bytes 1572872 | tf_op jit(solution)/shard_map/ppermute | solution.py:750
  575.1 21.1 %all-to-all-start.1 = ((bf16[8,36,1792]{2,1,0:T(8,128)(2,1)}), bf16[8,36,1792]{2,1,0:T(8,128)(2,1)S(1)}, u32[]{:S(2)}, u32[]{:S(2)}) async-start(bf16[8,36,1792]{2,1,0:T(8,128)(2,1)} %reshape.169), calls=%async_computation.3 | async-start | bytes 2293760 | tf_op jit(solution)/shard_map/all_to_all | solution.py:737
  (61 other events, 476.8 us)
Sparse Core Ops, SparseCore 0:
  10.2 57.9 all-gather.4
  69.7 84.6 all-gather.6
  409.4 51.3 reduce-scatter.9
  462.9 77.6 reduce-scatter.5
  573.0 23.1 reduce-scatter.7

commit v6 on v5

--- a/solution.py
+++ b/solution.py
@@ -215,7 +215,7 @@
 
 def send_far(far):
     half = far.shape[0] // 2
-    return swap(far[:half], "y").astype(F32), swap(far[half:], "x").astype(F32)
+    return swap(far[:half], "y"), swap(far[half:], "x")
 
 
 def sum_near(near, top, low):
@@ -259,6 +259,17 @@
     return jnp.concatenate([first, second], axis=1)
 
 
+def group_terms(term):
+    size = lax.axis_size("g")
+    place = lax.axis_index("g")
+    total = lax.dynamic_index_in_dim(term, place, 0, keepdims=False).astype(F32)
+    for k in range(1, size):
+        chunk = lax.dynamic_index_in_dim(term, lax.rem(place + k, size), 0, keepdims=False)
+        pairs = [(i, (i + k) % size) for i in range(size)]
+        total = total + lax.ppermute(chunk, "g", pairs).astype(F32)
+    return total
+
+
 def fold(term, axis, dim):
     place = lax.axis_index(axis)
     mine = lax.dynamic_index_in_dim(term, place, dim, keepdims=False)
@@ -305,11 +316,11 @@
 
 
 def project_kernel(
-    shard_rows, core, tokens, own, other, cosine, sine,
-    normed, query_raw, key_raw, queries, key_value, d_gains, h_gains,
+    shard_rows, core, tokens, earlier, own, other, cosine, sine,
+    normed, normed_earlier, query_raw, key_raw, queries, keys, values, d_gains, h_gains,
 ):
-    width = tokens.shape[1]
-    k_cols = key_raw.shape[1]
+    rows, width = tokens.shape
+    pad, k_cols = earlier.shape[0], key_raw.shape[1]
     half = query_raw.shape[1] // 2
     first_is_own = core[0] == 0
     block = jnp.where(
@@ -319,49 +330,59 @@
     d_gains[...] = flat
     chosen = matmul(flat.astype(BF), gain_places(width, k_cols, shard_rows))
     h_gains[...] = chosen
-    values = tokens[...].astype(F32)
-    low = (values * rms_scale(values) * flat[0:1]).astype(BF)
+    before = earlier[...].astype(F32)
+    low_before = (before * rms_scale(before) * flat[0:1]).astype(BF)
+    normed_earlier[...] = low_before
+    inputs = tokens[...].astype(F32)
+    low = (inputs * rms_scale(inputs) * flat[0:1]).astype(BF)
     normed[...] = low
     raw_own = matmul(low, own[:, : half + k_cols])
     raw_other = matmul(low, other[:, : half + k_cols])
+    before_own = matmul(low_before, own[:, half : half + k_cols])
+    before_other = matmul(low_before, other[:, half : half + k_cols])
     first = jnp.where(first_is_own, raw_own, raw_other)
     second = jnp.where(first_is_own, raw_other, raw_own)
     raw_query = jnp.concatenate([first[:, :half], second[:, :half]], axis=1)
-    raw_key = first[:, half:]
     query_raw[...] = raw_query
-    key_raw[...] = raw_key
-    cos, sin = cosine[...], sine[...]
+    values[:pad] = jnp.where(first_is_own, before_other, before_own).astype(BF)
+    values[pad:] = second[:, half:].astype(BF)
+    raw_before = jnp.where(first_is_own, before_own, before_other)
+    for raw, at in ((raw_before, slice(0, pad)), (first[:, half:], slice(pad, pad + rows))):
+        key_raw[at] = raw
+        part = raw * rms_scale(raw) * chosen[5:6]
+        keys[at] = turn_forward(part, cosine[at], sine[at]).astype(BF)
+    cos, sin = cosine[pad:], sine[pad:]
     for head in range(2 * half // k_cols):
         at = slice(head * k_cols, (head + 1) * k_cols)
         part = raw_query[:, at]
         part = part * rms_scale(part) * chosen[4:5]
         queries[:, at] = turn_forward(part, cos, sin).astype(BF)
-    part = raw_key * rms_scale(raw_key) * chosen[5:6]
-    key_value[:, :k_cols] = turn_forward(part, cos, sin).astype(BF)
-    key_value[:, k_cols:] = second[:, half:].astype(BF)
-
-
-def project(core, tokens, own, other, cosine, sine, shard_rows, q_cols, k_cols):
+
+
+def project(core, tokens, earlier, own, other, cosine, sine, shard_rows, q_cols, k_cols):
     rows, width = tokens.shape
+    seen = rows + earlier.shape[0]
     vmem = pl.BlockSpec(memory_space=pltpu.VMEM)
     return pl.pallas_call(
         functools.partial(project_kernel, shard_rows),
-        in_specs=[pl.BlockSpec(memory_space=pltpu.SMEM)] + [vmem] * 5,
-        out_specs=[vmem] * 7,
+        in_specs=[pl.BlockSpec(memory_space=pltpu.SMEM)] + [vmem] * 6,
+        out_specs=[vmem] * 9,
         out_shape=[
             jax.ShapeDtypeStruct((rows, width), BF),
+            jax.ShapeDtypeStruct(earlier.shape, BF),
             jax.ShapeDtypeStruct((rows, q_cols), F32),
-            jax.ShapeDtypeStruct((rows, k_cols), F32),
+            jax.ShapeDtypeStruct((seen, k_cols), F32),
             jax.ShapeDtypeStruct((rows, q_cols), BF),
-            jax.ShapeDtypeStruct((rows, 2 * k_cols), BF),
+            jax.ShapeDtypeStruct((seen, k_cols), BF),
+            jax.ShapeDtypeStruct((seen, k_cols), BF),
             jax.ShapeDtypeStruct((8, width), F32),
             jax.ShapeDtypeStruct((8, k_cols), F32),
         ],
         compiler_params=PARAMS,
         cost_estimate=pl.CostEstimate(
-            flops=2 * rows * width * (q_cols + 2 * k_cols), bytes_accessed=16 * rows * width, transcendentals=0
+            flops=2 * rows * width * (q_cols + 4 * k_cols), bytes_accessed=16 * rows * width, transcendentals=0
         ),
-    )(core, tokens, own, other, cosine, sine)
+    )(core, tokens, earlier, own, other, cosine, sine)
 
 
 def tile_mask(first, rows, first_key, keys, query_ids, key_ids, pad):
@@ -373,15 +394,11 @@
 
 
 def attend_kernel(
-    scale, queries, halo, key_value, query_ids, key_ids, w_o, tokens, d_gains,
-    attended, log_total, branch, middle, normed_mlp, keys, values,
+    scale, queries, keys, values, query_ids, key_ids, w_o, tokens, d_gains,
+    attended, log_total, branch, middle, normed_mlp,
 ):
-    pad, k_cols = halo.shape[0], halo.shape[1] // 2
     rows, q_cols = queries.shape
-    keys[:pad] = halo[:, :k_cols]
-    keys[pad:] = key_value[:, :k_cols]
-    values[:pad] = halo[:, k_cols:]
-    values[pad:] = key_value[:, k_cols:]
+    pad, k_cols = keys.shape[0] - rows, keys.shape[1]
     tile = rows // 2
     span = pad + tile
     lane = lax.broadcasted_iota(jnp.int32, (tile, 128), 1)
@@ -408,11 +425,9 @@
     normed_mlp[...] = (total * rms_scale(total) * d_gains[2:3]).astype(BF)
 
 
-def attend(queries, halo, key_value, query_ids, key_ids, w_o, tokens, d_gains, scale):
+def attend(queries, keys, values, query_ids, key_ids, w_o, tokens, d_gains, scale):
     rows, q_cols = queries.shape
     width = tokens.shape[1]
-    k_cols = halo.shape[1] // 2
-    pad = halo.shape[0]
     vmem = pl.BlockSpec(memory_space=pltpu.VMEM)
     return pl.pallas_call(
         functools.partial(attend_kernel, scale),
@@ -425,22 +440,20 @@
             jax.ShapeDtypeStruct((rows, width), F32),
             jax.ShapeDtypeStruct((rows, width), BF),
         ],
-        scratch_shapes=[pltpu.VMEM((pad + rows, k_cols), BF), pltpu.VMEM((pad + rows, k_cols), BF)],
         compiler_params=PARAMS,
         cost_estimate=pl.CostEstimate(
-            flops=2 * rows * q_cols * (width + 2 * (pad + rows)), bytes_accessed=20 * rows * width, transcendentals=0
+            flops=2 * rows * q_cols * (width + 2 * keys.shape[0]), bytes_accessed=20 * rows * width, transcendentals=0
         ),
-    )(queries, halo, key_value, query_ids, key_ids, w_o, tokens, d_gains)
+    )(queries, keys, values, query_ids, key_ids, w_o, tokens, d_gains)
 
 
 def attend_backward_kernel(
     scale, grad_normed_mlp, cotangent, middle, branch, d_gains, w_o,
-    queries, halo, key_value, query_ids, key_ids, log_total,
-    grad_middle, grad_branch, grad_queries, grad_key_value, returned, terms,
-    keys, values, grad_keys, grad_values, grad_attended,
+    queries, keys, values, query_ids, key_ids, log_total,
+    grad_middle, grad_branch, grad_queries, grad_keys, grad_values, terms, grad_attended,
 ):
-    pad, k_cols = halo.shape[0], halo.shape[1] // 2
     rows, q_cols = queries.shape
+    pad, k_cols = keys.shape[0] - rows, keys.shape[1]
     total = middle[...]
     from_mlp, mlp_terms = rms_backward(total, rms_scale(total), d_gains[2:3], grad_normed_mlp[...])
     grad_total = cotangent[...].astype(F32) + from_mlp
@@ -451,10 +464,6 @@
     grad_branch[...] = low
     terms[...] = jnp.concatenate([out_terms, mlp_terms, jnp.zeros((6, out.shape[1]), F32)], axis=0)
     grad_attended[...] = by_transpose(low, w_o[...]).astype(BF)
-    keys[:pad] = halo[:, :k_cols]
-    keys[pad:] = key_value[:, :k_cols]
-    values[:pad] = halo[:, k_cols:]
-    values[pad:] = key_value[:, k_cols:]
     grad_keys[...] = jnp.zeros_like(grad_keys)
     grad_values[...] = jnp.zeros_like(grad_values)
     tile = rows // 2
@@ -481,20 +490,14 @@
             value_total = value_total + over_rows(probabilities.astype(BF), grad)
         grad_keys[seen] = grad_keys[seen] + key_total * scale
         grad_values[seen] = grad_values[seen] + value_total
-    returned[:, :k_cols] = grad_keys[:pad].astype(BF)
-    returned[:, k_cols:] = grad_values[:pad].astype(BF)
-    grad_key_value[:, :k_cols] = grad_keys[pad:]
-    grad_key_value[:, k_cols:] = grad_values[pad:]
 
 
 def attend_backward(
     grad_normed_mlp, cotangent, middle, branch, d_gains, w_o,
-    queries, halo, key_value, query_ids, key_ids, log_total, scale,
+    queries, keys, values, query_ids, key_ids, log_total, scale,
 ):
     rows, q_cols = queries.shape
     width = middle.shape[1]
-    k_cols = halo.shape[1] // 2
-    pad = halo.shape[0]
     vmem = pl.BlockSpec(memory_space=pltpu.VMEM)
     return pl.pallas_call(
         functools.partial(attend_backward_kernel, scale),
@@ -504,37 +507,32 @@
             jax.ShapeDtypeStruct((rows, width), F32),
             jax.ShapeDtypeStruct((rows, width), BF),
             jax.ShapeDtypeStruct((rows, q_cols), F32),
-            jax.ShapeDtypeStruct((rows, 2 * k_cols), F32),
-            jax.ShapeDtypeStruct((pad, 2 * k_cols), BF),
+            jax.ShapeDtypeStruct(keys.shape, F32),
+            jax.ShapeDtypeStruct(keys.shape, F32),
             jax.ShapeDtypeStruct((8, width), F32),
         ],
-        scratch_shapes=[
-            pltpu.VMEM((pad + rows, k_cols), BF),
-            pltpu.VMEM((pad + rows, k_cols), BF),
-            pltpu.VMEM((pad + rows, k_cols), F32),
-            pltpu.VMEM((pad + rows, k_cols), F32),
-            pltpu.VMEM((rows, q_cols), BF),
-        ],
+        scratch_shapes=[pltpu.VMEM((rows, q_cols), BF)],
         compiler_params=PARAMS,
         cost_estimate=pl.CostEstimate(
-            flops=2 * rows * q_cols * (width + 5 * (pad + rows)), bytes_accessed=30 * rows * width, transcendentals=0
+            flops=2 * rows * q_cols * (width + 5 * keys.shape[0]), bytes_accessed=30 * rows * width, transcendentals=0
         ),
     )(
         grad_normed_mlp, cotangent, middle, branch, d_gains, w_o,
-        queries, halo, key_value, query_ids, key_ids, log_total,
+        queries, keys, values, query_ids, key_ids, log_total,
     )
 
 
 def project_backward_kernel(
-    shard_rows, core, grad_queries, grad_key_value, returned, query_raw, key_raw, cosine, sine,
-    h_gains, normed, own, other, grad_middle, tokens, d_gains, terms, mixed_terms,
-    grad_tokens, mine, sent,
+    shard_rows, core, grad_queries, grad_keys, grad_values, query_raw, key_raw, cosine, sine,
+    h_gains, normed, normed_earlier, own, other, tokens, earlier, d_gains, terms, mixed_terms,
+    grad_normed, returned, mine, sent,
 ):
-    width = tokens.shape[1]
-    k_cols = key_raw.shape[1]
+    rows, width = tokens.shape
+    pad, k_cols = earlier.shape[0], key_raw.shape[1]
     half = query_raw.shape[1] // 2
+    cols = half + k_cols
     first_is_own = core[0] == 0
-    cos, sin = cosine[...], sine[...]
+    cos, sin = cosine[pad:], sine[pad:]
     query_terms = jnp.zeros((1, k_cols), F32)
     parts = []
     for head in range(2 * half // k_cols):
@@ -544,22 +542,35 @@
         grad, term = rms_backward(raw, rms_scale(raw), h_gains[4:5], grad)
         query_terms = query_terms + term
         parts.append(grad.astype(BF))
-    total = grad_key_value[...] + returned[...].astype(F32)
     raw = key_raw[...]
-    grad = turn_backward(total[:, :k_cols], cos, sin)
+    grad = turn_backward(grad_keys[...], cosine[...], sine[...])
     grad, key_terms = rms_backward(raw, rms_scale(raw), h_gains[5:6], grad)
+    grad_key, grad_value = grad.astype(BF), grad_values[...].astype(BF)
+    returned[:, :k_cols] = grad_key[:pad]
+    returned[:, k_cols:] = grad_value[:pad]
+    kv_own = jnp.where(first_is_own, grad_key, grad_value)
+    kv_other = jnp.where(first_is_own, grad_value, grad_key)
     both = len(parts) // 2
-    first = jnp.concatenate(parts[:both] + [grad.astype(BF)], axis=1)
-    second = jnp.concatenate(parts[both:] + [total[:, k_cols:].astype(BF)], axis=1)
-    grad_own = jnp.where(first_is_own, first, second)
-    grad_other = jnp.where(first_is_own, second, first)
-    cols = half + k_cols
-    grad_normed = by_transpose(grad_own, own[:, :cols]) + by_transpose(grad_other, other[:, :cols])
+    first = jnp.concatenate(parts[:both], axis=1)
+    second = jnp.concatenate(parts[both:], axis=1)
+    q_own = jnp.where(first_is_own, first, second)
+    q_other = jnp.where(first_is_own, second, first)
+    grad_own = jnp.concatenate([q_own, kv_own[pad:]], axis=1)
+    grad_other = jnp.concatenate([q_other, kv_other[pad:]], axis=1)
+    total = by_transpose(grad_own, own[:, :cols]) + by_transpose(grad_other, other[:, :cols])
+    grad_normed[...] = total
     values = tokens[...].astype(F32)
-    from_attn, in_terms = rms_backward(values, rms_scale(values), d_gains[0:1], grad_normed)
-    grad_tokens[...] = (grad_middle[...] + from_attn).astype(BF)
-    mine[:, :cols] = over_rows(normed[...], grad_own).astype(BF)
-    sent[:, :cols] = over_rows(normed[...], grad_other).astype(BF)
+    in_terms = jnp.sum(total * values * rms_scale(values), axis=0, keepdims=True)
+    total = by_transpose(kv_own[:pad], own[:, half:cols])
+    total = total + by_transpose(kv_other[:pad], other[:, half:cols])
+    values = earlier[...].astype(F32)
+    in_terms = in_terms + jnp.sum(total * values * rms_scale(values), axis=0, keepdims=True)
+    low, low_before = normed[...], normed_earlier[...]
+    for out, query, key_value in ((mine, q_own, kv_own), (sent, q_other, kv_other)):
+        out[:, :half] = over_rows(low, query).astype(BF)
+        out[:, half:cols] = (
+            over_rows(low, key_value[pad:]) + over_rows(low_before, key_value[:pad])
+        ).astype(BF)
     heads = jnp.concatenate([query_terms, key_terms, jnp.zeros((6, k_cols), F32)], axis=0)
     placed = by_transpose(heads.astype(BF), gain_places(width, k_cols, shard_rows))
     block = jnp.concatenate(
@@ -570,28 +581,60 @@
 
 
 def project_backward(
-    core, grad_queries, grad_key_value, returned, query_raw, key_raw, cosine, sine,
-    h_gains, normed, own, other, grad_middle, tokens, d_gains, terms, mixed_terms, shard_rows,
+    core, grad_queries, grad_keys, grad_values, query_raw, key_raw, cosine, sine,
+    h_gains, normed, normed_earlier, own, other, tokens, earlier, d_gains, terms, mixed_terms,
+    shard_rows,
 ):
     rows, width = tokens.shape
+    pad, k_cols = earlier.shape[0], key_raw.shape[1]
     vmem = pl.BlockSpec(memory_space=pltpu.VMEM)
     return pl.pallas_call(
         functools.partial(project_backward_kernel, shard_rows),
-        in_specs=[pl.BlockSpec(memory_space=pltpu.SMEM)] + [vmem] * 16,
-        out_specs=[vmem] * 3,
+        in_specs=[pl.BlockSpec(memory_space=pltpu.SMEM)] + [vmem] * 17,
+        out_specs=[vmem] * 4,
         out_shape=[
-            jax.ShapeDtypeStruct((rows, width), BF),
+            jax.ShapeDtypeStruct((rows, width), F32),
+            jax.ShapeDtypeStruct((pad, 2 * k_cols), BF),
             jax.ShapeDtypeStruct(own.shape, BF),
             jax.ShapeDtypeStruct(own.shape, BF),
         ],
         compiler_params=PARAMS,
         cost_estimate=pl.CostEstimate(
-            flops=8 * rows * width * own.shape[1], bytes_accessed=30 * rows * width, transcendentals=0
+            flops=9 * rows * width * own.shape[1], bytes_accessed=30 * rows * width, transcendentals=0
         ),
     )(
-        core, grad_queries, grad_key_value, returned, query_raw, key_raw, cosine, sine,
-        h_gains, normed, own, other, grad_middle, tokens, d_gains, terms, mixed_terms,
-    )
+        core, grad_queries, grad_keys, grad_values, query_raw, key_raw, cosine, sine,
+        h_gains, normed, normed_earlier, own, other, tokens, earlier, d_gains, terms, mixed_terms,
+    )
+
+
+def grad_tokens_kernel(core, returned, grad_normed, own, other, tokens, d_gains, grad_middle, out):
+    k_cols = returned.shape[1] // 2
+    cols = own.shape[1] - 128
+    half = cols - k_cols
+    first_is_own = core[0] == 0
+    grad_key, grad_value = returned[:, :k_cols], returned[:, k_cols:]
+    kv_own = jnp.where(first_is_own, grad_key, grad_value)
+    kv_other = jnp.where(first_is_own, grad_value, grad_key)
+    total = grad_normed[...] + by_transpose(kv_own, own[:, half:cols])
+    total = total + by_transpose(kv_other, other[:, half:cols])
+    values = tokens[...].astype(F32)
+    from_attn, _ = rms_backward(values, rms_scale(values), d_gains[0:1], total)
+    out[...] = (grad_middle[...] + from_attn).astype(BF)
+
+
+def grad_tokens(core, returned, grad_normed, own, other, tokens, d_gains, grad_middle):
+    vmem = pl.BlockSpec(memory_space=pltpu.VMEM)
+    return pl.pallas_call(
+        grad_tokens_kernel,
+        in_specs=[pl.BlockSpec(memory_space=pltpu.SMEM)] + [vmem] * 7,
+        out_specs=vmem,
+        out_shape=jax.ShapeDtypeStruct(tokens.shape, BF),
+        compiler_params=PARAMS,
+        cost_estimate=pl.CostEstimate(
+            flops=2 * tokens.size * returned.shape[1], bytes_accessed=12 * tokens.size, transcendentals=0
+        ),
+    )(core, returned, grad_normed, own, other, tokens, d_gains, grad_middle)
 
 
 def on_device(
@@ -632,14 +675,16 @@
         block = jnp.stack(columns, axis=-1)
         return jnp.pad(block, ((0, 0), (0, 0), (0, 128 - len(columns))))
 
+    seq_place = lax.axis_index(("g", "y", "c"))
+    seq_size = lax.axis_size(("g", "y", "c"))
+    before = lax.ppermute(tokens[0], ("g", "y", "c"), [(i, i + 1) for i in range(seq_size - 1)])
+
     def spread(weight):
         cut = weight.reshape(shard_rows, 2, groups, members // 2, piece)
         cut = cut.transpose(1, 3, 0, 2, 4).reshape(members, shard_rows, hidden_own)
         return jnp.pad(cut, ((0, 0), (0, 0), (0, hidden_pad - hidden_own)))
 
     sent = jnp.concatenate([spread(w_gate), spread(w_up)], axis=2)
-    sent = lax.all_to_all(sent, PLANE, split_axis=0, concat_axis=0, tiled=True)
-    sent = sent.reshape(members * shard_rows, 2 * hidden_pad)
     core = lax.axis_index("c")
     half_cols = q_cols // 2 + k_cols + 128
     gains = gain_columns(
@@ -655,22 +700,22 @@
     mine = lax.dynamic_index_in_dim(halves, core, 0, keepdims=False)
     other = lax.dynamic_index_in_dim(halves, 1 - core, 0, keepdims=False)
     mine = in_order(mine, swap(other, "c"), core).reshape(2 * shard_rows, half_cols)
+    mine, before, sent = lax.optimization_barrier((mine, before, sent))
+    sent = lax.all_to_all(sent, PLANE, split_axis=0, concat_axis=0, tiled=True)
+    sent = sent.reshape(members * shard_rows, 2 * hidden_pad)
     mine, sent = lax.optimization_barrier((group_gather(mine), sent))
     mine = plane_weights(mine).reshape(width, half_cols)
     other = swap(mine, "c")
 
     down = lax.all_gather(jnp.concatenate([w_down, w_out]), "g", axis=0)
-    w_o = plane_weights(down[:, w_down.shape[0] :])
+    w_o = down[:, w_down.shape[0] :]
     down = down[:, : w_down.shape[0]].reshape(-1, width)
     down = jnp.pad(down, ((0, hidden_pad - hidden_own), (0, 0)))
-    w_o = in_order(w_o, swap(w_o, "c"), core).transpose(1, 2, 3, 0, 4, 5).reshape(q_cols, width)
 
     both = lax.all_gather(sent, "g", axis=0)
     both = both.reshape(groups, 2, members // 2 * shard_rows, 2 * hidden_pad)
     gate_up = both.transpose(1, 0, 2, 3).reshape(width, 2 * hidden_pad)
 
-    seq_place = lax.axis_index(("g", "y", "c"))
-    seq_size = lax.axis_size(("g", "y", "c"))
     first_row = seq_place * row_count
     ids_all = doc_ids[0]
     ids_own = lax.dynamic_slice_in_dim(ids_all, first_row, row_count, 0)
@@ -680,16 +725,17 @@
     ids_prev = jnp.where(seq_place > 0, ids_prev, -1)
     ids_pad = jnp.concatenate([ids_prev, ids_own])
     query_ids, key_ids = ids_own[:, None], ids_pad[None]
-    cosine_table, sine_table = rope_tables(first_row, row_count, HEAD)
+    cosine_table, sine_table = rope_tables(first_row - row_count, 2 * row_count, HEAD)
     places = jnp.full((1,), core, jnp.int32)
     layer_in, grad_out = tokens[0], cotangent[0]
 
-    normed, query_raw, key_raw, queries, key_value, d_gains, h_gains = project(
-        places, layer_in, mine, other, cosine_table, sine_table, shard_rows, q_cols, k_cols
-    )
-    halo = lax.ppermute(key_value, ("g", "y", "c"), [(i, i + 1) for i in range(seq_size - 1)])
+    normed, normed_before, query_raw, key_raw, queries, keys, values, d_gains, h_gains = project(
+        places, layer_in, before, mine, other, cosine_table, sine_table, shard_rows, q_cols, k_cols
+    )
+    w_o = plane_weights(after(w_o, keys))
+    w_o = in_order(w_o, swap(w_o, "c"), core).transpose(1, 2, 3, 0, 4, 5).reshape(q_cols, width)
     attended, log_total, branch, middle, normed_mlp = attend(
-        queries, halo, key_value, query_ids, key_ids, w_o, layer_in, d_gains, attn_scale
+        queries, keys, values, query_ids, key_ids, w_o, layer_in, d_gains, attn_scale
     )
 
     half = row_count // 2
@@ -700,7 +746,7 @@
     far_result = mlp_forward(normed_all[2], gate_up, down, normed_all[2])
     far_sum = core_sum(far_result[3]).astype(BF)
     near_result = mlp_forward(normed_all[1], gate_up, down, far_sum)
-    to_x, to_y = sum_near(near_result[3], *send_far(far_sum))
+    to_x, to_y = sum_near(*lax.optimization_barrier((near_result[3], *send_far(far_sum))))
     own_result = mlp_forward(normed_all[0], gate_up, down, to_x)
     mixed = sum_own(own_result[3], to_x, to_y)
     layer_out = middle + norm_gain(mixed, d_gains[3:4])
@@ -719,20 +765,20 @@
         [grad_own, grad_near, grad_far],
         hidden_own,
     )
-    grad_down = lax.psum_scatter(grad_down_terms, "g", scatter_dimension=0, tiled=True)
+    grad_down = group_terms(grad_down_terms.reshape(groups, -1, width))
     far_grads = mlp_backward(
         grad_far, far_result[1], far_result[2], gate_up, down, grad_down_terms
     )
     far_sum = core_sum(far_grads[1]).astype(BF)
     near_grads = mlp_backward(grad_near, near_result[1], near_result[2], gate_up, down, far_sum)
-    to_x, to_y = sum_near(near_grads[1], *send_far(far_sum))
+    to_x, to_y = sum_near(*lax.optimization_barrier((near_grads[1], *send_far(far_sum))))
     gate_up_terms = gate_terms(
         normed_all, [g[0] for g in (own_grads, near_grads, far_grads)], groups, to_x
     )
     grad_normed_mlp = sum_own(own_grads[1], to_x, to_y)
-    grad_normed_mlp = after(grad_normed_mlp, gate_up_terms, grad_down)
+    grad_normed_mlp = after(grad_normed_mlp, gate_up_terms)
     term = gate_up_terms.reshape(groups * members * shard_rows, 2 * hidden_pad)
-    gate_up_share = lax.psum_scatter(after(term, grad_down), "g", scatter_dimension=0, tiled=True)
+    gate_up_share = lax.psum_scatter(term, "g", scatter_dimension=0, tiled=True)
     term = gate_up_share.reshape(members, shard_rows, 2 * hidden_pad)
     term = lax.all_to_all(term, PLANE, split_axis=0, concat_axis=0, tiled=True)
 
@@ -743,28 +789,30 @@
     grad_w_gate = collect(term[:, :, :hidden_pad])
     grad_w_up = collect(term[:, :, hidden_pad:])
 
-    grad_middle, grad_branch, grad_queries, grad_key_value, returned, terms = attend_backward(
+    grad_middle, grad_branch, grad_queries, grad_keys, grad_values, terms = attend_backward(
         grad_normed_mlp, grad_out, middle, branch, d_gains, w_o,
-        queries, halo, key_value, query_ids, key_ids, log_total, attn_scale,
-    )
-    returned = lax.ppermute(returned, ("g", "y", "c"), [(i + 1, i) for i in range(seq_size - 1)])
+        queries, keys, values, query_ids, key_ids, log_total, attn_scale,
+    )
     out_terms = over_rows(attended, grad_branch).astype(BF)
     out_terms = out_terms.reshape(2, groups, 2, 2, w_out.shape[0], width)
     out_terms = plane_terms(fold(out_terms, "c", 3))
-    grad_in, mine, sent = project_backward(
-        places, grad_queries, grad_key_value, returned, query_raw, key_raw,
-        cosine_table, sine_table, h_gains, normed, mine, other,
-        grad_middle, layer_in, d_gains, terms, mixed_terms, shard_rows,
+    own_weights, other_weights = mine, other
+    grad_normed, returned, mine, sent = project_backward(
+        places, after(grad_queries, grad_down), grad_keys, grad_values, query_raw, key_raw,
+        cosine_table, sine_table, h_gains, normed, normed_before, own_weights, other_weights,
+        layer_in, before, d_gains, terms, mixed_terms, shard_rows,
+    )
+    returned = lax.ppermute(returned, ("g", "y", "c"), [(i + 1, i) for i in range(seq_size - 1)])
+    grad_in = grad_tokens(
+        places, returned, grad_normed, own_weights, other_weights, layer_in, d_gains, grad_middle
     )
     mine = (mine.astype(F32) + swap(sent, "c").astype(F32)).astype(BF)
     qkv_terms = plane_terms(mine.reshape(2, groups, 2, 2 * shard_rows, half_cols))
     qkv_terms = qkv_terms.reshape(groups, -1, width)
     share = jnp.concatenate([out_terms, qkv_terms], axis=1)
-    share = jnp.pad(share, ((0, 0), (0, -share.shape[1] % 32), (0, 0))).reshape(-1, width)
-    share = lax.psum_scatter(after(share, gate_up_share), "g", scatter_dimension=0, tiled=True)
-    grad_w_out = share[: w_out.shape[0]].astype(F32)
-    qkv_rows = qkv_terms.shape[1]
-    share = share[w_out.shape[0] :][:qkv_rows].reshape(2, shard_rows, half_cols)
+    share = group_terms(after(share, gate_up_share))
+    grad_w_out = share[: w_out.shape[0]]
+    share = share[w_out.shape[0] :].astype(BF).reshape(2, shard_rows, half_cols)
     mine = lax.dynamic_index_in_dim(share, core, 0, keepdims=False)
     other = lax.dynamic_index_in_dim(share, 1 - core, 0, keepdims=False)
     first, second = in_order(mine, swap(other, "c"), core).astype(F32)
@@ -779,7 +827,7 @@
         grad_w_out,
         grad_w_gate,
         grad_w_up,
-        grad_down.astype(F32),
+        grad_down,
         d_terms[:, 0],
         d_terms[:, 1],
         d_terms[:, 2],

time: 624 us -> 562 us (0.901)
  waiting for transfers between devices: 246 us -> 168 us
  Pallas kernels: 184 us -> 195 us
    ppermute x1, waiting for transfers between devices: 36.2 us -> 7.18 us  [on_device(): lax.ppermute(returned, ('g', 'y', 'c'), [(i + 1, i) for i in range(seq_si...]
    ppermute x1 -> x7, waiting for transfers between devices: 25.8 us -> 8.73 us  [the longest x6 6.56 us: group_terms(): total = total + lax.ppermute(chunk, 'g', pairs).astype(F32)]
    all_to_all x1, waiting for transfers between devices: 13.4 us -> 0.01 us  [on_device(): term = lax.all_to_all(term, PLANE, split_axis=0, concat_axis=0, tiled=True)]
    ppermute x50, waiting for transfers between devices: 143 us -> 135 us  [swap(): return lax.ppermute(array, axis, [(0, 1), (1, 0)])]
    ppermute x3, waiting for transfers between devices: 19.5 us -> 11.5 us  [group_gather(): lax.ppermute(own, 'g', [((i + k) % size, i) for i in range(size)])]
    unnamed x6 -> x3, waiting for transfers between devices: 7.55 us -> 0.05 us
    pallas_call x0 -> x1, Pallas kernels: none -> 6.52 us  [grad_tokens(): pl.pallas_call(grad_tokens_kernel, in_specs=[pl.BlockSpec(memory_space=pl...]
  transfers between devices with their start and end apart: 62 -> 66, of which waited for: 34 -> 31; matrix products, arithmetic and copies ran while one was open for 13% -> 14% of each run, Pallas kernels for 18% -> 28%
where the time goes in v6:
time: 562 us; the launch traced here: 557 us
  Pallas kernels  195 us (35%)
  waiting for transfers between devices  168 us (30%)
  starting transfers between devices  68.4 us (12%)
  local copies, waits for them, and re-layouts  66.1 us (12%)
  other arithmetic  40.8 us (7%)
  between operations  15.2 us (3%)
    ppermute x50, waiting for transfers between devices, swap(): return lax.ppermute(array, axis, [(0, 1), (1, 0)])  135 us
    pallas_call x3, Pallas kernels, mlp_backward(): pl.pallas_call(mlp_backward_kernel, grid=(rows // TILE,), in_specs=[row_b...  48.9 us
    pallas_call x3, Pallas kernels, mlp_forward(): pl.pallas_call(mlp_forward_kernel, grid=(rows // TILE,), in_specs=[row_bl...  48.3 us
    ppermute x50, starting transfers between devices, swap(): return lax.ppermute(array, axis, [(0, 1), (1, 0)])  38 us
    pallas_call x1, Pallas kernels, gate_terms(): pl.pallas_call(gate_terms_kernel, grid=(both // 256,), in_specs=[whole_bl...  24.4 us
    pallas_call x1, Pallas kernels, attend_backward(): pl.pallas_call(functools.partial(attend_backward_kernel, scale), in_specs...  16.9 us
    pallas_call x1, Pallas kernels, down_terms(): pl.pallas_call(down_terms_kernel, grid=(own // 128,), in_specs=[pl.BlockS...  16.6 us
    pallas_call x1, Pallas kernels, project_backward(): pl.pallas_call(functools.partial(project_backward_kernel, shard_rows), in...  15.2 us
  transfers between devices with their start and end apart: 66, of which 31 were waited for; matrix products, arithmetic and copies ran while one was open for 14% of the time, Pallas kernels for 28%

profile of v6, /device:TPU:13, one launch (start us, length us, event | category | flops | bytes accessed | tf_op | source)
XLA Modules:
  0.0 556.6 jit_solution(227238984450601330)
XLA Ops:
  28.2 8.9 %all-to-all-start = ((bf16[8,36,1792]{2,1,0:T(8,128)(2,1)}), bf16[8,36,1792]{2,1,0:T(8,128)(2,1)S(1)}, u32[]{:S(2)}, u32[]{:S(2)}) async-start(bf16[8,36,1792]{2,1,0:T(8,128)(2,1)} %copy.112), calls=%async_computation | async-start | bytes 2293760 | tf_op jit(solution)/shard_map/all_to_all | solution.py:704
  39.6 9.3 %collective-permute-done.4 = bf16[72,896]{1,0:T(8,128)(2,1)S(1)} collective-permute-done((bf16[72,896]{1,0:T(8,128)(2,1)S(1)}, bf16[72,896]{1,0:T(8,128)(2,1)S(1)}, u32[]{:S(2)}, u32[]{:S(2)}) %collective-permute-start.4) | collective-permute-done | bytes 129056 | tf_op jit(solution)/shard_map/ppermute | solution.py:242
  62.0 10.1 %collective-permute-done.8 = bf16[2,2,72,896]{3,2,1,0:T(8,128)(2,1)S(1)} collective-permute-done((bf16[2,2,72,896]{3,2,1,0:T(8,128)(2,1)S(1)}, bf16[2,2,72,896]{3,2,1,0:T(8,128)(2,1)S(1)}, u32[]{:S(2)}, u32[]{:S(2)}) %collective-permute-start.8) | collective-permute-done | bytes 516128 | tf_op jit(solution)/shard_map/ppermute | solution.py:51
  80.2 8.5 %shard_map.271 = (bf16[512,1152]{1,0:T(8,128)(2,1)}, bf16[512,1152]{1,0:T(8,128)(2,1)}, f32[512,1024]{1,0:T(8,128)}, f32[1024,256]{1,0:T(8,128)}, bf16[512,1024]...) custom-call(s32[1]{0:T(128)} %bitcast.core, ...), custom_call_target="tpu_custom_call" | custom-call | flops 2415919104 | bytes 9437184 | tf_op jit(solution)/shard_map/pallas_call | solution.py:366
  110.9 9.7 %shard_map.272 = (bf16[512,1024]{1,0:T(8,128)(2,1)}, f32[512,128]{1,0:T(8,128)}, f32[512,1152]{1,0:T(8,128)}, f32[512,1152]{1,0:T(8,128)}, bf16[512,1152]{1,0:T(8,128)(2,1)}) custom-call(bf16[512,1024]{1,0:T(8,128)(2,1)} %get-tuple-element.78.queries, bf16[1024,256]{1,0:T(8,128)(2,1)} %get-tuple-element.79.keys, bf16[1024,256]{1,0:T(8,128)(2,1)} %get-tuple-element.80.values, ...), custom_call_target="tpu_custom_call" | custom-call | flops 3355443200 | bytes 11796480 | tf_op jit(solution)/shard_map/pallas_call | solution.py:432
  121.7 26.3 %collective-permute-done.16 = bf16[512,1152]{1,0:T(8,128)(2,1)S(1)} collective-permute-done((bf16[512,1152]{1,0:T(8,128)(2,1)}, bf16[512,1152]{1,0:T(8,128)(2,1)S(1)}, u32[]{:S(2)}, u32[]{:S(2)}) %collective-permute-start.16) | collective-permute-done | bytes 1179680 | tf_op jit(solution)/shard_map/ppermute | solution.py:51
  149.4 12.4 %collective-permute-done.19 = bf16[256,1152]{1,0:T(8,128)(2,1)S(1)} collective-permute-done((bf16[256,1152]{1,0:T(8,128)(2,1)S(1)}, bf16[256,1152]{1,0:T(8,128)(2,1)S(1)}, u32[]{:S(2)}, u32[]{:S(2)}) %collective-permute-start.19) | collective-permute-done | bytes 589856 | tf_op jit(solution)/shard_map/ppermute | solution.py:51
  176.0 13.3 %shard_map.273 = (bf16[1024,896]{1,0:T(8,128)(2,1)}, bf16[1024,896]{1,0:T(8,128)(2,1)}, bf16[1024,896]{1,0:T(8,128)(2,1)}, bf16[1024,1152]{1,0:T(8,128)(2,1)}) custom-call(bf16[1024,1152]{1,0:T(8,128)(2,1)} %copy-done.24, bf16[1152,1792]{1,0:T(8,128)(2,1)} %bitcast.204, bf16[896,1152]{1,0:T(8,128)(2,1)} %pad.27.down._, bf16[1024,1152]{1,0:T(8,128)(2,1)} %copy-done.24), custom_call_target="tpu_custom_call" | custom-call | flops 6341787648 | bytes 10223616 | tf_op jit(solution)/shard_map/pallas_call | solution.py:88
  198.0 21.8 %shard_map.274 = (bf16[2048,896]{1,0:T(8,128)(2,1)}, bf16[2048,896]{1,0:T(8,128)(2,1)}, bf16[2048,896]{1,0:T(8,128)(2,1)}, bf16[2048,1152]{1,0:T(8,128)(2,1)}) custom-call(bf16[2048,1152]{1,0:T(8,128)(2,1)} %copy-done.22, bf16[1152,1792]{1,0:T(8,128)(2,1)} %bitcast.205, bf16[896,1152]{1,0:T(8,128)(2,1)} %pad.27.down._, bf16[512,1152]{1,0:T(8,128)(2,1)} %copy-done.3), custom_call_target="tpu_custom_call" | custom-call | flops 12683575296 | bytes 20447232 | tf_op jit(solution)/shard_map/pallas_call | solution.py:88
  233.0 13.1 %shard_map.275 = (bf16[1024,896]{1,0:T(8,128)(2,1)}, bf16[1024,896]{1,0:T(8,128)(2,1)}, bf16[1024,896]{1,0:T(8,128)(2,1)}, bf16[1024,1152]{1,0:T(8,128)(2,1)}) custom-call(bf16[1024,1152]{1,0:T(8,128)(2,1)} %copy-done.18, bf16[1152,1792]{1,0:T(8,128)(2,1)} %bitcast.206, bf16[896,1152]{1,0:T(8,128)(2,1)} %pad.27.down._, bf16[512,1152]{1,0:T(8,128)(2,1)} %copy-done.13), custom_call_target="tpu_custom_call" | custom-call | flops 6341787648 | bytes 10223616 | tf_op jit(solution)/shard_map/pallas_call | solution.py:88
  249.2 9.1 %collective-permute-done.28 = bf16[512,1152]{1,0:T(8,128)(2,1)S(1)} collective-permute-done((bf16[512,1152]{1,0:T(8,128)(2,1)S(1)}, bf16[512,1152]{1,0:T(8,128)(2,1)S(1)}, u32[]{:S(2)}, u32[]{:S(2)}) %collective-permute-start.28) | collective-permute-done | bytes 1179680 | tf_op jit(solution)/shard_map/ppermute | solution.py:51
  269.0 13.5 %shard_map.276 = (bf16[1024,1792]{1,0:T(8,128)(2,1)}, bf16[1024,1152]{1,0:T(8,128)(2,1)}) custom-call(bf16[1024,1152]{1,0:T(8,128)(2,1)} %pad_maximum_fusion.1.grad_mixed.refs_3_, bf16[1024,896]{1,0:T(8,128)(2,1)} %get-tuple-element.92.gelu, bf16[1024,896]{1,0:T(8,128)(2,1)} %get-tuple-element.93.slope, bf16[1152,1792]{1,0:T(8,128)(2,1)} %bitcast.207, ...), custom_call_target="tpu_custom_call" | custom-call | flops 6341787648 | bytes 12058624 | tf_op jit(solution)/shard_map/pallas_call | solution.py:121
  282.5 10.0 %collective-permute-done.31 = bf16[512,1152]{1,0:T(8,128)(2,1)S(1)} collective-permute-done((bf16[512,1152]{1,0:T(8,128)(2,1)S(1)}, bf16[512,1152]{1,0:T(8,128)(2,1)S(1)}, u32[]{:S(2)}, u32[]{:S(2)}) %collective-permute-start.31) | collective-permute-done | bytes 1179680 | tf_op jit(solution)/shard_map/ppermute | solution.py:51
  295.8 13.2 %collective-permute-done.34 = bf16[256,1152]{1,0:T(8,128)(2,1)S(1)} collective-permute-done((bf16[256,1152]{1,0:T(8,128)(2,1)S(1)}, bf16[256,1152]{1,0:T(8,128)(2,1)S(1)}, u32[]{:S(2)}, u32[]{:S(2)}) %collective-permute-start.34) | collective-permute-done | bytes 589856 | tf_op jit(solution)/shard_map/ppermute | solution.py:51
  317.6 16.6 %shard_map.277._ = bf16[864,1152]{1,0:T(8,128)(2,1)} custom-call(bf16[1024,896]{1,0:T(8,128)(2,1)} %get-tuple-element.101.refs_0_, bf16[2048,896]{1,0:T(8,128)(2,1)} %get-tuple-element.102.refs_1_, bf16[1024,896]{1,0:T(8,128)(2,1)} %get-tuple-element.103.refs_2_, bf16[1024,1152]{1,0:T(8,128)(2,1)} %pad_maximum_fusion.1.grad_mixed.refs_3_, ...), custom_call_target="tpu_custom_call" | custom-call | flops 8455716864 | bytes 16777216 | tf_op jit(solution)/shard_map/pallas_call | solution.py:156
  334.2 13.5 %shard_map.278 = (bf16[1024,1792]{1,0:T(8,128)(2,1)}, bf16[1024,1152]{1,0:T(8,128)(2,1)}) custom-call(bf16[1024,1152]{1,0:T(8,128)(2,1)} %copy-done.25, bf16[1024,896]{1,0:T(8,128)(2,1)} %get-tuple-element.99.gelu, bf16[1024,896]{1,0:T(8,128)(2,1)} %get-tuple-element.100.slope, bf16[1152,1792]{1,0:T(8,128)(2,1)} %bitcast.208, bf16[896,1152]{1,0:T(8,128)(2,1)} %pad.27.down._, ...), custom_call_target="tpu_custom_call" | custom-call | flops 6341787648 | bytes 12058624 | tf_op jit(solution)/shard_map/pallas_call | solution.py:121
  353.7 22.0 %shard_map.279 = (bf16[2048,1792]{1,0:T(8,128)(2,1)}, bf16[2048,1152]{1,0:T(8,128)(2,1)}) custom-call(bf16[2048,1152]{1,0:T(8,128)(2,1)} %copy-done.23, bf16[2048,896]{1,0:T(8,128)(2,1)} %get-tuple-element.97.gelu, bf16[2048,896]{1,0:T(8,128)(2,1)} %get-tuple-element.98.slope, bf16[1152,1792]{1,0:T(8,128)(2,1)} %bitcast.209, bf16[896,1152]{1,0:T(8,128)(2,1)} %pad.27.down._, ...), custom_call_target="tpu_custom_call" | custom-call | flops 12683575296 | bytes 24117248 | tf_op jit(solution)/shard_map/pallas_call | solution.py:121
  394.4 24.4 %shard_map.280 = bf16[4,2,144,1792]{3,2,1,0:T(8,128)(2,1)} custom-call(bf16[1024,1152]{1,0:T(8,128)(2,1)} %copy-done.18, bf16[2048,1152]{1,0:T(8,128)(2,1)} %copy-done.22, bf16[1024,1152]{1,0:T(8,128)(2,1)} %copy-done.24, bf16[1024,1792]{1,0:T(8,128)(2,1)} %get-tuple-element.109.refs_3_, bf16[2048,1792]{1,0:T(8,128)(2,1)} %get-tuple-element.110.refs_4_, ...), custom_call_target="tpu_custom_call" | custom-call | flops 16911433728 | bytes 24117248 | tf_op jit(solution)/shard_map/pallas_call | solution.py:188
  424.6 16.9 %shard_map.281 = (f32[512,1152]{1,0:T(8,128)}, bf16[512,1152]{1,0:T(8,128)(2,1)}, f32[512,1024]{1,0:T(8,128)}, f32[1024,256]{1,0:T(8,128)}, f32[1024,256]{1,0:T(8,128)}, /*index=5*/f32[8,1152]{1,0:T(8,128)}) custom-call(f32[512,1152]{1,0:T(8,128)} %convert_add_fusion.3.grad_normed_mlp, bf16[512,1152]{1,0:T(8,128)(2,1)} %bitcast.198, ...), custom_call_target="tpu_custom_call" | custom-call | flops 6576668672 | bytes 17694720 | tf_op jit(solution)/shard_map/pallas_call | solution.py:502
  449.2 15.2 %shard_map.282 = (f32[512,1152]{1,0:T(8,128)}, bf16[512,512]{1,0:T(8,128)(2,1)}, bf16[1152,896]{1,0:T(8,128)(2,1)}, bf16[1152,896]{1,0:T(8,128)(2,1)}) custom-call(s32[1]{0:T(128)} %bitcast.core, f32[512,1024]{1,0:T(8,128)} %get-tuple-element.116.grad_queries, f32[1024,256]{1,0:T(8,128)} %get-tuple-element.117.grad_keys, ...), custom_call_target="tpu_custom_call" | custom-call | flops 4756340736 | bytes 17694720 | tf_op jit(solution)/shard_map/pallas_call | solution.py:591
  466.9 7.1 %collective-permute-done.50 = bf16[2,2,32,1152]{3,2,1,0:T(8,128)(2,1)S(1)} collective-permute-done((bf16[2,2,32,1152]{3,2,1,0:T(8,128)(2,1)}, bf16[2,2,32,1152]{3,2,1,0:T(8,128)(2,1)S(1)}, u32[]{:S(2)}, u32[]{:S(2)}) %collective-permute-start.50) | collective-permute-done | bytes 294944 | tf_op jit(solution)/shard_map/ppermute | solution.py:51
  480.0 10.5 %collective-permute-done.55 = bf16[2,2,72,896]{3,2,1,0:T(8,128)(2,1)S(1)} collective-permute-done((bf16[2,2,72,896]{3,2,1,0:T(8,128)(2,1)S(1)}, bf16[2,2,72,896]{3,2,1,0:T(8,128)(2,1)S(1)}, u32[]{:S(2)}, u32[]{:S(2)}) %collective-permute-start.55) | collective-permute-done | bytes 516128 | tf_op jit(solution)/shard_map/ppermute | solution.py:51
  523.6 7.2 %collective-permute-done.46.returned = bf16[512,512]{1,0:T(8,128)(2,1)S(1)} collective-permute-done((bf16[512,512]{1,0:T(8,128)(2,1)}, bf16[512,512]{1,0:T(8,128)(2,1)S(1)}, u32[]{:S(2)}, u32[]{:S(2)}) %collective-permute-start.46) | collective-permute-done | bytes 524320 | tf_op jit(solution)/shard_map/ppermute | solution.py:805
  531.6 6.5 %shard_map.283 = bf16[512,1152]{1,0:T(8,128)(2,1)} custom-call(s32[1]{0:T(128)} %bitcast.core, bf16[512,512]{1,0:T(8,128)(2,1)} %copy-done.21, f32[512,1152]{1,0:T(8,128)} %get-tuple-element.126.grad_normed, bf16[1152,896]{1,0:T(8,128)(2,1)} %bitcast.196, bf16[1152,896]{1,0:T(8,128)(2,1)} %collective-permute-done.9.other, bf16[512,1152]{1,0:T(8,128)(2,1)} %bitcast.226, ...), custom_call_target="tpu_custom_call" | custom-call | flops 603979776 | bytes 7077888 | tf_op jit(solution)/shard_map/pallas_call | solution.py:628
  (345 shorter events, 222.2 us)
Async XLA Ops:
  7.2 72.0 %all-gather.5.cloned.1.call-start = ((), (), s32[]{:S(2)}) async-start(), calls=%async_computation.4 | async-start | bytes 2856960 | tf_op jit(solution)/shard_map/all_gather | solution.py:710
  27.0 21.8 %collective-permute-start.4 = (bf16[72,896]{1,0:T(8,128)(2,1)S(1)}, bf16[72,896]{1,0:T(8,128)(2,1)S(1)}, u32[]{:S(2)}, u32[]{:S(2)}) collective-permute-start(bf16[72,896]{1,0:T(8,128)(2,1)S(1)} %reshape.155), channel_id=1, source_target_pairs={{12,0},{0,4},{4,8},{8,12},{13,1},{1,5},{5,9},{9,13},{14,2},{2,6},{... | collective-permute-start | bytes 387080 | tf_op jit(solution)/shard_map/ppermute | solution.py:242
  28.2 23.5 %all-to-all-start = ((bf16[8,36,1792]{2,1,0:T(8,128)(2,1)}), bf16[8,36,1792]{2,1,0:T(8,128)(2,1)S(1)}, u32[]{:S(2)}, u32[]{:S(2)}) async-start(bf16[8,36,1792]{2,1,0:T(8,128)(2,1)} %copy.112), calls=%async_computation | async-start | bytes 2293760 | tf_op jit(solution)/shard_map/all_to_all | solution.py:704
  37.1 131.4 %all-gather.7.cloned.1.call-start = ((), (), s32[]{:S(2)}) async-start(), calls=%async_computation.5 | async-start | bytes 5160960 | tf_op jit(solution)/shard_map/all_gather | solution.py:715
  89.3 412.5 %reduce-scatter.2.cloned.1.call-start = ((), (), s32[]{:S(2)}) async-start(), calls=%async_computation.3 | async-start | bytes 5160960 | tf_op jit(solution)/shard_map/reduce_scatter | solution.py:781
  120.6 27.5 %collective-permute-start.16 = (bf16[512,1152]{1,0:T(8,128)(2,1)}, bf16[512,1152]{1,0:T(8,128)(2,1)S(1)}, u32[]{:S(2)}, u32[]{:S(2)}) collective-permute-start(bf16[512,1152]{1,0:T(8,128)(2,1)} %get-tuple-element.84), channel_id=1, source_target_pairs={{0,16},{16,0},{1,17},{17,1},{2,18},{18,2},{3,19},{19,3},{4,20},{20... | collective-permute-start | bytes 3538952 | tf_op jit(solution)/shard_map/ppermute | solution.py:51
  120.9 27.3 %collective-permute-start.17 = (bf16[512,1152]{1,0:T(8,128)(2,1)}, bf16[512,1152]{1,0:T(8,128)(2,1)S(1)}, u32[]{:S(2)}, u32[]{:S(2)}) collective-permute-start(bf16[512,1152]{1,0:T(8,128)(2,1)} %get-tuple-element.84), channel_id=1, source_target_pairs={{0,2},{2,0},{1,3},{3,1},{4,6},{6,4},{5,7},{7,5},{8,10},{10,8},{9,1... | collective-permute-start | bytes 3538952 | tf_op jit(solution)/shard_map/ppermute | solution.py:51
  166.9 25.0 %collective-permute-start.18 = (bf16[1024,1152]{1,0:T(8,128)(2,1)}, bf16[1024,1152]{1,0:T(8,128)(2,1)}, u32[]{:S(2)}, u32[]{:S(2)}) collective-permute-start(bf16[1024,1152]{1,0:T(8,128)(2,1)} %pad_maximum_fusion), channel_id=1, source_target_pairs={{0,1},{1,0},{2,3},{3,2},{4,5},{5,4},{6,7},{7,6},{8,9},{9,8},{10,11... | collective-permute-start | bytes 7077896 | tf_op jit(solution)/shard_map/ppermute | solution.py:51
  196.3 23.6 %collective-permute-start.23 = (bf16[256,1152]{1,0:T(8,128)(2,1)S(1)}, bf16[256,1152]{1,0:T(8,128)(2,1)S(1)}, u32[]{:S(2)}, u32[]{:S(2)}) collective-permute-start(bf16[256,1152]{1,0:T(8,128)(2,1)S(1)} %get-tuple-element.169), channel_id=1, source_target_pairs={{0,2},{2,0},{1,3},{3,1},{4,6},{6,4},{5,7},{7,5},{8,10},{10,8},{9,1... | collective-permute-start | bytes 1769480 | tf_op jit(solution)/shard_map/ppermute | solution.py:51
  197.7 22.2 %collective-permute-start.24 = (bf16[256,1152]{1,0:T(8,128)(2,1)S(1)}, bf16[256,1152]{1,0:T(8,128)(2,1)S(1)}, u32[]{:S(2)}, u32[]{:S(2)}) collective-permute-start(bf16[256,1152]{1,0:T(8,128)(2,1)S(1)} %get-tuple-element.168), channel_id=1, source_target_pairs={{0,16},{16,0},{1,17},{17,1},{2,18},{18,2},{3,19},{19,3},{4,20},{20... | collective-permute-start | bytes 1769480 | tf_op jit(solution)/shard_map/ppermute | solution.py:51
  231.0 27.2 %collective-permute-start.28 = (bf16[512,1152]{1,0:T(8,128)(2,1)S(1)}, bf16[512,1152]{1,0:T(8,128)(2,1)S(1)}, u32[]{:S(2)}, u32[]{:S(2)}) collective-permute-start(bf16[512,1152]{1,0:T(8,128)(2,1)S(1)} %pad_maximum_fusion.7), channel_id=1, source_target_pairs={{0,2},{2,0},{1,3},{3,1},{4,6},{6,4},{5,7},{7,5},{8,10},{10,8},{9,1... | collective-permute-start | bytes 3538952 | tf_op jit(solution)/shard_map/ppermute | solution.py:51
  232.0 26.9 %collective-permute-start.27 = (bf16[512,1152]{1,0:T(8,128)(2,1)S(1)}, bf16[512,1152]{1,0:T(8,128)(2,1)S(1)}, u32[]{:S(2)}, u32[]{:S(2)}) collective-permute-start(bf16[512,1152]{1,0:T(8,128)(2,1)S(1)} %pad_maximum_fusion.6._), channel_id=1, source_target_pairs={{0,16},{16,0},{1,17},{17,1},{2,18},{18,2},{3,19},{19,3},{4,20},{20... | collective-permute-start | bytes 3538952 | tf_op jit(solution)/shard_map/ppermute | solution.py:51
  264.9 27.6 %collective-permute-start.31 = (bf16[512,1152]{1,0:T(8,128)(2,1)S(1)}, bf16[512,1152]{1,0:T(8,128)(2,1)S(1)}, u32[]{:S(2)}, u32[]{:S(2)}) collective-permute-start(bf16[512,1152]{1,0:T(8,128)(2,1)S(1)} %get-tuple-element.151), channel_id=1, source_target_pairs={{0,16},{16,0},{1,17},{17,1},{2,18},{18,2},{3,19},{19,3},{4,20},{20... | collective-permute-start | bytes 3538952 | tf_op jit(solution)/shard_map/ppermute | solution.py:51
  265.3 27.3 %collective-permute-start.32 = (bf16[512,1152]{1,0:T(8,128)(2,1)S(1)}, bf16[512,1152]{1,0:T(8,128)(2,1)S(1)}, u32[]{:S(2)}, u32[]{:S(2)}) collective-permute-start(bf16[512,1152]{1,0:T(8,128)(2,1)S(1)} %get-tuple-element.151), channel_id=1, source_target_pairs={{0,2},{2,0},{1,3},{3,1},{4,6},{6,4},{5,7},{7,5},{8,10},{10,8},{9,1... | collective-permute-start | bytes 3538952 | tf_op jit(solution)/shard_map/ppermute | solution.py:51
  352.5 23.2 %collective-permute-start.38 = (bf16[256,1152]{1,0:T(8,128)(2,1)S(1)}, bf16[256,1152]{1,0:T(8,128)(2,1)S(1)}, u32[]{:S(2)}, u32[]{:S(2)}) collective-permute-start(bf16[256,1152]{1,0:T(8,128)(2,1)S(1)} %get-tuple-element.167), channel_id=1, source_target_pairs={{0,2},{2,0},{1,3},{3,1},{4,6},{6,4},{5,7},{7,5},{8,10},{10,8},{9,1... | collective-permute-start | bytes 1769480 | tf_op jit(solution)/shard_map/ppermute | solution.py:51
  352.6 23.0 %collective-permute-start.39 = (bf16[256,1152]{1,0:T(8,128)(2,1)S(1)}, bf16[256,1152]{1,0:T(8,128)(2,1)S(1)}, u32[]{:S(2)}, u32[]{:S(2)}) collective-permute-start(bf16[256,1152]{1,0:T(8,128)(2,1)S(1)} %get-tuple-element.166), channel_id=1, source_target_pairs={{0,16},{16,0},{1,17},{17,1},{2,18},{18,2},{3,19},{19,3},{4,20},{20... | collective-permute-start | bytes 1769480 | tf_op jit(solution)/shard_map/ppermute | solution.py:51
  381.5 37.3 %collective-permute-start.30 = (bf16[512,1152]{1,0:T(8,128)(2,1)}, bf16[512,1152]{1,0:T(8,128)(2,1)S(1)}, u32[]{:S(2)}, u32[]{:S(2)}) collective-permute-start(bf16[512,1152]{1,0:T(8,128)(2,1)} %slice.206), channel_id=1, source_target_pairs={{0,1},{1,0},{2,3},{3,2},{4,5},{5,4},{6,7},{7,6},{8,9},{9,8},{10,11... | collective-permute-start | bytes 3538952 | tf_op jit(solution)/shard_map/ppermute | solution.py:51
  384.8 61.7 %collective-permute-start.45 = (bf16[216,1152]{1,0:T(8,128)(2,1)}, bf16[216,1152]{1,0:T(8,128)(2,1)}, u32[]{:S(2)}, u32[]{:S(2)}) collective-permute-start(bf16[216,1152]{1,0:T(8,128)(2,1)} %get-tuple-element.162), channel_id=1, source_target_pairs={{0,12},{4,0},{8,4},{12,8},{1,13},{5,1},{9,5},{13,9},{2,14},{6,2},{... | collective-permute-start | bytes 1493000 | tf_op jit(solution)/shard_map/ppermute | solution.py:269
  385.3 61.2 %collective-permute-start.44 = (bf16[216,1152]{1,0:T(8,128)(2,1)}, bf16[216,1152]{1,0:T(8,128)(2,1)}, u32[]{:S(2)}, u32[]{:S(2)}) collective-permute-start(bf16[216,1152]{1,0:T(8,128)(2,1)} %get-tuple-element.163), channel_id=1, source_target_pairs={{0,8},{4,12},{8,0},{12,4},{1,9},{5,13},{9,1},{13,5},{2,10},{6,14},... | collective-permute-start | bytes 1493000 | tf_op jit(solution)/shard_map/ppermute | solution.py:269
  391.8 28.5 %collective-permute-start.42 = (bf16[512,1152]{1,0:T(8,128)(2,1)}, bf16[512,1152]{1,0:T(8,128)(2,1)}, u32[]{:S(2)}, u32[]{:S(2)}) collective-permute-start(bf16[512,1152]{1,0:T(8,128)(2,1)} %pad_maximum_fusion.10), channel_id=1, source_target_pairs={{0,2},{2,0},{1,3},{3,1},{4,6},{6,4},{5,7},{7,5},{8,10},{10,8},{9,1... | collective-permute-start | bytes 3538952 | tf_op jit(solution)/shard_map/ppermute | solution.py:51
  394.0 26.9 %collective-permute-start.41 = (bf16[512,1152]{1,0:T(8,128)(2,1)}, bf16[512,1152]{1,0:T(8,128)(2,1)}, u32[]{:S(2)}, u32[]{:S(2)}) collective-permute-start(bf16[512,1152]{1,0:T(8,128)(2,1)} %pad_maximum_fusion.9.refs_6_), channel_id=1, source_target_pairs={{0,16},{16,0},{1,17},{17,1},{2,18},{18,2},{3,19},{19,3},{4,20},{20... | collective-permute-start | bytes 3538952 | tf_op jit(solution)/shard_map/ppermute | solution.py:51
  418.8 27.7 %collective-permute-start.43 = (bf16[216,1152]{1,0:T(8,128)(2,1)}, bf16[216,1152]{1,0:T(8,128)(2,1)}, u32[]{:S(2)}, u32[]{:S(2)}) collective-permute-start(bf16[216,1152]{1,0:T(8,128)(2,1)} %get-tuple-element.161), channel_id=1, source_target_pairs={{0,4},{4,8},{8,12},{12,0},{1,5},{5,9},{9,13},{13,1},{2,6},{6,10},{... | collective-permute-start | bytes 1493000 | tf_op jit(solution)/shard_map/ppermute | solution.py:269
  505.3 25.5 %collective-permute-start.46 = (bf16[512,512]{1,0:T(8,128)(2,1)}, bf16[512,512]{1,0:T(8,128)(2,1)S(1)}, u32[]{:S(2)}, u32[]{:S(2)}) collective-permute-start(bf16[512,512]{1,0:T(8,128)(2,1)} %get-tuple-element.125), channel_id=1, source_target_pairs={{1,0},{2,1},{3,2},{4,3},{5,4},{6,5},{7,6},{8,7},{9,8},{10,9},{11,1... | collective-permute-start | bytes 1572872 | tf_op jit(solution)/shard_map/ppermute | solution.py:805
  510.7 31.7 %all-to-all-start.1 = ((bf16[8,36,1792]{2,1,0:T(8,128)(2,1)}), bf16[8,36,1792]{2,1,0:T(8,128)(2,1)S(1)}, u32[]{:S(2)}, u32[]{:S(2)}) async-start(bf16[8,36,1792]{2,1,0:T(8,128)(2,1)} %reshape.173), calls=%async_computation.2 | async-start | bytes 2293760 | tf_op jit(solution)/shard_map/all_to_all | solution.py:783
  (71 other events, 598.1 us)
Sparse Core Ops, SparseCore 0:
  17.2 55.7 all-gather.4
  89.4 76.4 all-gather.6
  418.9 82.8 reduce-scatter.1

commit v7 on v6

--- a/solution.py
+++ b/solution.py
@@ -53,7 +53,7 @@
 
 GELU_A = 0.7978845608028654
 GELU_B = 0.044715
-TILE = 512
+STEP = 256
 PARAMS = pltpu.CompilerParams(vmem_limit_bytes=58 << 20)
 
 
@@ -65,9 +65,63 @@
     return pl.BlockSpec((rows, columns), lambda i: (i, 0))
 
 
-def mlp_forward_kernel(normed, gate_up, down, _, hidden, gelu, slope, mixed):
+def place_weights(blocks, out, sems):
+    groups, sides, rows, _ = blocks.shape
+    copies = []
+    for side in range(sides):
+        for group in range(groups):
+            at = side * groups + group
+            copies.append(
+                pltpu.make_async_copy(
+                    blocks.at[group, side], out.at[pl.ds(at * rows, rows)], sems.at[at]
+                )
+            )
+    return copies
+
+
+def fetch_tile(tiles, step, buffer, sems):
+    for at, tile in enumerate(tiles):
+
+        @pl.when(step == at)
+        def _():
+            pltpu.make_async_copy(tile, buffer.at[at % 2], sems.at[at % 2]).start()
+
+
+def next_tile(tiles, buffer, sems, blocks, gate_up, weight_sems):
+    step = pl.program_id(0)
+
+    @pl.when(step == 0)
+    def _():
+        copies = place_weights(blocks, gate_up, weight_sems)
+        for copy in copies:
+            copy.start()
+        fetch_tile(tiles, step, buffer, sems)
+        for copy in copies:
+            copy.wait()
+
+    fetch_tile(tiles, step + 1, buffer, sems)
+    slot = lax.rem(step, 2)
+    pltpu.make_async_copy(tiles[0], buffer.at[slot], sems.at[slot]).wait()
+    return buffer[slot]
+
+
+def store_half(value, mine, other, count):
+    step = pl.program_id(0)
+
+    @pl.when(step < count // 2)
+    def _():
+        mine[...] = value
+
+    @pl.when(step >= count // 2)
+    def _():
+        other[...] = value
+
+
+def mlp_forward_kernel(count, *refs):
+    tiles, refs = refs[:count], refs[count:]
+    blocks, down, _, hidden, gelu, slope, mine, other, buffer, gate_up, sems, weight_sems = refs
     own = down.shape[0]
-    raw = matmul(normed[...], gate_up[...])
+    raw = matmul(next_tile(tiles, buffer, sems, blocks, gate_up, weight_sems), gate_up[...])
     gate_raw, up_raw = raw[:, :own], raw[:, own:]
     square = gate_raw * gate_raw
     bend = jnp.tanh(GELU_A * (gate_raw + GELU_B * square * gate_raw))
@@ -78,75 +132,101 @@
     hidden[...] = low
     gelu[...] = active.astype(BF)
     slope[...] = ((half + turn) * up_raw).astype(BF)
-    mixed[...] = matmul(low, down[...]).astype(BF)
-
-
-def mlp_forward(normed, gate_up, down, earlier):
-    rows, width = normed.shape
+    store_half(matmul(low, down[...]).astype(BF), mine, other, count)
+
+
+def half_blocks(rows, columns, count):
+    return [
+        pl.BlockSpec((rows, columns), lambda i: (jnp.minimum(i, count // 2 - 1), 0)),
+        pl.BlockSpec((rows, columns), lambda i: (jnp.maximum(i - count // 2, 0), 0)),
+    ]
+
+
+def tile_scratch(tiles, blocks):
+    return [
+        pltpu.VMEM((2,) + tiles[0].shape, BF),
+        pltpu.VMEM((tiles[0].shape[1], blocks.shape[3]), BF),
+        pltpu.SemaphoreType.DMA((2,)),
+        pltpu.SemaphoreType.DMA((blocks.shape[0] * blocks.shape[1],)),
+    ]
+
+
+def mlp_forward(tiles, blocks, down, earlier):
+    count = len(tiles)
+    rows, width = tiles[0].shape
     own = down.shape[0]
-    flat = jax.ShapeDtypeStruct((rows, own), BF)
+    total = count * rows
+    flat = jax.ShapeDtypeStruct((total, own), BF)
+    part = jax.ShapeDtypeStruct((total // 2, width), BF)
+    anywhere = pl.BlockSpec(memory_space=pl.ANY)
     return pl.pallas_call(
-        mlp_forward_kernel,
-        grid=(rows // TILE,),
-        in_specs=[
-            row_block(TILE, width),
-            whole_block(gate_up.shape),
-            whole_block(down.shape),
-            pl.BlockSpec(memory_space=pl.ANY),
-        ],
-        out_specs=[row_block(TILE, own)] * 3 + [row_block(TILE, width)],
-        out_shape=[flat, flat, flat, jax.ShapeDtypeStruct((rows, width), BF)],
+        functools.partial(mlp_forward_kernel, count),
+        grid=(count,),
+        in_specs=[anywhere] * (count + 1) + [whole_block(down.shape), anywhere],
+        out_specs=[row_block(rows, own)] * 3 + half_blocks(rows, width, count),
+        out_shape=[flat, flat, flat, part, part],
+        scratch_shapes=tile_scratch(tiles, blocks),
         compiler_params=PARAMS,
         cost_estimate=pl.CostEstimate(
-            flops=6 * rows * width * own, bytes_accessed=rows * (4 * width + 6 * own), transcendentals=0
+            flops=6 * total * width * own, bytes_accessed=total * (4 * width + 6 * own), transcendentals=0
         ),
-    )(normed, gate_up, down, earlier)
-
-
-def mlp_backward_kernel(grad_mixed, gelu, slope, gate_up, down, _, grad_raw, grad_normed):
+    )(*tiles, blocks, down, earlier)
+
+
+def mlp_backward_kernel(count, *refs):
+    tiles, refs = refs[:count], refs[count:]
+    gelu, slope, blocks, down, _, grad_raw, mine, other, buffer, gate_up, sems, weight_sems = refs
     own = down.shape[0]
-    grad_hidden = by_transpose(grad_mixed[...], down[...])
+    grad_mixed = next_tile(tiles, buffer, sems, blocks, gate_up, weight_sems)
+    grad_hidden = by_transpose(grad_mixed, down[...])
     grad_gate = (grad_hidden * slope[...].astype(F32)).astype(BF)
     grad_up = (grad_hidden * gelu[...].astype(F32)).astype(BF)
     grad_raw[:, :own] = grad_gate
     grad_raw[:, own:] = grad_up
-    grad_normed[...] = (
-        by_transpose(grad_gate, gate_up[:, :own]) + by_transpose(grad_up, gate_up[:, own:])
-    ).astype(BF)
-
-
-def mlp_backward(grad_mixed, gelu, slope, gate_up, down, earlier):
-    rows, width = grad_mixed.shape
+    total = by_transpose(grad_gate, gate_up[:, :own]) + by_transpose(grad_up, gate_up[:, own:])
+    store_half(total.astype(BF), mine, other, count)
+
+
+def mlp_backward(tiles, gelu, slope, blocks, down, earlier):
+    count = len(tiles)
+    rows, width = tiles[0].shape
     own = down.shape[0]
+    total = count * rows
+    part = jax.ShapeDtypeStruct((total // 2, width), BF)
+    anywhere = pl.BlockSpec(memory_space=pl.ANY)
     return pl.pallas_call(
-        mlp_backward_kernel,
-        grid=(rows // TILE,),
-        in_specs=[
-            row_block(TILE, width),
-            row_block(TILE, own),
-            row_block(TILE, own),
-            whole_block(gate_up.shape),
-            whole_block(down.shape),
-            pl.BlockSpec(memory_space=pl.ANY),
-        ],
-        out_specs=[row_block(TILE, 2 * own), row_block(TILE, width)],
-        out_shape=[
-            jax.ShapeDtypeStruct((rows, 2 * own), BF),
-            jax.ShapeDtypeStruct((rows, width), BF),
-        ],
+        functools.partial(mlp_backward_kernel, count),
+        grid=(count,),
+        in_specs=[anywhere] * count
+        + [row_block(rows, own)] * 2
+        + [anywhere, whole_block(down.shape), anywhere],
+        out_specs=[row_block(rows, 2 * own)] + half_blocks(rows, width, count),
+        out_shape=[jax.ShapeDtypeStruct((total, 2 * own), BF), part, part],
+        scratch_shapes=tile_scratch(tiles, blocks),
         compiler_params=PARAMS,
         cost_estimate=pl.CostEstimate(
-            flops=6 * rows * width * own, bytes_accessed=rows * (4 * width + 8 * own), transcendentals=0
+            flops=6 * total * width * own, bytes_accessed=total * (4 * width + 8 * own), transcendentals=0
         ),
-    )(grad_mixed, gelu, slope, gate_up, down, earlier)
-
-
-def down_terms_kernel(*refs):
+    )(*tiles, gelu, slope, blocks, down, earlier)
+
+
+def rows_of(segments, tiles):
+    at = 0
+    for segment in segments:
+        first = 0
+        while first < segment.shape[0]:
+            rows = tiles[at].shape[0]
+            yield segment, first, tiles[at]
+            first += rows
+            at += 1
+
+
+def down_terms_kernel(count, *refs):
     *ins, out = refs
-    half = len(ins) // 2
-    total = over_rows(ins[0][...], ins[half][...])
-    for left, right in zip(ins[1:half], ins[half + 1 :]):
-        total = total + over_rows(left[...], right[...])
+    total = None
+    for segment, first, tile in rows_of(ins[:count], ins[count:]):
+        part = over_rows(segment[first : first + tile.shape[0], :], tile[...])
+        total = part if total is None else total + part
     out[...] = total.astype(BF)
 
 
@@ -154,7 +234,7 @@
     own, width = hidden[0].shape[1], grad_mixed[0].shape[1]
     rows = sum(part.shape[0] for part in hidden)
     return pl.pallas_call(
-        down_terms_kernel,
+        functools.partial(down_terms_kernel, len(hidden)),
         grid=(own // 128,),
         in_specs=[pl.BlockSpec((part.shape[0], 128), lambda i: (0, i)) for part in hidden]
         + [whole_block(part.shape) for part in grad_mixed],
@@ -167,12 +247,12 @@
     )(*hidden, *grad_mixed)
 
 
-def gate_terms_kernel(*refs):
+def gate_terms_kernel(count, *refs):
     *ins, _, out = refs
-    half = len(ins) // 2
-    total = over_rows(ins[0][...], ins[half][...])
-    for left, right in zip(ins[1:half], ins[half + 1 :]):
-        total = total + over_rows(left[...], right[...])
+    total = None
+    for segment, first, tile in rows_of(ins[:count], ins[count:]):
+        part = over_rows(tile[...], segment[first : first + tile.shape[0], :])
+        total = part if total is None else total + part
     total = total.astype(BF)
     groups, sides, rows, _ = out.shape
     for side in range(sides):
@@ -181,36 +261,38 @@
             out[group, side] = total[first : first + rows]
 
 
-def gate_terms(normed, grad_raw, groups, earlier):
-    width, both = normed[0].shape[1], grad_raw[0].shape[1]
-    rows = sum(part.shape[0] for part in normed)
+def gate_terms(normed, grad_raw, groups, first, steps, earlier):
+    width = normed[0].shape[1]
+    rows = sum(part.shape[0] for part in grad_raw)
     shape = (groups, 2, width // (2 * groups))
+    columns = steps * STEP
     return pl.pallas_call(
-        gate_terms_kernel,
-        grid=(both // 256,),
-        in_specs=[whole_block(part.shape) for part in normed]
-        + [pl.BlockSpec((part.shape[0], 256), lambda i: (0, i)) for part in grad_raw]
+        functools.partial(gate_terms_kernel, len(grad_raw)),
+        grid=(steps,),
+        in_specs=[
+            pl.BlockSpec((part.shape[0], STEP), lambda i: (0, first + i)) for part in grad_raw
+        ]
+        + [whole_block(part.shape) for part in normed]
         + [pl.BlockSpec(memory_space=pl.ANY)],
-        out_specs=pl.BlockSpec(shape + (256,), lambda i: (0, 0, 0, i)),
-        out_shape=jax.ShapeDtypeStruct(shape + (both,), BF),
+        out_specs=pl.BlockSpec(shape + (STEP,), lambda i: (0, 0, 0, i)),
+        out_shape=jax.ShapeDtypeStruct(shape + (columns,), BF),
         compiler_params=PARAMS,
         cost_estimate=pl.CostEstimate(
-            flops=2 * rows * width * both, bytes_accessed=2 * rows * (width + both), transcendentals=0
+            flops=2 * rows * width * columns, bytes_accessed=2 * rows * (width + columns), transcendentals=0
         ),
-    )(*normed, *grad_raw, earlier)
+    )(*grad_raw, *normed, earlier)
 
 
 def after(value, *earlier):
     return lax.optimization_barrier((value, *earlier))[0]
 
 
-def with_core(part):
-    return jnp.concatenate([part, swap(part, "c")])
-
-
-def core_sum(part):
-    half = part.shape[0] // 2
-    return part[:half].astype(F32) + swap(part[half:], "c").astype(F32)
+def core_sum(mine, other):
+    return mine.astype(F32) + swap(other, "c").astype(F32)
+
+
+def with_core(*tiles):
+    return list(tiles) + [swap(tile, "c") for tile in tiles]
 
 
 def send_far(far):
@@ -218,8 +300,9 @@
     return swap(far[:half], "y"), swap(far[half:], "x")
 
 
-def sum_near(near, top, low):
-    near = core_sum(near)
+def sum_near(mine, other, top, low):
+    mine, other, top, low = lax.optimization_barrier((mine, other, top, low))
+    near = core_sum(mine, other)
     rows = near.shape[0] // 2
     half = rows // 2
     to_x = jnp.concatenate([near[:half] + top, near[half:rows]]).astype(BF)
@@ -227,8 +310,9 @@
     return to_x, to_y
 
 
-def sum_own(own, to_x, to_y):
-    return core_sum(own) + swap(to_x, "x").astype(F32) + swap(to_y, "y").astype(F32)
+def sum_own(mine, other, to_x, to_y):
+    total = core_sum(mine, other)
+    return total + swap(to_x, "x").astype(F32) + swap(to_y, "y").astype(F32)
 
 
 def in_order(own, other, place):
@@ -246,12 +330,13 @@
     return lax.dynamic_slice_in_dim(both, lax.rem(size - place, size), size, 0)
 
 
-def plane_weights(blocks):
+def plane_weights(blocks, *earlier):
     x, y = lax.axis_index("x"), lax.axis_index("y")
     half = blocks.shape[0] // 2
     first, second = blocks[:half], blocks[half:]
     first = in_order(first, swap(first, "x"), x)
     second = in_order(second, swap(second, "y"), y)
+    first, second = lax.optimization_barrier((first, second, *earlier))[:2]
     first = in_order(first, swap(first, "y"), y)
     second = in_order(second, swap(second, "x"), x)
     first = first.transpose(1, 2, 0, 3, 4)
@@ -713,8 +798,9 @@
     down = jnp.pad(down, ((0, hidden_pad - hidden_own), (0, 0)))
 
     both = lax.all_gather(sent, "g", axis=0)
-    both = both.reshape(groups, 2, members // 2 * shard_rows, 2 * hidden_pad)
-    gate_up = both.transpose(1, 0, 2, 3).reshape(width, 2 * hidden_pad)
+    gate_up = both.reshape(groups, 2, members // 2 * shard_rows, 2 * hidden_pad)
+    if gate_up.shape[2] % 16:
+        gate_up = gate_up.transpose(1, 0, 2, 3).reshape(1, 1, width, 2 * hidden_pad)
 
     first_row = seq_place * row_count
     ids_all = doc_ids[0]
@@ -732,23 +818,24 @@
     normed, normed_before, query_raw, key_raw, queries, keys, values, d_gains, h_gains = project(
         places, layer_in, before, mine, other, cosine_table, sine_table, shard_rows, q_cols, k_cols
     )
-    w_o = plane_weights(after(w_o, keys))
+    w_o = plane_weights(w_o, keys)
     w_o = in_order(w_o, swap(w_o, "c"), core).transpose(1, 2, 3, 0, 4, 5).reshape(q_cols, width)
+    w_o = after(w_o, down)
     attended, log_total, branch, middle, normed_mlp = attend(
         queries, keys, values, query_ids, key_ids, w_o, layer_in, d_gains, attn_scale
     )
 
     half = row_count // 2
     from_x, from_y = swap(normed_mlp, "x"), swap(normed_mlp, "y")
-    normed_far = jnp.concatenate([swap(from_x[:half], "y"), swap(from_y[half:], "x")])
-    normed_near = jnp.concatenate([from_x, from_y])
-    normed_all = [with_core(part) for part in (normed_mlp, normed_near, normed_far)]
-    far_result = mlp_forward(normed_all[2], gate_up, down, normed_all[2])
-    far_sum = core_sum(far_result[3]).astype(BF)
-    near_result = mlp_forward(normed_all[1], gate_up, down, far_sum)
-    to_x, to_y = sum_near(*lax.optimization_barrier((near_result[3], *send_far(far_sum))))
-    own_result = mlp_forward(normed_all[0], gate_up, down, to_x)
-    mixed = sum_own(own_result[3], to_x, to_y)
+    normed_own = with_core(normed_mlp)
+    normed_near = with_core(from_x, from_y)
+    normed_far = with_core(swap(from_x[:half], "y"), swap(from_y[half:], "x"))
+    far_result = mlp_forward(normed_far, gate_up, down, normed_own[1])
+    far_sum = core_sum(*far_result[3:]).astype(BF)
+    near_result = mlp_forward(normed_near, gate_up, down, far_sum)
+    to_x, to_y = sum_near(*near_result[3:], *send_far(far_sum))
+    own_result = mlp_forward(normed_own, gate_up, down, to_x)
+    mixed = sum_own(*own_result[3:], to_x, to_y)
     layer_out = middle + norm_gain(mixed, d_gains[3:4])
 
     _, pullback = jax.vjp(norm_gain, mixed, d_gains[3:4])
@@ -758,29 +845,49 @@
     grad_own = with_core(grad_mixed)
     own_grads = mlp_backward(grad_own, own_result[1], own_result[2], gate_up, down, down)
     from_x, from_y = lax.optimization_barrier((from_x, from_y, own_grads[1]))[:2]
-    grad_far = with_core(jnp.concatenate([swap(from_x[:half], "y"), swap(from_y[half:], "x")]))
-    grad_near = with_core(jnp.concatenate([from_x, from_y]))
+    grad_near = with_core(from_x, from_y)
+    grad_far = with_core(swap(from_x[:half], "y"), swap(from_y[half:], "x"))
     grad_down_terms = down_terms(
         [r[0] for r in (own_result, near_result, far_result)],
-        [grad_own, grad_near, grad_far],
+        grad_own + grad_near + grad_far,
         hidden_own,
     )
     grad_down = group_terms(grad_down_terms.reshape(groups, -1, width))
     far_grads = mlp_backward(
         grad_far, far_result[1], far_result[2], gate_up, down, grad_down_terms
     )
-    far_sum = core_sum(far_grads[1]).astype(BF)
+    far_sum = core_sum(*far_grads[1:]).astype(BF)
     near_grads = mlp_backward(grad_near, near_result[1], near_result[2], gate_up, down, far_sum)
-    to_x, to_y = sum_near(*lax.optimization_barrier((near_grads[1], *send_far(far_sum))))
-    gate_up_terms = gate_terms(
-        normed_all, [g[0] for g in (own_grads, near_grads, far_grads)], groups, to_x
-    )
-    grad_normed_mlp = sum_own(own_grads[1], to_x, to_y)
-    grad_normed_mlp = after(grad_normed_mlp, gate_up_terms)
-    term = gate_up_terms.reshape(groups * members * shard_rows, 2 * hidden_pad)
-    gate_up_share = lax.psum_scatter(term, "g", scatter_dimension=0, tiled=True)
-    term = gate_up_share.reshape(members, shard_rows, 2 * hidden_pad)
-    term = lax.all_to_all(term, PLANE, split_axis=0, concat_axis=0, tiled=True)
+    to_x, to_y = sum_near(*near_grads[1:], *send_far(far_sum))
+    raw_grads = [g[0] for g in (own_grads, near_grads, far_grads)]
+    steps = 2 * hidden_pad // STEP
+    first_steps = steps // 2 + steps % 2
+    first_terms = gate_terms(
+        normed_own + normed_near + normed_far, raw_grads, groups, 0, first_steps, to_x
+    )
+    second_terms = gate_terms(
+        normed_own + normed_near + normed_far,
+        raw_grads,
+        groups,
+        first_steps,
+        steps - first_steps,
+        first_terms,
+    )
+    grad_normed_mlp = sum_own(*own_grads[1:], to_x, to_y)
+    grad_normed_mlp = after(grad_normed_mlp, second_terms)
+
+    def scatter(term):
+        term = term.reshape(groups * members * shard_rows, term.shape[3])
+        return lax.psum_scatter(term, "g", scatter_dimension=0, tiled=True)
+
+    def to_owner(term):
+        term = term.reshape(members, shard_rows, term.shape[1])
+        return lax.all_to_all(term, PLANE, split_axis=0, concat_axis=0, tiled=True)
+
+    first_share = scatter(first_terms)
+    second_share = scatter(after(second_terms, first_share))
+    first_share = to_owner(first_share)
+    term = jnp.concatenate([first_share, to_owner(second_share)], axis=2)
 
     def collect(cut):
         cut = cut[:, :, :hidden_own].reshape(2, members // 2, shard_rows, groups, piece)
@@ -810,7 +917,7 @@
     qkv_terms = plane_terms(mine.reshape(2, groups, 2, 2 * shard_rows, half_cols))
     qkv_terms = qkv_terms.reshape(groups, -1, width)
     share = jnp.concatenate([out_terms, qkv_terms], axis=1)
-    share = group_terms(after(share, gate_up_share))
+    share = group_terms(after(share, first_share, second_share, grad_in))
     grad_w_out = share[: w_out.shape[0]]
     share = share[w_out.shape[0] :].astype(BF).reshape(2, shard_rows, half_cols)
     mine = lax.dynamic_index_in_dim(share, core, 0, keepdims=False)

time: 562 us -> 616 us (1.096)
  the two profiles are of different devices: /device:TPU:13 before, /device:TPU:0 now
where the time goes in v7:
time: 616 us; the launch traced here: 608 us
  Pallas kernels  213 us (35%)
  waiting for transfers between devices  206 us (33%)
  starting transfers between devices  84.8 us (14%)
  other arithmetic  47.1 us (8%)
  local copies, waits for them, and re-layouts  39.2 us (6%)
  between operations  15.3 us (2%)
    ppermute x54, waiting for transfers between devices, swap(): return lax.ppermute(array, axis, [(0, 1), (1, 0)])  133 us
    pallas_call x3, Pallas kernels, mlp_backward(): pl.pallas_call(functools.partial(mlp_backward_kernel, count), grid=(count...  55.4 us
    pallas_call x3, Pallas kernels, mlp_forward(): pl.pallas_call(functools.partial(mlp_forward_kernel, count), grid=(count,...  55.2 us
    ppermute x54, starting transfers between devices, swap(): return lax.ppermute(array, axis, [(0, 1), (1, 0)])  50.1 us
    ppermute x6, waiting for transfers between devices, group_terms(): total = total + lax.ppermute(chunk, 'g', pairs).astype(F32)  43.2 us
    pallas_call x2, Pallas kernels, gate_terms(): pl.pallas_call(functools.partial(gate_terms_kernel, len(grad_raw)), grid=...  30.2 us
    pallas_call x1, Pallas kernels, down_terms(): pl.pallas_call(functools.partial(down_terms_kernel, len(hidden)), grid=(o...  16.6 us
    pallas_call x1, Pallas kernels, attend_backward(): pl.pallas_call(functools.partial(attend_backward_kernel, scale), in_specs...  16.4 us
  transfers between devices with their start and end apart: 72, of which 36 were waited for; matrix products, arithmetic and copies ran while one was open for 11% of the time, Pallas kernels for 27%

profile of v7, /device:TPU:0, one launch (start us, length us, event | category | flops | bytes accessed | tf_op | source)
XLA Modules:
  0.0 608.5 jit_solution(13415376028015138248)
XLA Ops:
  65.1 11.1 %collective-permute-done.7 = bf16[2,2,72,896]{3,2,1,0:T(8,128)(2,1)S(1)} collective-permute-done((bf16[2,2,72,896]{3,2,1,0:T(8,128)(2,1)S(1)}, bf16[2,2,72,896]{3,2,1,0:T(8,128)(2,1)S(1)}, u32[]{:S(2)}, u32[]{:S(2)}) %collective-permute-start.7) | collective-permute-done | bytes 516128 | tf_op jit(solution)/shard_map/ppermute | solution.py:51
  90.2 8.5 %shard_map.271 = (bf16[512,1152]{1,0:T(8,128)(2,1)}, bf16[512,1152]{1,0:T(8,128)(2,1)}, f32[512,1024]{1,0:T(8,128)}, f32[1024,256]{1,0:T(8,128)}, bf16[512,1024]...) custom-call(s32[1]{0:T(128)} %bitcast.core, ...), custom_call_target="tpu_custom_call" | custom-call | flops 2415919104 | bytes 9437184 | tf_op jit(solution)/shard_map/pallas_call | solution.py:451
  117.2 9.7 %shard_map.272 = (bf16[512,1024]{1,0:T(8,128)(2,1)}, f32[512,128]{1,0:T(8,128)}, f32[512,1152]{1,0:T(8,128)}, f32[512,1152]{1,0:T(8,128)}, bf16[512,1152]{1,0:T(8,128)(2,1)}) custom-call(bf16[512,1024]{1,0:T(8,128)(2,1)} %get-tuple-element.93.queries, bf16[1024,256]{1,0:T(8,128)(2,1)} %get-tuple-element.94.keys, bf16[1024,256]{1,0:T(8,128)(2,1)} %get-tuple-element.95.values, ...), custom_call_target="tpu_custom_call" | custom-call | flops 3355443200 | bytes 11796480 | tf_op jit(solution)/shard_map/pallas_call | solution.py:517
  128.3 27.2 %collective-permute-done.17.refs_1_.refs_6_ = bf16[512,1152]{1,0:T(8,128)(2,1)S(1)} collective-permute-done((bf16[512,1152]{1,0:T(8,128)(2,1)}, bf16[512,1152]{1,0:T(8,128)(2,1)S(1)}, u32[]{:S(2)}, u32[]{:S(2)}) %collective-permute-start.17) | collective-permute-done | bytes 1179680 | tf_op jit(solution)/shard_map/ppermute | solution.py:51
  157.3 13.4 %collective-permute-done.21.refs_1_.refs_10_ = bf16[256,1152]{1,0:T(8,128)(2,1)} collective-permute-done((bf16[256,1152]{1,0:T(8,128)(2,1)S(1)}, bf16[256,1152]{1,0:T(8,128)(2,1)}, u32[]{:S(2)}, u32[]{:S(2)}) %collective-permute-start.21) | collective-permute-done | bytes 589856 | tf_op jit(solution)/shard_map/ppermute | solution.py:51
  174.4 14.9 %shard_map.273 = (bf16[1024,896]{1,0:T(8,128)(2,1)}, bf16[1024,896]{1,0:T(8,128)(2,1)}, bf16[1024,896]{1,0:T(8,128)(2,1)}, bf16[512,1152]{1,0:T(8,128)(2,1)}, bf16[512,1152]{1,0:T(8,128)(2,1)}) custom-call(bf16[256,1152]{1,0:T(8,128)(2,1)} %collective-permute-done.20.refs_0_.refs_9_, bf16[256,1152]{1,0:T(8,128)(2,1)} %collective-permute-done.21.refs_1_.refs_10_, ...), custom_call_target="tpu_custom_call" | custom-call | flops 6341787648 | bytes 10223616 | tf_op jit(solution)/shard_map/pallas_call | solution.py:162
  199.0 24.6 %shard_map.274 = (bf16[2048,896]{1,0:T(8,128)(2,1)}, bf16[2048,896]{1,0:T(8,128)(2,1)}, bf16[2048,896]{1,0:T(8,128)(2,1)}, bf16[1024,1152]{1,0:T(8,128)(2,1)}, bf16[1024,1152]{1,0:T(8,128)(2,1)}) custom-call(bf16[512,1152]{1,0:T(8,128)(2,1)} %copy-done.5, bf16[512,1152]{1,0:T(8,128)(2,1)} %copy-done.4, bf16[512,1152]{1,0:T(8,128)(2,1)} %copy-done.12, ...), custom_call_target="tpu_custom_call" | custom-call | flops 12683575296 | bytes 20447232 | tf_op jit(solution)/shard_map/pallas_call | solution.py:162
  235.3 15.6 %shard_map.275 = (bf16[1024,896]{1,0:T(8,128)(2,1)}, bf16[1024,896]{1,0:T(8,128)(2,1)}, bf16[1024,896]{1,0:T(8,128)(2,1)}, bf16[512,1152]{1,0:T(8,128)(2,1)}, bf16[512,1152]{1,0:T(8,128)(2,1)}) custom-call(bf16[512,1152]{1,0:T(8,128)(2,1)} %get-tuple-element.101.refs_0_.refs_3_, bf16[512,1152]{1,0:T(8,128)(2,1)} %copy-done.10, ...), custom_call_target="tpu_custom_call" | custom-call | flops 6341787648 | bytes 10223616 | tf_op jit(solution)/shard_map/pallas_call | solution.py:162
  251.9 8.6 %collective-permute-done.30 = bf16[512,1152]{1,0:T(8,128)(2,1)S(1)} collective-permute-done((bf16[512,1152]{1,0:T(8,128)(2,1)S(1)}, bf16[512,1152]{1,0:T(8,128)(2,1)S(1)}, u32[]{:S(2)}, u32[]{:S(2)}) %collective-permute-start.30) | collective-permute-done | bytes 1179680 | tf_op jit(solution)/shard_map/ppermute | solution.py:51
  271.3 15.5 %shard_map.276 = (bf16[1024,1792]{1,0:T(8,128)(2,1)}, bf16[512,1152]{1,0:T(8,128)(2,1)}, bf16[512,1152]{1,0:T(8,128)(2,1)}) custom-call(bf16[512,1152]{1,0:T(8,128)(2,1)} %copy-done.13, bf16[512,1152]{1,0:T(8,128)(2,1)} %copy-done.24, bf16[1024,896]{1,0:T(8,128)(2,1)} %get-tuple-element.113.refs_2_, bf16[1024,896]{1,0:T(8,128)(2,1)} %get-tuple-element.114.refs_3_, ...), custom_call_target="tpu_custom_call" | custom-call | flops 6341787648 | bytes 12058624 | tf_op jit(solution)/shard_map/pallas_call | solution.py:197
  286.8 8.9 %collective-permute-done.34.refs_6_.refs_1_ = bf16[512,1152]{1,0:T(8,128)(2,1)S(1)} collective-permute-done((bf16[512,1152]{1,0:T(8,128)(2,1)S(1)}, bf16[512,1152]{1,0:T(8,128)(2,1)S(1)}, u32[]{:S(2)}, u32[]{:S(2)}) %collective-permute-start.34) | collective-permute-done | bytes 1179680 | tf_op jit(solution)/shard_map/ppermute | solution.py:51
  299.7 11.3 %collective-permute-done.38.refs_10_.refs_1_ = bf16[256,1152]{1,0:T(8,128)(2,1)S(1)} collective-permute-done((bf16[256,1152]{1,0:T(8,128)(2,1)S(1)}, bf16[256,1152]{1,0:T(8,128)(2,1)S(1)}, u32[]{:S(2)}, u32[]{:S(2)}) %collective-permute-start.38) | collective-permute-done | bytes 589856 | tf_op jit(solution)/shard_map/ppermute | solution.py:51
  315.7 16.6 %shard_map.277.refs_8_ = bf16[864,1152]{1,0:T(8,128)(2,1)} custom-call(bf16[1024,896]{1,0:T(8,128)(2,1)} %get-tuple-element.123.refs_0_, bf16[2048,896]{1,0:T(8,128)(2,1)} %get-tuple-element.124.refs_1_, bf16[1024,896]{1,0:T(8,128)(2,1)} %get-tuple-element.125.refs_2_, bf16[512,1152]{1,0:T(8,128)(2,1)} %copy-done.13, bf16[512,1152]{1,0:T(8,128)(2,1)} %copy-done.24, ...), custom_call_target="tpu_custom_call" | custom-call | flops 8455716864 | bytes 16777216 | tf_op jit(solution)/shard_map/pallas_call | solution.py:236
  332.3 15.4 %shard_map.278 = (bf16[1024,1792]{1,0:T(8,128)(2,1)}, bf16[512,1152]{1,0:T(8,128)(2,1)}, bf16[512,1152]{1,0:T(8,128)(2,1)}) custom-call(bf16[256,1152]{1,0:T(8,128)(2,1)} %copy-done.26, bf16[256,1152]{1,0:T(8,128)(2,1)} %copy-done.25, bf16[256,1152]{1,0:T(8,128)(2,1)} %copy-done.28, bf16[256,1152]{1,0:T(8,128)(2,1)} %copy-done.27, ...), custom_call_target="tpu_custom_call" | custom-call | flops 6341787648 | bytes 12058624 | tf_op jit(solution)/shard_map/pallas_call | solution.py:197
  355.0 24.4 %shard_map.279 = (bf16[2048,1792]{1,0:T(8,128)(2,1)}, bf16[1024,1152]{1,0:T(8,128)(2,1)}, bf16[1024,1152]{1,0:T(8,128)(2,1)}) custom-call(bf16[512,1152]{1,0:T(8,128)(2,1)} %copy-done.21, bf16[512,1152]{1,0:T(8,128)(2,1)} %copy-done.20, bf16[512,1152]{1,0:T(8,128)(2,1)} %copy-done.22, bf16[512,1152]{1,0:T(8,128)(2,1)} %copy-done.23, ...), custom_call_target="tpu_custom_call" | custom-call | flops 12683575296 | bytes 24117248 | tf_op jit(solution)/shard_map/pallas_call | solution.py:197
  394.5 16.3 %shard_map.280.refs_13_ = bf16[4,2,144,1024]{3,2,1,0:T(8,128)(2,1)} custom-call(bf16[1024,1792]{1,0:T(8,128)(2,1)} %get-tuple-element.134.refs_0_, bf16[2048,1792]{1,0:T(8,128)(2,1)} %get-tuple-element.135.refs_1_, bf16[1024,1792]{1,0:T(8,128)(2,1)} %get-tuple-element.136.refs_2_, bf16[512,1152]{1,0:T(8,128)(2,1)} %get-tuple-element.101.refs_0_.refs_3_, ...), custom_call_target="tpu_custom_call" | custom-call | flops 9663676416 | bytes 17825792 | tf_op jit(solution)/shard_map/pallas_call | solution.py:269
  410.9 13.9 %shard_map.281 = bf16[4,2,144,768]{3,2,1,0:T(8,128)(2,1)} custom-call(bf16[1024,1792]{1,0:T(8,128)(2,1)} %get-tuple-element.134.refs_0_, bf16[2048,1792]{1,0:T(8,128)(2,1)} %get-tuple-element.135.refs_1_, bf16[1024,1792]{1,0:T(8,128)(2,1)} %get-tuple-element.136.refs_2_, bf16[512,1152]{1,0:T(8,128)(2,1)} %get-tuple-element.101.refs_0_.refs_3_, ...), custom_call_target="tpu_custom_call" | custom-call | flops 7247757312 | bytes 15728640 | tf_op jit(solution)/shard_map/pallas_call | solution.py:269
  429.6 16.4 %shard_map.282 = (f32[512,1152]{1,0:T(8,128)}, bf16[512,1152]{1,0:T(8,128)(2,1)}, f32[512,1024]{1,0:T(8,128)}, f32[1024,256]{1,0:T(8,128)}, f32[1024,256]{1,0:T(8,128)}, /*index=5*/f32[8,1152]{1,0:T(8,128)}) custom-call(f32[512,1152]{1,0:T(8,128)} %convert_add_fusion.3.grad_normed_mlp, bf16[512,1152]{1,0:T(8,128)(2,1)} %bitcast.196, ...), custom_call_target="tpu_custom_call" | custom-call | flops 6576668672 | bytes 17694720 | tf_op jit(solution)/shard_map/pallas_call | solution.py:587
  449.8 25.7 %collective-permute-done.48 = bf16[216,1152]{1,0:T(8,128)(2,1)} collective-permute-done((bf16[216,1152]{1,0:T(8,128)(2,1)}, bf16[216,1152]{1,0:T(8,128)(2,1)}, u32[]{:S(2)}, u32[]{:S(2)}) %collective-permute-start.48) | collective-permute-done | bytes 497696 | tf_op jit(solution)/shard_map/ppermute | solution.py:354
  478.3 15.0 %shard_map.283 = (f32[512,1152]{1,0:T(8,128)}, bf16[512,512]{1,0:T(8,128)(2,1)}, bf16[1152,896]{1,0:T(8,128)(2,1)}, bf16[1152,896]{1,0:T(8,128)(2,1)}) custom-call(s32[1]{0:T(128)} %bitcast.core, f32[512,1024]{1,0:T(8,128)} %get-tuple-element.141.grad_queries, f32[1024,256]{1,0:T(8,128)} %get-tuple-element.142.grad_keys, ...), custom_call_target="tpu_custom_call" | custom-call | flops 4756340736 | bytes 17694720 | tf_op jit(solution)/shard_map/pallas_call | solution.py:676
  512.7 10.7 %collective-permute-start.53 = (bf16[2,32,1152]{2,1,0:T(8,128)(2,1)S(1)}, bf16[2,32,1152]{2,1,0:T(8,128)(2,1)}, u32[]{:S(2)}, u32[]{:S(2)}) collective-permute-start(bf16[2,32,1152]{2,1,0:T(8,128)(2,1)S(1)} %dynamic-slice_bitcast_fusion.12), channel_id=1, source_target_pairs={{0,2},{2,0},{1,3},{3,1},{4,6},{6,4},{5,7},{7,5},{8,10},{10,8},{9,1... | collective-permute-start | bytes 442376 | tf_op jit(solution)/shard_map/ppermute | solution.py:51
  528.2 9.3 %collective-permute-done.59 = bf16[2,2,72,896]{3,2,1,0:T(8,128)(2,1)S(1)} collective-permute-done((bf16[2,2,72,896]{3,2,1,0:T(8,128)(2,1)S(1)}, bf16[2,2,72,896]{3,2,1,0:T(8,128)(2,1)S(1)}, u32[]{:S(2)}, u32[]{:S(2)}) %collective-permute-start.59) | collective-permute-done | bytes 516128 | tf_op jit(solution)/shard_map/ppermute | solution.py:51
  549.8 9.4 %all-to-all-done.1 = bf16[8,36,1024]{2,1,0:T(8,128)(2,1)S(1)} async-done(((bf16[8,36,1024]{2,1,0:T(8,128)(2,1)}), bf16[8,36,1024]{2,1,0:T(8,128)(2,1)S(1)}, u32[]{:S(2)}, u32[]{:S(2)}) %all-to-all-start.1) | async-done | bytes 589856 | tf_op jit(solution)/shard_map/all_to_all | solution.py:885
  572.0 8.7 %collective-permute-done.62 = bf16[88,1152]{1,0:T(8,128)(2,1)S(1)} collective-permute-done((bf16[88,1152]{1,0:T(8,128)(2,1)S(1)}, bf16[88,1152]{1,0:T(8,128)(2,1)S(1)}, u32[]{:S(2)}, u32[]{:S(2)}) %collective-permute-start.62) | collective-permute-done | bytes 202784 | tf_op jit(solution)/shard_map/ppermute | solution.py:354
  (330 shorter events, 241.9 us)
Async XLA Ops:
  7.2 71.4 %all-gather.5.cloned.1.call-start = ((), (), s32[]{:S(2)}) async-start(), calls=%async_computation.7 | async-start | bytes 2856960 | tf_op jit(solution)/shard_map/all_gather | solution.py:795
  37.8 133.9 %all-gather.7.cloned.1.call-start = ((), (), s32[]{:S(2)}) async-start(), calls=%async_computation.8 | async-start | bytes 5160960 | tf_op jit(solution)/shard_map/all_gather | solution.py:800
  78.0 445.4 %reduce-scatter.3.cloned.1.call-start = ((), (), s32[]{:S(2)}) async-start(), calls=%async_computation.5 | async-start | bytes 2949120 | tf_op jit(solution)/shard_map/reduce_scatter | solution.py:881
  126.9 28.6 %collective-permute-start.17 = (bf16[512,1152]{1,0:T(8,128)(2,1)}, bf16[512,1152]{1,0:T(8,128)(2,1)S(1)}, u32[]{:S(2)}, u32[]{:S(2)}) collective-permute-start(bf16[512,1152]{1,0:T(8,128)(2,1)} %get-tuple-element.101.refs_0_.refs_3_), channel_id=1, source_target_pairs={{0,2},{2,0},{1,3},{3,1},{4,6},{6,4},{5,7},{7,5},{8,10},{10,8},{9,1... | collective-permute-start | bytes 3538952 | tf_op jit(solution)/shard_map/ppermute | solution.py:51
  127.6 28.6 %collective-permute-start.16 = (bf16[512,1152]{1,0:T(8,128)(2,1)}, bf16[512,1152]{1,0:T(8,128)(2,1)S(1)}, u32[]{:S(2)}, u32[]{:S(2)}) collective-permute-start(bf16[512,1152]{1,0:T(8,128)(2,1)} %get-tuple-element.101.refs_0_.refs_3_), channel_id=1, source_target_pairs={{0,16},{16,0},{1,17},{17,1},{2,18},{18,2},{3,19},{19,3},{4,20},{20... | collective-permute-start | bytes 3538952 | tf_op jit(solution)/shard_map/ppermute | solution.py:51
  128.3 43.4 %collective-permute-start.15 = (bf16[512,1152]{1,0:T(8,128)(2,1)}, bf16[512,1152]{1,0:T(8,128)(2,1)S(1)}, u32[]{:S(2)}, u32[]{:S(2)}) collective-permute-start(bf16[512,1152]{1,0:T(8,128)(2,1)} %get-tuple-element.101.refs_0_.refs_3_), channel_id=1, source_target_pairs={{0,1},{1,0},{2,3},{3,2},{4,5},{5,4},{6,7},{7,6},{8,9},{9,8},{10,11... | collective-permute-start | bytes 3538952 | tf_op jit(solution)/shard_map/ppermute | solution.py:51
  195.6 28.0 %collective-permute-start.26 = (bf16[256,1152]{1,0:T(8,128)(2,1)}, bf16[256,1152]{1,0:T(8,128)(2,1)}, u32[]{:S(2)}, u32[]{:S(2)}) collective-permute-start(bf16[256,1152]{1,0:T(8,128)(2,1)} %get-tuple-element.198), channel_id=1, source_target_pairs={{0,16},{16,0},{1,17},{17,1},{2,18},{18,2},{3,19},{19,3},{4,20},{20... | collective-permute-start | bytes 1769480 | tf_op jit(solution)/shard_map/ppermute | solution.py:51
  196.2 27.4 %collective-permute-start.25 = (bf16[256,1152]{1,0:T(8,128)(2,1)}, bf16[256,1152]{1,0:T(8,128)(2,1)}, u32[]{:S(2)}, u32[]{:S(2)}) collective-permute-start(bf16[256,1152]{1,0:T(8,128)(2,1)} %get-tuple-element.199), channel_id=1, source_target_pairs={{0,2},{2,0},{1,3},{3,1},{4,6},{6,4},{5,7},{7,5},{8,10},{10,8},{9,1... | collective-permute-start | bytes 1769480 | tf_op jit(solution)/shard_map/ppermute | solution.py:51
  232.4 28.1 %collective-permute-start.30 = (bf16[512,1152]{1,0:T(8,128)(2,1)S(1)}, bf16[512,1152]{1,0:T(8,128)(2,1)S(1)}, u32[]{:S(2)}, u32[]{:S(2)}) collective-permute-start(bf16[512,1152]{1,0:T(8,128)(2,1)S(1)} %pad_maximum_fusion.3), channel_id=1, source_target_pairs={{0,2},{2,0},{1,3},{3,1},{4,6},{6,4},{5,7},{7,5},{8,10},{10,8},{9,1... | collective-permute-start | bytes 3538952 | tf_op jit(solution)/shard_map/ppermute | solution.py:51
  233.8 27.8 %collective-permute-start.29 = (bf16[512,1152]{1,0:T(8,128)(2,1)S(1)}, bf16[512,1152]{1,0:T(8,128)(2,1)S(1)}, u32[]{:S(2)}, u32[]{:S(2)}) collective-permute-start(bf16[512,1152]{1,0:T(8,128)(2,1)S(1)} %pad_maximum_fusion.2.refs_4_), channel_id=1, source_target_pairs={{0,16},{16,0},{1,17},{17,1},{2,18},{18,2},{3,19},{19,3},{4,20},{20... | collective-permute-start | bytes 3538952 | tf_op jit(solution)/shard_map/ppermute | solution.py:51
  267.4 28.4 %collective-permute-start.34 = (bf16[512,1152]{1,0:T(8,128)(2,1)S(1)}, bf16[512,1152]{1,0:T(8,128)(2,1)S(1)}, u32[]{:S(2)}, u32[]{:S(2)}) collective-permute-start(bf16[512,1152]{1,0:T(8,128)(2,1)S(1)} %get-tuple-element.177.refs_0_.refs_3_), channel_id=1, source_target_pairs={{0,2},{2,0},{1,3},{3,1},{4,6},{6,4},{5,7},{7,5},{8,10},{10,8},{9,1... | collective-permute-start | bytes 3538952 | tf_op jit(solution)/shard_map/ppermute | solution.py:51
  268.1 28.1 %collective-permute-start.33 = (bf16[512,1152]{1,0:T(8,128)(2,1)S(1)}, bf16[512,1152]{1,0:T(8,128)(2,1)S(1)}, u32[]{:S(2)}, u32[]{:S(2)}) collective-permute-start(bf16[512,1152]{1,0:T(8,128)(2,1)S(1)} %get-tuple-element.177.refs_0_.refs_3_), channel_id=1, source_target_pairs={{0,16},{16,0},{1,17},{17,1},{2,18},{18,2},{3,19},{19,3},{4,20},{20... | collective-permute-start | bytes 3538952 | tf_op jit(solution)/shard_map/ppermute | solution.py:51
  352.5 26.9 %collective-permute-start.43 = (bf16[256,1152]{1,0:T(8,128)(2,1)S(1)}, bf16[256,1152]{1,0:T(8,128)(2,1)}, u32[]{:S(2)}, u32[]{:S(2)}) collective-permute-start(bf16[256,1152]{1,0:T(8,128)(2,1)S(1)} %get-tuple-element.196), channel_id=1, source_target_pairs={{0,16},{16,0},{1,17},{17,1},{2,18},{18,2},{3,19},{19,3},{4,20},{20... | collective-permute-start | bytes 1769480 | tf_op jit(solution)/shard_map/ppermute | solution.py:51
  353.6 25.8 %collective-permute-start.42 = (bf16[256,1152]{1,0:T(8,128)(2,1)S(1)}, bf16[256,1152]{1,0:T(8,128)(2,1)}, u32[]{:S(2)}, u32[]{:S(2)}) collective-permute-start(bf16[256,1152]{1,0:T(8,128)(2,1)S(1)} %get-tuple-element.197), channel_id=1, source_target_pairs={{0,2},{2,0},{1,3},{3,1},{4,6},{6,4},{5,7},{7,5},{8,10},{10,8},{9,1... | collective-permute-start | bytes 1769480 | tf_op jit(solution)/shard_map/ppermute | solution.py:51
  379.5 45.2 %collective-permute-start.32 = (bf16[512,1152]{1,0:T(8,128)(2,1)}, bf16[512,1152]{1,0:T(8,128)(2,1)S(1)}, u32[]{:S(2)}, u32[]{:S(2)}) collective-permute-start(bf16[512,1152]{1,0:T(8,128)(2,1)} %get-tuple-element.116), channel_id=1, source_target_pairs={{0,1},{1,0},{2,3},{3,2},{4,5},{5,4},{6,7},{7,6},{8,9},{9,8},{10,11... | collective-permute-start | bytes 3538952 | tf_op jit(solution)/shard_map/ppermute | solution.py:51
  382.6 67.2 %collective-permute-start.47 = (bf16[216,1152]{1,0:T(8,128)(2,1)}, bf16[216,1152]{1,0:T(8,128)(2,1)}, u32[]{:S(2)}, u32[]{:S(2)}) collective-permute-start(bf16[216,1152]{1,0:T(8,128)(2,1)} %get-tuple-element.191), channel_id=1, source_target_pairs={{0,4},{4,8},{8,12},{12,0},{1,5},{5,9},{9,13},{13,1},{2,6},{6,10},{... | collective-permute-start | bytes 1493000 | tf_op jit(solution)/shard_map/ppermute | solution.py:354
  386.2 63.7 %collective-permute-start.49 = (bf16[216,1152]{1,0:T(8,128)(2,1)}, bf16[216,1152]{1,0:T(8,128)(2,1)}, u32[]{:S(2)}, u32[]{:S(2)}) collective-permute-start(bf16[216,1152]{1,0:T(8,128)(2,1)} %get-tuple-element.192), channel_id=1, source_target_pairs={{0,12},{4,0},{8,4},{12,8},{1,13},{5,1},{9,5},{13,9},{2,14},{6,2},{... | collective-permute-start | bytes 1493000 | tf_op jit(solution)/shard_map/ppermute | solution.py:354
  391.5 34.8 %collective-permute-start.46 = (bf16[512,1152]{1,0:T(8,128)(2,1)}, bf16[512,1152]{1,0:T(8,128)(2,1)S(1)}, u32[]{:S(2)}, u32[]{:S(2)}) collective-permute-start(bf16[512,1152]{1,0:T(8,128)(2,1)} %pad_maximum_fusion.5), channel_id=1, source_target_pairs={{0,2},{2,0},{1,3},{3,1},{4,6},{6,4},{5,7},{7,5},{8,10},{10,8},{9,1... | collective-permute-start | bytes 3538952 | tf_op jit(solution)/shard_map/ppermute | solution.py:51
  393.5 32.8 %collective-permute-start.45 = (bf16[512,1152]{1,0:T(8,128)(2,1)}, bf16[512,1152]{1,0:T(8,128)(2,1)}, u32[]{:S(2)}, u32[]{:S(2)}) collective-permute-start(bf16[512,1152]{1,0:T(8,128)(2,1)} %pad_maximum_fusion.4.refs_13_), channel_id=1, source_target_pairs={{0,16},{16,0},{1,17},{17,1},{2,18},{18,2},{3,19},{19,3},{4,20},{20... | collective-permute-start | bytes 3538952 | tf_op jit(solution)/shard_map/ppermute | solution.py:51
  410.8 148.3 %reduce-scatter.5.cloned.1.call-start = ((), (), s32[]{:S(2)}) async-start(), calls=%async_computation.6 | async-start | bytes 2211840 | tf_op jit(solution)/shard_map/reduce_scatter | solution.py:881
  424.8 50.8 %collective-permute-start.48 = (bf16[216,1152]{1,0:T(8,128)(2,1)}, bf16[216,1152]{1,0:T(8,128)(2,1)}, u32[]{:S(2)}, u32[]{:S(2)}) collective-permute-start(bf16[216,1152]{1,0:T(8,128)(2,1)} %get-tuple-element.193), channel_id=1, source_target_pairs={{0,8},{4,12},{8,0},{12,4},{1,9},{5,13},{9,1},{13,5},{2,10},{6,14},... | collective-permute-start | bytes 1493000 | tf_op jit(solution)/shard_map/ppermute | solution.py:354
  449.2 46.6 %collective-permute-start.51 = (bf16[2,4,2,32,1152]{4,3,1,0,2:T(8,128)(2,1)S(1)}, bf16[2,4,2,32,1152]{4,3,1,0,2:T(8,128)(2,1)S(1)}, u32[]{:S(2)}, u32[]{:S(2)}) collective-permute-start(bf16[2,4,2,32,1152]{4,3,1,0,2:T(8,128)(2,1)S(1)} %bitcast.210), channel_id=1, source_target_pairs={{0,1},{1,0},{2,3},{3,2},{4,5},{5,4},{6,7},{7,6},{8,9},{9,8},{10,11... | collective-permute-start | bytes 3538952 | tf_op jit(solution)/shard_map/ppermute | solution.py:51
  494.6 28.8 %collective-permute-start.56 = (bf16[1152,896]{1,0:T(8,128)(2,1)}, bf16[1152,896]{1,0:T(8,128)(2,1)}, u32[]{:S(2)}, u32[]{:S(2)}) collective-permute-start(bf16[1152,896]{1,0:T(8,128)(2,1)} %get-tuple-element.156), channel_id=1, source_target_pairs={{0,1},{1,0},{2,3},{3,2},{4,5},{5,4},{6,7},{7,6},{8,9},{9,8},{10,11... | collective-permute-start | bytes 6193160 | tf_op jit(solution)/shard_map/ppermute | solution.py:51
  512.7 28.1 %collective-permute-start.53 = (bf16[2,32,1152]{2,1,0:T(8,128)(2,1)S(1)}, bf16[2,32,1152]{2,1,0:T(8,128)(2,1)}, u32[]{:S(2)}, u32[]{:S(2)}) collective-permute-start(bf16[2,32,1152]{2,1,0:T(8,128)(2,1)S(1)} %dynamic-slice_bitcast_fusion.12), channel_id=1, source_target_pairs={{0,2},{2,0},{1,3},{3,1},{4,6},{6,4},{5,7},{7,5},{8,10},{10,8},{9,1... | collective-permute-start | bytes 442376 | tf_op jit(solution)/shard_map/ppermute | solution.py:51
  (78 other events, 733.8 us)
Sparse Core Ops, SparseCore 0:
  18.4 60.1 all-gather.4
  80.2 79.3 all-gather.6
  410.9 65.0 reduce-scatter.2
  523.5 35.3 reduce-scatter.4

commit v8 on v6

--- a/solution.py
+++ b/solution.py
@@ -54,6 +54,7 @@
 GELU_A = 0.7978845608028654
 GELU_B = 0.044715
 TILE = 512
+STEP = 256
 PARAMS = pltpu.CompilerParams(vmem_limit_bytes=58 << 20)
 
 
@@ -65,7 +66,27 @@
     return pl.BlockSpec((rows, columns), lambda i: (i, 0))
 
 
-def mlp_forward_kernel(normed, gate_up, down, _, hidden, gelu, slope, mixed):
+def store_half(value, mine, other):
+    step, half = pl.program_id(0), pl.num_programs(0) // 2
+
+    @pl.when(step < half)
+    def _():
+        mine[...] = value
+
+    @pl.when(step >= half)
+    def _():
+        other[...] = value
+
+
+def half_blocks(rows, columns):
+    half = rows // TILE // 2
+    return [
+        pl.BlockSpec((TILE, columns), lambda i: (jnp.minimum(i, half - 1), 0)),
+        pl.BlockSpec((TILE, columns), lambda i: (jnp.maximum(i - half, 0), 0)),
+    ]
+
+
+def mlp_forward_kernel(normed, gate_up, down, _, hidden, gelu, slope, mine, other):
     own = down.shape[0]
     raw = matmul(normed[...], gate_up[...])
     gate_raw, up_raw = raw[:, :own], raw[:, own:]
@@ -78,13 +99,14 @@
     hidden[...] = low
     gelu[...] = active.astype(BF)
     slope[...] = ((half + turn) * up_raw).astype(BF)
-    mixed[...] = matmul(low, down[...]).astype(BF)
+    store_half(matmul(low, down[...]).astype(BF), mine, other)
 
 
 def mlp_forward(normed, gate_up, down, earlier):
     rows, width = normed.shape
     own = down.shape[0]
     flat = jax.ShapeDtypeStruct((rows, own), BF)
+    part = jax.ShapeDtypeStruct((rows // 2, width), BF)
     return pl.pallas_call(
         mlp_forward_kernel,
         grid=(rows // TILE,),
@@ -94,8 +116,8 @@
             whole_block(down.shape),
             pl.BlockSpec(memory_space=pl.ANY),
         ],
-        out_specs=[row_block(TILE, own)] * 3 + [row_block(TILE, width)],
-        out_shape=[flat, flat, flat, jax.ShapeDtypeStruct((rows, width), BF)],
+        out_specs=[row_block(TILE, own)] * 3 + half_blocks(rows, width),
+        out_shape=[flat, flat, flat, part, part],
         compiler_params=PARAMS,
         cost_estimate=pl.CostEstimate(
             flops=6 * rows * width * own, bytes_accessed=rows * (4 * width + 6 * own), transcendentals=0
@@ -103,16 +125,15 @@
     )(normed, gate_up, down, earlier)
 
 
-def mlp_backward_kernel(grad_mixed, gelu, slope, gate_up, down, _, grad_raw, grad_normed):
+def mlp_backward_kernel(grad_mixed, gelu, slope, gate_up, down, _, grad_raw, mine, other):
     own = down.shape[0]
     grad_hidden = by_transpose(grad_mixed[...], down[...])
     grad_gate = (grad_hidden * slope[...].astype(F32)).astype(BF)
     grad_up = (grad_hidden * gelu[...].astype(F32)).astype(BF)
     grad_raw[:, :own] = grad_gate
     grad_raw[:, own:] = grad_up
-    grad_normed[...] = (
-        by_transpose(grad_gate, gate_up[:, :own]) + by_transpose(grad_up, gate_up[:, own:])
-    ).astype(BF)
+    total = by_transpose(grad_gate, gate_up[:, :own]) + by_transpose(grad_up, gate_up[:, own:])
+    store_half(total.astype(BF), mine, other)
 
 
 def mlp_backward(grad_mixed, gelu, slope, gate_up, down, earlier):
@@ -129,10 +150,11 @@
             whole_block(down.shape),
             pl.BlockSpec(memory_space=pl.ANY),
         ],
-        out_specs=[row_block(TILE, 2 * own), row_block(TILE, width)],
+        out_specs=[row_block(TILE, 2 * own)] + half_blocks(rows, width),
         out_shape=[
             jax.ShapeDtypeStruct((rows, 2 * own), BF),
-            jax.ShapeDtypeStruct((rows, width), BF),
+            jax.ShapeDtypeStruct((rows // 2, width), BF),
+            jax.ShapeDtypeStruct((rows // 2, width), BF),
         ],
         compiler_params=PARAMS,
         cost_estimate=pl.CostEstimate(
@@ -181,17 +203,17 @@
             out[group, side] = total[first : first + rows]
 
 
-def gate_terms(normed, grad_raw, groups, earlier):
-    width, both = normed[0].shape[1], grad_raw[0].shape[1]
+def gate_terms(normed, grad_raw, groups, first, steps, earlier):
+    width, both = normed[0].shape[1], steps * STEP
     rows = sum(part.shape[0] for part in normed)
     shape = (groups, 2, width // (2 * groups))
     return pl.pallas_call(
         gate_terms_kernel,
-        grid=(both // 256,),
+        grid=(steps,),
         in_specs=[whole_block(part.shape) for part in normed]
-        + [pl.BlockSpec((part.shape[0], 256), lambda i: (0, i)) for part in grad_raw]
+        + [pl.BlockSpec((part.shape[0], STEP), lambda i: (0, first + i)) for part in grad_raw]
         + [pl.BlockSpec(memory_space=pl.ANY)],
-        out_specs=pl.BlockSpec(shape + (256,), lambda i: (0, 0, 0, i)),
+        out_specs=pl.BlockSpec(shape + (STEP,), lambda i: (0, 0, 0, i)),
         out_shape=jax.ShapeDtypeStruct(shape + (both,), BF),
         compiler_params=PARAMS,
         cost_estimate=pl.CostEstimate(
@@ -208,9 +230,8 @@
     return jnp.concatenate([part, swap(part, "c")])
 
 
-def core_sum(part):
-    half = part.shape[0] // 2
-    return part[:half].astype(F32) + swap(part[half:], "c").astype(F32)
+def core_sum(mine, other):
+    return mine.astype(F32) + swap(other, "c").astype(F32)
 
 
 def send_far(far):
@@ -218,8 +239,9 @@
     return swap(far[:half], "y"), swap(far[half:], "x")
 
 
-def sum_near(near, top, low):
-    near = core_sum(near)
+def sum_near(mine, other, top, low):
+    mine, other, top, low = lax.optimization_barrier((mine, other, top, low))
+    near = core_sum(mine, other)
     rows = near.shape[0] // 2
     half = rows // 2
     to_x = jnp.concatenate([near[:half] + top, near[half:rows]]).astype(BF)
@@ -227,8 +249,9 @@
     return to_x, to_y
 
 
-def sum_own(own, to_x, to_y):
-    return core_sum(own) + swap(to_x, "x").astype(F32) + swap(to_y, "y").astype(F32)
+def sum_own(mine, other, to_x, to_y):
+    total = core_sum(mine, other)
+    return total + swap(to_x, "x").astype(F32) + swap(to_y, "y").astype(F32)
 
 
 def in_order(own, other, place):
@@ -246,12 +269,13 @@
     return lax.dynamic_slice_in_dim(both, lax.rem(size - place, size), size, 0)
 
 
-def plane_weights(blocks):
+def plane_weights(blocks, *earlier):
     x, y = lax.axis_index("x"), lax.axis_index("y")
     half = blocks.shape[0] // 2
     first, second = blocks[:half], blocks[half:]
     first = in_order(first, swap(first, "x"), x)
     second = in_order(second, swap(second, "y"), y)
+    first, second = lax.optimization_barrier((first, second, *earlier))[:2]
     first = in_order(first, swap(first, "y"), y)
     second = in_order(second, swap(second, "x"), x)
     first = first.transpose(1, 2, 0, 3, 4)
@@ -732,8 +756,9 @@
     normed, normed_before, query_raw, key_raw, queries, keys, values, d_gains, h_gains = project(
         places, layer_in, before, mine, other, cosine_table, sine_table, shard_rows, q_cols, k_cols
     )
-    w_o = plane_weights(after(w_o, keys))
+    w_o = plane_weights(w_o, keys)
     w_o = in_order(w_o, swap(w_o, "c"), core).transpose(1, 2, 3, 0, 4, 5).reshape(q_cols, width)
+    w_o = after(w_o, down)
     attended, log_total, branch, middle, normed_mlp = attend(
         queries, keys, values, query_ids, key_ids, w_o, layer_in, d_gains, attn_scale
     )
@@ -742,13 +767,14 @@
     from_x, from_y = swap(normed_mlp, "x"), swap(normed_mlp, "y")
     normed_far = jnp.concatenate([swap(from_x[:half], "y"), swap(from_y[half:], "x")])
     normed_near = jnp.concatenate([from_x, from_y])
+    normed_far, gate_up = lax.optimization_barrier((normed_far, gate_up))
     normed_all = [with_core(part) for part in (normed_mlp, normed_near, normed_far)]
-    far_result = mlp_forward(normed_all[2], gate_up, down, normed_all[2])
-    far_sum = core_sum(far_result[3]).astype(BF)
+    far_result = mlp_forward(normed_all[2], gate_up, down, normed_all[0])
+    far_sum = core_sum(*far_result[3:]).astype(BF)
     near_result = mlp_forward(normed_all[1], gate_up, down, far_sum)
-    to_x, to_y = sum_near(*lax.optimization_barrier((near_result[3], *send_far(far_sum))))
+    to_x, to_y = sum_near(*near_result[3:], *send_far(far_sum))
     own_result = mlp_forward(normed_all[0], gate_up, down, to_x)
-    mixed = sum_own(own_result[3], to_x, to_y)
+    mixed = sum_own(*own_result[3:], to_x, to_y)
     layer_out = middle + norm_gain(mixed, d_gains[3:4])
 
     _, pullback = jax.vjp(norm_gain, mixed, d_gains[3:4])
@@ -769,18 +795,17 @@
     far_grads = mlp_backward(
         grad_far, far_result[1], far_result[2], gate_up, down, grad_down_terms
     )
-    far_sum = core_sum(far_grads[1]).astype(BF)
+    far_sum = core_sum(*far_grads[1:]).astype(BF)
     near_grads = mlp_backward(grad_near, near_result[1], near_result[2], gate_up, down, far_sum)
-    to_x, to_y = sum_near(*lax.optimization_barrier((near_grads[1], *send_far(far_sum))))
-    gate_up_terms = gate_terms(
-        normed_all, [g[0] for g in (own_grads, near_grads, far_grads)], groups, to_x
-    )
-    grad_normed_mlp = sum_own(own_grads[1], to_x, to_y)
+    to_x, to_y = sum_near(*near_grads[1:], *send_far(far_sum))
+    raw_grads = [g[0] for g in (own_grads, near_grads, far_grads)]
+    gate_up_terms = gate_terms(normed_all, raw_grads, groups, 0, 2 * hidden_pad // STEP, to_x)
+    grad_normed_mlp = sum_own(*own_grads[1:], to_x, to_y)
     grad_normed_mlp = after(grad_normed_mlp, gate_up_terms)
     term = gate_up_terms.reshape(groups * members * shard_rows, 2 * hidden_pad)
-    gate_up_share = lax.psum_scatter(term, "g", scatter_dimension=0, tiled=True)
-    term = gate_up_share.reshape(members, shard_rows, 2 * hidden_pad)
-    term = lax.all_to_all(term, PLANE, split_axis=0, concat_axis=0, tiled=True)
+    term = lax.psum_scatter(term, "g", scatter_dimension=0, tiled=True)
+    gate_up_share = term.reshape(members, shard_rows, 2 * hidden_pad)
+    term = lax.all_to_all(gate_up_share, PLANE, split_axis=0, concat_axis=0, tiled=True)
 
     def collect(cut):
         cut = cut[:, :, :hidden_own].reshape(2, members // 2, shard_rows, groups, piece)

time: 562 us -> 580 us (1.032)
  waiting for transfers between devices: 168 us -> 185 us
  local copies, waits for them, and re-layouts: 66.1 us -> 50.1 us
  Pallas kernels: 195 us -> 204 us
    ppermute x50, waiting for transfers between devices: 135 us -> 152 us  [swap(): return lax.ppermute(array, axis, [(0, 1), (1, 0)])]
    slice x7 -> x0, local copies, waits for them, and re-layouts: 12.2 us -> none  [the longest x6 11.2 us: core_sum(): return part[:half].astype(F32) + swap(part[half:], 'c').astype(F32)]
    unnamed x74 -> x57, local copies, waits for them, and re-layouts: 12.2 us -> 8.97 us
  transfers between devices with their start and end apart: 66 -> 66, of which waited for: 31 -> 33; matrix products, arithmetic and copies ran while one was open for 14% -> 13% of each run, Pallas kernels for 28% -> 30%
where the time goes in v8:
time: 580 us; the launch traced here: 572 us
  Pallas kernels  204 us (35%)
  waiting for transfers between devices  185 us (32%)
  starting transfers between devices  69.4 us (12%)
  local copies, waits for them, and re-layouts  50.1 us (9%)
  other arithmetic  45.6 us (8%)
  between operations  15.2 us (3%)
    ppermute x50, waiting for transfers between devices, swap(): return lax.ppermute(array, axis, [(0, 1), (1, 0)])  152 us
    pallas_call x3, Pallas kernels, mlp_backward(): pl.pallas_call(mlp_backward_kernel, grid=(rows // TILE,), in_specs=[row_b...  53.5 us
    pallas_call x3, Pallas kernels, mlp_forward(): pl.pallas_call(mlp_forward_kernel, grid=(rows // TILE,), in_specs=[row_bl...  52.8 us
    ppermute x50, starting transfers between devices, swap(): return lax.ppermute(array, axis, [(0, 1), (1, 0)])  39 us
    pallas_call x1, Pallas kernels, gate_terms(): pl.pallas_call(gate_terms_kernel, grid=(steps,), in_specs=[whole_block(pa...  24.4 us
    pallas_call x1, Pallas kernels, attend_backward(): pl.pallas_call(functools.partial(attend_backward_kernel, scale), in_specs...  17 us
    pallas_call x1, Pallas kernels, down_terms(): pl.pallas_call(down_terms_kernel, grid=(own // 128,), in_specs=[pl.BlockS...  16.2 us
    pallas_call x1, Pallas kernels, project_backward(): pl.pallas_call(functools.partial(project_backward_kernel, shard_rows), in...  15.1 us
  transfers between devices with their start and end apart: 66, of which 33 were waited for; matrix products, arithmetic and copies ran while one was open for 13% of the time, Pallas kernels for 30%

profile of v8, /device:TPU:13, one launch (start us, length us, event | category | flops | bytes accessed | tf_op | source)
XLA Modules:
  0.0 572.1 jit_solution(4237289940696680007)
XLA Ops:
  28.2 8.9 %all-to-all-start = ((bf16[8,36,1792]{2,1,0:T(8,128)(2,1)}), bf16[8,36,1792]{2,1,0:T(8,128)(2,1)S(1)}, u32[]{:S(2)}, u32[]{:S(2)}) async-start(bf16[8,36,1792]{2,1,0:T(8,128)(2,1)} %copy.116), calls=%async_computation | async-start | bytes 2293760 | tf_op jit(solution)/shard_map/all_to_all | solution.py:728
  39.5 9.3 %collective-permute-done.4 = bf16[72,896]{1,0:T(8,128)(2,1)S(1)} collective-permute-done((bf16[72,896]{1,0:T(8,128)(2,1)S(1)}, bf16[72,896]{1,0:T(8,128)(2,1)S(1)}, u32[]{:S(2)}, u32[]{:S(2)}) %collective-permute-start.4) | collective-permute-done | bytes 129056 | tf_op jit(solution)/shard_map/ppermute | solution.py:265
  53.5 6.4 %collective-permute-done.5 = bf16[2,72,896]{2,1,0:T(8,128)(2,1)S(1)} collective-permute-done((bf16[2,72,896]{2,1,0:T(8,128)(2,1)S(1)}, bf16[2,72,896]{2,1,0:T(8,128)(2,1)S(1)}, u32[]{:S(2)}, u32[]{:S(2)}) %collective-permute-start.5) | collective-permute-done | bytes 258080 | tf_op jit(solution)/shard_map/ppermute | solution.py:51
  61.5 10.9 %collective-permute-done.8 = bf16[2,2,72,896]{3,2,1,0:T(8,128)(2,1)S(1)} collective-permute-done((bf16[2,2,72,896]{3,2,1,0:T(8,128)(2,1)S(1)}, bf16[2,2,72,896]{3,2,1,0:T(8,128)(2,1)S(1)}, u32[]{:S(2)}, u32[]{:S(2)}) %collective-permute-start.8) | collective-permute-done | bytes 516128 | tf_op jit(solution)/shard_map/ppermute | solution.py:51
  86.7 8.6 %shard_map.271 = (bf16[512,1152]{1,0:T(8,128)(2,1)}, bf16[512,1152]{1,0:T(8,128)(2,1)}, f32[512,1024]{1,0:T(8,128)}, f32[1024,256]{1,0:T(8,128)}, bf16[512,1024]...) custom-call(s32[1]{0:T(128)} %bitcast.core, ...), custom_call_target="tpu_custom_call" | custom-call | flops 2415919104 | bytes 9437184 | tf_op jit(solution)/shard_map/pallas_call | solution.py:390
  115.0 9.8 %shard_map.272 = (bf16[512,1024]{1,0:T(8,128)(2,1)}, f32[512,128]{1,0:T(8,128)}, f32[512,1152]{1,0:T(8,128)}, f32[512,1152]{1,0:T(8,128)}, bf16[512,1152]{1,0:T(8,128)(2,1)}) custom-call(bf16[512,1024]{1,0:T(8,128)(2,1)} %get-tuple-element.94.queries, bf16[1024,256]{1,0:T(8,128)(2,1)} %get-tuple-element.95.keys, bf16[1024,256]{1,0:T(8,128)(2,1)} %get-tuple-element.96.values, ...), custom_call_target="tpu_custom_call" | custom-call | flops 3355443200 | bytes 11796480 | tf_op jit(solution)/shard_map/pallas_call | solution.py:456
  125.4 27.3 %collective-permute-done.18 = bf16[512,1152]{1,0:T(8,128)(2,1)S(1)} collective-permute-done((bf16[512,1152]{1,0:T(8,128)(2,1)}, bf16[512,1152]{1,0:T(8,128)(2,1)S(1)}, u32[]{:S(2)}, u32[]{:S(2)}) %collective-permute-start.18) | collective-permute-done | bytes 1179680 | tf_op jit(solution)/shard_map/ppermute | solution.py:51
  155.2 11.7 %collective-permute-done.19 = bf16[256,1152]{1,0:T(8,128)(2,1)S(1)} collective-permute-done((bf16[256,1152]{1,0:T(8,128)(2,1)S(1)}, bf16[256,1152]{1,0:T(8,128)(2,1)S(1)}, u32[]{:S(2)}, u32[]{:S(2)}) %collective-permute-start.19) | collective-permute-done | bytes 589856 | tf_op jit(solution)/shard_map/ppermute | solution.py:51
  181.7 14.5 %shard_map.273 = (bf16[1024,896]{1,0:T(8,128)(2,1)}, bf16[1024,896]{1,0:T(8,128)(2,1)}, bf16[1024,896]{1,0:T(8,128)(2,1)}, bf16[512,1152]{1,0:T(8,128)(2,1)}, bf16[512,1152]{1,0:T(8,128)(2,1)}) custom-call(bf16[1024,1152]{1,0:T(8,128)(2,1)} %constant_dynamic-update-slice_fusion.5.normed.refs_2_, bf16[1152,1792]{1,0:T(8,128)(2,1)} %bitcast.200, ...), custom_call_target="tpu_custom_call" | custom-call | flops 6341787648 | bytes 10223616 | tf_op jit(solution)/shard_map/pallas_call | solution.py:110
  200.9 23.6 %shard_map.274 = (bf16[2048,896]{1,0:T(8,128)(2,1)}, bf16[2048,896]{1,0:T(8,128)(2,1)}, bf16[2048,896]{1,0:T(8,128)(2,1)}, bf16[1024,1152]{1,0:T(8,128)(2,1)}, bf16[1024,1152]{1,0:T(8,128)(2,1)}) custom-call(bf16[2048,1152]{1,0:T(8,128)(2,1)} %copy-done.16, bf16[1152,1792]{1,0:T(8,128)(2,1)} %bitcast.201, bf16[896,1152]{1,0:T(8,128)(2,1)} %pad.27.down._, ...), custom_call_target="tpu_custom_call" | custom-call | flops 12683575296 | bytes 20447232 | tf_op jit(solution)/shard_map/pallas_call | solution.py:110
  233.7 14.7 %shard_map.275 = (bf16[1024,896]{1,0:T(8,128)(2,1)}, bf16[1024,896]{1,0:T(8,128)(2,1)}, bf16[1024,896]{1,0:T(8,128)(2,1)}, bf16[512,1152]{1,0:T(8,128)(2,1)}, bf16[512,1152]{1,0:T(8,128)(2,1)}) custom-call(bf16[1024,1152]{1,0:T(8,128)(2,1)} %copy-done.12, bf16[1152,1792]{1,0:T(8,128)(2,1)} %bitcast.202, bf16[896,1152]{1,0:T(8,128)(2,1)} %pad.27.down._, ...), custom_call_target="tpu_custom_call" | custom-call | flops 6341787648 | bytes 10223616 | tf_op jit(solution)/shard_map/pallas_call | solution.py:110
  251.3 24.2 %collective-permute-done.28 = bf16[512,1152]{1,0:T(8,128)(2,1)S(1)} collective-permute-done((bf16[512,1152]{1,0:T(8,128)(2,1)S(1)}, bf16[512,1152]{1,0:T(8,128)(2,1)S(1)}, u32[]{:S(2)}, u32[]{:S(2)}) %collective-permute-start.28) | collective-permute-done | bytes 1179680 | tf_op jit(solution)/shard_map/ppermute | solution.py:51
  285.6 15.2 %shard_map.276 = (bf16[1024,1792]{1,0:T(8,128)(2,1)}, bf16[512,1152]{1,0:T(8,128)(2,1)}, bf16[512,1152]{1,0:T(8,128)(2,1)}) custom-call(bf16[1024,1152]{1,0:T(8,128)(2,1)} %pad_maximum_fusion.1.grad_mixed.refs_3_, bf16[1024,896]{1,0:T(8,128)(2,1)} %get-tuple-element.116.gelu, bf16[1024,896]{1,0:T(8,128)(2,1)} %get-tuple-element.117.slope, ...), custom_call_target="tpu_custom_call" | custom-call | flops 6341787648 | bytes 12058624 | tf_op jit(solution)/shard_map/pallas_call | solution.py:142
  300.8 8.3 %collective-permute-done.31 = bf16[512,1152]{1,0:T(8,128)(2,1)S(1)} collective-permute-done((bf16[512,1152]{1,0:T(8,128)(2,1)S(1)}, bf16[512,1152]{1,0:T(8,128)(2,1)S(1)}, u32[]{:S(2)}, u32[]{:S(2)}) %collective-permute-start.31) | collective-permute-done | bytes 1179680 | tf_op jit(solution)/shard_map/ppermute | solution.py:51
  313.1 13.0 %collective-permute-done.34 = bf16[256,1152]{1,0:T(8,128)(2,1)S(1)} collective-permute-done((bf16[256,1152]{1,0:T(8,128)(2,1)S(1)}, bf16[256,1152]{1,0:T(8,128)(2,1)S(1)}, u32[]{:S(2)}, u32[]{:S(2)}) %collective-permute-start.34) | collective-permute-done | bytes 589856 | tf_op jit(solution)/shard_map/ppermute | solution.py:51
  334.3 16.2 %shard_map.277._ = bf16[864,1152]{1,0:T(8,128)(2,1)} custom-call(bf16[1024,896]{1,0:T(8,128)(2,1)} %get-tuple-element.126.refs_0_, bf16[2048,896]{1,0:T(8,128)(2,1)} %get-tuple-element.127.refs_1_, bf16[1024,896]{1,0:T(8,128)(2,1)} %get-tuple-element.128.refs_2_, bf16[1024,1152]{1,0:T(8,128)(2,1)} %pad_maximum_fusion.1.grad_mixed.refs_3_, ...), custom_call_target="tpu_custom_call" | custom-call | flops 8455716864 | bytes 16777216 | tf_op jit(solution)/shard_map/pallas_call | solution.py:178
  350.5 14.8 %shard_map.278 = (bf16[1024,1792]{1,0:T(8,128)(2,1)}, bf16[512,1152]{1,0:T(8,128)(2,1)}, bf16[512,1152]{1,0:T(8,128)(2,1)}) custom-call(bf16[1024,1152]{1,0:T(8,128)(2,1)} %copy-done.18, bf16[1024,896]{1,0:T(8,128)(2,1)} %get-tuple-element.124.gelu, bf16[1024,896]{1,0:T(8,128)(2,1)} %get-tuple-element.125.slope, bf16[1152,1792]{1,0:T(8,128)(2,1)} %bitcast.204, ...), custom_call_target="tpu_custom_call" | custom-call | flops 6341787648 | bytes 12058624 | tf_op jit(solution)/shard_map/pallas_call | solution.py:142
  371.1 23.5 %shard_map.279 = (bf16[2048,1792]{1,0:T(8,128)(2,1)}, bf16[1024,1152]{1,0:T(8,128)(2,1)}, bf16[1024,1152]{1,0:T(8,128)(2,1)}) custom-call(bf16[2048,1152]{1,0:T(8,128)(2,1)} %copy-done.17, bf16[2048,896]{1,0:T(8,128)(2,1)} %get-tuple-element.122.gelu, bf16[2048,896]{1,0:T(8,128)(2,1)} %get-tuple-element.123.slope, bf16[1152,1792]{1,0:T(8,128)(2,1)} %bitcast.205, ...), custom_call_target="tpu_custom_call" | custom-call | flops 12683575296 | bytes 24117248 | tf_op jit(solution)/shard_map/pallas_call | solution.py:142
  409.9 24.4 %shard_map.280 = bf16[4,2,144,1792]{3,2,1,0:T(8,128)(2,1)} custom-call(bf16[1024,1152]{1,0:T(8,128)(2,1)} %copy-done.12, bf16[2048,1152]{1,0:T(8,128)(2,1)} %copy-done.16, bf16[1024,1152]{1,0:T(8,128)(2,1)} %constant_dynamic-update-slice_fusion.5.normed.refs_2_, bf16[1024,1792]{1,0:T(8,128)(2,1)} %get-tuple-element.137.refs_3_, ...), custom_call_target="tpu_custom_call" | custom-call | flops 16911433728 | bytes 24117248 | tf_op jit(solution)/shard_map/pallas_call | solution.py:210
  439.7 17.0 %shard_map.281 = (f32[512,1152]{1,0:T(8,128)}, bf16[512,1152]{1,0:T(8,128)(2,1)}, f32[512,1024]{1,0:T(8,128)}, f32[1024,256]{1,0:T(8,128)}, f32[1024,256]{1,0:T(8,128)}, /*index=5*/f32[8,1152]{1,0:T(8,128)}) custom-call(f32[512,1152]{1,0:T(8,128)} %convert_add_fusion.3.grad_normed_mlp, bf16[512,1152]{1,0:T(8,128)(2,1)} %bitcast.196, ...), custom_call_target="tpu_custom_call" | custom-call | flops 6576668672 | bytes 17694720 | tf_op jit(solution)/shard_map/pallas_call | solution.py:526
  464.3 15.1 %shard_map.282 = (f32[512,1152]{1,0:T(8,128)}, bf16[512,512]{1,0:T(8,128)(2,1)}, bf16[1152,896]{1,0:T(8,128)(2,1)}, bf16[1152,896]{1,0:T(8,128)(2,1)}) custom-call(s32[1]{0:T(128)} %bitcast.core, f32[512,1024]{1,0:T(8,128)} %get-tuple-element.144.grad_queries, f32[1024,256]{1,0:T(8,128)} %get-tuple-element.145.grad_keys, ...), custom_call_target="tpu_custom_call" | custom-call | flops 4756340736 | bytes 17694720 | tf_op jit(solution)/shard_map/pallas_call | solution.py:615
  481.9 7.1 %collective-permute-done.50 = bf16[2,2,32,1152]{3,2,1,0:T(8,128)(2,1)S(1)} collective-permute-done((bf16[2,2,32,1152]{3,2,1,0:T(8,128)(2,1)}, bf16[2,2,32,1152]{3,2,1,0:T(8,128)(2,1)S(1)}, u32[]{:S(2)}, u32[]{:S(2)}) %collective-permute-start.50) | collective-permute-done | bytes 294944 | tf_op jit(solution)/shard_map/ppermute | solution.py:51
  495.0 11.0 %collective-permute-done.55 = bf16[2,2,72,896]{3,2,1,0:T(8,128)(2,1)S(1)} collective-permute-done((bf16[2,2,72,896]{3,2,1,0:T(8,128)(2,1)S(1)}, bf16[2,2,72,896]{3,2,1,0:T(8,128)(2,1)S(1)}, u32[]{:S(2)}, u32[]{:S(2)}) %collective-permute-start.55) | collective-permute-done | bytes 516128 | tf_op jit(solution)/shard_map/ppermute | solution.py:51
  546.9 6.5 %shard_map.283 = bf16[512,1152]{1,0:T(8,128)(2,1)} custom-call(s32[1]{0:T(128)} %bitcast.core, bf16[512,512]{1,0:T(8,128)(2,1)} %copy-done.15, f32[512,1152]{1,0:T(8,128)} %get-tuple-element.154.grad_normed, bf16[1152,896]{1,0:T(8,128)(2,1)} %bitcast.194, bf16[1152,896]{1,0:T(8,128)(2,1)} %collective-permute-done.9.other, bf16[512,1152]{1,0:T(8,128)(2,1)} %bitcast.225, ...), custom_call_target="tpu_custom_call" | custom-call | flops 603979776 | bytes 7077888 | tf_op jit(solution)/shard_map/pallas_call | solution.py:652
  (316 shorter events, 214.9 us)
Async XLA Ops:
  7.2 69.6 %all-gather.5.cloned.1.call-start = ((), (), s32[]{:S(2)}) async-start(), calls=%async_computation.4 | async-start | bytes 2856960 | tf_op jit(solution)/shard_map/all_gather | solution.py:734
  28.2 23.5 %all-to-all-start = ((bf16[8,36,1792]{2,1,0:T(8,128)(2,1)}), bf16[8,36,1792]{2,1,0:T(8,128)(2,1)S(1)}, u32[]{:S(2)}, u32[]{:S(2)}) async-start(bf16[8,36,1792]{2,1,0:T(8,128)(2,1)} %copy.116), calls=%async_computation | async-start | bytes 2293760 | tf_op jit(solution)/shard_map/all_to_all | solution.py:728
  37.1 130.8 %all-gather.7.cloned.1.call-start = ((), (), s32[]{:S(2)}) async-start(), calls=%async_computation.5 | async-start | bytes 5160960 | tf_op jit(solution)/shard_map/all_gather | solution.py:739
  76.7 440.0 %reduce-scatter.2.cloned.1.call-start = ((), (), s32[]{:S(2)}) async-start(), calls=%async_computation.3 | async-start | bytes 5160960 | tf_op jit(solution)/shard_map/reduce_scatter | solution.py:806
  124.8 27.9 %collective-permute-start.18 = (bf16[512,1152]{1,0:T(8,128)(2,1)}, bf16[512,1152]{1,0:T(8,128)(2,1)S(1)}, u32[]{:S(2)}, u32[]{:S(2)}) collective-permute-start(bf16[512,1152]{1,0:T(8,128)(2,1)} %get-tuple-element.102), channel_id=1, source_target_pairs={{0,2},{2,0},{1,3},{3,1},{4,6},{6,4},{5,7},{7,5},{8,10},{10,8},{9,1... | collective-permute-start | bytes 3538952 | tf_op jit(solution)/shard_map/ppermute | solution.py:51
  124.8 28.5 %collective-permute-start.16 = (bf16[512,1152]{1,0:T(8,128)(2,1)}, bf16[512,1152]{1,0:T(8,128)(2,1)S(1)}, u32[]{:S(2)}, u32[]{:S(2)}) collective-permute-start(bf16[512,1152]{1,0:T(8,128)(2,1)} %get-tuple-element.102), channel_id=1, source_target_pairs={{0,16},{16,0},{1,17},{17,1},{2,18},{18,2},{3,19},{19,3},{4,20},{20... | collective-permute-start | bytes 3538952 | tf_op jit(solution)/shard_map/ppermute | solution.py:51
  153.9 23.4 %collective-permute-start.15 = (bf16[512,1152]{1,0:T(8,128)(2,1)}, bf16[512,1152]{1,0:T(8,128)(2,1)}, u32[]{:S(2)}, u32[]{:S(2)}) collective-permute-start(bf16[512,1152]{1,0:T(8,128)(2,1)} %get-tuple-element.102), channel_id=1, source_target_pairs={{0,1},{1,0},{2,3},{3,2},{4,5},{5,4},{6,7},{7,6},{8,9},{9,8},{10,11... | collective-permute-start | bytes 3538952 | tf_op jit(solution)/shard_map/ppermute | solution.py:51
  199.8 24.7 %collective-permute-start.23 = (bf16[256,1152]{1,0:T(8,128)(2,1)S(1)}, bf16[256,1152]{1,0:T(8,128)(2,1)S(1)}, u32[]{:S(2)}, u32[]{:S(2)}) collective-permute-start(bf16[256,1152]{1,0:T(8,128)(2,1)S(1)} %get-tuple-element.201), channel_id=1, source_target_pairs={{0,2},{2,0},{1,3},{3,1},{4,6},{6,4},{5,7},{7,5},{8,10},{10,8},{9,1... | collective-permute-start | bytes 1769480 | tf_op jit(solution)/shard_map/ppermute | solution.py:51
  200.3 24.2 %collective-permute-start.24 = (bf16[256,1152]{1,0:T(8,128)(2,1)S(1)}, bf16[256,1152]{1,0:T(8,128)(2,1)S(1)}, u32[]{:S(2)}, u32[]{:S(2)}) collective-permute-start(bf16[256,1152]{1,0:T(8,128)(2,1)S(1)} %get-tuple-element.200), channel_id=1, source_target_pairs={{0,16},{16,0},{1,17},{17,1},{2,18},{18,2},{3,19},{19,3},{4,20},{20... | collective-permute-start | bytes 1769480 | tf_op jit(solution)/shard_map/ppermute | solution.py:51
  232.7 42.8 %collective-permute-start.27 = (bf16[512,1152]{1,0:T(8,128)(2,1)S(1)}, bf16[512,1152]{1,0:T(8,128)(2,1)S(1)}, u32[]{:S(2)}, u32[]{:S(2)}) collective-permute-start(bf16[512,1152]{1,0:T(8,128)(2,1)S(1)} %pad_maximum_fusion.6._), channel_id=1, source_target_pairs={{0,16},{16,0},{1,17},{17,1},{2,18},{18,2},{3,19},{19,3},{4,20},{20... | collective-permute-start | bytes 3538952 | tf_op jit(solution)/shard_map/ppermute | solution.py:51
  248.5 27.0 %collective-permute-start.28 = (bf16[512,1152]{1,0:T(8,128)(2,1)S(1)}, bf16[512,1152]{1,0:T(8,128)(2,1)S(1)}, u32[]{:S(2)}, u32[]{:S(2)}) collective-permute-start(bf16[512,1152]{1,0:T(8,128)(2,1)S(1)} %pad_maximum_fusion.7), channel_id=1, source_target_pairs={{0,2},{2,0},{1,3},{3,1},{4,6},{6,4},{5,7},{7,5},{8,10},{10,8},{9,1... | collective-permute-start | bytes 3538952 | tf_op jit(solution)/shard_map/ppermute | solution.py:51
  249.9 25.6 %collective-permute-start.26 = (bf16[512,1152]{1,0:T(8,128)(2,1)S(1)}, bf16[512,1152]{1,0:T(8,128)(2,1)S(1)}, u32[]{:S(2)}, u32[]{:S(2)}) collective-permute-start(bf16[512,1152]{1,0:T(8,128)(2,1)S(1)} %copy-done.19), channel_id=1, source_target_pairs={{0,1},{1,0},{2,3},{3,2},{4,5},{5,4},{6,7},{7,6},{8,9},{9,8},{10,11... | collective-permute-start | bytes 3538952 | tf_op jit(solution)/shard_map/ppermute | solution.py:51
  281.5 27.6 %collective-permute-start.31 = (bf16[512,1152]{1,0:T(8,128)(2,1)S(1)}, bf16[512,1152]{1,0:T(8,128)(2,1)S(1)}, u32[]{:S(2)}, u32[]{:S(2)}) collective-permute-start(bf16[512,1152]{1,0:T(8,128)(2,1)S(1)} %get-tuple-element.179), channel_id=1, source_target_pairs={{0,16},{16,0},{1,17},{17,1},{2,18},{18,2},{3,19},{19,3},{4,20},{20... | collective-permute-start | bytes 3538952 | tf_op jit(solution)/shard_map/ppermute | solution.py:51
  282.4 27.3 %collective-permute-start.32 = (bf16[512,1152]{1,0:T(8,128)(2,1)S(1)}, bf16[512,1152]{1,0:T(8,128)(2,1)S(1)}, u32[]{:S(2)}, u32[]{:S(2)}) collective-permute-start(bf16[512,1152]{1,0:T(8,128)(2,1)S(1)} %get-tuple-element.179), channel_id=1, source_target_pairs={{0,2},{2,0},{1,3},{3,1},{4,6},{6,4},{5,7},{7,5},{8,10},{10,8},{9,1... | collective-permute-start | bytes 3538952 | tf_op jit(solution)/shard_map/ppermute | solution.py:51
  370.0 24.6 %collective-permute-start.38 = (bf16[256,1152]{1,0:T(8,128)(2,1)S(1)}, bf16[256,1152]{1,0:T(8,128)(2,1)}, u32[]{:S(2)}, u32[]{:S(2)}) collective-permute-start(bf16[256,1152]{1,0:T(8,128)(2,1)S(1)} %get-tuple-element.199), channel_id=1, source_target_pairs={{0,2},{2,0},{1,3},{3,1},{4,6},{6,4},{5,7},{7,5},{8,10},{10,8},{9,1... | collective-permute-start | bytes 1769480 | tf_op jit(solution)/shard_map/ppermute | solution.py:51
  370.5 24.1 %collective-permute-start.39 = (bf16[256,1152]{1,0:T(8,128)(2,1)S(1)}, bf16[256,1152]{1,0:T(8,128)(2,1)}, u32[]{:S(2)}, u32[]{:S(2)}) collective-permute-start(bf16[256,1152]{1,0:T(8,128)(2,1)S(1)} %get-tuple-element.198), channel_id=1, source_target_pairs={{0,16},{16,0},{1,17},{17,1},{2,18},{18,2},{3,19},{19,3},{4,20},{20... | collective-permute-start | bytes 1769480 | tf_op jit(solution)/shard_map/ppermute | solution.py:51
  395.6 38.8 %collective-permute-start.30 = (bf16[512,1152]{1,0:T(8,128)(2,1)}, bf16[512,1152]{1,0:T(8,128)(2,1)S(1)}, u32[]{:S(2)}, u32[]{:S(2)}) collective-permute-start(bf16[512,1152]{1,0:T(8,128)(2,1)} %get-tuple-element.119), channel_id=1, source_target_pairs={{0,1},{1,0},{2,3},{3,2},{4,5},{5,4},{6,7},{7,6},{8,9},{9,8},{10,11... | collective-permute-start | bytes 3538952 | tf_op jit(solution)/shard_map/ppermute | solution.py:51
  398.1 63.5 %collective-permute-start.45 = (bf16[216,1152]{1,0:T(8,128)(2,1)}, bf16[216,1152]{1,0:T(8,128)(2,1)}, u32[]{:S(2)}, u32[]{:S(2)}) collective-permute-start(bf16[216,1152]{1,0:T(8,128)(2,1)} %get-tuple-element.194), channel_id=1, source_target_pairs={{0,12},{4,0},{8,4},{12,8},{1,13},{5,1},{9,5},{13,9},{2,14},{6,2},{... | collective-permute-start | bytes 1493000 | tf_op jit(solution)/shard_map/ppermute | solution.py:293
  398.9 62.7 %collective-permute-start.44 = (bf16[216,1152]{1,0:T(8,128)(2,1)}, bf16[216,1152]{1,0:T(8,128)(2,1)}, u32[]{:S(2)}, u32[]{:S(2)}) collective-permute-start(bf16[216,1152]{1,0:T(8,128)(2,1)} %get-tuple-element.195), channel_id=1, source_target_pairs={{0,8},{4,12},{8,0},{12,4},{1,9},{5,13},{9,1},{13,5},{2,10},{6,14},... | collective-permute-start | bytes 1493000 | tf_op jit(solution)/shard_map/ppermute | solution.py:293
  406.9 28.7 %collective-permute-start.42 = (bf16[512,1152]{1,0:T(8,128)(2,1)}, bf16[512,1152]{1,0:T(8,128)(2,1)S(1)}, u32[]{:S(2)}, u32[]{:S(2)}) collective-permute-start(bf16[512,1152]{1,0:T(8,128)(2,1)} %pad_maximum_fusion.10), channel_id=1, source_target_pairs={{0,2},{2,0},{1,3},{3,1},{4,6},{6,4},{5,7},{7,5},{8,10},{10,8},{9,1... | collective-permute-start | bytes 3538952 | tf_op jit(solution)/shard_map/ppermute | solution.py:51
  409.3 27.2 %collective-permute-start.41 = (bf16[512,1152]{1,0:T(8,128)(2,1)}, bf16[512,1152]{1,0:T(8,128)(2,1)}, u32[]{:S(2)}, u32[]{:S(2)}) collective-permute-start(bf16[512,1152]{1,0:T(8,128)(2,1)} %pad_maximum_fusion.9.refs_6_), channel_id=1, source_target_pairs={{0,16},{16,0},{1,17},{17,1},{2,18},{18,2},{3,19},{19,3},{4,20},{20... | collective-permute-start | bytes 3538952 | tf_op jit(solution)/shard_map/ppermute | solution.py:51
  434.3 27.3 %collective-permute-start.43 = (bf16[216,1152]{1,0:T(8,128)(2,1)}, bf16[216,1152]{1,0:T(8,128)(2,1)}, u32[]{:S(2)}, u32[]{:S(2)}) collective-permute-start(bf16[216,1152]{1,0:T(8,128)(2,1)} %get-tuple-element.193), channel_id=1, source_target_pairs={{0,4},{4,8},{8,12},{12,0},{1,5},{5,9},{9,13},{13,1},{2,6},{6,10},{... | collective-permute-start | bytes 1493000 | tf_op jit(solution)/shard_map/ppermute | solution.py:293
  523.0 23.1 %collective-permute-start.46 = (bf16[512,512]{1,0:T(8,128)(2,1)}, bf16[512,512]{1,0:T(8,128)(2,1)S(1)}, u32[]{:S(2)}, u32[]{:S(2)}) collective-permute-start(bf16[512,512]{1,0:T(8,128)(2,1)} %get-tuple-element.153), channel_id=1, source_target_pairs={{1,0},{2,1},{3,2},{4,3},{5,4},{6,5},{7,6},{8,7},{9,8},{10,9},{11,1... | collective-permute-start | bytes 1572872 | tf_op jit(solution)/shard_map/ppermute | solution.py:830
  526.2 31.5 %all-to-all-start.1 = ((bf16[8,36,1792]{2,1,0:T(8,128)(2,1)}), bf16[8,36,1792]{2,1,0:T(8,128)(2,1)S(1)}, u32[]{:S(2)}, u32[]{:S(2)}) async-start(bf16[8,36,1792]{2,1,0:T(8,128)(2,1)} %reshape.172), calls=%async_computation.2 | async-start | bytes 2293760 | tf_op jit(solution)/shard_map/all_to_all | solution.py:808
  (63 other events, 569.2 us)
Sparse Core Ops, SparseCore 0:
  17.2 55.7 all-gather.4
  76.8 76.9 all-gather.6
  434.5 82.2 reduce-scatter.1

commit v9 on v6

--- a/solution.py
+++ b/solution.py
@@ -246,14 +246,17 @@
     return lax.dynamic_slice_in_dim(both, lax.rem(size - place, size), size, 0)
 
 
-def plane_weights(blocks):
-    x, y = lax.axis_index("x"), lax.axis_index("y")
+def plane_near(blocks):
     half = blocks.shape[0] // 2
     first, second = blocks[:half], blocks[half:]
-    first = in_order(first, swap(first, "x"), x)
-    second = in_order(second, swap(second, "y"), y)
-    first = in_order(first, swap(first, "y"), y)
-    second = in_order(second, swap(second, "x"), x)
+    first = in_order(first, swap(first, "x"), lax.axis_index("x"))
+    second = in_order(second, swap(second, "y"), lax.axis_index("y"))
+    return first, second
+
+
+def plane_far(first, second):
+    first = in_order(first, swap(first, "y"), lax.axis_index("y"))
+    second = in_order(second, swap(second, "x"), lax.axis_index("x"))
     first = first.transpose(1, 2, 0, 3, 4)
     second = second.transpose(0, 2, 1, 3, 4)
     return jnp.concatenate([first, second], axis=1)
@@ -637,6 +640,35 @@
     )(core, returned, grad_normed, own, other, tokens, d_gains, grad_middle)
 
 
+def owner_rows_kernel(groups, piece, term, gate, up):
+    sides, lanes = term.shape[0] // 2, term.shape[2] // 2
+    for out, first in ((gate, 0), (up, lanes)):
+        parts = []
+        for side in range(2):
+            rows = [
+                term[side * sides + member, :, first : first + lanes].astype(F32)
+                for member in range(sides)
+            ]
+            for group in range(groups):
+                parts += [row[:, group * piece : (group + 1) * piece] for row in rows]
+        out[...] = jnp.concatenate(parts, axis=1)
+
+
+def owner_rows(term, groups, piece):
+    vmem = pl.BlockSpec(memory_space=pltpu.VMEM)
+    shape = jax.ShapeDtypeStruct((term.shape[1], term.shape[0] * groups * piece), F32)
+    return pl.pallas_call(
+        functools.partial(owner_rows_kernel, groups, piece),
+        in_specs=[vmem],
+        out_specs=[vmem, vmem],
+        out_shape=[shape, shape],
+        compiler_params=PARAMS,
+        cost_estimate=pl.CostEstimate(
+            flops=term.size, bytes_accessed=6 * term.size, transcendentals=0
+        ),
+    )(term)
+
+
 def on_device(
     tokens,
     cotangent,
@@ -703,13 +735,16 @@
     mine, before, sent = lax.optimization_barrier((mine, before, sent))
     sent = lax.all_to_all(sent, PLANE, split_axis=0, concat_axis=0, tiled=True)
     sent = sent.reshape(members * shard_rows, 2 * hidden_pad)
+    w_o = group_gather(after(w_out, mine))
     mine, sent = lax.optimization_barrier((group_gather(mine), sent))
-    mine = plane_weights(mine).reshape(width, half_cols)
+    near, w_o = lax.optimization_barrier((plane_near(mine), w_o))
+    w_o = plane_near(w_o)
+    mine, w_o = lax.optimization_barrier((plane_far(*near), w_o))
+    mine = mine.reshape(width, half_cols)
+    w_o = plane_far(*w_o)
     other = swap(mine, "c")
 
-    down = lax.all_gather(jnp.concatenate([w_down, w_out]), "g", axis=0)
-    w_o = down[:, w_down.shape[0] :]
-    down = down[:, : w_down.shape[0]].reshape(-1, width)
+    down = lax.all_gather(w_down, "g", axis=0, tiled=True)
     down = jnp.pad(down, ((0, hidden_pad - hidden_own), (0, 0)))
 
     both = lax.all_gather(sent, "g", axis=0)
@@ -732,7 +767,7 @@
     normed, normed_before, query_raw, key_raw, queries, keys, values, d_gains, h_gains = project(
         places, layer_in, before, mine, other, cosine_table, sine_table, shard_rows, q_cols, k_cols
     )
-    w_o = plane_weights(after(w_o, keys))
+    w_o = after(w_o, keys)
     w_o = in_order(w_o, swap(w_o, "c"), core).transpose(1, 2, 3, 0, 4, 5).reshape(q_cols, width)
     attended, log_total, branch, middle, normed_mlp = attend(
         queries, keys, values, query_ids, key_ids, w_o, layer_in, d_gains, attn_scale
@@ -779,15 +814,10 @@
     grad_normed_mlp = after(grad_normed_mlp, gate_up_terms)
     term = gate_up_terms.reshape(groups * members * shard_rows, 2 * hidden_pad)
     gate_up_share = lax.psum_scatter(term, "g", scatter_dimension=0, tiled=True)
-    term = gate_up_share.reshape(members, shard_rows, 2 * hidden_pad)
-    term = lax.all_to_all(term, PLANE, split_axis=0, concat_axis=0, tiled=True)
-
-    def collect(cut):
-        cut = cut[:, :, :hidden_own].reshape(2, members // 2, shard_rows, groups, piece)
-        return cut.transpose(2, 0, 3, 1, 4).reshape(shard_rows, hidden_all).astype(F32)
-
-    grad_w_gate = collect(term[:, :, :hidden_pad])
-    grad_w_up = collect(term[:, :, hidden_pad:])
+    gate_up_share = gate_up_share.reshape(members, shard_rows, 2 * hidden_pad)
+    term = lax.all_to_all(gate_up_share, PLANE, split_axis=0, concat_axis=0, tiled=True)
+
+    grad_w_gate, grad_w_up = owner_rows(term, groups, piece)
 
     grad_middle, grad_branch, grad_queries, grad_keys, grad_values, terms = attend_backward(
         grad_normed_mlp, grad_out, middle, branch, d_gains, w_o,

time: 562 us -> 574 us (1.021)
  starting transfers between devices: 68.4 us -> 78.1 us
    ppermute x3 -> x6, waiting for transfers between devices: 11.5 us -> 25.8 us  [group_gather(): lax.ppermute(own, 'g', [((i + k) % size, i) for i in range(size)])]
    ppermute x50, waiting for transfers between devices: 135 us -> 126 us  [swap(): return lax.ppermute(array, axis, [(0, 1), (1, 0)])]
    ppermute x50, starting transfers between devices: 38 us -> 46.8 us  [swap(): return lax.ppermute(array, axis, [(0, 1), (1, 0)])]
    convert_element_type x6 -> x0, local copies, waits for them, and re-layouts: 7.23 us -> none  [collect(): cut.transpose(2, 0, 3, 1, 4).reshape(shard_rows, hidden_all).astype(F32)]
    unnamed x74 -> x78, local copies, waits for them, and re-layouts: 12.2 us -> 13.1 us
  transfers between devices with their start and end apart: 66 -> 69, of which waited for: 31 -> 32; matrix products, arithmetic and copies ran while one was open for 14% -> 14% of each run, Pallas kernels for 28% -> 29%
where the time goes in v9:
time: 574 us; the launch traced here: 566 us
  Pallas kernels  198 us (34%)
  waiting for transfers between devices  171 us (30%)
  starting transfers between devices  78.1 us (14%)
  local copies, waits for them, and re-layouts  64.1 us (11%)
  other arithmetic  37.1 us (6%)
  between operations  15.1 us (3%)
    ppermute x50, waiting for transfers between devices, swap(): return lax.ppermute(array, axis, [(0, 1), (1, 0)])  126 us
    pallas_call x3, Pallas kernels, mlp_backward(): pl.pallas_call(mlp_backward_kernel, grid=(rows // TILE,), in_specs=[row_b...  48.9 us
    pallas_call x3, Pallas kernels, mlp_forward(): pl.pallas_call(mlp_forward_kernel, grid=(rows // TILE,), in_specs=[row_bl...  48.1 us
    ppermute x50, starting transfers between devices, swap(): return lax.ppermute(array, axis, [(0, 1), (1, 0)])  46.8 us
    ppermute x6, waiting for transfers between devices, group_gather(): lax.ppermute(own, 'g', [((i + k) % size, i) for i in range(size)])  25.8 us
    pallas_call x1, Pallas kernels, gate_terms(): pl.pallas_call(gate_terms_kernel, grid=(both // 256,), in_specs=[whole_bl...  24.4 us
    pallas_call x1, Pallas kernels, attend_backward(): pl.pallas_call(functools.partial(attend_backward_kernel, scale), in_specs...  16.8 us
    pallas_call x1, Pallas kernels, down_terms(): pl.pallas_call(down_terms_kernel, grid=(own // 128,), in_specs=[pl.BlockS...  16.4 us
  transfers between devices with their start and end apart: 69, of which 32 were waited for; matrix products, arithmetic and copies ran while one was open for 14% of the time, Pallas kernels for 29%

profile of v9, /device:TPU:13, one launch (start us, length us, event | category | flops | bytes accessed | tf_op | source)
XLA Modules:
  0.0 565.8 jit_solution(791314933663703696)
XLA Ops:
  30.9 8.5 %all-to-all-start = ((bf16[8,36,1792]{2,1,0:T(8,128)(2,1)}), bf16[8,36,1792]{2,1,0:T(8,128)(2,1)S(1)}, u32[]{:S(2)}, u32[]{:S(2)}) async-start(bf16[8,36,1792]{2,1,0:T(8,128)(2,1)} %copy.70), calls=%async_computation | async-start | bytes 2293760 | tf_op jit(solution)/shard_map/all_to_all | solution.py:736
  39.4 19.5 %collective-permute-done.7 = bf16[32,1152]{1,0:T(8,128)(2,1)S(1)} collective-permute-done((bf16[32,1152]{1,0:T(8,128)(2,1)S(1)}, bf16[32,1152]{1,0:T(8,128)(2,1)S(1)}, u32[]{:S(2)}, u32[]{:S(2)}) %collective-permute-start.7) | collective-permute-done | bytes 73760 | tf_op jit(solution)/shard_map/ppermute | solution.py:242
  78.6 7.0 %collective-permute-done.13 = bf16[2,32,1152]{2,1,0:T(8,128)(2,1)S(1)} collective-permute-done((bf16[2,32,1152]{2,1,0:T(8,128)(2,1)S(1)}, bf16[2,32,1152]{2,1,0:T(8,128)(2,1)S(1)}, u32[]{:S(2)}, u32[]{:S(2)}) %collective-permute-start.13) | collective-permute-done | bytes 147488 | tf_op jit(solution)/shard_map/ppermute | solution.py:51
  87.3 8.3 %collective-permute-start.14 = (bf16[1152,896]{1,0:T(8,128)(2,1)S(1)}, bf16[1152,896]{1,0:T(8,128)(2,1)}, u32[]{:S(2)}, u32[]{:S(2)}) collective-permute-start(bf16[1152,896]{1,0:T(8,128)(2,1)S(1)} %bitcast.189), channel_id=1, source_target_pairs={{0,1},{1,0},{2,3},{3,2},{4,5},{5,4},{6,7},{7,6},{8,9},{9,8},{10,11... | collective-permute-start | bytes 6193160 | tf_op jit(solution)/shard_map/ppermute | solution.py:51
  106.0 8.8 %shard_map.271 = (bf16[512,1152]{1,0:T(8,128)(2,1)}, bf16[512,1152]{1,0:T(8,128)(2,1)}, f32[512,1024]{1,0:T(8,128)}, f32[1024,256]{1,0:T(8,128)}, bf16[512,1024]...) custom-call(s32[1]{0:T(128)} %bitcast.core, ...), custom_call_target="tpu_custom_call" | custom-call | flops 2415919104 | bytes 9437184 | tf_op jit(solution)/shard_map/pallas_call | solution.py:369
  121.1 9.7 %shard_map.272 = (bf16[512,1024]{1,0:T(8,128)(2,1)}, f32[512,128]{1,0:T(8,128)}, f32[512,1152]{1,0:T(8,128)}, f32[512,1152]{1,0:T(8,128)}, bf16[512,1152]{1,0:T(8,128)(2,1)}) custom-call(bf16[512,1024]{1,0:T(8,128)(2,1)} %get-tuple-element.92.queries, bf16[1024,256]{1,0:T(8,128)(2,1)} %get-tuple-element.93.keys, bf16[1024,256]{1,0:T(8,128)(2,1)} %get-tuple-element.94.values, ...), custom_call_target="tpu_custom_call" | custom-call | flops 3355443200 | bytes 11796480 | tf_op jit(solution)/shard_map/pallas_call | solution.py:435
  132.8 25.4 %collective-permute-done.19 = bf16[512,1152]{1,0:T(8,128)(2,1)S(1)} collective-permute-done((bf16[512,1152]{1,0:T(8,128)(2,1)}, bf16[512,1152]{1,0:T(8,128)(2,1)S(1)}, u32[]{:S(2)}, u32[]{:S(2)}) %collective-permute-start.19) | collective-permute-done | bytes 1179680 | tf_op jit(solution)/shard_map/ppermute | solution.py:51
  160.4 11.6 %collective-permute-done.22 = bf16[256,1152]{1,0:T(8,128)(2,1)S(1)} collective-permute-done((bf16[256,1152]{1,0:T(8,128)(2,1)S(1)}, bf16[256,1152]{1,0:T(8,128)(2,1)S(1)}, u32[]{:S(2)}, u32[]{:S(2)}) %collective-permute-start.22) | collective-permute-done | bytes 589856 | tf_op jit(solution)/shard_map/ppermute | solution.py:51
  190.1 12.9 %shard_map.273 = (bf16[1024,896]{1,0:T(8,128)(2,1)}, bf16[1024,896]{1,0:T(8,128)(2,1)}, bf16[1024,896]{1,0:T(8,128)(2,1)}, bf16[1024,1152]{1,0:T(8,128)(2,1)}) custom-call(bf16[1024,1152]{1,0:T(8,128)(2,1)} %constant_dynamic-update-slice_fusion.5.normed._.refs_2_, bf16[1152,1792]{1,0:T(8,128)(2,1)} %bitcast.198, bf16[896,1152]{1,0:T(8,128)(2,1)} %pad.27.down._, ...), custom_call_target="tpu_custom_call" | custom-call | flops 6341787648 | bytes 10223616 | tf_op jit(solution)/shard_map/pallas_call | solution.py:88
  210.7 21.8 %shard_map.274 = (bf16[2048,896]{1,0:T(8,128)(2,1)}, bf16[2048,896]{1,0:T(8,128)(2,1)}, bf16[2048,896]{1,0:T(8,128)(2,1)}, bf16[2048,1152]{1,0:T(8,128)(2,1)}) custom-call(bf16[2048,1152]{1,0:T(8,128)(2,1)} %copy-done.21, bf16[1152,1792]{1,0:T(8,128)(2,1)} %bitcast.199, bf16[896,1152]{1,0:T(8,128)(2,1)} %pad.27.down._, bf16[512,1152]{1,0:T(8,128)(2,1)} %copy-done.3), custom_call_target="tpu_custom_call" | custom-call | flops 12683575296 | bytes 20447232 | tf_op jit(solution)/shard_map/pallas_call | solution.py:88
  246.0 13.4 %shard_map.275 = (bf16[1024,896]{1,0:T(8,128)(2,1)}, bf16[1024,896]{1,0:T(8,128)(2,1)}, bf16[1024,896]{1,0:T(8,128)(2,1)}, bf16[1024,1152]{1,0:T(8,128)(2,1)}) custom-call(bf16[1024,1152]{1,0:T(8,128)(2,1)} %copy-done.18, bf16[1152,1792]{1,0:T(8,128)(2,1)} %bitcast.200, bf16[896,1152]{1,0:T(8,128)(2,1)} %pad.27.down._, bf16[512,1152]{1,0:T(8,128)(2,1)} %copy-done.13), custom_call_target="tpu_custom_call" | custom-call | flops 6341787648 | bytes 10223616 | tf_op jit(solution)/shard_map/pallas_call | solution.py:88
  262.5 8.4 %collective-permute-done.31 = bf16[512,1152]{1,0:T(8,128)(2,1)S(1)} collective-permute-done((bf16[512,1152]{1,0:T(8,128)(2,1)S(1)}, bf16[512,1152]{1,0:T(8,128)(2,1)S(1)}, u32[]{:S(2)}, u32[]{:S(2)}) %collective-permute-start.31) | collective-permute-done | bytes 1179680 | tf_op jit(solution)/shard_map/ppermute | solution.py:51
  282.0 13.5 %shard_map.276 = (bf16[1024,1792]{1,0:T(8,128)(2,1)}, bf16[1024,1152]{1,0:T(8,128)(2,1)}) custom-call(bf16[1024,1152]{1,0:T(8,128)(2,1)} %pad_maximum_fusion.1.grad_mixed.refs_3_, bf16[1024,896]{1,0:T(8,128)(2,1)} %get-tuple-element.108.gelu, bf16[1024,896]{1,0:T(8,128)(2,1)} %get-tuple-element.109.slope, bf16[1152,1792]{1,0:T(8,128)(2,1)} %bitcast.201, ...), custom_call_target="tpu_custom_call" | custom-call | flops 6341787648 | bytes 12058624 | tf_op jit(solution)/shard_map/pallas_call | solution.py:121
  295.4 10.0 %collective-permute-done.34 = bf16[512,1152]{1,0:T(8,128)(2,1)S(1)} collective-permute-done((bf16[512,1152]{1,0:T(8,128)(2,1)S(1)}, bf16[512,1152]{1,0:T(8,128)(2,1)S(1)}, u32[]{:S(2)}, u32[]{:S(2)}) %collective-permute-start.34) | collective-permute-done | bytes 1179680 | tf_op jit(solution)/shard_map/ppermute | solution.py:51
  308.5 13.9 %collective-permute-done.37 = bf16[256,1152]{1,0:T(8,128)(2,1)S(1)} collective-permute-done((bf16[256,1152]{1,0:T(8,128)(2,1)S(1)}, bf16[256,1152]{1,0:T(8,128)(2,1)S(1)}, u32[]{:S(2)}, u32[]{:S(2)}) %collective-permute-start.37) | collective-permute-done | bytes 589856 | tf_op jit(solution)/shard_map/ppermute | solution.py:51
  329.9 16.4 %shard_map.277._ = bf16[864,1152]{1,0:T(8,128)(2,1)} custom-call(bf16[1024,896]{1,0:T(8,128)(2,1)} %get-tuple-element.117.refs_0_, bf16[2048,896]{1,0:T(8,128)(2,1)} %get-tuple-element.118.refs_1_, bf16[1024,896]{1,0:T(8,128)(2,1)} %get-tuple-element.119.refs_2_, bf16[1024,1152]{1,0:T(8,128)(2,1)} %pad_maximum_fusion.1.grad_mixed.refs_3_, ...), custom_call_target="tpu_custom_call" | custom-call | flops 8455716864 | bytes 16777216 | tf_op jit(solution)/shard_map/pallas_call | solution.py:156
  346.3 13.5 %shard_map.278 = (bf16[1024,1792]{1,0:T(8,128)(2,1)}, bf16[1024,1152]{1,0:T(8,128)(2,1)}) custom-call(bf16[1024,1152]{1,0:T(8,128)(2,1)} %copy-done.24, bf16[1024,896]{1,0:T(8,128)(2,1)} %get-tuple-element.115.gelu, bf16[1024,896]{1,0:T(8,128)(2,1)} %get-tuple-element.116.slope, bf16[1152,1792]{1,0:T(8,128)(2,1)} %bitcast.202, ...), custom_call_target="tpu_custom_call" | custom-call | flops 6341787648 | bytes 12058624 | tf_op jit(solution)/shard_map/pallas_call | solution.py:121
  366.4 22.0 %shard_map.279 = (bf16[2048,1792]{1,0:T(8,128)(2,1)}, bf16[2048,1152]{1,0:T(8,128)(2,1)}) custom-call(bf16[2048,1152]{1,0:T(8,128)(2,1)} %copy-done.22, bf16[2048,896]{1,0:T(8,128)(2,1)} %get-tuple-element.113.gelu, bf16[2048,896]{1,0:T(8,128)(2,1)} %get-tuple-element.114.slope, bf16[1152,1792]{1,0:T(8,128)(2,1)} %bitcast.203, ...), custom_call_target="tpu_custom_call" | custom-call | flops 12683575296 | bytes 24117248 | tf_op jit(solution)/shard_map/pallas_call | solution.py:121
  407.8 24.4 %shard_map.280 = bf16[4,2,144,1792]{3,2,1,0:T(8,128)(2,1)} custom-call(bf16[1024,1152]{1,0:T(8,128)(2,1)} %copy-done.18, bf16[2048,1152]{1,0:T(8,128)(2,1)} %copy-done.21, bf16[1024,1152]{1,0:T(8,128)(2,1)} %constant_dynamic-update-slice_fusion.5.normed._.refs_2_, bf16[1024,1792]{1,0:T(8,128)(2,1)} %get-tuple-element.125.refs_3_, ...), custom_call_target="tpu_custom_call" | custom-call | flops 16911433728 | bytes 24117248 | tf_op jit(solution)/shard_map/pallas_call | solution.py:188
  437.4 16.8 %shard_map.281 = (f32[512,1152]{1,0:T(8,128)}, bf16[512,1152]{1,0:T(8,128)(2,1)}, f32[512,1024]{1,0:T(8,128)}, f32[1024,256]{1,0:T(8,128)}, f32[1024,256]{1,0:T(8,128)}, /*index=5*/f32[8,1152]{1,0:T(8,128)}) custom-call(f32[512,1152]{1,0:T(8,128)} %convert_add_fusion.3.grad_normed_mlp, bf16[512,1152]{1,0:T(8,128)(2,1)} %bitcast.193, ...), custom_call_target="tpu_custom_call" | custom-call | flops 6576668672 | bytes 17694720 | tf_op jit(solution)/shard_map/pallas_call | solution.py:505
  461.9 15.1 %shard_map.282 = (f32[512,1152]{1,0:T(8,128)}, bf16[512,512]{1,0:T(8,128)(2,1)}, bf16[1152,896]{1,0:T(8,128)(2,1)}, bf16[1152,896]{1,0:T(8,128)(2,1)}) custom-call(s32[1]{0:T(128)} %bitcast.core, f32[512,1024]{1,0:T(8,128)} %get-tuple-element.132.grad_queries, f32[1024,256]{1,0:T(8,128)} %get-tuple-element.133.grad_keys, ...), custom_call_target="tpu_custom_call" | custom-call | flops 4756340736 | bytes 17694720 | tf_op jit(solution)/shard_map/pallas_call | solution.py:594
  479.4 7.3 %collective-permute-done.53 = bf16[2,2,32,1152]{3,2,1,0:T(8,128)(2,1)S(1)} collective-permute-done((bf16[2,2,32,1152]{3,2,1,0:T(8,128)(2,1)}, bf16[2,2,32,1152]{3,2,1,0:T(8,128)(2,1)S(1)}, u32[]{:S(2)}, u32[]{:S(2)}) %collective-permute-start.53) | collective-permute-done | bytes 294944 | tf_op jit(solution)/shard_map/ppermute | solution.py:51
  492.6 11.4 %collective-permute-done.58 = bf16[2,2,72,896]{3,2,1,0:T(8,128)(2,1)S(1)} collective-permute-done((bf16[2,2,72,896]{3,2,1,0:T(8,128)(2,1)S(1)}, bf16[2,2,72,896]{3,2,1,0:T(8,128)(2,1)S(1)}, u32[]{:S(2)}, u32[]{:S(2)}) %collective-permute-start.58) | collective-permute-done | bytes 516128 | tf_op jit(solution)/shard_map/ppermute | solution.py:51
  544.5 6.5 %shard_map.283 = bf16[512,1152]{1,0:T(8,128)(2,1)} custom-call(s32[1]{0:T(128)} %bitcast.core, bf16[512,512]{1,0:T(8,128)(2,1)} %copy-done.20, f32[512,1152]{1,0:T(8,128)} %get-tuple-element.142.grad_normed, bf16[1152,896]{1,0:T(8,128)(2,1)} %bitcast.192, bf16[1152,896]{1,0:T(8,128)(2,1)} %collective-permute-done.14.other, bf16[512,1152]{1,0:T(8,128)(2,1)} %bitcast.222, ...), custom_call_target="tpu_custom_call" | custom-call | flops 603979776 | bytes 7077888 | tf_op jit(solution)/shard_map/pallas_call | solution.py:631
  (344 shorter events, 224.8 us)
Async XLA Ops:
  7.2 171.1 %all-gather.4.cloned.1.call-start = ((), (), s32[]{:S(2)}) async-start(), calls=%async_computation.3 | async-start | bytes 2488320 | tf_op jit(solution)/shard_map/all_gather | solution.py:747
  24.6 40.7 %collective-permute-start.2 = (bf16[72,896]{1,0:T(8,128)(2,1)S(1)}, bf16[72,896]{1,0:T(8,128)(2,1)S(1)}, u32[]{:S(2)}, u32[]{:S(2)}) collective-permute-start(bf16[72,896]{1,0:T(8,128)(2,1)S(1)} %reshape.140), channel_id=1, source_target_pairs={{4,0},{8,4},{12,8},{0,12},{5,1},{9,5},{13,9},{1,13},{6,2},{10,6},{... | collective-permute-start | bytes 387080 | tf_op jit(solution)/shard_map/ppermute | solution.py:242
  25.1 40.2 %collective-permute-start.3 = (bf16[72,896]{1,0:T(8,128)(2,1)S(1)}, bf16[72,896]{1,0:T(8,128)(2,1)S(1)}, u32[]{:S(2)}, u32[]{:S(2)}) collective-permute-start(bf16[72,896]{1,0:T(8,128)(2,1)S(1)} %reshape.140), channel_id=1, source_target_pairs={{8,0},{12,4},{0,8},{4,12},{9,1},{13,5},{1,9},{5,13},{10,2},{14,6},... | collective-permute-start | bytes 387080 | tf_op jit(solution)/shard_map/ppermute | solution.py:242
  27.5 37.8 %collective-permute-start.4 = (bf16[72,896]{1,0:T(8,128)(2,1)S(1)}, bf16[72,896]{1,0:T(8,128)(2,1)S(1)}, u32[]{:S(2)}, u32[]{:S(2)}) collective-permute-start(bf16[72,896]{1,0:T(8,128)(2,1)S(1)} %reshape.140), channel_id=1, source_target_pairs={{12,0},{0,4},{4,8},{8,12},{13,1},{1,5},{5,9},{9,13},{14,2},{2,6},{... | collective-permute-start | bytes 387080 | tf_op jit(solution)/shard_map/ppermute | solution.py:242
  27.5 31.4 %collective-permute-start.7 = (bf16[32,1152]{1,0:T(8,128)(2,1)S(1)}, bf16[32,1152]{1,0:T(8,128)(2,1)S(1)}, u32[]{:S(2)}, u32[]{:S(2)}) collective-permute-start(bf16[32,1152]{1,0:T(8,128)(2,1)S(1)} %copy-done.23), channel_id=1, source_target_pairs={{4,0},{8,4},{12,8},{0,12},{5,1},{9,5},{13,9},{1,13},{6,2},{10,6},{... | collective-permute-start | bytes 221192 | tf_op jit(solution)/shard_map/ppermute | solution.py:242
  29.0 31.0 %collective-permute-start.8 = (bf16[32,1152]{1,0:T(8,128)(2,1)S(1)}, bf16[32,1152]{1,0:T(8,128)(2,1)S(1)}, u32[]{:S(2)}, u32[]{:S(2)}) collective-permute-start(bf16[32,1152]{1,0:T(8,128)(2,1)S(1)} %copy-done.23), channel_id=1, source_target_pairs={{8,0},{12,4},{0,8},{4,12},{9,1},{13,5},{1,9},{5,13},{10,2},{14,6},... | collective-permute-start | bytes 221192 | tf_op jit(solution)/shard_map/ppermute | solution.py:242
  30.9 34.6 %all-to-all-start = ((bf16[8,36,1792]{2,1,0:T(8,128)(2,1)}), bf16[8,36,1792]{2,1,0:T(8,128)(2,1)S(1)}, u32[]{:S(2)}, u32[]{:S(2)}) async-start(bf16[8,36,1792]{2,1,0:T(8,128)(2,1)} %copy.70), calls=%async_computation | async-start | bytes 2293760 | tf_op jit(solution)/shard_map/all_to_all | solution.py:736
  39.4 143.8 %all-gather.6.cloned.1.call-start = ((), (), s32[]{:S(2)}) async-start(), calls=%async_computation.5 | async-start | bytes 5160960 | tf_op jit(solution)/shard_map/all_gather | solution.py:750
  96.6 418.0 %reduce-scatter.2.cloned.1.call-start = ((), (), s32[]{:S(2)}) async-start(), calls=%async_computation.4 | async-start | bytes 5160960 | tf_op jit(solution)/shard_map/reduce_scatter | solution.py:816
  130.8 27.4 %collective-permute-start.19 = (bf16[512,1152]{1,0:T(8,128)(2,1)}, bf16[512,1152]{1,0:T(8,128)(2,1)S(1)}, u32[]{:S(2)}, u32[]{:S(2)}) collective-permute-start(bf16[512,1152]{1,0:T(8,128)(2,1)} %get-tuple-element.100), channel_id=1, source_target_pairs={{0,16},{16,0},{1,17},{17,1},{2,18},{18,2},{3,19},{19,3},{4,20},{20... | collective-permute-start | bytes 3538952 | tf_op jit(solution)/shard_map/ppermute | solution.py:51
  131.5 28.0 %collective-permute-start.20 = (bf16[512,1152]{1,0:T(8,128)(2,1)}, bf16[512,1152]{1,0:T(8,128)(2,1)S(1)}, u32[]{:S(2)}, u32[]{:S(2)}) collective-permute-start(bf16[512,1152]{1,0:T(8,128)(2,1)} %get-tuple-element.100), channel_id=1, source_target_pairs={{0,2},{2,0},{1,3},{3,1},{4,6},{6,4},{5,7},{7,5},{8,10},{10,8},{9,1... | collective-permute-start | bytes 3538952 | tf_op jit(solution)/shard_map/ppermute | solution.py:51
  178.3 27.0 %collective-permute-start.21 = (bf16[1024,1152]{1,0:T(8,128)(2,1)}, bf16[1024,1152]{1,0:T(8,128)(2,1)}, u32[]{:S(2)}, u32[]{:S(2)}) collective-permute-start(bf16[1024,1152]{1,0:T(8,128)(2,1)} %pad_maximum_fusion), channel_id=1, source_target_pairs={{0,1},{1,0},{2,3},{3,2},{4,5},{5,4},{6,7},{7,6},{8,9},{9,8},{10,11... | collective-permute-start | bytes 7077896 | tf_op jit(solution)/shard_map/ppermute | solution.py:51
  243.7 27.2 %collective-permute-start.31 = (bf16[512,1152]{1,0:T(8,128)(2,1)S(1)}, bf16[512,1152]{1,0:T(8,128)(2,1)S(1)}, u32[]{:S(2)}, u32[]{:S(2)}) collective-permute-start(bf16[512,1152]{1,0:T(8,128)(2,1)S(1)} %pad_maximum_fusion.7), channel_id=1, source_target_pairs={{0,2},{2,0},{1,3},{3,1},{4,6},{6,4},{5,7},{7,5},{8,10},{10,8},{9,1... | collective-permute-start | bytes 3538952 | tf_op jit(solution)/shard_map/ppermute | solution.py:51
  245.0 26.9 %collective-permute-start.30 = (bf16[512,1152]{1,0:T(8,128)(2,1)S(1)}, bf16[512,1152]{1,0:T(8,128)(2,1)S(1)}, u32[]{:S(2)}, u32[]{:S(2)}) collective-permute-start(bf16[512,1152]{1,0:T(8,128)(2,1)S(1)} %pad_maximum_fusion.6._), channel_id=1, source_target_pairs={{0,16},{16,0},{1,17},{17,1},{2,18},{18,2},{3,19},{19,3},{4,20},{20... | collective-permute-start | bytes 3538952 | tf_op jit(solution)/shard_map/ppermute | solution.py:51
  277.9 27.6 %collective-permute-start.34 = (bf16[512,1152]{1,0:T(8,128)(2,1)S(1)}, bf16[512,1152]{1,0:T(8,128)(2,1)S(1)}, u32[]{:S(2)}, u32[]{:S(2)}) collective-permute-start(bf16[512,1152]{1,0:T(8,128)(2,1)S(1)} %get-tuple-element.169), channel_id=1, source_target_pairs={{0,16},{16,0},{1,17},{17,1},{2,18},{18,2},{3,19},{19,3},{4,20},{20... | collective-permute-start | bytes 3538952 | tf_op jit(solution)/shard_map/ppermute | solution.py:51
  278.6 27.3 %collective-permute-start.35 = (bf16[512,1152]{1,0:T(8,128)(2,1)S(1)}, bf16[512,1152]{1,0:T(8,128)(2,1)S(1)}, u32[]{:S(2)}, u32[]{:S(2)}) collective-permute-start(bf16[512,1152]{1,0:T(8,128)(2,1)S(1)} %get-tuple-element.169), channel_id=1, source_target_pairs={{0,2},{2,0},{1,3},{3,1},{4,6},{6,4},{5,7},{7,5},{8,10},{10,8},{9,1... | collective-permute-start | bytes 3538952 | tf_op jit(solution)/shard_map/ppermute | solution.py:51
  364.6 23.9 %collective-permute-start.41 = (bf16[256,1152]{1,0:T(8,128)(2,1)S(1)}, bf16[256,1152]{1,0:T(8,128)(2,1)S(1)}, u32[]{:S(2)}, u32[]{:S(2)}) collective-permute-start(bf16[256,1152]{1,0:T(8,128)(2,1)S(1)} %get-tuple-element.185), channel_id=1, source_target_pairs={{0,2},{2,0},{1,3},{3,1},{4,6},{6,4},{5,7},{7,5},{8,10},{10,8},{9,1... | collective-permute-start | bytes 1769480 | tf_op jit(solution)/shard_map/ppermute | solution.py:51
  394.3 37.9 %collective-permute-start.33 = (bf16[512,1152]{1,0:T(8,128)(2,1)}, bf16[512,1152]{1,0:T(8,128)(2,1)S(1)}, u32[]{:S(2)}, u32[]{:S(2)}) collective-permute-start(bf16[512,1152]{1,0:T(8,128)(2,1)} %slice.188), channel_id=1, source_target_pairs={{0,1},{1,0},{2,3},{3,2},{4,5},{5,4},{6,7},{7,6},{8,9},{9,8},{10,11... | collective-permute-start | bytes 3538952 | tf_op jit(solution)/shard_map/ppermute | solution.py:51
  397.5 61.8 %collective-permute-start.48 = (bf16[216,1152]{1,0:T(8,128)(2,1)}, bf16[216,1152]{1,0:T(8,128)(2,1)}, u32[]{:S(2)}, u32[]{:S(2)}) collective-permute-start(bf16[216,1152]{1,0:T(8,128)(2,1)} %get-tuple-element.180), channel_id=1, source_target_pairs={{0,12},{4,0},{8,4},{12,8},{1,13},{5,1},{9,5},{13,9},{2,14},{6,2},{... | collective-permute-start | bytes 1493000 | tf_op jit(solution)/shard_map/ppermute | solution.py:272
  397.5 61.8 %collective-permute-start.47 = (bf16[216,1152]{1,0:T(8,128)(2,1)}, bf16[216,1152]{1,0:T(8,128)(2,1)}, u32[]{:S(2)}, u32[]{:S(2)}) collective-permute-start(bf16[216,1152]{1,0:T(8,128)(2,1)} %get-tuple-element.181), channel_id=1, source_target_pairs={{0,8},{4,12},{8,0},{12,4},{1,9},{5,13},{9,1},{13,5},{2,10},{6,14},... | collective-permute-start | bytes 1493000 | tf_op jit(solution)/shard_map/ppermute | solution.py:272
  404.7 27.9 %collective-permute-start.45 = (bf16[512,1152]{1,0:T(8,128)(2,1)}, bf16[512,1152]{1,0:T(8,128)(2,1)}, u32[]{:S(2)}, u32[]{:S(2)}) collective-permute-start(bf16[512,1152]{1,0:T(8,128)(2,1)} %pad_maximum_fusion.10), channel_id=1, source_target_pairs={{0,2},{2,0},{1,3},{3,1},{4,6},{6,4},{5,7},{7,5},{8,10},{10,8},{9,1... | collective-permute-start | bytes 3538952 | tf_op jit(solution)/shard_map/ppermute | solution.py:51
  406.8 26.9 %collective-permute-start.44 = (bf16[512,1152]{1,0:T(8,128)(2,1)}, bf16[512,1152]{1,0:T(8,128)(2,1)}, u32[]{:S(2)}, u32[]{:S(2)}) collective-permute-start(bf16[512,1152]{1,0:T(8,128)(2,1)} %pad_maximum_fusion.9.refs_6_), channel_id=1, source_target_pairs={{0,16},{16,0},{1,17},{17,1},{2,18},{18,2},{3,19},{19,3},{4,20},{20... | collective-permute-start | bytes 3538952 | tf_op jit(solution)/shard_map/ppermute | solution.py:51
  432.2 27.1 %collective-permute-start.46 = (bf16[216,1152]{1,0:T(8,128)(2,1)}, bf16[216,1152]{1,0:T(8,128)(2,1)}, u32[]{:S(2)}, u32[]{:S(2)}) collective-permute-start(bf16[216,1152]{1,0:T(8,128)(2,1)} %get-tuple-element.179), channel_id=1, source_target_pairs={{0,4},{4,8},{8,12},{12,0},{1,5},{5,9},{9,13},{13,1},{2,6},{6,10},{... | collective-permute-start | bytes 1493000 | tf_op jit(solution)/shard_map/ppermute | solution.py:272
  524.2 31.0 %all-to-all-start.1 = ((bf16[8,36,1792]{2,1,0:T(8,128)(2,1)}), bf16[8,36,1792]{2,1,0:T(8,128)(2,1)S(1)}, u32[]{:S(2)}, u32[]{:S(2)}) async-start(bf16[8,36,1792]{2,1,0:T(8,128)(2,1)} %reshape.156), calls=%async_computation.2 | async-start | bytes 2293760 | tf_op jit(solution)/shard_map/all_to_all | solution.py:818
  (73 other events, 680.6 us)
Sparse Core Ops, SparseCore 0:
  15.1 58.6 all-gather.3
  96.7 77.2 all-gather.5
  432.3 82.2 reduce-scatter.1

commit v10 on v9

--- a/solution.py
+++ b/solution.py
@@ -246,17 +246,18 @@
     return lax.dynamic_slice_in_dim(both, lax.rem(size - place, size), size, 0)
 
 
-def plane_near(blocks):
+def plane_start(blocks):
     half = blocks.shape[0] // 2
-    first, second = blocks[:half], blocks[half:]
-    first = in_order(first, swap(first, "x"), lax.axis_index("x"))
-    second = in_order(second, swap(second, "y"), lax.axis_index("y"))
-    return first, second
-
-
-def plane_far(first, second):
-    first = in_order(first, swap(first, "y"), lax.axis_index("y"))
-    second = in_order(second, swap(second, "x"), lax.axis_index("x"))
+    return swap(blocks[:half], "x"), swap(blocks[half:], "y")
+
+
+def plane_weights(blocks, from_x, from_y):
+    x, y = lax.axis_index("x"), lax.axis_index("y")
+    half = blocks.shape[0] // 2
+    first = in_order(blocks[:half], from_x, x)
+    second = in_order(blocks[half:], from_y, y)
+    first = in_order(first, swap(first, "y"), y)
+    second = in_order(second, swap(second, "x"), x)
     first = first.transpose(1, 2, 0, 3, 4)
     second = second.transpose(0, 2, 1, 3, 4)
     return jnp.concatenate([first, second], axis=1)
@@ -735,16 +736,13 @@
     mine, before, sent = lax.optimization_barrier((mine, before, sent))
     sent = lax.all_to_all(sent, PLANE, split_axis=0, concat_axis=0, tiled=True)
     sent = sent.reshape(members * shard_rows, 2 * hidden_pad)
-    w_o = group_gather(after(w_out, mine))
     mine, sent = lax.optimization_barrier((group_gather(mine), sent))
-    near, w_o = lax.optimization_barrier((plane_near(mine), w_o))
-    w_o = plane_near(w_o)
-    mine, w_o = lax.optimization_barrier((plane_far(*near), w_o))
-    mine = mine.reshape(width, half_cols)
-    w_o = plane_far(*w_o)
+    mine = plane_weights(mine, *plane_start(mine)).reshape(width, half_cols)
     other = swap(mine, "c")
 
-    down = lax.all_gather(w_down, "g", axis=0, tiled=True)
+    down = lax.all_gather(jnp.concatenate([w_down, w_out]), "g", axis=0)
+    w_o = down[:, w_down.shape[0] :]
+    down = down[:, : w_down.shape[0]].reshape(-1, width)
     down = jnp.pad(down, ((0, hidden_pad - hidden_own), (0, 0)))
 
     both = lax.all_gather(sent, "g", axis=0)
@@ -767,7 +765,7 @@
     normed, normed_before, query_raw, key_raw, queries, keys, values, d_gains, h_gains = project(
         places, layer_in, before, mine, other, cosine_table, sine_table, shard_rows, q_cols, k_cols
     )
-    w_o = after(w_o, keys)
+    w_o = plane_weights(*lax.optimization_barrier((w_o, *plane_start(w_o), keys))[:3])
     w_o = in_order(w_o, swap(w_o, "c"), core).transpose(1, 2, 3, 0, 4, 5).reshape(q_cols, width)
     attended, log_total, branch, middle, normed_mlp = attend(
         queries, keys, values, query_ids, key_ids, w_o, layer_in, d_gains, attn_scale
@@ -814,8 +812,8 @@
     grad_normed_mlp = after(grad_normed_mlp, gate_up_terms)
     term = gate_up_terms.reshape(groups * members * shard_rows, 2 * hidden_pad)
     gate_up_share = lax.psum_scatter(term, "g", scatter_dimension=0, tiled=True)
-    gate_up_share = gate_up_share.reshape(members, shard_rows, 2 * hidden_pad)
-    term = lax.all_to_all(gate_up_share, PLANE, split_axis=0, concat_axis=0, tiled=True)
+    term = gate_up_share.reshape(members, shard_rows, 2 * hidden_pad)
+    term = lax.all_to_all(term, PLANE, split_axis=0, concat_axis=0, tiled=True)
 
     grad_w_gate, grad_w_up = owner_rows(term, groups, piece)
 

time: 574 us -> 559 us (0.974)
  waiting for transfers between devices: 171 us -> 161 us
    ppermute x6 -> x3, waiting for transfers between devices: 25.8 us -> 11.7 us  [group_gather(): lax.ppermute(own, 'g', [((i + k) % size, i) for i in range(size)])]
    unnamed x78 -> x74, local copies, waits for them, and re-layouts: 13.1 us -> 13.6 us
  transfers between devices with their start and end apart: 69 -> 66, of which waited for: 32 -> 30; matrix products, arithmetic and copies ran while one was open for 14% -> 15% of each run, Pallas kernels for 29% -> 30%
where the time goes in v10:
time: 559 us; the launch traced here: 551 us
  Pallas kernels  198 us (35%)
  waiting for transfers between devices  161 us (29%)
  starting transfers between devices  72.5 us (13%)
  local copies, waits for them, and re-layouts  61 us (11%)
  other arithmetic  40.6 us (7%)
  between operations  15.1 us (3%)
    ppermute x50, waiting for transfers between devices, swap(): return lax.ppermute(array, axis, [(0, 1), (1, 0)])  127 us
    pallas_call x3, Pallas kernels, mlp_backward(): pl.pallas_call(mlp_backward_kernel, grid=(rows // TILE,), in_specs=[row_b...  48.9 us
    pallas_call x3, Pallas kernels, mlp_forward(): pl.pallas_call(mlp_forward_kernel, grid=(rows // TILE,), in_specs=[row_bl...  48.1 us
    ppermute x50, starting transfers between devices, swap(): return lax.ppermute(array, axis, [(0, 1), (1, 0)])  42.3 us
    pallas_call x1, Pallas kernels, gate_terms(): pl.pallas_call(gate_terms_kernel, grid=(both // 256,), in_specs=[whole_bl...  24.4 us
    pallas_call x1, Pallas kernels, attend_backward(): pl.pallas_call(functools.partial(attend_backward_kernel, scale), in_specs...  17.1 us
    pallas_call x1, Pallas kernels, down_terms(): pl.pallas_call(down_terms_kernel, grid=(own // 128,), in_specs=[pl.BlockS...  16.4 us
    pallas_call x1, Pallas kernels, project_backward(): pl.pallas_call(functools.partial(project_backward_kernel, shard_rows), in...  15.1 us
  transfers between devices with their start and end apart: 66, of which 30 were waited for; matrix products, arithmetic and copies ran while one was open for 15% of the time, Pallas kernels for 30%

profile of v10, /device:TPU:13, one launch (start us, length us, event | category | flops | bytes accessed | tf_op | source)
XLA Modules:
  0.0 551.1 jit_solution(15143110373807423910)
XLA Ops:
  28.2 8.9 %all-to-all-start = ((bf16[8,36,1792]{2,1,0:T(8,128)(2,1)}), bf16[8,36,1792]{2,1,0:T(8,128)(2,1)S(1)}, u32[]{:S(2)}, u32[]{:S(2)}) async-start(bf16[8,36,1792]{2,1,0:T(8,128)(2,1)} %copy.71), calls=%async_computation | async-start | bytes 2293760 | tf_op jit(solution)/shard_map/all_to_all | solution.py:737
  39.5 9.3 %collective-permute-done.4 = bf16[72,896]{1,0:T(8,128)(2,1)S(1)} collective-permute-done((bf16[72,896]{1,0:T(8,128)(2,1)S(1)}, bf16[72,896]{1,0:T(8,128)(2,1)S(1)}, u32[]{:S(2)}, u32[]{:S(2)}) %collective-permute-start.4) | collective-permute-done | bytes 129056 | tf_op jit(solution)/shard_map/ppermute | solution.py:242
  62.0 10.1 %collective-permute-done.8 = bf16[2,2,72,896]{3,2,1,0:T(8,128)(2,1)S(1)} collective-permute-done((bf16[2,2,72,896]{3,2,1,0:T(8,128)(2,1)S(1)}, bf16[2,2,72,896]{3,2,1,0:T(8,128)(2,1)S(1)}, u32[]{:S(2)}, u32[]{:S(2)}) %collective-permute-start.8) | collective-permute-done | bytes 516128 | tf_op jit(solution)/shard_map/ppermute | solution.py:51
  83.1 8.8 %shard_map.271 = (bf16[512,1152]{1,0:T(8,128)(2,1)}, bf16[512,1152]{1,0:T(8,128)(2,1)}, f32[512,1024]{1,0:T(8,128)}, f32[1024,256]{1,0:T(8,128)}, bf16[512,1024]...) custom-call(s32[1]{0:T(128)} %bitcast.core, ...), custom_call_target="tpu_custom_call" | custom-call | flops 2415919104 | bytes 9437184 | tf_op jit(solution)/shard_map/pallas_call | solution.py:370
  108.0 9.7 %shard_map.272 = (bf16[512,1024]{1,0:T(8,128)(2,1)}, f32[512,128]{1,0:T(8,128)}, f32[512,1152]{1,0:T(8,128)}, f32[512,1152]{1,0:T(8,128)}, bf16[512,1152]{1,0:T(8,128)(2,1)}) custom-call(bf16[512,1024]{1,0:T(8,128)(2,1)} %get-tuple-element.82.queries, bf16[1024,256]{1,0:T(8,128)(2,1)} %get-tuple-element.83.keys, bf16[1024,256]{1,0:T(8,128)(2,1)} %get-tuple-element.84.values, ...), custom_call_target="tpu_custom_call" | custom-call | flops 3355443200 | bytes 11796480 | tf_op jit(solution)/shard_map/pallas_call | solution.py:436
  120.5 24.6 %collective-permute-done.16 = bf16[512,1152]{1,0:T(8,128)(2,1)S(1)} collective-permute-done((bf16[512,1152]{1,0:T(8,128)(2,1)}, bf16[512,1152]{1,0:T(8,128)(2,1)S(1)}, u32[]{:S(2)}, u32[]{:S(2)}) %collective-permute-start.16) | collective-permute-done | bytes 1179680 | tf_op jit(solution)/shard_map/ppermute | solution.py:51
  148.3 10.5 %collective-permute-done.19 = bf16[256,1152]{1,0:T(8,128)(2,1)S(1)} collective-permute-done((bf16[256,1152]{1,0:T(8,128)(2,1)S(1)}, bf16[256,1152]{1,0:T(8,128)(2,1)S(1)}, u32[]{:S(2)}, u32[]{:S(2)}) %collective-permute-start.19) | collective-permute-done | bytes 589856 | tf_op jit(solution)/shard_map/ppermute | solution.py:51
  174.5 12.9 %shard_map.273 = (bf16[1024,896]{1,0:T(8,128)(2,1)}, bf16[1024,896]{1,0:T(8,128)(2,1)}, bf16[1024,896]{1,0:T(8,128)(2,1)}, bf16[1024,1152]{1,0:T(8,128)(2,1)}) custom-call(bf16[1024,1152]{1,0:T(8,128)(2,1)} %constant_dynamic-update-slice_fusion.5.normed._.refs_2_, bf16[1152,1792]{1,0:T(8,128)(2,1)} %bitcast.196, bf16[896,1152]{1,0:T(8,128)(2,1)} %pad.27.down._, ...), custom_call_target="tpu_custom_call" | custom-call | flops 6341787648 | bytes 10223616 | tf_op jit(solution)/shard_map/pallas_call | solution.py:88
  195.8 21.8 %shard_map.274 = (bf16[2048,896]{1,0:T(8,128)(2,1)}, bf16[2048,896]{1,0:T(8,128)(2,1)}, bf16[2048,896]{1,0:T(8,128)(2,1)}, bf16[2048,1152]{1,0:T(8,128)(2,1)}) custom-call(bf16[2048,1152]{1,0:T(8,128)(2,1)} %copy-done.23, bf16[1152,1792]{1,0:T(8,128)(2,1)} %bitcast.197, bf16[896,1152]{1,0:T(8,128)(2,1)} %pad.27.down._, bf16[512,1152]{1,0:T(8,128)(2,1)} %copy-done.3), custom_call_target="tpu_custom_call" | custom-call | flops 12683575296 | bytes 20447232 | tf_op jit(solution)/shard_map/pallas_call | solution.py:88
  231.3 13.4 %shard_map.275 = (bf16[1024,896]{1,0:T(8,128)(2,1)}, bf16[1024,896]{1,0:T(8,128)(2,1)}, bf16[1024,896]{1,0:T(8,128)(2,1)}, bf16[1024,1152]{1,0:T(8,128)(2,1)}) custom-call(bf16[1024,1152]{1,0:T(8,128)(2,1)} %copy-done.19, bf16[1152,1792]{1,0:T(8,128)(2,1)} %bitcast.198, bf16[896,1152]{1,0:T(8,128)(2,1)} %pad.27.down._, bf16[512,1152]{1,0:T(8,128)(2,1)} %copy-done.14), custom_call_target="tpu_custom_call" | custom-call | flops 6341787648 | bytes 10223616 | tf_op jit(solution)/shard_map/pallas_call | solution.py:88
  247.7 8.2 %collective-permute-done.28 = bf16[512,1152]{1,0:T(8,128)(2,1)S(1)} collective-permute-done((bf16[512,1152]{1,0:T(8,128)(2,1)S(1)}, bf16[512,1152]{1,0:T(8,128)(2,1)S(1)}, u32[]{:S(2)}, u32[]{:S(2)}) %collective-permute-start.28) | collective-permute-done | bytes 1179680 | tf_op jit(solution)/shard_map/ppermute | solution.py:51
  267.4 13.5 %shard_map.276 = (bf16[1024,1792]{1,0:T(8,128)(2,1)}, bf16[1024,1152]{1,0:T(8,128)(2,1)}) custom-call(bf16[1024,1152]{1,0:T(8,128)(2,1)} %pad_maximum_fusion.1.grad_mixed.refs_3_, bf16[1024,896]{1,0:T(8,128)(2,1)} %get-tuple-element.98.gelu, bf16[1024,896]{1,0:T(8,128)(2,1)} %get-tuple-element.99.slope, bf16[1152,1792]{1,0:T(8,128)(2,1)} %bitcast.199, ...), custom_call_target="tpu_custom_call" | custom-call | flops 6341787648 | bytes 12058624 | tf_op jit(solution)/shard_map/pallas_call | solution.py:121
  280.8 10.0 %collective-permute-done.31 = bf16[512,1152]{1,0:T(8,128)(2,1)S(1)} collective-permute-done((bf16[512,1152]{1,0:T(8,128)(2,1)S(1)}, bf16[512,1152]{1,0:T(8,128)(2,1)S(1)}, u32[]{:S(2)}, u32[]{:S(2)}) %collective-permute-start.31) | collective-permute-done | bytes 1179680 | tf_op jit(solution)/shard_map/ppermute | solution.py:51
  293.6 13.5 %collective-permute-done.34 = bf16[256,1152]{1,0:T(8,128)(2,1)S(1)} collective-permute-done((bf16[256,1152]{1,0:T(8,128)(2,1)S(1)}, bf16[256,1152]{1,0:T(8,128)(2,1)S(1)}, u32[]{:S(2)}, u32[]{:S(2)}) %collective-permute-start.34) | collective-permute-done | bytes 589856 | tf_op jit(solution)/shard_map/ppermute | solution.py:51
  315.3 16.4 %shard_map.277._ = bf16[864,1152]{1,0:T(8,128)(2,1)} custom-call(bf16[1024,896]{1,0:T(8,128)(2,1)} %get-tuple-element.107.refs_0_, bf16[2048,896]{1,0:T(8,128)(2,1)} %get-tuple-element.108.refs_1_, bf16[1024,896]{1,0:T(8,128)(2,1)} %get-tuple-element.109.refs_2_, bf16[1024,1152]{1,0:T(8,128)(2,1)} %pad_maximum_fusion.1.grad_mixed.refs_3_, ...), custom_call_target="tpu_custom_call" | custom-call | flops 8455716864 | bytes 16777216 | tf_op jit(solution)/shard_map/pallas_call | solution.py:156
  331.7 13.5 %shard_map.278 = (bf16[1024,1792]{1,0:T(8,128)(2,1)}, bf16[1024,1152]{1,0:T(8,128)(2,1)}) custom-call(bf16[1024,1152]{1,0:T(8,128)(2,1)} %copy-done.25, bf16[1024,896]{1,0:T(8,128)(2,1)} %get-tuple-element.105.gelu, bf16[1024,896]{1,0:T(8,128)(2,1)} %get-tuple-element.106.slope, bf16[1152,1792]{1,0:T(8,128)(2,1)} %bitcast.200, ...), custom_call_target="tpu_custom_call" | custom-call | flops 6341787648 | bytes 12058624 | tf_op jit(solution)/shard_map/pallas_call | solution.py:121
  351.8 22.0 %shard_map.279 = (bf16[2048,1792]{1,0:T(8,128)(2,1)}, bf16[2048,1152]{1,0:T(8,128)(2,1)}) custom-call(bf16[2048,1152]{1,0:T(8,128)(2,1)} %copy-done.24, bf16[2048,896]{1,0:T(8,128)(2,1)} %get-tuple-element.103.gelu, bf16[2048,896]{1,0:T(8,128)(2,1)} %get-tuple-element.104.slope, bf16[1152,1792]{1,0:T(8,128)(2,1)} %bitcast.201, ...), custom_call_target="tpu_custom_call" | custom-call | flops 12683575296 | bytes 24117248 | tf_op jit(solution)/shard_map/pallas_call | solution.py:121
  391.9 24.4 %shard_map.280 = bf16[4,2,144,1792]{3,2,1,0:T(8,128)(2,1)} custom-call(bf16[1024,1152]{1,0:T(8,128)(2,1)} %copy-done.19, bf16[2048,1152]{1,0:T(8,128)(2,1)} %copy-done.23, bf16[1024,1152]{1,0:T(8,128)(2,1)} %constant_dynamic-update-slice_fusion.5.normed._.refs_2_, bf16[1024,1792]{1,0:T(8,128)(2,1)} %get-tuple-element.115.refs_3_, ...), custom_call_target="tpu_custom_call" | custom-call | flops 16911433728 | bytes 24117248 | tf_op jit(solution)/shard_map/pallas_call | solution.py:188
  421.8 17.1 %shard_map.281 = (f32[512,1152]{1,0:T(8,128)}, bf16[512,1152]{1,0:T(8,128)(2,1)}, f32[512,1024]{1,0:T(8,128)}, f32[1024,256]{1,0:T(8,128)}, f32[1024,256]{1,0:T(8,128)}, /*index=5*/f32[8,1152]{1,0:T(8,128)}) custom-call(f32[512,1152]{1,0:T(8,128)} %convert_add_fusion.3.grad_normed_mlp, bf16[512,1152]{1,0:T(8,128)(2,1)} %bitcast.192, ...), custom_call_target="tpu_custom_call" | custom-call | flops 6576668672 | bytes 17694720 | tf_op jit(solution)/shard_map/pallas_call | solution.py:506
  446.5 15.1 %shard_map.282 = (f32[512,1152]{1,0:T(8,128)}, bf16[512,512]{1,0:T(8,128)(2,1)}, bf16[1152,896]{1,0:T(8,128)(2,1)}, bf16[1152,896]{1,0:T(8,128)(2,1)}) custom-call(s32[1]{0:T(128)} %bitcast.core, f32[512,1024]{1,0:T(8,128)} %get-tuple-element.122.grad_queries, f32[1024,256]{1,0:T(8,128)} %get-tuple-element.123.grad_keys, ...), custom_call_target="tpu_custom_call" | custom-call | flops 4756340736 | bytes 17694720 | tf_op jit(solution)/shard_map/pallas_call | solution.py:595
  464.7 6.5 %collective-permute-done.50 = bf16[2,2,32,1152]{3,2,1,0:T(8,128)(2,1)S(1)} collective-permute-done((bf16[2,2,32,1152]{3,2,1,0:T(8,128)(2,1)}, bf16[2,2,32,1152]{3,2,1,0:T(8,128)(2,1)S(1)}, u32[]{:S(2)}, u32[]{:S(2)}) %collective-permute-start.50) | collective-permute-done | bytes 294944 | tf_op jit(solution)/shard_map/ppermute | solution.py:51
  477.2 10.5 %collective-permute-done.55 = bf16[2,2,72,896]{3,2,1,0:T(8,128)(2,1)S(1)} collective-permute-done((bf16[2,2,72,896]{3,2,1,0:T(8,128)(2,1)S(1)}, bf16[2,2,72,896]{3,2,1,0:T(8,128)(2,1)S(1)}, u32[]{:S(2)}, u32[]{:S(2)}) %collective-permute-start.55) | collective-permute-done | bytes 516128 | tf_op jit(solution)/shard_map/ppermute | solution.py:51
  521.2 7.7 %collective-permute-done.46.returned = bf16[512,512]{1,0:T(8,128)(2,1)S(1)} collective-permute-done((bf16[512,512]{1,0:T(8,128)(2,1)}, bf16[512,512]{1,0:T(8,128)(2,1)S(1)}, u32[]{:S(2)}, u32[]{:S(2)}) %collective-permute-start.46) | collective-permute-done | bytes 524320 | tf_op jit(solution)/shard_map/ppermute | solution.py:833
  529.7 6.5 %shard_map.283 = bf16[512,1152]{1,0:T(8,128)(2,1)} custom-call(s32[1]{0:T(128)} %bitcast.core, bf16[512,512]{1,0:T(8,128)(2,1)} %copy-done.22, f32[512,1152]{1,0:T(8,128)} %get-tuple-element.132.grad_normed, bf16[1152,896]{1,0:T(8,128)(2,1)} %bitcast.190, bf16[1152,896]{1,0:T(8,128)(2,1)} %collective-permute-done.9.other, bf16[512,1152]{1,0:T(8,128)(2,1)} %bitcast.219, ...), custom_call_target="tpu_custom_call" | custom-call | flops 603979776 | bytes 7077888 | tf_op jit(solution)/shard_map/pallas_call | solution.py:632
  (338 shorter events, 221.1 us)
Async XLA Ops:
  7.2 72.6 %all-gather.5.cloned.1.call-start = ((), (), s32[]{:S(2)}) async-start(), calls=%async_computation.4 | async-start | bytes 2856960 | tf_op jit(solution)/shard_map/all_gather | solution.py:743
  27.0 21.8 %collective-permute-start.4 = (bf16[72,896]{1,0:T(8,128)(2,1)S(1)}, bf16[72,896]{1,0:T(8,128)(2,1)S(1)}, u32[]{:S(2)}, u32[]{:S(2)}) collective-permute-start(bf16[72,896]{1,0:T(8,128)(2,1)S(1)} %reshape.143), channel_id=1, source_target_pairs={{12,0},{0,4},{4,8},{8,12},{13,1},{1,5},{5,9},{9,13},{14,2},{2,6},{... | collective-permute-start | bytes 387080 | tf_op jit(solution)/shard_map/ppermute | solution.py:242
  28.2 23.5 %all-to-all-start = ((bf16[8,36,1792]{2,1,0:T(8,128)(2,1)}), bf16[8,36,1792]{2,1,0:T(8,128)(2,1)S(1)}, u32[]{:S(2)}, u32[]{:S(2)}) async-start(bf16[8,36,1792]{2,1,0:T(8,128)(2,1)} %copy.71), calls=%async_computation | async-start | bytes 2293760 | tf_op jit(solution)/shard_map/all_to_all | solution.py:737
  37.1 131.8 %all-gather.7.cloned.1.call-start = ((), (), s32[]{:S(2)}) async-start(), calls=%async_computation.5 | async-start | bytes 5160960 | tf_op jit(solution)/shard_map/all_gather | solution.py:748
  79.2 420.3 %reduce-scatter.2.cloned.1.call-start = ((), (), s32[]{:S(2)}) async-start(), calls=%async_computation.3 | async-start | bytes 5160960 | tf_op jit(solution)/shard_map/reduce_scatter | solution.py:814
  117.7 27.4 %collective-permute-start.16 = (bf16[512,1152]{1,0:T(8,128)(2,1)}, bf16[512,1152]{1,0:T(8,128)(2,1)S(1)}, u32[]{:S(2)}, u32[]{:S(2)}) collective-permute-start(bf16[512,1152]{1,0:T(8,128)(2,1)} %get-tuple-element.90), channel_id=1, source_target_pairs={{0,16},{16,0},{1,17},{17,1},{2,18},{18,2},{3,19},{19,3},{4,20},{20... | collective-permute-start | bytes 3538952 | tf_op jit(solution)/shard_map/ppermute | solution.py:51
  119.0 27.7 %collective-permute-start.17 = (bf16[512,1152]{1,0:T(8,128)(2,1)}, bf16[512,1152]{1,0:T(8,128)(2,1)S(1)}, u32[]{:S(2)}, u32[]{:S(2)}) collective-permute-start(bf16[512,1152]{1,0:T(8,128)(2,1)} %get-tuple-element.90), channel_id=1, source_target_pairs={{0,2},{2,0},{1,3},{3,1},{4,6},{6,4},{5,7},{7,5},{8,10},{10,8},{9,1... | collective-permute-start | bytes 3538952 | tf_op jit(solution)/shard_map/ppermute | solution.py:51
  165.5 24.4 %collective-permute-start.18 = (bf16[1024,1152]{1,0:T(8,128)(2,1)}, bf16[1024,1152]{1,0:T(8,128)(2,1)}, u32[]{:S(2)}, u32[]{:S(2)}) collective-permute-start(bf16[1024,1152]{1,0:T(8,128)(2,1)} %pad_maximum_fusion), channel_id=1, source_target_pairs={{0,1},{1,0},{2,3},{3,2},{4,5},{5,4},{6,7},{7,6},{8,9},{9,8},{10,11... | collective-permute-start | bytes 7077896 | tf_op jit(solution)/shard_map/ppermute | solution.py:51
  194.4 23.2 %collective-permute-start.23 = (bf16[256,1152]{1,0:T(8,128)(2,1)S(1)}, bf16[256,1152]{1,0:T(8,128)(2,1)S(1)}, u32[]{:S(2)}, u32[]{:S(2)}) collective-permute-start(bf16[256,1152]{1,0:T(8,128)(2,1)S(1)} %get-tuple-element.179), channel_id=1, source_target_pairs={{0,2},{2,0},{1,3},{3,1},{4,6},{6,4},{5,7},{7,5},{8,10},{10,8},{9,1... | collective-permute-start | bytes 1769480 | tf_op jit(solution)/shard_map/ppermute | solution.py:51
  195.4 22.2 %collective-permute-start.24 = (bf16[256,1152]{1,0:T(8,128)(2,1)S(1)}, bf16[256,1152]{1,0:T(8,128)(2,1)S(1)}, u32[]{:S(2)}, u32[]{:S(2)}) collective-permute-start(bf16[256,1152]{1,0:T(8,128)(2,1)S(1)} %get-tuple-element.178), channel_id=1, source_target_pairs={{0,16},{16,0},{1,17},{17,1},{2,18},{18,2},{3,19},{19,3},{4,20},{20... | collective-permute-start | bytes 1769480 | tf_op jit(solution)/shard_map/ppermute | solution.py:51
  228.7 27.2 %collective-permute-start.28 = (bf16[512,1152]{1,0:T(8,128)(2,1)S(1)}, bf16[512,1152]{1,0:T(8,128)(2,1)S(1)}, u32[]{:S(2)}, u32[]{:S(2)}) collective-permute-start(bf16[512,1152]{1,0:T(8,128)(2,1)S(1)} %pad_maximum_fusion.7), channel_id=1, source_target_pairs={{0,2},{2,0},{1,3},{3,1},{4,6},{6,4},{5,7},{7,5},{8,10},{10,8},{9,1... | collective-permute-start | bytes 3538952 | tf_op jit(solution)/shard_map/ppermute | solution.py:51
  230.3 26.9 %collective-permute-start.27 = (bf16[512,1152]{1,0:T(8,128)(2,1)S(1)}, bf16[512,1152]{1,0:T(8,128)(2,1)S(1)}, u32[]{:S(2)}, u32[]{:S(2)}) collective-permute-start(bf16[512,1152]{1,0:T(8,128)(2,1)S(1)} %pad_maximum_fusion.6._), channel_id=1, source_target_pairs={{0,16},{16,0},{1,17},{17,1},{2,18},{18,2},{3,19},{19,3},{4,20},{20... | collective-permute-start | bytes 3538952 | tf_op jit(solution)/shard_map/ppermute | solution.py:51
  263.3 27.6 %collective-permute-start.31 = (bf16[512,1152]{1,0:T(8,128)(2,1)S(1)}, bf16[512,1152]{1,0:T(8,128)(2,1)S(1)}, u32[]{:S(2)}, u32[]{:S(2)}) collective-permute-start(bf16[512,1152]{1,0:T(8,128)(2,1)S(1)} %get-tuple-element.159), channel_id=1, source_target_pairs={{0,16},{16,0},{1,17},{17,1},{2,18},{18,2},{3,19},{19,3},{4,20},{20... | collective-permute-start | bytes 3538952 | tf_op jit(solution)/shard_map/ppermute | solution.py:51
  263.4 27.5 %collective-permute-start.32 = (bf16[512,1152]{1,0:T(8,128)(2,1)S(1)}, bf16[512,1152]{1,0:T(8,128)(2,1)S(1)}, u32[]{:S(2)}, u32[]{:S(2)}) collective-permute-start(bf16[512,1152]{1,0:T(8,128)(2,1)S(1)} %get-tuple-element.159), channel_id=1, source_target_pairs={{0,2},{2,0},{1,3},{3,1},{4,6},{6,4},{5,7},{7,5},{8,10},{10,8},{9,1... | collective-permute-start | bytes 3538952 | tf_op jit(solution)/shard_map/ppermute | solution.py:51
  350.0 23.8 %collective-permute-start.38 = (bf16[256,1152]{1,0:T(8,128)(2,1)S(1)}, bf16[256,1152]{1,0:T(8,128)(2,1)S(1)}, u32[]{:S(2)}, u32[]{:S(2)}) collective-permute-start(bf16[256,1152]{1,0:T(8,128)(2,1)S(1)} %get-tuple-element.177), channel_id=1, source_target_pairs={{0,2},{2,0},{1,3},{3,1},{4,6},{6,4},{5,7},{7,5},{8,10},{10,8},{9,1... | collective-permute-start | bytes 1769480 | tf_op jit(solution)/shard_map/ppermute | solution.py:51
  350.5 23.3 %collective-permute-start.39 = (bf16[256,1152]{1,0:T(8,128)(2,1)S(1)}, bf16[256,1152]{1,0:T(8,128)(2,1)S(1)}, u32[]{:S(2)}, u32[]{:S(2)}) collective-permute-start(bf16[256,1152]{1,0:T(8,128)(2,1)S(1)} %get-tuple-element.176), channel_id=1, source_target_pairs={{0,16},{16,0},{1,17},{17,1},{2,18},{18,2},{3,19},{19,3},{4,20},{20... | collective-permute-start | bytes 1769480 | tf_op jit(solution)/shard_map/ppermute | solution.py:51
  379.7 36.6 %collective-permute-start.30 = (bf16[512,1152]{1,0:T(8,128)(2,1)}, bf16[512,1152]{1,0:T(8,128)(2,1)S(1)}, u32[]{:S(2)}, u32[]{:S(2)}) collective-permute-start(bf16[512,1152]{1,0:T(8,128)(2,1)} %slice.208), channel_id=1, source_target_pairs={{0,1},{1,0},{2,3},{3,2},{4,5},{5,4},{6,7},{7,6},{8,9},{9,8},{10,11... | collective-permute-start | bytes 3538952 | tf_op jit(solution)/shard_map/ppermute | solution.py:51
  382.9 60.9 %collective-permute-start.45 = (bf16[216,1152]{1,0:T(8,128)(2,1)}, bf16[216,1152]{1,0:T(8,128)(2,1)}, u32[]{:S(2)}, u32[]{:S(2)}) collective-permute-start(bf16[216,1152]{1,0:T(8,128)(2,1)} %get-tuple-element.172), channel_id=1, source_target_pairs={{0,12},{4,0},{8,4},{12,8},{1,13},{5,1},{9,5},{13,9},{2,14},{6,2},{... | collective-permute-start | bytes 1493000 | tf_op jit(solution)/shard_map/ppermute | solution.py:273
  383.5 60.3 %collective-permute-start.44 = (bf16[216,1152]{1,0:T(8,128)(2,1)}, bf16[216,1152]{1,0:T(8,128)(2,1)}, u32[]{:S(2)}, u32[]{:S(2)}) collective-permute-start(bf16[216,1152]{1,0:T(8,128)(2,1)} %get-tuple-element.173), channel_id=1, source_target_pairs={{0,8},{4,12},{8,0},{12,4},{1,9},{5,13},{9,1},{13,5},{2,10},{6,14},... | collective-permute-start | bytes 1493000 | tf_op jit(solution)/shard_map/ppermute | solution.py:273
  389.5 28.0 %collective-permute-start.42 = (bf16[512,1152]{1,0:T(8,128)(2,1)}, bf16[512,1152]{1,0:T(8,128)(2,1)}, u32[]{:S(2)}, u32[]{:S(2)}) collective-permute-start(bf16[512,1152]{1,0:T(8,128)(2,1)} %pad_maximum_fusion.10), channel_id=1, source_target_pairs={{0,2},{2,0},{1,3},{3,1},{4,6},{6,4},{5,7},{7,5},{8,10},{10,8},{9,1... | collective-permute-start | bytes 3538952 | tf_op jit(solution)/shard_map/ppermute | solution.py:51
  391.2 26.9 %collective-permute-start.41 = (bf16[512,1152]{1,0:T(8,128)(2,1)}, bf16[512,1152]{1,0:T(8,128)(2,1)}, u32[]{:S(2)}, u32[]{:S(2)}) collective-permute-start(bf16[512,1152]{1,0:T(8,128)(2,1)} %pad_maximum_fusion.9.refs_6_), channel_id=1, source_target_pairs={{0,16},{16,0},{1,17},{17,1},{2,18},{18,2},{3,19},{19,3},{4,20},{20... | collective-permute-start | bytes 3538952 | tf_op jit(solution)/shard_map/ppermute | solution.py:51
  416.3 27.5 %collective-permute-start.43 = (bf16[216,1152]{1,0:T(8,128)(2,1)}, bf16[216,1152]{1,0:T(8,128)(2,1)}, u32[]{:S(2)}, u32[]{:S(2)}) collective-permute-start(bf16[216,1152]{1,0:T(8,128)(2,1)} %get-tuple-element.171), channel_id=1, source_target_pairs={{0,4},{4,8},{8,12},{12,0},{1,5},{5,9},{9,13},{13,1},{2,6},{6,10},{... | collective-permute-start | bytes 1493000 | tf_op jit(solution)/shard_map/ppermute | solution.py:273
  503.0 25.9 %collective-permute-start.46 = (bf16[512,512]{1,0:T(8,128)(2,1)}, bf16[512,512]{1,0:T(8,128)(2,1)S(1)}, u32[]{:S(2)}, u32[]{:S(2)}) collective-permute-start(bf16[512,512]{1,0:T(8,128)(2,1)} %get-tuple-element.131), channel_id=1, source_target_pairs={{1,0},{2,1},{3,2},{4,3},{5,4},{6,5},{7,6},{8,7},{9,8},{10,9},{11,1... | collective-permute-start | bytes 1572872 | tf_op jit(solution)/shard_map/ppermute | solution.py:833
  508.4 32.0 %all-to-all-start.1 = ((bf16[8,36,1792]{2,1,0:T(8,128)(2,1)}), bf16[8,36,1792]{2,1,0:T(8,128)(2,1)S(1)}, u32[]{:S(2)}, u32[]{:S(2)}) async-start(bf16[8,36,1792]{2,1,0:T(8,128)(2,1)} %reshape.161), calls=%async_computation.2 | async-start | bytes 2293760 | tf_op jit(solution)/shard_map/all_to_all | solution.py:816
  (71 other events, 611.1 us)
Sparse Core Ops, SparseCore 0:
  17.2 55.7 all-gather.4
  79.3 76.2 all-gather.6
  416.4 83.0 reduce-scatter.1

commit v11 on v10

--- a/solution.py
+++ b/solution.py
@@ -710,7 +710,6 @@
 
     seq_place = lax.axis_index(("g", "y", "c"))
     seq_size = lax.axis_size(("g", "y", "c"))
-    before = lax.ppermute(tokens[0], ("g", "y", "c"), [(i, i + 1) for i in range(seq_size - 1)])
 
     def spread(weight):
         cut = weight.reshape(shard_rows, 2, groups, members // 2, piece)
@@ -733,10 +732,13 @@
     mine = lax.dynamic_index_in_dim(halves, core, 0, keepdims=False)
     other = lax.dynamic_index_in_dim(halves, 1 - core, 0, keepdims=False)
     mine = in_order(mine, swap(other, "c"), core).reshape(2 * shard_rows, half_cols)
-    mine, before, sent = lax.optimization_barrier((mine, before, sent))
+    mine, sent = lax.optimization_barrier((mine, sent))
     sent = lax.all_to_all(sent, PLANE, split_axis=0, concat_axis=0, tiled=True)
     sent = sent.reshape(members * shard_rows, 2 * hidden_pad)
-    mine, sent = lax.optimization_barrier((group_gather(mine), sent))
+    before = lax.ppermute(
+        after(tokens[0], mine), ("g", "y", "c"), [(i, i + 1) for i in range(seq_size - 1)]
+    )
+    mine, sent, before = lax.optimization_barrier((group_gather(mine), sent, before))
     mine = plane_weights(mine, *plane_start(mine)).reshape(width, half_cols)
     other = swap(mine, "c")
 
@@ -772,7 +774,9 @@
     )
 
     half = row_count // 2
-    from_x, from_y = swap(normed_mlp, "x"), swap(normed_mlp, "y")
+    from_x, from_y, down = lax.optimization_barrier(
+        (swap(normed_mlp, "x"), swap(normed_mlp, "y"), down)
+    )
     normed_far = jnp.concatenate([swap(from_x[:half], "y"), swap(from_y[half:], "x")])
     normed_near = jnp.concatenate([from_x, from_y])
     normed_all = [with_core(part) for part in (normed_mlp, normed_near, normed_far)]

time: 559 us -> 587 us (1.050)
  waiting for transfers between devices: 161 us -> 189 us
    ppermute x1, waiting for transfers between devices: 2.18 us -> 37.2 us  [on_device(): lax.ppermute(after(tokens[0], mine), ('g', 'y', 'c'), [(i, i + 1) for i i...]
    unnamed x74 -> x76, local copies, waits for them, and re-layouts: 13.6 us -> 12.9 us
  transfers between devices with their start and end apart: 66 -> 66, of which waited for: 30 -> 30; matrix products, arithmetic and copies ran while one was open for 15% -> 13% of each run, Pallas kernels for 30% -> 28%
where the time goes in v11:
time: 587 us; the launch traced here: 579 us
  Pallas kernels  198 us (34%)
  waiting for transfers between devices  189 us (32%)
  starting transfers between devices  73.6 us (13%)
  local copies, waits for them, and re-layouts  60.3 us (10%)
  other arithmetic  40.6 us (7%)
  between operations  15.1 us (3%)
    ppermute x50, waiting for transfers between devices, swap(): return lax.ppermute(array, axis, [(0, 1), (1, 0)])  123 us
    pallas_call x3, Pallas kernels, mlp_backward(): pl.pallas_call(mlp_backward_kernel, grid=(rows // TILE,), in_specs=[row_b...  48.9 us
    pallas_call x3, Pallas kernels, mlp_forward(): pl.pallas_call(mlp_forward_kernel, grid=(rows // TILE,), in_specs=[row_bl...  48.1 us
    ppermute x50, starting transfers between devices, swap(): return lax.ppermute(array, axis, [(0, 1), (1, 0)])  42.2 us
    ppermute x1, waiting for transfers between devices, on_device(): lax.ppermute(after(tokens[0], mine), ('g', 'y', 'c'), [(i, i + 1) for i i...  37.2 us
    pallas_call x1, Pallas kernels, gate_terms(): pl.pallas_call(gate_terms_kernel, grid=(both // 256,), in_specs=[whole_bl...  24.3 us
    pallas_call x1, Pallas kernels, attend_backward(): pl.pallas_call(functools.partial(attend_backward_kernel, scale), in_specs...  16.9 us
    pallas_call x1, Pallas kernels, down_terms(): pl.pallas_call(down_terms_kernel, grid=(own // 128,), in_specs=[pl.BlockS...  16.4 us
  transfers between devices with their start and end apart: 66, of which 30 were waited for; matrix products, arithmetic and copies ran while one was open for 13% of the time, Pallas kernels for 28%

profile of v11, /device:TPU:13, one launch (start us, length us, event | category | flops | bytes accessed | tf_op | source)
XLA Modules:
  0.0 579.0 jit_solution(13189671322114034447)
XLA Ops:
  33.1 7.9 %collective-permute-done.3 = bf16[72,896]{1,0:T(8,128)(2,1)S(1)} collective-permute-done((bf16[72,896]{1,0:T(8,128)(2,1)S(1)}, bf16[72,896]{1,0:T(8,128)(2,1)S(1)}, u32[]{:S(2)}, u32[]{:S(2)}) %collective-permute-start.3) | collective-permute-done | bytes 129056 | tf_op jit(solution)/shard_map/ppermute | solution.py:242
  45.5 37.2 %collective-permute-done.4.earlier = bf16[512,1152]{1,0:T(8,128)(2,1)} collective-permute-done((bf16[512,1152]{1,0:T(8,128)(2,1)S(1)}, bf16[512,1152]{1,0:T(8,128)(2,1)}, u32[]{:S(2)}, u32[]{:S(2)}) %collective-permute-start.4) | collective-permute-done | bytes 1179680 | tf_op jit(solution)/shard_map/ppermute | solution.py:738
  91.1 8.2 %collective-permute-done.8 = bf16[2,2,72,896]{3,2,1,0:T(8,128)(2,1)S(1)} collective-permute-done((bf16[2,2,72,896]{3,2,1,0:T(8,128)(2,1)S(1)}, bf16[2,2,72,896]{3,2,1,0:T(8,128)(2,1)S(1)}, u32[]{:S(2)}, u32[]{:S(2)}) %collective-permute-start.8) | collective-permute-done | bytes 516128 | tf_op jit(solution)/shard_map/ppermute | solution.py:51
  109.2 8.5 %shard_map.271 = (bf16[512,1152]{1,0:T(8,128)(2,1)}, bf16[512,1152]{1,0:T(8,128)(2,1)}, f32[512,1024]{1,0:T(8,128)}, f32[1024,256]{1,0:T(8,128)}, bf16[512,1024]...) custom-call(s32[1]{0:T(128)} %bitcast.core, ...), custom_call_target="tpu_custom_call" | custom-call | flops 2415919104 | bytes 9437184 | tf_op jit(solution)/shard_map/pallas_call | solution.py:370
  134.4 9.9 %shard_map.272 = (bf16[512,1024]{1,0:T(8,128)(2,1)}, f32[512,128]{1,0:T(8,128)}, f32[512,1152]{1,0:T(8,128)}, f32[512,1152]{1,0:T(8,128)}, bf16[512,1152]{1,0:T(8,128)(2,1)}) custom-call(bf16[512,1024]{1,0:T(8,128)(2,1)} %get-tuple-element.87.queries, bf16[1024,256]{1,0:T(8,128)(2,1)} %get-tuple-element.88.keys, bf16[1024,256]{1,0:T(8,128)(2,1)} %get-tuple-element.89.values, ...), custom_call_target="tpu_custom_call" | custom-call | flops 3355443200 | bytes 11796480 | tf_op jit(solution)/shard_map/pallas_call | solution.py:436
  147.3 24.5 %collective-permute-done.16 = bf16[512,1152]{1,0:T(8,128)(2,1)S(1)} collective-permute-done((bf16[512,1152]{1,0:T(8,128)(2,1)}, bf16[512,1152]{1,0:T(8,128)(2,1)S(1)}, u32[]{:S(2)}, u32[]{:S(2)}) %collective-permute-start.16) | collective-permute-done | bytes 1179680 | tf_op jit(solution)/shard_map/ppermute | solution.py:51
  173.3 12.2 %collective-permute-done.19 = bf16[256,1152]{1,0:T(8,128)(2,1)S(1)} collective-permute-done((bf16[256,1152]{1,0:T(8,128)(2,1)S(1)}, bf16[256,1152]{1,0:T(8,128)(2,1)S(1)}, u32[]{:S(2)}, u32[]{:S(2)}) %collective-permute-start.19) | collective-permute-done | bytes 589856 | tf_op jit(solution)/shard_map/ppermute | solution.py:51
  198.9 12.9 %shard_map.273 = (bf16[1024,896]{1,0:T(8,128)(2,1)}, bf16[1024,896]{1,0:T(8,128)(2,1)}, bf16[1024,896]{1,0:T(8,128)(2,1)}, bf16[1024,1152]{1,0:T(8,128)(2,1)}) custom-call(bf16[1024,1152]{1,0:T(8,128)(2,1)} %constant_dynamic-update-slice_fusion.5.normed._.refs_2_, bf16[1152,1792]{1,0:T(8,128)(2,1)} %bitcast.196, bf16[896,1152]{1,0:T(8,128)(2,1)} %pad.27.down._, ...), custom_call_target="tpu_custom_call" | custom-call | flops 6341787648 | bytes 10223616 | tf_op jit(solution)/shard_map/pallas_call | solution.py:88
  220.2 21.8 %shard_map.274 = (bf16[2048,896]{1,0:T(8,128)(2,1)}, bf16[2048,896]{1,0:T(8,128)(2,1)}, bf16[2048,896]{1,0:T(8,128)(2,1)}, bf16[2048,1152]{1,0:T(8,128)(2,1)}) custom-call(bf16[2048,1152]{1,0:T(8,128)(2,1)} %copy-done.24, bf16[1152,1792]{1,0:T(8,128)(2,1)} %bitcast.197, bf16[896,1152]{1,0:T(8,128)(2,1)} %pad.27.down._, bf16[512,1152]{1,0:T(8,128)(2,1)} %copy-done.3), custom_call_target="tpu_custom_call" | custom-call | flops 12683575296 | bytes 20447232 | tf_op jit(solution)/shard_map/pallas_call | solution.py:88
  254.6 13.4 %shard_map.275 = (bf16[1024,896]{1,0:T(8,128)(2,1)}, bf16[1024,896]{1,0:T(8,128)(2,1)}, bf16[1024,896]{1,0:T(8,128)(2,1)}, bf16[1024,1152]{1,0:T(8,128)(2,1)}) custom-call(bf16[1024,1152]{1,0:T(8,128)(2,1)} %copy-done.20, bf16[1152,1792]{1,0:T(8,128)(2,1)} %bitcast.198, bf16[896,1152]{1,0:T(8,128)(2,1)} %pad.27.down._, bf16[512,1152]{1,0:T(8,128)(2,1)} %copy-done.14), custom_call_target="tpu_custom_call" | custom-call | flops 6341787648 | bytes 10223616 | tf_op jit(solution)/shard_map/pallas_call | solution.py:88
  271.3 9.1 %collective-permute-done.28 = bf16[512,1152]{1,0:T(8,128)(2,1)S(1)} collective-permute-done((bf16[512,1152]{1,0:T(8,128)(2,1)S(1)}, bf16[512,1152]{1,0:T(8,128)(2,1)S(1)}, u32[]{:S(2)}, u32[]{:S(2)}) %collective-permute-start.28) | collective-permute-done | bytes 1179680 | tf_op jit(solution)/shard_map/ppermute | solution.py:51
  290.4 13.5 %shard_map.276 = (bf16[1024,1792]{1,0:T(8,128)(2,1)}, bf16[1024,1152]{1,0:T(8,128)(2,1)}) custom-call(bf16[1024,1152]{1,0:T(8,128)(2,1)} %pad_maximum_fusion.1.grad_mixed.refs_3_, bf16[1024,896]{1,0:T(8,128)(2,1)} %get-tuple-element.106.gelu, bf16[1024,896]{1,0:T(8,128)(2,1)} %get-tuple-element.107.slope, bf16[1152,1792]{1,0:T(8,128)(2,1)} %bitcast.199, ...), custom_call_target="tpu_custom_call" | custom-call | flops 6341787648 | bytes 12058624 | tf_op jit(solution)/shard_map/pallas_call | solution.py:121
  303.9 10.0 %collective-permute-done.31 = bf16[512,1152]{1,0:T(8,128)(2,1)S(1)} collective-permute-done((bf16[512,1152]{1,0:T(8,128)(2,1)S(1)}, bf16[512,1152]{1,0:T(8,128)(2,1)S(1)}, u32[]{:S(2)}, u32[]{:S(2)}) %collective-permute-start.31) | collective-permute-done | bytes 1179680 | tf_op jit(solution)/shard_map/ppermute | solution.py:51
  317.9 13.2 %collective-permute-done.34 = bf16[256,1152]{1,0:T(8,128)(2,1)S(1)} collective-permute-done((bf16[256,1152]{1,0:T(8,128)(2,1)S(1)}, bf16[256,1152]{1,0:T(8,128)(2,1)S(1)}, u32[]{:S(2)}, u32[]{:S(2)}) %collective-permute-start.34) | collective-permute-done | bytes 589856 | tf_op jit(solution)/shard_map/ppermute | solution.py:51
  338.9 16.4 %shard_map.277._ = bf16[864,1152]{1,0:T(8,128)(2,1)} custom-call(bf16[1024,896]{1,0:T(8,128)(2,1)} %get-tuple-element.115.refs_0_, bf16[2048,896]{1,0:T(8,128)(2,1)} %get-tuple-element.116.refs_1_, bf16[1024,896]{1,0:T(8,128)(2,1)} %get-tuple-element.117.refs_2_, bf16[1024,1152]{1,0:T(8,128)(2,1)} %pad_maximum_fusion.1.grad_mixed.refs_3_, ...), custom_call_target="tpu_custom_call" | custom-call | flops 8455716864 | bytes 16777216 | tf_op jit(solution)/shard_map/pallas_call | solution.py:156
  355.3 13.5 %shard_map.278 = (bf16[1024,1792]{1,0:T(8,128)(2,1)}, bf16[1024,1152]{1,0:T(8,128)(2,1)}) custom-call(bf16[1024,1152]{1,0:T(8,128)(2,1)} %copy-done.26, bf16[1024,896]{1,0:T(8,128)(2,1)} %get-tuple-element.113.gelu, bf16[1024,896]{1,0:T(8,128)(2,1)} %get-tuple-element.114.slope, bf16[1152,1792]{1,0:T(8,128)(2,1)} %bitcast.200, ...), custom_call_target="tpu_custom_call" | custom-call | flops 6341787648 | bytes 12058624 | tf_op jit(solution)/shard_map/pallas_call | solution.py:121
  374.9 22.0 %shard_map.279 = (bf16[2048,1792]{1,0:T(8,128)(2,1)}, bf16[2048,1152]{1,0:T(8,128)(2,1)}) custom-call(bf16[2048,1152]{1,0:T(8,128)(2,1)} %copy-done.25, bf16[2048,896]{1,0:T(8,128)(2,1)} %get-tuple-element.111.gelu, bf16[2048,896]{1,0:T(8,128)(2,1)} %get-tuple-element.112.slope, bf16[1152,1792]{1,0:T(8,128)(2,1)} %bitcast.201, ...), custom_call_target="tpu_custom_call" | custom-call | flops 12683575296 | bytes 24117248 | tf_op jit(solution)/shard_map/pallas_call | solution.py:121
  405.9 6.5 %collective-permute-start.44 = (bf16[216,1152]{1,0:T(8,128)(2,1)}, bf16[216,1152]{1,0:T(8,128)(2,1)}, u32[]{:S(2)}, u32[]{:S(2)}) collective-permute-start(bf16[216,1152]{1,0:T(8,128)(2,1)} %get-tuple-element.181), channel_id=1, source_target_pairs={{0,8},{4,12},{8,0},{12,4},{1,9},{5,13},{9,1},{13,5},{2,10},{6,14},... | collective-permute-start | bytes 1493000 | tf_op jit(solution)/shard_map/ppermute | solution.py:273
  419.7 24.3 %shard_map.280 = bf16[4,2,144,1792]{3,2,1,0:T(8,128)(2,1)} custom-call(bf16[1024,1152]{1,0:T(8,128)(2,1)} %copy-done.20, bf16[2048,1152]{1,0:T(8,128)(2,1)} %copy-done.24, bf16[1024,1152]{1,0:T(8,128)(2,1)} %constant_dynamic-update-slice_fusion.5.normed._.refs_2_, bf16[1024,1792]{1,0:T(8,128)(2,1)} %get-tuple-element.123.refs_3_, ...), custom_call_target="tpu_custom_call" | custom-call | flops 16911433728 | bytes 24117248 | tf_op jit(solution)/shard_map/pallas_call | solution.py:188
  449.2 16.9 %shard_map.281 = (f32[512,1152]{1,0:T(8,128)}, bf16[512,1152]{1,0:T(8,128)(2,1)}, f32[512,1024]{1,0:T(8,128)}, f32[1024,256]{1,0:T(8,128)}, f32[1024,256]{1,0:T(8,128)}, /*index=5*/f32[8,1152]{1,0:T(8,128)}) custom-call(f32[512,1152]{1,0:T(8,128)} %convert_add_fusion.3.grad_normed_mlp, bf16[512,1152]{1,0:T(8,128)(2,1)} %bitcast.192, ...), custom_call_target="tpu_custom_call" | custom-call | flops 6576668672 | bytes 17694720 | tf_op jit(solution)/shard_map/pallas_call | solution.py:506
  473.7 15.1 %shard_map.282 = (f32[512,1152]{1,0:T(8,128)}, bf16[512,512]{1,0:T(8,128)(2,1)}, bf16[1152,896]{1,0:T(8,128)(2,1)}, bf16[1152,896]{1,0:T(8,128)(2,1)}) custom-call(s32[1]{0:T(128)} %bitcast.core, f32[512,1024]{1,0:T(8,128)} %get-tuple-element.130.grad_queries, f32[1024,256]{1,0:T(8,128)} %get-tuple-element.131.grad_keys, ...), custom_call_target="tpu_custom_call" | custom-call | flops 4756340736 | bytes 17694720 | tf_op jit(solution)/shard_map/pallas_call | solution.py:595
  504.8 10.4 %collective-permute-done.55 = bf16[2,2,72,896]{3,2,1,0:T(8,128)(2,1)S(1)} collective-permute-done((bf16[2,2,72,896]{3,2,1,0:T(8,128)(2,1)S(1)}, bf16[2,2,72,896]{3,2,1,0:T(8,128)(2,1)S(1)}, u32[]{:S(2)}, u32[]{:S(2)}) %collective-permute-start.55) | collective-permute-done | bytes 516128 | tf_op jit(solution)/shard_map/ppermute | solution.py:51
  548.3 8.5 %collective-permute-done.46.returned = bf16[512,512]{1,0:T(8,128)(2,1)S(1)} collective-permute-done((bf16[512,512]{1,0:T(8,128)(2,1)}, bf16[512,512]{1,0:T(8,128)(2,1)S(1)}, u32[]{:S(2)}, u32[]{:S(2)}) %collective-permute-start.46) | collective-permute-done | bytes 524320 | tf_op jit(solution)/shard_map/ppermute | solution.py:837
  557.6 6.5 %shard_map.283 = bf16[512,1152]{1,0:T(8,128)(2,1)} custom-call(s32[1]{0:T(128)} %bitcast.core, bf16[512,512]{1,0:T(8,128)(2,1)} %copy-done.23, f32[512,1152]{1,0:T(8,128)} %get-tuple-element.140.grad_normed, bf16[1152,896]{1,0:T(8,128)(2,1)} %bitcast.190, bf16[1152,896]{1,0:T(8,128)(2,1)} %collective-permute-done.9.other, bf16[512,1152]{1,0:T(8,128)(2,1)} %bitcast.218, ...), custom_call_target="tpu_custom_call" | custom-call | flops 603979776 | bytes 7077888 | tf_op jit(solution)/shard_map/pallas_call | solution.py:632
  (340 shorter events, 221.4 us)
Async XLA Ops:
  7.2 98.1 %all-gather.5.cloned.1.call-start = ((), (), s32[]{:S(2)}) async-start(), calls=%async_computation.4 | async-start | bytes 2856960 | tf_op jit(solution)/shard_map/all_gather | solution.py:745
  29.9 163.4 %all-gather.7.cloned.1.call-start = ((), (), s32[]{:S(2)}) async-start(), calls=%async_computation.5 | async-start | bytes 5160960 | tf_op jit(solution)/shard_map/all_gather | solution.py:750
  29.9 52.8 %collective-permute-start.4 = (bf16[512,1152]{1,0:T(8,128)(2,1)S(1)}, bf16[512,1152]{1,0:T(8,128)(2,1)}, u32[]{:S(2)}, u32[]{:S(2)}) collective-permute-start(bf16[512,1152]{1,0:T(8,128)(2,1)S(1)} %bitcast.219), channel_id=1, source_target_pairs={{0,1},{1,2},{2,3},{3,4},{4,5},{5,6},{6,7},{7,8},{8,9},{9,10},{10,1... | collective-permute-start | bytes 3538952 | tf_op jit(solution)/shard_map/ppermute | solution.py:738
  104.7 421.8 %reduce-scatter.2.cloned.1.call-start = ((), (), s32[]{:S(2)}) async-start(), calls=%async_computation.3 | async-start | bytes 5160960 | tf_op jit(solution)/shard_map/reduce_scatter | solution.py:818
  144.4 27.5 %collective-permute-start.16 = (bf16[512,1152]{1,0:T(8,128)(2,1)}, bf16[512,1152]{1,0:T(8,128)(2,1)S(1)}, u32[]{:S(2)}, u32[]{:S(2)}) collective-permute-start(bf16[512,1152]{1,0:T(8,128)(2,1)} %get-tuple-element.95), channel_id=1, source_target_pairs={{0,16},{16,0},{1,17},{17,1},{2,18},{18,2},{3,19},{19,3},{4,20},{20... | collective-permute-start | bytes 3538952 | tf_op jit(solution)/shard_map/ppermute | solution.py:51
  144.7 27.2 %collective-permute-start.17 = (bf16[512,1152]{1,0:T(8,128)(2,1)}, bf16[512,1152]{1,0:T(8,128)(2,1)S(1)}, u32[]{:S(2)}, u32[]{:S(2)}) collective-permute-start(bf16[512,1152]{1,0:T(8,128)(2,1)} %get-tuple-element.95), channel_id=1, source_target_pairs={{0,2},{2,0},{1,3},{3,1},{4,6},{6,4},{5,7},{7,5},{8,10},{10,8},{9,1... | collective-permute-start | bytes 3538952 | tf_op jit(solution)/shard_map/ppermute | solution.py:51
  191.5 22.5 %collective-permute-start.18 = (bf16[1024,1152]{1,0:T(8,128)(2,1)}, bf16[1024,1152]{1,0:T(8,128)(2,1)}, u32[]{:S(2)}, u32[]{:S(2)}) collective-permute-start(bf16[1024,1152]{1,0:T(8,128)(2,1)} %pad_maximum_fusion), channel_id=1, source_target_pairs={{0,1},{1,0},{2,3},{3,2},{4,5},{5,4},{6,7},{7,6},{8,9},{9,8},{10,11... | collective-permute-start | bytes 7077896 | tf_op jit(solution)/shard_map/ppermute | solution.py:51
  218.5 23.5 %collective-permute-start.23 = (bf16[256,1152]{1,0:T(8,128)(2,1)S(1)}, bf16[256,1152]{1,0:T(8,128)(2,1)S(1)}, u32[]{:S(2)}, u32[]{:S(2)}) collective-permute-start(bf16[256,1152]{1,0:T(8,128)(2,1)S(1)} %get-tuple-element.187), channel_id=1, source_target_pairs={{0,2},{2,0},{1,3},{3,1},{4,6},{6,4},{5,7},{7,5},{8,10},{10,8},{9,1... | collective-permute-start | bytes 1769480 | tf_op jit(solution)/shard_map/ppermute | solution.py:51
  219.0 23.0 %collective-permute-start.24 = (bf16[256,1152]{1,0:T(8,128)(2,1)S(1)}, bf16[256,1152]{1,0:T(8,128)(2,1)S(1)}, u32[]{:S(2)}, u32[]{:S(2)}) collective-permute-start(bf16[256,1152]{1,0:T(8,128)(2,1)S(1)} %get-tuple-element.186), channel_id=1, source_target_pairs={{0,16},{16,0},{1,17},{17,1},{2,18},{18,2},{3,19},{19,3},{4,20},{20... | collective-permute-start | bytes 1769480 | tf_op jit(solution)/shard_map/ppermute | solution.py:51
  253.2 27.2 %collective-permute-start.28 = (bf16[512,1152]{1,0:T(8,128)(2,1)S(1)}, bf16[512,1152]{1,0:T(8,128)(2,1)S(1)}, u32[]{:S(2)}, u32[]{:S(2)}) collective-permute-start(bf16[512,1152]{1,0:T(8,128)(2,1)S(1)} %pad_maximum_fusion.7), channel_id=1, source_target_pairs={{0,2},{2,0},{1,3},{3,1},{4,6},{6,4},{5,7},{7,5},{8,10},{10,8},{9,1... | collective-permute-start | bytes 3538952 | tf_op jit(solution)/shard_map/ppermute | solution.py:51
  253.4 27.0 %collective-permute-start.27 = (bf16[512,1152]{1,0:T(8,128)(2,1)S(1)}, bf16[512,1152]{1,0:T(8,128)(2,1)S(1)}, u32[]{:S(2)}, u32[]{:S(2)}) collective-permute-start(bf16[512,1152]{1,0:T(8,128)(2,1)S(1)} %pad_maximum_fusion.6._), channel_id=1, source_target_pairs={{0,16},{16,0},{1,17},{17,1},{2,18},{18,2},{3,19},{19,3},{4,20},{20... | collective-permute-start | bytes 3538952 | tf_op jit(solution)/shard_map/ppermute | solution.py:51
  286.3 27.6 %collective-permute-start.31 = (bf16[512,1152]{1,0:T(8,128)(2,1)S(1)}, bf16[512,1152]{1,0:T(8,128)(2,1)S(1)}, u32[]{:S(2)}, u32[]{:S(2)}) collective-permute-start(bf16[512,1152]{1,0:T(8,128)(2,1)S(1)} %get-tuple-element.167), channel_id=1, source_target_pairs={{0,16},{16,0},{1,17},{17,1},{2,18},{18,2},{3,19},{19,3},{4,20},{20... | collective-permute-start | bytes 3538952 | tf_op jit(solution)/shard_map/ppermute | solution.py:51
  287.4 27.3 %collective-permute-start.32 = (bf16[512,1152]{1,0:T(8,128)(2,1)S(1)}, bf16[512,1152]{1,0:T(8,128)(2,1)S(1)}, u32[]{:S(2)}, u32[]{:S(2)}) collective-permute-start(bf16[512,1152]{1,0:T(8,128)(2,1)S(1)} %get-tuple-element.167), channel_id=1, source_target_pairs={{0,2},{2,0},{1,3},{3,1},{4,6},{6,4},{5,7},{7,5},{8,10},{10,8},{9,1... | collective-permute-start | bytes 3538952 | tf_op jit(solution)/shard_map/ppermute | solution.py:51
  314.9 20.5 %collective-permute-start.33 = (bf16[1024,1152]{1,0:T(8,128)(2,1)S(1)}, bf16[1024,1152]{1,0:T(8,128)(2,1)S(1)}, u32[]{:S(2)}, u32[]{:S(2)}) collective-permute-start(bf16[1024,1152]{1,0:T(8,128)(2,1)S(1)} %pad_maximum_fusion.2), channel_id=1, source_target_pairs={{0,1},{1,0},{2,3},{3,2},{4,5},{5,4},{6,7},{7,6},{8,9},{9,8},{10,11... | collective-permute-start | bytes 7077896 | tf_op jit(solution)/shard_map/ppermute | solution.py:51
  373.6 23.3 %collective-permute-start.38 = (bf16[256,1152]{1,0:T(8,128)(2,1)S(1)}, bf16[256,1152]{1,0:T(8,128)(2,1)S(1)}, u32[]{:S(2)}, u32[]{:S(2)}) collective-permute-start(bf16[256,1152]{1,0:T(8,128)(2,1)S(1)} %get-tuple-element.185), channel_id=1, source_target_pairs={{0,2},{2,0},{1,3},{3,1},{4,6},{6,4},{5,7},{7,5},{8,10},{10,8},{9,1... | collective-permute-start | bytes 1769480 | tf_op jit(solution)/shard_map/ppermute | solution.py:51
  374.5 22.3 %collective-permute-start.39 = (bf16[256,1152]{1,0:T(8,128)(2,1)S(1)}, bf16[256,1152]{1,0:T(8,128)(2,1)S(1)}, u32[]{:S(2)}, u32[]{:S(2)}) collective-permute-start(bf16[256,1152]{1,0:T(8,128)(2,1)S(1)} %get-tuple-element.184), channel_id=1, source_target_pairs={{0,16},{16,0},{1,17},{17,1},{2,18},{18,2},{3,19},{19,3},{4,20},{20... | collective-permute-start | bytes 1769480 | tf_op jit(solution)/shard_map/ppermute | solution.py:51
  402.7 41.4 %collective-permute-start.30 = (bf16[512,1152]{1,0:T(8,128)(2,1)}, bf16[512,1152]{1,0:T(8,128)(2,1)S(1)}, u32[]{:S(2)}, u32[]{:S(2)}) collective-permute-start(bf16[512,1152]{1,0:T(8,128)(2,1)} %slice.208), channel_id=1, source_target_pairs={{0,1},{1,0},{2,3},{3,2},{4,5},{5,4},{6,7},{7,6},{8,9},{9,8},{10,11... | collective-permute-start | bytes 3538952 | tf_op jit(solution)/shard_map/ppermute | solution.py:51
  405.9 65.1 %collective-permute-start.45 = (bf16[216,1152]{1,0:T(8,128)(2,1)}, bf16[216,1152]{1,0:T(8,128)(2,1)}, u32[]{:S(2)}, u32[]{:S(2)}) collective-permute-start(bf16[216,1152]{1,0:T(8,128)(2,1)} %get-tuple-element.180), channel_id=1, source_target_pairs={{0,12},{4,0},{8,4},{12,8},{1,13},{5,1},{9,5},{13,9},{2,14},{6,2},{... | collective-permute-start | bytes 1493000 | tf_op jit(solution)/shard_map/ppermute | solution.py:273
  405.9 65.1 %collective-permute-start.44 = (bf16[216,1152]{1,0:T(8,128)(2,1)}, bf16[216,1152]{1,0:T(8,128)(2,1)}, u32[]{:S(2)}, u32[]{:S(2)}) collective-permute-start(bf16[216,1152]{1,0:T(8,128)(2,1)} %get-tuple-element.181), channel_id=1, source_target_pairs={{0,8},{4,12},{8,0},{12,4},{1,9},{5,13},{9,1},{13,5},{2,10},{6,14},... | collective-permute-start | bytes 1493000 | tf_op jit(solution)/shard_map/ppermute | solution.py:273
  417.3 27.2 %collective-permute-start.42 = (bf16[512,1152]{1,0:T(8,128)(2,1)}, bf16[512,1152]{1,0:T(8,128)(2,1)}, u32[]{:S(2)}, u32[]{:S(2)}) collective-permute-start(bf16[512,1152]{1,0:T(8,128)(2,1)} %pad_maximum_fusion.10), channel_id=1, source_target_pairs={{0,2},{2,0},{1,3},{3,1},{4,6},{6,4},{5,7},{7,5},{8,10},{10,8},{9,1... | collective-permute-start | bytes 3538952 | tf_op jit(solution)/shard_map/ppermute | solution.py:51
  418.6 26.9 %collective-permute-start.41 = (bf16[512,1152]{1,0:T(8,128)(2,1)}, bf16[512,1152]{1,0:T(8,128)(2,1)}, u32[]{:S(2)}, u32[]{:S(2)}) collective-permute-start(bf16[512,1152]{1,0:T(8,128)(2,1)} %pad_maximum_fusion.9.refs_6_), channel_id=1, source_target_pairs={{0,16},{16,0},{1,17},{17,1},{2,18},{18,2},{3,19},{19,3},{4,20},{20... | collective-permute-start | bytes 3538952 | tf_op jit(solution)/shard_map/ppermute | solution.py:51
  444.1 27.0 %collective-permute-start.43 = (bf16[216,1152]{1,0:T(8,128)(2,1)}, bf16[216,1152]{1,0:T(8,128)(2,1)}, u32[]{:S(2)}, u32[]{:S(2)}) collective-permute-start(bf16[216,1152]{1,0:T(8,128)(2,1)} %get-tuple-element.179), channel_id=1, source_target_pairs={{0,4},{4,8},{8,12},{12,0},{1,5},{5,9},{9,13},{13,1},{2,6},{6,10},{... | collective-permute-start | bytes 1493000 | tf_op jit(solution)/shard_map/ppermute | solution.py:273
  530.8 26.0 %collective-permute-start.46 = (bf16[512,512]{1,0:T(8,128)(2,1)}, bf16[512,512]{1,0:T(8,128)(2,1)S(1)}, u32[]{:S(2)}, u32[]{:S(2)}) collective-permute-start(bf16[512,512]{1,0:T(8,128)(2,1)} %get-tuple-element.139), channel_id=1, source_target_pairs={{1,0},{2,1},{3,2},{4,3},{5,4},{6,5},{7,6},{8,7},{9,8},{10,9},{11,1... | collective-permute-start | bytes 1572872 | tf_op jit(solution)/shard_map/ppermute | solution.py:837
  536.1 32.2 %all-to-all-start.1 = ((bf16[8,36,1792]{2,1,0:T(8,128)(2,1)}), bf16[8,36,1792]{2,1,0:T(8,128)(2,1)S(1)}, u32[]{:S(2)}, u32[]{:S(2)}) async-start(bf16[8,36,1792]{2,1,0:T(8,128)(2,1)} %reshape.161), calls=%async_computation.2 | async-start | bytes 2293760 | tf_op jit(solution)/shard_map/all_to_all | solution.py:820
  (72 other events, 628.1 us)
Sparse Core Ops, SparseCore 0:
  14.0 67.9 all-gather.4
  104.8 80.5 all-gather.6
  444.2 82.2 reduce-scatter.1

commit v12 on v10

--- a/solution.py
+++ b/solution.py
@@ -141,30 +141,33 @@
     )(grad_mixed, gelu, slope, gate_up, down, earlier)
 
 
-def down_terms_kernel(*refs):
+def down_terms_kernel(count, *refs):
     *ins, out = refs
-    half = len(ins) // 2
-    total = over_rows(ins[0][...], ins[half][...])
-    for left, right in zip(ins[1:half], ins[half + 1 :]):
-        total = total + over_rows(left[...], right[...])
-    out[...] = total.astype(BF)
-
-
-def down_terms(hidden, grad_mixed, keep):
+    total = None
+    for left, right in zip(ins[:count], ins[count : 2 * count]):
+        part = over_rows(left[...], right[...])
+        total = part if total is None else total + part
+    for base in ins[2 * count :]:
+        total = total + base[...]
+    out[...] = total.astype(out.dtype)
+
+
+def down_terms(hidden, grad_mixed, base, keep, kind):
     own, width = hidden[0].shape[1], grad_mixed[0].shape[1]
     rows = sum(part.shape[0] for part in hidden)
     return pl.pallas_call(
-        down_terms_kernel,
+        functools.partial(down_terms_kernel, len(hidden)),
         grid=(own // 128,),
         in_specs=[pl.BlockSpec((part.shape[0], 128), lambda i: (0, i)) for part in hidden]
-        + [whole_block(part.shape) for part in grad_mixed],
+        + [whole_block(part.shape) for part in grad_mixed]
+        + [row_block(128, width) for _ in base],
         out_specs=row_block(128, width),
-        out_shape=jax.ShapeDtypeStruct((keep, width), BF),
+        out_shape=jax.ShapeDtypeStruct((keep, width), kind),
         compiler_params=PARAMS,
         cost_estimate=pl.CostEstimate(
             flops=2 * rows * width * own, bytes_accessed=2 * rows * (width + own), transcendentals=0
         ),
-    )(*hidden, *grad_mixed)
+    )(*hidden, *grad_mixed, *base)
 
 
 def gate_terms_kernel(*refs):
@@ -772,7 +775,9 @@
     )
 
     half = row_count // 2
-    from_x, from_y = swap(normed_mlp, "x"), swap(normed_mlp, "y")
+    from_x, from_y, down = lax.optimization_barrier(
+        (swap(normed_mlp, "x"), swap(normed_mlp, "y"), down)
+    )
     normed_far = jnp.concatenate([swap(from_x[:half], "y"), swap(from_y[half:], "x")])
     normed_near = jnp.concatenate([from_x, from_y])
     normed_all = [with_core(part) for part in (normed_mlp, normed_near, normed_far)]
@@ -791,13 +796,15 @@
     grad_own = with_core(grad_mixed)
     own_grads = mlp_backward(grad_own, own_result[1], own_result[2], gate_up, down, down)
     from_x, from_y = lax.optimization_barrier((from_x, from_y, own_grads[1]))[:2]
-    grad_far = with_core(jnp.concatenate([swap(from_x[:half], "y"), swap(from_y[half:], "x")]))
     grad_near = with_core(jnp.concatenate([from_x, from_y]))
-    grad_down_terms = down_terms(
-        [r[0] for r in (own_result, near_result, far_result)],
-        [grad_own, grad_near, grad_far],
-        hidden_own,
-    )
+    near_terms = down_terms(
+        [own_result[0], near_result[0]], [grad_own, grad_near], [], hidden_pad, F32
+    )
+    grad_far = lax.optimization_barrier(
+        (swap(from_x[:half], "y"), swap(from_y[half:], "x"), near_terms)
+    )
+    grad_far = with_core(jnp.concatenate(grad_far[:2]))
+    grad_down_terms = down_terms([far_result[0]], [grad_far], [near_terms], hidden_own, BF)
     grad_down = group_terms(grad_down_terms.reshape(groups, -1, width))
     far_grads = mlp_backward(
         grad_far, far_result[1], far_result[2], gate_up, down, grad_down_terms

time: 559 us -> 553 us (0.989)
  waiting for transfers between devices: 161 us -> 150 us
  Pallas kernels: 198 us -> 204 us
    ppermute x50, waiting for transfers between devices: 127 us -> 118 us  [swap(): return lax.ppermute(array, axis, [(0, 1), (1, 0)])]
    pallas_call x1 -> x2, Pallas kernels: 16.4 us -> 22 us  [down_terms(): pl.pallas_call(functools.partial(down_terms_kernel, len(hidden)), grid=(o...]
    unnamed x74 -> x72, local copies, waits for them, and re-layouts: 13.6 us -> 13.7 us
  transfers between devices with their start and end apart: 66 -> 66, of which waited for: 30 -> 31; matrix products, arithmetic and copies ran while one was open for 15% -> 15% of each run, Pallas kernels for 30% -> 33%
where the time goes in v12:
time: 553 us; the launch traced here: 545 us
  Pallas kernels  204 us (37%)
  waiting for transfers between devices  150 us (27%)
  starting transfers between devices  69.5 us (13%)
  local copies, waits for them, and re-layouts  61.7 us (11%)
  other arithmetic  42.6 us (8%)
  between operations  15.1 us (3%)
    ppermute x50, waiting for transfers between devices, swap(): return lax.ppermute(array, axis, [(0, 1), (1, 0)])  118 us
    pallas_call x3, Pallas kernels, mlp_backward(): pl.pallas_call(mlp_backward_kernel, grid=(rows // TILE,), in_specs=[row_b...  49 us
    pallas_call x3, Pallas kernels, mlp_forward(): pl.pallas_call(mlp_forward_kernel, grid=(rows // TILE,), in_specs=[row_bl...  48.2 us
    ppermute x50, starting transfers between devices, swap(): return lax.ppermute(array, axis, [(0, 1), (1, 0)])  37 us
    pallas_call x1, Pallas kernels, gate_terms(): pl.pallas_call(gate_terms_kernel, grid=(both // 256,), in_specs=[whole_bl...  24.4 us
    pallas_call x2, Pallas kernels, down_terms(): pl.pallas_call(functools.partial(down_terms_kernel, len(hidden)), grid=(o...  22 us
    pallas_call x1, Pallas kernels, attend_backward(): pl.pallas_call(functools.partial(attend_backward_kernel, scale), in_specs...  17.1 us
    pallas_call x1, Pallas kernels, project_backward(): pl.pallas_call(functools.partial(project_backward_kernel, shard_rows), in...  15.2 us
  transfers between devices with their start and end apart: 66, of which 31 were waited for; matrix products, arithmetic and copies ran while one was open for 15% of the time, Pallas kernels for 33%

profile of v12, /device:TPU:13, one launch (start us, length us, event | category | flops | bytes accessed | tf_op | source)
XLA Modules:
  0.0 545.1 jit_solution(18099398196847410725)
XLA Ops:
  28.2 8.9 %all-to-all-start = ((bf16[8,36,1792]{2,1,0:T(8,128)(2,1)}), bf16[8,36,1792]{2,1,0:T(8,128)(2,1)S(1)}, u32[]{:S(2)}, u32[]{:S(2)}) async-start(bf16[8,36,1792]{2,1,0:T(8,128)(2,1)} %copy.71), calls=%async_computation | async-start | bytes 2293760 | tf_op jit(solution)/shard_map/all_to_all | solution.py:740
  39.6 9.3 %collective-permute-done.4 = bf16[72,896]{1,0:T(8,128)(2,1)S(1)} collective-permute-done((bf16[72,896]{1,0:T(8,128)(2,1)S(1)}, bf16[72,896]{1,0:T(8,128)(2,1)S(1)}, u32[]{:S(2)}, u32[]{:S(2)}) %collective-permute-start.4) | collective-permute-done | bytes 129056 | tf_op jit(solution)/shard_map/ppermute | solution.py:245
  62.0 10.0 %collective-permute-done.8 = bf16[2,2,72,896]{3,2,1,0:T(8,128)(2,1)S(1)} collective-permute-done((bf16[2,2,72,896]{3,2,1,0:T(8,128)(2,1)S(1)}, bf16[2,2,72,896]{3,2,1,0:T(8,128)(2,1)S(1)}, u32[]{:S(2)}, u32[]{:S(2)}) %collective-permute-start.8) | collective-permute-done | bytes 516128 | tf_op jit(solution)/shard_map/ppermute | solution.py:51
  83.1 8.7 %shard_map.271 = (bf16[512,1152]{1,0:T(8,128)(2,1)}, bf16[512,1152]{1,0:T(8,128)(2,1)}, f32[512,1024]{1,0:T(8,128)}, f32[1024,256]{1,0:T(8,128)}, bf16[512,1024]...) custom-call(s32[1]{0:T(128)} %bitcast.core, ...), custom_call_target="tpu_custom_call" | custom-call | flops 2415919104 | bytes 9437184 | tf_op jit(solution)/shard_map/pallas_call | solution.py:373
  108.1 9.9 %shard_map.272 = (bf16[512,1024]{1,0:T(8,128)(2,1)}, f32[512,128]{1,0:T(8,128)}, f32[512,1152]{1,0:T(8,128)}, f32[512,1152]{1,0:T(8,128)}, bf16[512,1152]{1,0:T(8,128)(2,1)}) custom-call(bf16[512,1024]{1,0:T(8,128)(2,1)} %get-tuple-element.87.queries, bf16[1024,256]{1,0:T(8,128)(2,1)} %get-tuple-element.88.keys, bf16[1024,256]{1,0:T(8,128)(2,1)} %get-tuple-element.89.values, ...), custom_call_target="tpu_custom_call" | custom-call | flops 3355443200 | bytes 11796480 | tf_op jit(solution)/shard_map/pallas_call | solution.py:439
  122.5 22.9 %collective-permute-done.16 = bf16[512,1152]{1,0:T(8,128)(2,1)S(1)} collective-permute-done((bf16[512,1152]{1,0:T(8,128)(2,1)}, bf16[512,1152]{1,0:T(8,128)(2,1)S(1)}, u32[]{:S(2)}, u32[]{:S(2)}) %collective-permute-start.16) | collective-permute-done | bytes 1179680 | tf_op jit(solution)/shard_map/ppermute | solution.py:51
  148.4 11.5 %collective-permute-done.19 = bf16[256,1152]{1,0:T(8,128)(2,1)S(1)} collective-permute-done((bf16[256,1152]{1,0:T(8,128)(2,1)S(1)}, bf16[256,1152]{1,0:T(8,128)(2,1)S(1)}, u32[]{:S(2)}, u32[]{:S(2)}) %collective-permute-start.19) | collective-permute-done | bytes 589856 | tf_op jit(solution)/shard_map/ppermute | solution.py:51
  173.8 13.0 %shard_map.273 = (bf16[1024,896]{1,0:T(8,128)(2,1)}, bf16[1024,896]{1,0:T(8,128)(2,1)}, bf16[1024,896]{1,0:T(8,128)(2,1)}, bf16[1024,1152]{1,0:T(8,128)(2,1)}) custom-call(bf16[1024,1152]{1,0:T(8,128)(2,1)} %constant_dynamic-update-slice_fusion.5.normed._.refs_2_, bf16[1152,1792]{1,0:T(8,128)(2,1)} %bitcast.198, bf16[896,1152]{1,0:T(8,128)(2,1)} %pad.27.down._, ...), custom_call_target="tpu_custom_call" | custom-call | flops 6341787648 | bytes 10223616 | tf_op jit(solution)/shard_map/pallas_call | solution.py:88
  193.8 21.8 %shard_map.274 = (bf16[2048,896]{1,0:T(8,128)(2,1)}, bf16[2048,896]{1,0:T(8,128)(2,1)}, bf16[2048,896]{1,0:T(8,128)(2,1)}, bf16[2048,1152]{1,0:T(8,128)(2,1)}) custom-call(bf16[2048,1152]{1,0:T(8,128)(2,1)} %copy-done.23, bf16[1152,1792]{1,0:T(8,128)(2,1)} %bitcast.199, bf16[896,1152]{1,0:T(8,128)(2,1)} %pad.27.down._, bf16[512,1152]{1,0:T(8,128)(2,1)} %copy-done.4), custom_call_target="tpu_custom_call" | custom-call | flops 12683575296 | bytes 20447232 | tf_op jit(solution)/shard_map/pallas_call | solution.py:88
  229.6 13.5 %shard_map.275 = (bf16[1024,896]{1,0:T(8,128)(2,1)}, bf16[1024,896]{1,0:T(8,128)(2,1)}, bf16[1024,896]{1,0:T(8,128)(2,1)}, bf16[1024,1152]{1,0:T(8,128)(2,1)}) custom-call(bf16[1024,1152]{1,0:T(8,128)(2,1)} %copy-done.19, bf16[1152,1792]{1,0:T(8,128)(2,1)} %bitcast.200, bf16[896,1152]{1,0:T(8,128)(2,1)} %pad.27.down._, bf16[512,1152]{1,0:T(8,128)(2,1)} %copy-done.14), custom_call_target="tpu_custom_call" | custom-call | flops 6341787648 | bytes 10223616 | tf_op jit(solution)/shard_map/pallas_call | solution.py:88
  246.4 7.6 %collective-permute-done.28 = bf16[512,1152]{1,0:T(8,128)(2,1)S(1)} collective-permute-done((bf16[512,1152]{1,0:T(8,128)(2,1)S(1)}, bf16[512,1152]{1,0:T(8,128)(2,1)S(1)}, u32[]{:S(2)}, u32[]{:S(2)}) %collective-permute-start.28) | collective-permute-done | bytes 1179680 | tf_op jit(solution)/shard_map/ppermute | solution.py:51
  265.3 13.5 %shard_map.276 = (bf16[1024,1792]{1,0:T(8,128)(2,1)}, bf16[1024,1152]{1,0:T(8,128)(2,1)}) custom-call(bf16[1024,1152]{1,0:T(8,128)(2,1)} %pad_maximum_fusion.1.grad_mixed.refs_2_, bf16[1024,896]{1,0:T(8,128)(2,1)} %get-tuple-element.106.gelu, bf16[1024,896]{1,0:T(8,128)(2,1)} %get-tuple-element.107.slope, bf16[1152,1792]{1,0:T(8,128)(2,1)} %bitcast.201, ...), custom_call_target="tpu_custom_call" | custom-call | flops 6341787648 | bytes 12058624 | tf_op jit(solution)/shard_map/pallas_call | solution.py:121
  278.9 10.0 %collective-permute-done.31 = bf16[512,1152]{1,0:T(8,128)(2,1)S(1)} collective-permute-done((bf16[512,1152]{1,0:T(8,128)(2,1)S(1)}, bf16[512,1152]{1,0:T(8,128)(2,1)S(1)}, u32[]{:S(2)}, u32[]{:S(2)}) %collective-permute-start.31) | collective-permute-done | bytes 1179680 | tf_op jit(solution)/shard_map/ppermute | solution.py:51
  297.7 13.3 %shard_map.277.refs_2_ = f32[896,1152]{1,0:T(8,128)} custom-call(bf16[1024,896]{1,0:T(8,128)(2,1)} %get-tuple-element.113.refs_0_, bf16[2048,896]{1,0:T(8,128)(2,1)} %get-tuple-element.114.refs_1_, bf16[1024,1152]{1,0:T(8,128)(2,1)} %pad_maximum_fusion.1.grad_mixed.refs_2_, bf16[2048,1152]{1,0:T(8,128)(2,1)} %copy-done.24), custom_call_target="tpu_custom_call" | custom-call | flops 6341787648 | bytes 12582912 | tf_op jit(solution)/shard_map/pallas_call | solution.py:158
  315.7 8.7 %shard_map.278._ = bf16[864,1152]{1,0:T(8,128)(2,1)} custom-call(bf16[1024,896]{1,0:T(8,128)(2,1)} %get-tuple-element.119.refs_0_, bf16[1024,1152]{1,0:T(8,128)(2,1)} %copy-done.6, f32[896,1152]{1,0:T(8,128)} %shard_map.277.refs_2_), custom_call_target="tpu_custom_call" | custom-call | flops 2113929216 | bytes 4194304 | tf_op jit(solution)/shard_map/pallas_call | solution.py:158
  324.4 13.5 %shard_map.279 = (bf16[1024,1792]{1,0:T(8,128)(2,1)}, bf16[1024,1152]{1,0:T(8,128)(2,1)}) custom-call(bf16[1024,1152]{1,0:T(8,128)(2,1)} %copy-done.6, bf16[1024,896]{1,0:T(8,128)(2,1)} %get-tuple-element.117.gelu, bf16[1024,896]{1,0:T(8,128)(2,1)} %get-tuple-element.118.slope, bf16[1152,1792]{1,0:T(8,128)(2,1)} %bitcast.202, bf16[896,1152]{1,0:T(8,128)(2,1)} %pad.27.down._, ...), custom_call_target="tpu_custom_call" | custom-call | flops 6341787648 | bytes 12058624 | tf_op jit(solution)/shard_map/pallas_call | solution.py:121
  343.6 22.0 %shard_map.280 = (bf16[2048,1792]{1,0:T(8,128)(2,1)}, bf16[2048,1152]{1,0:T(8,128)(2,1)}) custom-call(bf16[2048,1152]{1,0:T(8,128)(2,1)} %copy-done.24, bf16[2048,896]{1,0:T(8,128)(2,1)} %get-tuple-element.111.gelu, bf16[2048,896]{1,0:T(8,128)(2,1)} %get-tuple-element.112.slope, bf16[1152,1792]{1,0:T(8,128)(2,1)} %bitcast.203, ...), custom_call_target="tpu_custom_call" | custom-call | flops 12683575296 | bytes 24117248 | tf_op jit(solution)/shard_map/pallas_call | solution.py:121
  384.6 24.4 %shard_map.281 = bf16[4,2,144,1792]{3,2,1,0:T(8,128)(2,1)} custom-call(bf16[1024,1152]{1,0:T(8,128)(2,1)} %copy-done.19, bf16[2048,1152]{1,0:T(8,128)(2,1)} %copy-done.23, bf16[1024,1152]{1,0:T(8,128)(2,1)} %constant_dynamic-update-slice_fusion.5.normed._.refs_2_, bf16[1024,1792]{1,0:T(8,128)(2,1)} %get-tuple-element.125.refs_3_, ...), custom_call_target="tpu_custom_call" | custom-call | flops 16911433728 | bytes 24117248 | tf_op jit(solution)/shard_map/pallas_call | solution.py:191
  414.7 17.1 %shard_map.282 = (f32[512,1152]{1,0:T(8,128)}, bf16[512,1152]{1,0:T(8,128)(2,1)}, f32[512,1024]{1,0:T(8,128)}, f32[1024,256]{1,0:T(8,128)}, f32[1024,256]{1,0:T(8,128)}, /*index=5*/f32[8,1152]{1,0:T(8,128)}) custom-call(f32[512,1152]{1,0:T(8,128)} %convert_add_fusion.3.grad_normed_mlp, bf16[512,1152]{1,0:T(8,128)(2,1)} %bitcast.194, ...), custom_call_target="tpu_custom_call" | custom-call | flops 6576668672 | bytes 17694720 | tf_op jit(solution)/shard_map/pallas_call | solution.py:509
  440.6 15.2 %shard_map.283 = (f32[512,1152]{1,0:T(8,128)}, bf16[512,512]{1,0:T(8,128)(2,1)}, bf16[1152,896]{1,0:T(8,128)(2,1)}, bf16[1152,896]{1,0:T(8,128)(2,1)}) custom-call(s32[1]{0:T(128)} %bitcast.core, f32[512,1024]{1,0:T(8,128)} %get-tuple-element.132.grad_queries, f32[1024,256]{1,0:T(8,128)} %get-tuple-element.133.grad_keys, ...), custom_call_target="tpu_custom_call" | custom-call | flops 4756340736 | bytes 17694720 | tf_op jit(solution)/shard_map/pallas_call | solution.py:598
  459.3 7.3 %collective-permute-done.50 = bf16[2,2,32,1152]{3,2,1,0:T(8,128)(2,1)S(1)} collective-permute-done((bf16[2,2,32,1152]{3,2,1,0:T(8,128)(2,1)}, bf16[2,2,32,1152]{3,2,1,0:T(8,128)(2,1)S(1)}, u32[]{:S(2)}, u32[]{:S(2)}) %collective-permute-start.50) | collective-permute-done | bytes 294944 | tf_op jit(solution)/shard_map/ppermute | solution.py:51
  472.6 11.1 %collective-permute-done.55 = bf16[2,2,72,896]{3,2,1,0:T(8,128)(2,1)S(1)} collective-permute-done((bf16[2,2,72,896]{3,2,1,0:T(8,128)(2,1)S(1)}, bf16[2,2,72,896]{3,2,1,0:T(8,128)(2,1)S(1)}, u32[]{:S(2)}, u32[]{:S(2)}) %collective-permute-start.55) | collective-permute-done | bytes 516128 | tf_op jit(solution)/shard_map/ppermute | solution.py:51
  514.1 8.9 %collective-permute-done.46.returned = bf16[512,512]{1,0:T(8,128)(2,1)S(1)} collective-permute-done((bf16[512,512]{1,0:T(8,128)(2,1)}, bf16[512,512]{1,0:T(8,128)(2,1)S(1)}, u32[]{:S(2)}, u32[]{:S(2)}) %collective-permute-start.46) | collective-permute-done | bytes 524320 | tf_op jit(solution)/shard_map/ppermute | solution.py:840
  523.8 6.5 %shard_map.284 = bf16[512,1152]{1,0:T(8,128)(2,1)} custom-call(s32[1]{0:T(128)} %bitcast.core, bf16[512,512]{1,0:T(8,128)(2,1)} %copy-done.22, f32[512,1152]{1,0:T(8,128)} %get-tuple-element.142.grad_normed, bf16[1152,896]{1,0:T(8,128)(2,1)} %bitcast.190, bf16[1152,896]{1,0:T(8,128)(2,1)} %collective-permute-done.9.other, bf16[512,1152]{1,0:T(8,128)(2,1)} %bitcast.218, ...), custom_call_target="tpu_custom_call" | custom-call | flops 603979776 | bytes 7077888 | tf_op jit(solution)/shard_map/pallas_call | solution.py:635
  (337 shorter events, 221.5 us)
Async XLA Ops:
  7.2 72.6 %all-gather.5.cloned.1.call-start = ((), (), s32[]{:S(2)}) async-start(), calls=%async_computation.4 | async-start | bytes 2856960 | tf_op jit(solution)/shard_map/all_gather | solution.py:746
  27.0 21.8 %collective-permute-start.4 = (bf16[72,896]{1,0:T(8,128)(2,1)S(1)}, bf16[72,896]{1,0:T(8,128)(2,1)S(1)}, u32[]{:S(2)}, u32[]{:S(2)}) collective-permute-start(bf16[72,896]{1,0:T(8,128)(2,1)S(1)} %reshape.143), channel_id=1, source_target_pairs={{12,0},{0,4},{4,8},{8,12},{13,1},{1,5},{5,9},{9,13},{14,2},{2,6},{... | collective-permute-start | bytes 387080 | tf_op jit(solution)/shard_map/ppermute | solution.py:245
  28.2 23.5 %all-to-all-start = ((bf16[8,36,1792]{2,1,0:T(8,128)(2,1)}), bf16[8,36,1792]{2,1,0:T(8,128)(2,1)S(1)}, u32[]{:S(2)}, u32[]{:S(2)}) async-start(bf16[8,36,1792]{2,1,0:T(8,128)(2,1)} %copy.71), calls=%async_computation | async-start | bytes 2293760 | tf_op jit(solution)/shard_map/all_to_all | solution.py:740
  37.1 131.2 %all-gather.7.cloned.1.call-start = ((), (), s32[]{:S(2)}) async-start(), calls=%async_computation.5 | async-start | bytes 5160960 | tf_op jit(solution)/shard_map/all_gather | solution.py:751
  79.2 413.2 %reduce-scatter.2.cloned.1.call-start = ((), (), s32[]{:S(2)}) async-start(), calls=%async_computation.3 | async-start | bytes 5160960 | tf_op jit(solution)/shard_map/reduce_scatter | solution.py:821
  117.9 27.4 %collective-permute-start.16 = (bf16[512,1152]{1,0:T(8,128)(2,1)}, bf16[512,1152]{1,0:T(8,128)(2,1)S(1)}, u32[]{:S(2)}, u32[]{:S(2)}) collective-permute-start(bf16[512,1152]{1,0:T(8,128)(2,1)} %get-tuple-element.95), channel_id=1, source_target_pairs={{0,16},{16,0},{1,17},{17,1},{2,18},{18,2},{3,19},{19,3},{4,20},{20... | collective-permute-start | bytes 3538952 | tf_op jit(solution)/shard_map/ppermute | solution.py:51
  119.2 27.2 %collective-permute-start.17 = (bf16[512,1152]{1,0:T(8,128)(2,1)}, bf16[512,1152]{1,0:T(8,128)(2,1)S(1)}, u32[]{:S(2)}, u32[]{:S(2)}) collective-permute-start(bf16[512,1152]{1,0:T(8,128)(2,1)} %get-tuple-element.95), channel_id=1, source_target_pairs={{0,2},{2,0},{1,3},{3,1},{4,6},{6,4},{5,7},{7,5},{8,10},{10,8},{9,1... | collective-permute-start | bytes 3538952 | tf_op jit(solution)/shard_map/ppermute | solution.py:51
  166.5 22.5 %collective-permute-start.18 = (bf16[1024,1152]{1,0:T(8,128)(2,1)}, bf16[1024,1152]{1,0:T(8,128)(2,1)}, u32[]{:S(2)}, u32[]{:S(2)}) collective-permute-start(bf16[1024,1152]{1,0:T(8,128)(2,1)} %pad_maximum_fusion), channel_id=1, source_target_pairs={{0,1},{1,0},{2,3},{3,2},{4,5},{5,4},{6,7},{7,6},{8,9},{9,8},{10,11... | collective-permute-start | bytes 7077896 | tf_op jit(solution)/shard_map/ppermute | solution.py:51
  193.4 22.1 %collective-permute-start.23 = (bf16[256,1152]{1,0:T(8,128)(2,1)S(1)}, bf16[256,1152]{1,0:T(8,128)(2,1)S(1)}, u32[]{:S(2)}, u32[]{:S(2)}) collective-permute-start(bf16[256,1152]{1,0:T(8,128)(2,1)S(1)} %get-tuple-element.189), channel_id=1, source_target_pairs={{0,2},{2,0},{1,3},{3,1},{4,6},{6,4},{5,7},{7,5},{8,10},{10,8},{9,1... | collective-permute-start | bytes 1769480 | tf_op jit(solution)/shard_map/ppermute | solution.py:51
  193.5 22.1 %collective-permute-start.24 = (bf16[256,1152]{1,0:T(8,128)(2,1)S(1)}, bf16[256,1152]{1,0:T(8,128)(2,1)S(1)}, u32[]{:S(2)}, u32[]{:S(2)}) collective-permute-start(bf16[256,1152]{1,0:T(8,128)(2,1)S(1)} %get-tuple-element.188), channel_id=1, source_target_pairs={{0,16},{16,0},{1,17},{17,1},{2,18},{18,2},{3,19},{19,3},{4,20},{20... | collective-permute-start | bytes 1769480 | tf_op jit(solution)/shard_map/ppermute | solution.py:51
  226.7 27.2 %collective-permute-start.28 = (bf16[512,1152]{1,0:T(8,128)(2,1)S(1)}, bf16[512,1152]{1,0:T(8,128)(2,1)S(1)}, u32[]{:S(2)}, u32[]{:S(2)}) collective-permute-start(bf16[512,1152]{1,0:T(8,128)(2,1)S(1)} %pad_maximum_fusion.7), channel_id=1, source_target_pairs={{0,2},{2,0},{1,3},{3,1},{4,6},{6,4},{5,7},{7,5},{8,10},{10,8},{9,1... | collective-permute-start | bytes 3538952 | tf_op jit(solution)/shard_map/ppermute | solution.py:51
  228.4 26.9 %collective-permute-start.27 = (bf16[512,1152]{1,0:T(8,128)(2,1)S(1)}, bf16[512,1152]{1,0:T(8,128)(2,1)S(1)}, u32[]{:S(2)}, u32[]{:S(2)}) collective-permute-start(bf16[512,1152]{1,0:T(8,128)(2,1)S(1)} %pad_maximum_fusion.6._), channel_id=1, source_target_pairs={{0,16},{16,0},{1,17},{17,1},{2,18},{18,2},{3,19},{19,3},{4,20},{20... | collective-permute-start | bytes 3538952 | tf_op jit(solution)/shard_map/ppermute | solution.py:51
  261.3 27.6 %collective-permute-start.31 = (bf16[512,1152]{1,0:T(8,128)(2,1)S(1)}, bf16[512,1152]{1,0:T(8,128)(2,1)S(1)}, u32[]{:S(2)}, u32[]{:S(2)}) collective-permute-start(bf16[512,1152]{1,0:T(8,128)(2,1)S(1)} %get-tuple-element.169), channel_id=1, source_target_pairs={{0,16},{16,0},{1,17},{17,1},{2,18},{18,2},{3,19},{19,3},{4,20},{20... | collective-permute-start | bytes 3538952 | tf_op jit(solution)/shard_map/ppermute | solution.py:51
  262.4 27.3 %collective-permute-start.32 = (bf16[512,1152]{1,0:T(8,128)(2,1)S(1)}, bf16[512,1152]{1,0:T(8,128)(2,1)S(1)}, u32[]{:S(2)}, u32[]{:S(2)}) collective-permute-start(bf16[512,1152]{1,0:T(8,128)(2,1)S(1)} %get-tuple-element.169), channel_id=1, source_target_pairs={{0,2},{2,0},{1,3},{3,1},{4,6},{6,4},{5,7},{7,5},{8,10},{10,8},{9,1... | collective-permute-start | bytes 3538952 | tf_op jit(solution)/shard_map/ppermute | solution.py:51
  342.7 22.9 %collective-permute-start.38 = (bf16[256,1152]{1,0:T(8,128)(2,1)S(1)}, bf16[256,1152]{1,0:T(8,128)(2,1)S(1)}, u32[]{:S(2)}, u32[]{:S(2)}) collective-permute-start(bf16[256,1152]{1,0:T(8,128)(2,1)S(1)} %get-tuple-element.187), channel_id=1, source_target_pairs={{0,2},{2,0},{1,3},{3,1},{4,6},{6,4},{5,7},{7,5},{8,10},{10,8},{9,1... | collective-permute-start | bytes 1769480 | tf_op jit(solution)/shard_map/ppermute | solution.py:51
  342.8 22.8 %collective-permute-start.39 = (bf16[256,1152]{1,0:T(8,128)(2,1)S(1)}, bf16[256,1152]{1,0:T(8,128)(2,1)S(1)}, u32[]{:S(2)}, u32[]{:S(2)}) collective-permute-start(bf16[256,1152]{1,0:T(8,128)(2,1)S(1)} %get-tuple-element.186), channel_id=1, source_target_pairs={{0,16},{16,0},{1,17},{17,1},{2,18},{18,2},{3,19},{19,3},{4,20},{20... | collective-permute-start | bytes 1769480 | tf_op jit(solution)/shard_map/ppermute | solution.py:51
  372.4 36.7 %collective-permute-start.30 = (bf16[512,1152]{1,0:T(8,128)(2,1)}, bf16[512,1152]{1,0:T(8,128)(2,1)S(1)}, u32[]{:S(2)}, u32[]{:S(2)}) collective-permute-start(bf16[512,1152]{1,0:T(8,128)(2,1)} %slice.208), channel_id=1, source_target_pairs={{0,1},{1,0},{2,3},{3,2},{4,5},{5,4},{6,7},{7,6},{8,9},{9,8},{10,11... | collective-permute-start | bytes 3538952 | tf_op jit(solution)/shard_map/ppermute | solution.py:51
  373.7 64.4 %collective-permute-start.45 = (bf16[216,1152]{1,0:T(8,128)(2,1)}, bf16[216,1152]{1,0:T(8,128)(2,1)}, u32[]{:S(2)}, u32[]{:S(2)}) collective-permute-start(bf16[216,1152]{1,0:T(8,128)(2,1)} %get-tuple-element.182), channel_id=1, source_target_pairs={{0,12},{4,0},{8,4},{12,8},{1,13},{5,1},{9,5},{13,9},{2,14},{6,2},{... | collective-permute-start | bytes 1493000 | tf_op jit(solution)/shard_map/ppermute | solution.py:276
  374.2 63.8 %collective-permute-start.44 = (bf16[216,1152]{1,0:T(8,128)(2,1)}, bf16[216,1152]{1,0:T(8,128)(2,1)}, u32[]{:S(2)}, u32[]{:S(2)}) collective-permute-start(bf16[216,1152]{1,0:T(8,128)(2,1)} %get-tuple-element.183), channel_id=1, source_target_pairs={{0,8},{4,12},{8,0},{12,4},{1,9},{5,13},{9,1},{13,5},{2,10},{6,14},... | collective-permute-start | bytes 1493000 | tf_op jit(solution)/shard_map/ppermute | solution.py:276
  381.8 28.7 %collective-permute-start.42 = (bf16[512,1152]{1,0:T(8,128)(2,1)}, bf16[512,1152]{1,0:T(8,128)(2,1)}, u32[]{:S(2)}, u32[]{:S(2)}) collective-permute-start(bf16[512,1152]{1,0:T(8,128)(2,1)} %pad_maximum_fusion.10), channel_id=1, source_target_pairs={{0,2},{2,0},{1,3},{3,1},{4,6},{6,4},{5,7},{7,5},{8,10},{10,8},{9,1... | collective-permute-start | bytes 3538952 | tf_op jit(solution)/shard_map/ppermute | solution.py:51
  384.2 26.6 %collective-permute-start.41 = (bf16[512,1152]{1,0:T(8,128)(2,1)}, bf16[512,1152]{1,0:T(8,128)(2,1)}, u32[]{:S(2)}, u32[]{:S(2)}) collective-permute-start(bf16[512,1152]{1,0:T(8,128)(2,1)} %pad_maximum_fusion.9.refs_6_), channel_id=1, source_target_pairs={{0,16},{16,0},{1,17},{17,1},{2,18},{18,2},{3,19},{19,3},{4,20},{20... | collective-permute-start | bytes 3538952 | tf_op jit(solution)/shard_map/ppermute | solution.py:51
  409.0 29.0 %collective-permute-start.43 = (bf16[216,1152]{1,0:T(8,128)(2,1)}, bf16[216,1152]{1,0:T(8,128)(2,1)}, u32[]{:S(2)}, u32[]{:S(2)}) collective-permute-start(bf16[216,1152]{1,0:T(8,128)(2,1)} %get-tuple-element.181), channel_id=1, source_target_pairs={{0,4},{4,8},{8,12},{12,0},{1,5},{5,9},{9,13},{13,1},{2,6},{6,10},{... | collective-permute-start | bytes 1493000 | tf_op jit(solution)/shard_map/ppermute | solution.py:276
  495.9 27.1 %collective-permute-start.46 = (bf16[512,512]{1,0:T(8,128)(2,1)}, bf16[512,512]{1,0:T(8,128)(2,1)S(1)}, u32[]{:S(2)}, u32[]{:S(2)}) collective-permute-start(bf16[512,512]{1,0:T(8,128)(2,1)} %get-tuple-element.141), channel_id=1, source_target_pairs={{1,0},{2,1},{3,2},{4,3},{5,4},{6,5},{7,6},{8,7},{9,8},{10,9},{11,1... | collective-permute-start | bytes 1572872 | tf_op jit(solution)/shard_map/ppermute | solution.py:840
  503.7 30.8 %all-to-all-start.1 = ((bf16[8,36,1792]{2,1,0:T(8,128)(2,1)}), bf16[8,36,1792]{2,1,0:T(8,128)(2,1)S(1)}, u32[]{:S(2)}, u32[]{:S(2)}) async-start(bf16[8,36,1792]{2,1,0:T(8,128)(2,1)} %reshape.161), calls=%async_computation.2 | async-start | bytes 2293760 | tf_op jit(solution)/shard_map/all_to_all | solution.py:823
  (70 other events, 606.0 us)
Sparse Core Ops, SparseCore 0:
  17.2 55.7 all-gather.4
  79.3 76.2 all-gather.6
  409.2 83.2 reduce-scatter.1

commit v13 on v12

--- a/solution.py
+++ b/solution.py
@@ -63,6 +63,26 @@
 
 def row_block(rows, columns):
     return pl.BlockSpec((rows, columns), lambda i: (i, 0))
+
+
+def store_half(value, mine, other):
+    step, half = pl.program_id(0), pl.num_programs(0) // 2
+
+    @pl.when(step < half)
+    def _():
+        mine[...] = value
+
+    @pl.when(step >= half)
+    def _():
+        other[...] = value
+
+
+def half_blocks(rows, columns):
+    half = rows // TILE // 2
+    return [
+        pl.BlockSpec((TILE, columns), lambda i: (jnp.minimum(i, half - 1), 0)),
+        pl.BlockSpec((TILE, columns), lambda i: (jnp.maximum(i - half, 0), 0)),
+    ]
 
 
 def mlp_forward_kernel(normed, gate_up, down, _, hidden, gelu, slope, mixed):
@@ -103,16 +123,15 @@
     )(normed, gate_up, down, earlier)
 
 
-def mlp_backward_kernel(grad_mixed, gelu, slope, gate_up, down, _, grad_raw, grad_normed):
+def mlp_backward_kernel(grad_mixed, gelu, slope, gate_up, down, _, grad_raw, mine, other):
     own = down.shape[0]
     grad_hidden = by_transpose(grad_mixed[...], down[...])
     grad_gate = (grad_hidden * slope[...].astype(F32)).astype(BF)
     grad_up = (grad_hidden * gelu[...].astype(F32)).astype(BF)
     grad_raw[:, :own] = grad_gate
     grad_raw[:, own:] = grad_up
-    grad_normed[...] = (
-        by_transpose(grad_gate, gate_up[:, :own]) + by_transpose(grad_up, gate_up[:, own:])
-    ).astype(BF)
+    total = by_transpose(grad_gate, gate_up[:, :own]) + by_transpose(grad_up, gate_up[:, own:])
+    store_half(total.astype(BF), mine, other)
 
 
 def mlp_backward(grad_mixed, gelu, slope, gate_up, down, earlier):
@@ -129,10 +148,11 @@
             whole_block(down.shape),
             pl.BlockSpec(memory_space=pl.ANY),
         ],
-        out_specs=[row_block(TILE, 2 * own), row_block(TILE, width)],
+        out_specs=[row_block(TILE, 2 * own)] + half_blocks(rows, width),
         out_shape=[
             jax.ShapeDtypeStruct((rows, 2 * own), BF),
-            jax.ShapeDtypeStruct((rows, width), BF),
+            jax.ShapeDtypeStruct((rows // 2, width), BF),
+            jax.ShapeDtypeStruct((rows // 2, width), BF),
         ],
         compiler_params=PARAMS,
         cost_estimate=pl.CostEstimate(
@@ -211,9 +231,13 @@
     return jnp.concatenate([part, swap(part, "c")])
 
 
-def core_sum(part):
+def two_cores(part):
     half = part.shape[0] // 2
-    return part[:half].astype(F32) + swap(part[half:], "c").astype(F32)
+    return part[:half], part[half:]
+
+
+def core_sum(parts):
+    return parts[0].astype(F32) + swap(parts[1], "c").astype(F32)
 
 
 def send_far(far):
@@ -782,11 +806,11 @@
     normed_near = jnp.concatenate([from_x, from_y])
     normed_all = [with_core(part) for part in (normed_mlp, normed_near, normed_far)]
     far_result = mlp_forward(normed_all[2], gate_up, down, normed_all[2])
-    far_sum = core_sum(far_result[3]).astype(BF)
+    far_sum = core_sum(two_cores(far_result[3])).astype(BF)
     near_result = mlp_forward(normed_all[1], gate_up, down, far_sum)
-    to_x, to_y = sum_near(*lax.optimization_barrier((near_result[3], *send_far(far_sum))))
+    to_x, to_y = sum_near(*lax.optimization_barrier((two_cores(near_result[3]), *send_far(far_sum))))
     own_result = mlp_forward(normed_all[0], gate_up, down, to_x)
-    mixed = sum_own(own_result[3], to_x, to_y)
+    mixed = sum_own(two_cores(own_result[3]), to_x, to_y)
     layer_out = middle + norm_gain(mixed, d_gains[3:4])
 
     _, pullback = jax.vjp(norm_gain, mixed, d_gains[3:4])
@@ -809,13 +833,13 @@
     far_grads = mlp_backward(
         grad_far, far_result[1], far_result[2], gate_up, down, grad_down_terms
     )
-    far_sum = core_sum(far_grads[1]).astype(BF)
+    far_sum = core_sum(far_grads[1:]).astype(BF)
     near_grads = mlp_backward(grad_near, near_result[1], near_result[2], gate_up, down, far_sum)
-    to_x, to_y = sum_near(*lax.optimization_barrier((near_grads[1], *send_far(far_sum))))
+    to_x, to_y = sum_near(*lax.optimization_barrier((tuple(near_grads[1:]), *send_far(far_sum))))
     gate_up_terms = gate_terms(
         normed_all, [g[0] for g in (own_grads, near_grads, far_grads)], groups, to_x
     )
-    grad_normed_mlp = sum_own(own_grads[1], to_x, to_y)
+    grad_normed_mlp = sum_own(own_grads[1:], to_x, to_y)
     grad_normed_mlp = after(grad_normed_mlp, gate_up_terms)
     term = gate_up_terms.reshape(groups * members * shard_rows, 2 * hidden_pad)
     gate_up_share = lax.psum_scatter(term, "g", scatter_dimension=0, tiled=True)

time: 553 us -> 577 us (1.043)
  waiting for transfers between devices: 150 us -> 173 us
  local copies, waits for them, and re-layouts: 61.7 us -> 53 us
    ppermute x6, waiting for transfers between devices: 4.75 us -> 23.2 us  [group_terms(): total = total + lax.ppermute(chunk, 'g', pairs).astype(F32)]
    slice x6 -> x3, local copies, waits for them, and re-layouts: 12.6 us -> 5.7 us  [two_cores(): return (part[:half], part[half:])]
    ppermute x3, waiting for transfers between devices: 11.7 us -> 17.7 us  [group_gather(): lax.ppermute(own, 'g', [((i + k) % size, i) for i in range(size)])]
    unnamed x72 -> x62, local copies, waits for them, and re-layouts: 13.7 us -> 12.1 us
  transfers between devices with their start and end apart: 66 -> 66, of which waited for: 31 -> 30; matrix products, arithmetic and copies ran while one was open for 15% -> 14% of each run, Pallas kernels for 33% -> 32%
where the time goes in v13:
time: 577 us; the launch traced here: 569 us
  Pallas kernels  208 us (36%)
  waiting for transfers between devices  173 us (30%)
  starting transfers between devices  73.7 us (13%)
  local copies, waits for them, and re-layouts  53 us (9%)
  other arithmetic  43.2 us (7%)
  between operations  15 us (3%)
    ppermute x50, waiting for transfers between devices, swap(): return lax.ppermute(array, axis, [(0, 1), (1, 0)])  118 us
    pallas_call x3, Pallas kernels, mlp_backward(): pl.pallas_call(mlp_backward_kernel, grid=(rows // TILE,), in_specs=[row_b...  53 us
    pallas_call x3, Pallas kernels, mlp_forward(): pl.pallas_call(mlp_forward_kernel, grid=(rows // TILE,), in_specs=[row_bl...  48.1 us
    ppermute x50, starting transfers between devices, swap(): return lax.ppermute(array, axis, [(0, 1), (1, 0)])  42.3 us
    pallas_call x1, Pallas kernels, gate_terms(): pl.pallas_call(gate_terms_kernel, grid=(both // 256,), in_specs=[whole_bl...  24.8 us
    ppermute x6, waiting for transfers between devices, group_terms(): total = total + lax.ppermute(chunk, 'g', pairs).astype(F32)  23.2 us
    pallas_call x2, Pallas kernels, down_terms(): pl.pallas_call(functools.partial(down_terms_kernel, len(hidden)), grid=(o...  22 us
    ppermute x3, waiting for transfers between devices, group_gather(): lax.ppermute(own, 'g', [((i + k) % size, i) for i in range(size)])  17.7 us
  transfers between devices with their start and end apart: 66, of which 30 were waited for; matrix products, arithmetic and copies ran while one was open for 14% of the time, Pallas kernels for 32%

profile of v13, /device:TPU:13, one launch (start us, length us, event | category | flops | bytes accessed | tf_op | source)
XLA Modules:
  0.0 569.0 jit_solution(599073008285099831)
XLA Ops:
  28.2 8.0 %all-to-all-start = ((bf16[8,36,1792]{2,1,0:T(8,128)(2,1)}), bf16[8,36,1792]{2,1,0:T(8,128)(2,1)S(1)}, u32[]{:S(2)}, u32[]{:S(2)}) async-start(bf16[8,36,1792]{2,1,0:T(8,128)(2,1)} %copy.71), calls=%async_computation | async-start | bytes 2293760 | tf_op jit(solution)/shard_map/all_to_all | solution.py:764
  36.2 17.7 %collective-permute-done.2 = bf16[72,896]{1,0:T(8,128)(2,1)S(1)} collective-permute-done((bf16[72,896]{1,0:T(8,128)(2,1)S(1)}, bf16[72,896]{1,0:T(8,128)(2,1)S(1)}, u32[]{:S(2)}, u32[]{:S(2)}) %collective-permute-start.2) | collective-permute-done | bytes 129056 | tf_op jit(solution)/shard_map/ppermute | solution.py:269
  65.7 9.7 %collective-permute-done.6 = bf16[2,2,72,896]{3,2,1,0:T(8,128)(2,1)S(1)} collective-permute-done((bf16[2,2,72,896]{3,2,1,0:T(8,128)(2,1)S(1)}, bf16[2,2,72,896]{3,2,1,0:T(8,128)(2,1)S(1)}, u32[]{:S(2)}, u32[]{:S(2)}) %collective-permute-start.6) | collective-permute-done | bytes 516128 | tf_op jit(solution)/shard_map/ppermute | solution.py:51
  87.4 9.1 %shard_map.271 = (bf16[512,1152]{1,0:T(8,128)(2,1)}, bf16[512,1152]{1,0:T(8,128)(2,1)}, f32[512,1024]{1,0:T(8,128)}, f32[1024,256]{1,0:T(8,128)}, bf16[512,1024]...) custom-call(s32[1]{0:T(128)} %bitcast.core, ...), custom_call_target="tpu_custom_call" | custom-call | flops 2415919104 | bytes 9437184 | tf_op jit(solution)/shard_map/pallas_call | solution.py:397
  112.2 9.9 %shard_map.272 = (bf16[512,1024]{1,0:T(8,128)(2,1)}, f32[512,128]{1,0:T(8,128)}, f32[512,1152]{1,0:T(8,128)}, f32[512,1152]{1,0:T(8,128)}, bf16[512,1152]{1,0:T(8,128)(2,1)}) custom-call(bf16[512,1024]{1,0:T(8,128)(2,1)} %get-tuple-element.92.queries, bf16[1024,256]{1,0:T(8,128)(2,1)} %get-tuple-element.93.keys, bf16[1024,256]{1,0:T(8,128)(2,1)} %get-tuple-element.94.values, ...), custom_call_target="tpu_custom_call" | custom-call | flops 3355443200 | bytes 11796480 | tf_op jit(solution)/shard_map/pallas_call | solution.py:463
  125.6 24.0 %collective-permute-done.17 = bf16[512,1152]{1,0:T(8,128)(2,1)S(1)} collective-permute-done((bf16[512,1152]{1,0:T(8,128)(2,1)}, bf16[512,1152]{1,0:T(8,128)(2,1)S(1)}, u32[]{:S(2)}, u32[]{:S(2)}) %collective-permute-start.17) | collective-permute-done | bytes 1179680 | tf_op jit(solution)/shard_map/ppermute | solution.py:51
  152.3 11.1 %collective-permute-done.20 = bf16[256,1152]{1,0:T(8,128)(2,1)S(1)} collective-permute-done((bf16[256,1152]{1,0:T(8,128)(2,1)S(1)}, bf16[256,1152]{1,0:T(8,128)(2,1)S(1)}, u32[]{:S(2)}, u32[]{:S(2)}) %collective-permute-start.20) | collective-permute-done | bytes 589856 | tf_op jit(solution)/shard_map/ppermute | solution.py:51
  176.9 12.9 %shard_map.273 = (bf16[1024,896]{1,0:T(8,128)(2,1)}, bf16[1024,896]{1,0:T(8,128)(2,1)}, bf16[1024,896]{1,0:T(8,128)(2,1)}, bf16[1024,1152]{1,0:T(8,128)(2,1)}) custom-call(bf16[1024,1152]{1,0:T(8,128)(2,1)} %constant_dynamic-update-slice_fusion.5.normed._.refs_2_, bf16[1152,1792]{1,0:T(8,128)(2,1)} %bitcast.196, bf16[896,1152]{1,0:T(8,128)(2,1)} %pad.27.down._, ...), custom_call_target="tpu_custom_call" | custom-call | flops 6341787648 | bytes 10223616 | tf_op jit(solution)/shard_map/pallas_call | solution.py:108
  197.7 21.8 %shard_map.274 = (bf16[2048,896]{1,0:T(8,128)(2,1)}, bf16[2048,896]{1,0:T(8,128)(2,1)}, bf16[2048,896]{1,0:T(8,128)(2,1)}, bf16[2048,1152]{1,0:T(8,128)(2,1)}) custom-call(bf16[2048,1152]{1,0:T(8,128)(2,1)} %copy-done.20, bf16[1152,1792]{1,0:T(8,128)(2,1)} %bitcast.197, bf16[896,1152]{1,0:T(8,128)(2,1)} %pad.27.down._, bf16[512,1152]{1,0:T(8,128)(2,1)} %copy-done.4), custom_call_target="tpu_custom_call" | custom-call | flops 12683575296 | bytes 20447232 | tf_op jit(solution)/shard_map/pallas_call | solution.py:108
  233.4 13.4 %shard_map.275 = (bf16[1024,896]{1,0:T(8,128)(2,1)}, bf16[1024,896]{1,0:T(8,128)(2,1)}, bf16[1024,896]{1,0:T(8,128)(2,1)}, bf16[1024,1152]{1,0:T(8,128)(2,1)}) custom-call(bf16[1024,1152]{1,0:T(8,128)(2,1)} %copy-done.16, bf16[1152,1792]{1,0:T(8,128)(2,1)} %bitcast.198, bf16[896,1152]{1,0:T(8,128)(2,1)} %pad.27.down._, bf16[512,1152]{1,0:T(8,128)(2,1)} %copy-done.15), custom_call_target="tpu_custom_call" | custom-call | flops 6341787648 | bytes 10223616 | tf_op jit(solution)/shard_map/pallas_call | solution.py:108
  250.1 8.6 %collective-permute-done.28 = bf16[512,1152]{1,0:T(8,128)(2,1)S(1)} collective-permute-done((bf16[512,1152]{1,0:T(8,128)(2,1)S(1)}, bf16[512,1152]{1,0:T(8,128)(2,1)S(1)}, u32[]{:S(2)}, u32[]{:S(2)}) %collective-permute-start.28) | collective-permute-done | bytes 1179680 | tf_op jit(solution)/shard_map/ppermute | solution.py:51
  269.1 14.7 %shard_map.276 = (bf16[1024,1792]{1,0:T(8,128)(2,1)}, bf16[512,1152]{1,0:T(8,128)(2,1)}, bf16[512,1152]{1,0:T(8,128)(2,1)}) custom-call(bf16[1024,1152]{1,0:T(8,128)(2,1)} %pad_maximum_fusion.1.grad_mixed.refs_2_, bf16[1024,896]{1,0:T(8,128)(2,1)} %get-tuple-element.112.gelu, bf16[1024,896]{1,0:T(8,128)(2,1)} %get-tuple-element.113.slope, ...), custom_call_target="tpu_custom_call" | custom-call | flops 6341787648 | bytes 12058624 | tf_op jit(solution)/shard_map/pallas_call | solution.py:140
  283.8 8.9 %collective-permute-done.32 = bf16[512,1152]{1,0:T(8,128)(2,1)S(1)} collective-permute-done((bf16[512,1152]{1,0:T(8,128)(2,1)S(1)}, bf16[512,1152]{1,0:T(8,128)(2,1)S(1)}, u32[]{:S(2)}, u32[]{:S(2)}) %collective-permute-start.32) | collective-permute-done | bytes 1179680 | tf_op jit(solution)/shard_map/ppermute | solution.py:51
  301.3 13.4 %shard_map.277.refs_2_ = f32[896,1152]{1,0:T(8,128)} custom-call(bf16[1024,896]{1,0:T(8,128)(2,1)} %get-tuple-element.120.refs_0_, bf16[2048,896]{1,0:T(8,128)(2,1)} %get-tuple-element.121.refs_1_, bf16[1024,1152]{1,0:T(8,128)(2,1)} %pad_maximum_fusion.1.grad_mixed.refs_2_, bf16[2048,1152]{1,0:T(8,128)(2,1)} %copy-done.21), custom_call_target="tpu_custom_call" | custom-call | flops 6341787648 | bytes 12582912 | tf_op jit(solution)/shard_map/pallas_call | solution.py:178
  319.3 8.7 %shard_map.278._ = bf16[864,1152]{1,0:T(8,128)(2,1)} custom-call(bf16[1024,896]{1,0:T(8,128)(2,1)} %get-tuple-element.126.refs_0_, bf16[1024,1152]{1,0:T(8,128)(2,1)} %copy-done.6, f32[896,1152]{1,0:T(8,128)} %shard_map.277.refs_2_), custom_call_target="tpu_custom_call" | custom-call | flops 2113929216 | bytes 4194304 | tf_op jit(solution)/shard_map/pallas_call | solution.py:178
  328.0 14.7 %shard_map.279 = (bf16[1024,1792]{1,0:T(8,128)(2,1)}, bf16[512,1152]{1,0:T(8,128)(2,1)}, bf16[512,1152]{1,0:T(8,128)(2,1)}) custom-call(bf16[1024,1152]{1,0:T(8,128)(2,1)} %copy-done.6, bf16[1024,896]{1,0:T(8,128)(2,1)} %get-tuple-element.124.gelu, bf16[1024,896]{1,0:T(8,128)(2,1)} %get-tuple-element.125.slope, bf16[1152,1792]{1,0:T(8,128)(2,1)} %bitcast.200, ...), custom_call_target="tpu_custom_call" | custom-call | flops 6341787648 | bytes 12058624 | tf_op jit(solution)/shard_map/pallas_call | solution.py:140
  349.2 23.6 %shard_map.280 = (bf16[2048,1792]{1,0:T(8,128)(2,1)}, bf16[1024,1152]{1,0:T(8,128)(2,1)}, bf16[1024,1152]{1,0:T(8,128)(2,1)}) custom-call(bf16[2048,1152]{1,0:T(8,128)(2,1)} %copy-done.21, bf16[2048,896]{1,0:T(8,128)(2,1)} %get-tuple-element.118.gelu, bf16[2048,896]{1,0:T(8,128)(2,1)} %get-tuple-element.119.slope, bf16[1152,1792]{1,0:T(8,128)(2,1)} %bitcast.201, ...), custom_call_target="tpu_custom_call" | custom-call | flops 12683575296 | bytes 24117248 | tf_op jit(solution)/shard_map/pallas_call | solution.py:140
  384.5 24.8 %shard_map.281 = bf16[4,2,144,1792]{3,2,1,0:T(8,128)(2,1)} custom-call(bf16[1024,1152]{1,0:T(8,128)(2,1)} %copy-done.16, bf16[2048,1152]{1,0:T(8,128)(2,1)} %copy-done.20, bf16[1024,1152]{1,0:T(8,128)(2,1)} %constant_dynamic-update-slice_fusion.5.normed._.refs_2_, bf16[1024,1792]{1,0:T(8,128)(2,1)} %get-tuple-element.135.refs_3_, ...), custom_call_target="tpu_custom_call" | custom-call | flops 16911433728 | bytes 24117248 | tf_op jit(solution)/shard_map/pallas_call | solution.py:211
  415.5 16.6 %shard_map.282 = (f32[512,1152]{1,0:T(8,128)}, bf16[512,1152]{1,0:T(8,128)(2,1)}, f32[512,1024]{1,0:T(8,128)}, f32[1024,256]{1,0:T(8,128)}, f32[1024,256]{1,0:T(8,128)}, /*index=5*/f32[8,1152]{1,0:T(8,128)}) custom-call(f32[512,1152]{1,0:T(8,128)} %convert_add_fusion.3.grad_normed_mlp, bf16[512,1152]{1,0:T(8,128)(2,1)} %bitcast.194, ...), custom_call_target="tpu_custom_call" | custom-call | flops 6576668672 | bytes 17694720 | tf_op jit(solution)/shard_map/pallas_call | solution.py:533
  438.1 22.3 %collective-permute-done.44 = bf16[216,1152]{1,0:T(8,128)(2,1)} collective-permute-done((bf16[216,1152]{1,0:T(8,128)(2,1)}, bf16[216,1152]{1,0:T(8,128)(2,1)}, u32[]{:S(2)}, u32[]{:S(2)}) %collective-permute-start.44) | collective-permute-done | bytes 497696 | tf_op jit(solution)/shard_map/ppermute | solution.py:300
  462.9 15.0 %shard_map.283 = (f32[512,1152]{1,0:T(8,128)}, bf16[512,512]{1,0:T(8,128)(2,1)}, bf16[1152,896]{1,0:T(8,128)(2,1)}, bf16[1152,896]{1,0:T(8,128)(2,1)}) custom-call(s32[1]{0:T(128)} %bitcast.core, f32[512,1024]{1,0:T(8,128)} %get-tuple-element.142.grad_queries, f32[1024,256]{1,0:T(8,128)} %get-tuple-element.143.grad_keys, ...), custom_call_target="tpu_custom_call" | custom-call | flops 4756340736 | bytes 17694720 | tf_op jit(solution)/shard_map/pallas_call | solution.py:622
  482.8 7.1 %collective-permute-done.50 = bf16[2,2,32,1152]{3,2,1,0:T(8,128)(2,1)S(1)} collective-permute-done((bf16[2,2,32,1152]{3,2,1,0:T(8,128)(2,1)}, bf16[2,2,32,1152]{3,2,1,0:T(8,128)(2,1)S(1)}, u32[]{:S(2)}, u32[]{:S(2)}) %collective-permute-start.50) | collective-permute-done | bytes 294944 | tf_op jit(solution)/shard_map/ppermute | solution.py:51
  495.9 11.3 %collective-permute-done.55 = bf16[2,2,72,896]{3,2,1,0:T(8,128)(2,1)S(1)} collective-permute-done((bf16[2,2,72,896]{3,2,1,0:T(8,128)(2,1)S(1)}, bf16[2,2,72,896]{3,2,1,0:T(8,128)(2,1)S(1)}, u32[]{:S(2)}, u32[]{:S(2)}) %collective-permute-start.55) | collective-permute-done | bytes 516128 | tf_op jit(solution)/shard_map/ppermute | solution.py:51
  535.1 11.7 %collective-permute-done.46.returned = bf16[512,512]{1,0:T(8,128)(2,1)S(1)} collective-permute-done((bf16[512,512]{1,0:T(8,128)(2,1)}, bf16[512,512]{1,0:T(8,128)(2,1)S(1)}, u32[]{:S(2)}, u32[]{:S(2)}) %collective-permute-start.46) | collective-permute-done | bytes 524320 | tf_op jit(solution)/shard_map/ppermute | solution.py:864
  (323 shorter events, 215.2 us)
Async XLA Ops:
  7.2 75.8 %all-gather.5.cloned.1.call-start = ((), (), s32[]{:S(2)}) async-start(), calls=%async_computation.4 | async-start | bytes 2856960 | tf_op jit(solution)/shard_map/all_gather | solution.py:770
  24.5 29.4 %collective-permute-start.4 = (bf16[72,896]{1,0:T(8,128)(2,1)S(1)}, bf16[72,896]{1,0:T(8,128)(2,1)S(1)}, u32[]{:S(2)}, u32[]{:S(2)}) collective-permute-start(bf16[72,896]{1,0:T(8,128)(2,1)S(1)} %reshape.143), channel_id=1, source_target_pairs={{12,0},{0,4},{4,8},{8,12},{13,1},{1,5},{5,9},{9,13},{14,2},{2,6},{... | collective-permute-start | bytes 387080 | tf_op jit(solution)/shard_map/ppermute | solution.py:269
  25.8 28.1 %collective-permute-start.3 = (bf16[72,896]{1,0:T(8,128)(2,1)S(1)}, bf16[72,896]{1,0:T(8,128)(2,1)S(1)}, u32[]{:S(2)}, u32[]{:S(2)}) collective-permute-start(bf16[72,896]{1,0:T(8,128)(2,1)S(1)} %reshape.143), channel_id=1, source_target_pairs={{8,0},{12,4},{0,8},{4,12},{9,1},{13,5},{1,9},{5,13},{10,2},{14,6},... | collective-permute-start | bytes 387080 | tf_op jit(solution)/shard_map/ppermute | solution.py:269
  26.8 27.1 %collective-permute-start.2 = (bf16[72,896]{1,0:T(8,128)(2,1)S(1)}, bf16[72,896]{1,0:T(8,128)(2,1)S(1)}, u32[]{:S(2)}, u32[]{:S(2)}) collective-permute-start(bf16[72,896]{1,0:T(8,128)(2,1)S(1)} %reshape.143), channel_id=1, source_target_pairs={{4,0},{8,4},{12,8},{0,12},{5,1},{9,5},{13,9},{1,13},{6,2},{10,6},{... | collective-permute-start | bytes 387080 | tf_op jit(solution)/shard_map/ppermute | solution.py:269
  28.2 25.9 %all-to-all-start = ((bf16[8,36,1792]{2,1,0:T(8,128)(2,1)}), bf16[8,36,1792]{2,1,0:T(8,128)(2,1)S(1)}, u32[]{:S(2)}, u32[]{:S(2)}) async-start(bf16[8,36,1792]{2,1,0:T(8,128)(2,1)} %copy.71), calls=%async_computation | async-start | bytes 2293760 | tf_op jit(solution)/shard_map/all_to_all | solution.py:764
  36.2 135.2 %all-gather.7.cloned.1.call-start = ((), (), s32[]{:S(2)}) async-start(), calls=%async_computation.5 | async-start | bytes 5160960 | tf_op jit(solution)/shard_map/all_gather | solution.py:775
  82.4 431.8 %reduce-scatter.2.cloned.1.call-start = ((), (), s32[]{:S(2)}) async-start(), calls=%async_computation.3 | async-start | bytes 5160960 | tf_op jit(solution)/shard_map/reduce_scatter | solution.py:845
  122.1 27.5 %collective-permute-start.17 = (bf16[512,1152]{1,0:T(8,128)(2,1)}, bf16[512,1152]{1,0:T(8,128)(2,1)S(1)}, u32[]{:S(2)}, u32[]{:S(2)}) collective-permute-start(bf16[512,1152]{1,0:T(8,128)(2,1)} %get-tuple-element.100), channel_id=1, source_target_pairs={{0,2},{2,0},{1,3},{3,1},{4,6},{6,4},{5,7},{7,5},{8,10},{10,8},{9,1... | collective-permute-start | bytes 3538952 | tf_op jit(solution)/shard_map/ppermute | solution.py:51
  122.6 27.2 %collective-permute-start.16 = (bf16[512,1152]{1,0:T(8,128)(2,1)}, bf16[512,1152]{1,0:T(8,128)(2,1)S(1)}, u32[]{:S(2)}, u32[]{:S(2)}) collective-permute-start(bf16[512,1152]{1,0:T(8,128)(2,1)} %get-tuple-element.100), channel_id=1, source_target_pairs={{0,16},{16,0},{1,17},{17,1},{2,18},{18,2},{3,19},{19,3},{4,20},{20... | collective-permute-start | bytes 3538952 | tf_op jit(solution)/shard_map/ppermute | solution.py:51
  196.5 25.8 %collective-permute-start.24 = (bf16[256,1152]{1,0:T(8,128)(2,1)S(1)}, bf16[256,1152]{1,0:T(8,128)(2,1)S(1)}, u32[]{:S(2)}, u32[]{:S(2)}) collective-permute-start(bf16[256,1152]{1,0:T(8,128)(2,1)S(1)} %get-tuple-element.200), channel_id=1, source_target_pairs={{0,16},{16,0},{1,17},{17,1},{2,18},{18,2},{3,19},{19,3},{4,20},{20... | collective-permute-start | bytes 1769480 | tf_op jit(solution)/shard_map/ppermute | solution.py:51
  196.8 25.6 %collective-permute-start.23 = (bf16[256,1152]{1,0:T(8,128)(2,1)S(1)}, bf16[256,1152]{1,0:T(8,128)(2,1)S(1)}, u32[]{:S(2)}, u32[]{:S(2)}) collective-permute-start(bf16[256,1152]{1,0:T(8,128)(2,1)S(1)} %get-tuple-element.201), channel_id=1, source_target_pairs={{0,2},{2,0},{1,3},{3,1},{4,6},{6,4},{5,7},{7,5},{8,10},{10,8},{9,1... | collective-permute-start | bytes 1769480 | tf_op jit(solution)/shard_map/ppermute | solution.py:51
  231.5 27.2 %collective-permute-start.28 = (bf16[512,1152]{1,0:T(8,128)(2,1)S(1)}, bf16[512,1152]{1,0:T(8,128)(2,1)S(1)}, u32[]{:S(2)}, u32[]{:S(2)}) collective-permute-start(bf16[512,1152]{1,0:T(8,128)(2,1)S(1)} %pad_maximum_fusion.7), channel_id=1, source_target_pairs={{0,2},{2,0},{1,3},{3,1},{4,6},{6,4},{5,7},{7,5},{8,10},{10,8},{9,1... | collective-permute-start | bytes 3538952 | tf_op jit(solution)/shard_map/ppermute | solution.py:51
  232.2 26.9 %collective-permute-start.27 = (bf16[512,1152]{1,0:T(8,128)(2,1)S(1)}, bf16[512,1152]{1,0:T(8,128)(2,1)S(1)}, u32[]{:S(2)}, u32[]{:S(2)}) collective-permute-start(bf16[512,1152]{1,0:T(8,128)(2,1)S(1)} %pad_maximum_fusion.6._), channel_id=1, source_target_pairs={{0,16},{16,0},{1,17},{17,1},{2,18},{18,2},{3,19},{19,3},{4,20},{20... | collective-permute-start | bytes 3538952 | tf_op jit(solution)/shard_map/ppermute | solution.py:51
  265.1 27.6 %collective-permute-start.32 = (bf16[512,1152]{1,0:T(8,128)(2,1)S(1)}, bf16[512,1152]{1,0:T(8,128)(2,1)S(1)}, u32[]{:S(2)}, u32[]{:S(2)}) collective-permute-start(bf16[512,1152]{1,0:T(8,128)(2,1)S(1)} %get-tuple-element.181), channel_id=1, source_target_pairs={{0,2},{2,0},{1,3},{3,1},{4,6},{6,4},{5,7},{7,5},{8,10},{10,8},{9,1... | collective-permute-start | bytes 3538952 | tf_op jit(solution)/shard_map/ppermute | solution.py:51
  266.0 27.3 %collective-permute-start.31 = (bf16[512,1152]{1,0:T(8,128)(2,1)S(1)}, bf16[512,1152]{1,0:T(8,128)(2,1)S(1)}, u32[]{:S(2)}, u32[]{:S(2)}) collective-permute-start(bf16[512,1152]{1,0:T(8,128)(2,1)S(1)} %get-tuple-element.181), channel_id=1, source_target_pairs={{0,16},{16,0},{1,17},{17,1},{2,18},{18,2},{3,19},{19,3},{4,20},{20... | collective-permute-start | bytes 3538952 | tf_op jit(solution)/shard_map/ppermute | solution.py:51
  373.8 35.5 %collective-permute-start.30 = (bf16[512,1152]{1,0:T(8,128)(2,1)}, bf16[512,1152]{1,0:T(8,128)(2,1)}, u32[]{:S(2)}, u32[]{:S(2)}) collective-permute-start(bf16[512,1152]{1,0:T(8,128)(2,1)} %get-tuple-element.115), channel_id=1, source_target_pairs={{0,1},{1,0},{2,3},{3,2},{4,5},{5,4},{6,7},{7,6},{8,9},{9,8},{10,11... | collective-permute-start | bytes 3538952 | tf_op jit(solution)/shard_map/ppermute | solution.py:51
  375.1 63.0 %collective-permute-start.43 = (bf16[216,1152]{1,0:T(8,128)(2,1)}, bf16[216,1152]{1,0:T(8,128)(2,1)}, u32[]{:S(2)}, u32[]{:S(2)}) collective-permute-start(bf16[216,1152]{1,0:T(8,128)(2,1)} %get-tuple-element.193), channel_id=1, source_target_pairs={{0,4},{4,8},{8,12},{12,0},{1,5},{5,9},{9,13},{13,1},{2,6},{6,10},{... | collective-permute-start | bytes 1493000 | tf_op jit(solution)/shard_map/ppermute | solution.py:300
  375.1 63.0 %collective-permute-start.45 = (bf16[216,1152]{1,0:T(8,128)(2,1)}, bf16[216,1152]{1,0:T(8,128)(2,1)}, u32[]{:S(2)}, u32[]{:S(2)}) collective-permute-start(bf16[216,1152]{1,0:T(8,128)(2,1)} %get-tuple-element.194), channel_id=1, source_target_pairs={{0,12},{4,0},{8,4},{12,8},{1,13},{5,1},{9,5},{13,9},{2,14},{6,2},{... | collective-permute-start | bytes 1493000 | tf_op jit(solution)/shard_map/ppermute | solution.py:300
  382.1 27.5 %collective-permute-start.42 = (bf16[512,1152]{1,0:T(8,128)(2,1)}, bf16[512,1152]{1,0:T(8,128)(2,1)}, u32[]{:S(2)}, u32[]{:S(2)}) collective-permute-start(bf16[512,1152]{1,0:T(8,128)(2,1)} %pad_maximum_fusion.10), channel_id=1, source_target_pairs={{0,2},{2,0},{1,3},{3,1},{4,6},{6,4},{5,7},{7,5},{8,10},{10,8},{9,1... | collective-permute-start | bytes 3538952 | tf_op jit(solution)/shard_map/ppermute | solution.py:51
  384.4 27.2 %collective-permute-start.41 = (bf16[512,1152]{1,0:T(8,128)(2,1)}, bf16[512,1152]{1,0:T(8,128)(2,1)}, u32[]{:S(2)}, u32[]{:S(2)}) collective-permute-start(bf16[512,1152]{1,0:T(8,128)(2,1)} %pad_maximum_fusion.9.refs_6_), channel_id=1, source_target_pairs={{0,16},{16,0},{1,17},{17,1},{2,18},{18,2},{3,19},{19,3},{4,20},{20... | collective-permute-start | bytes 3538952 | tf_op jit(solution)/shard_map/ppermute | solution.py:51
  409.3 51.1 %collective-permute-start.44 = (bf16[216,1152]{1,0:T(8,128)(2,1)}, bf16[216,1152]{1,0:T(8,128)(2,1)}, u32[]{:S(2)}, u32[]{:S(2)}) collective-permute-start(bf16[216,1152]{1,0:T(8,128)(2,1)} %get-tuple-element.195), channel_id=1, source_target_pairs={{0,8},{4,12},{8,0},{12,4},{1,9},{5,13},{9,1},{13,5},{2,10},{6,14},... | collective-permute-start | bytes 1493000 | tf_op jit(solution)/shard_map/ppermute | solution.py:300
  436.3 42.3 %collective-permute-start.47 = (bf16[2,4,2,32,1152]{4,3,1,0,2:T(8,128)(2,1)}, bf16[2,4,2,32,1152]{4,3,1,0,2:T(8,128)(2,1)}, u32[]{:S(2)}, u32[]{:S(2)}) collective-permute-start(bf16[2,4,2,32,1152]{4,3,1,0,2:T(8,128)(2,1)} %bitcast.182), channel_id=1, source_target_pairs={{0,1},{1,0},{2,3},{3,2},{4,5},{5,4},{6,7},{7,6},{8,9},{9,8},{10,11... | collective-permute-start | bytes 3538952 | tf_op jit(solution)/shard_map/ppermute | solution.py:51
  519.2 27.6 %collective-permute-start.46 = (bf16[512,512]{1,0:T(8,128)(2,1)}, bf16[512,512]{1,0:T(8,128)(2,1)S(1)}, u32[]{:S(2)}, u32[]{:S(2)}) collective-permute-start(bf16[512,512]{1,0:T(8,128)(2,1)} %get-tuple-element.151), channel_id=1, source_target_pairs={{1,0},{2,1},{3,2},{4,3},{5,4},{6,5},{7,6},{8,7},{9,8},{10,9},{11,1... | collective-permute-start | bytes 1572872 | tf_op jit(solution)/shard_map/ppermute | solution.py:864
  527.1 31.3 %all-to-all-start.1 = ((bf16[8,36,1792]{2,1,0:T(8,128)(2,1)}), bf16[8,36,1792]{2,1,0:T(8,128)(2,1)S(1)}, u32[]{:S(2)}, u32[]{:S(2)}) async-start(bf16[8,36,1792]{2,1,0:T(8,128)(2,1)} %reshape.161), calls=%async_computation.2 | async-start | bytes 2293760 | tf_op jit(solution)/shard_map/all_to_all | solution.py:847
  (65 other events, 616.2 us)
Sparse Core Ops, SparseCore 0:
  17.2 56.9 all-gather.4
  82.6 75.6 all-gather.6
  409.4 89.8 reduce-scatter.1
